TPU v7x, 32 devices: a whole 2x2x4 slice. The times are simulated.
32 devices in a mesh: groups: 2 (over x), tensor: 16 (over z, y, core).
Axes of the slice: x: 2, y: 2, z: 4, core: 2. Of those that a mesh axis runs over, the one named last changes fastest.
Arguments:
- tokens: bfloat16 [256, 8192], P('groups', 'tensor'), parts along dimension 0, may hold values from -6 to 6
- weight: bfloat16 [8192, 16384], P('tensor'), may hold values from -0.0625 to 0.0625
- generators: float32 [8, 8192, 32], P('groups', 'tensor'), parts along dimension 0, may hold values from -2 to 2
- orders: int32 [4, 32], replicated, may hold values from 0 to 31, each once within a row
- cotangent: bfloat16 [256, 16384], P('groups', 'tensor'), parts along dimension 0, may hold values from -1.5 to 1.5
Outputs:
- outputs: float32 [256, 16384], P('groups', 'tensor'), parts along dimension 0
- grad_tokens: float32 [256, 8192], P('groups', 'tensor'), parts along dimension 0
- grad_generators: float32 [8, 8192, 32], P('groups', 'tensor'), parts along dimension 0
There are 2 independent parts, one for each index of `groups`. A program takes and returns all parts, laid end to end along the dimension named above; an argument that names none is the same for every part. Nothing has to cross between parts.
Inputs may be any that keep to these rules, and one draw needn't show every extreme that they name: Each row of orders is a permutation of 0 to 31.
All inputs are finite; a program needn't handle non-finite values.
Results may differ from a plain program's by a relative error of at most 0.0003.
Values may be sent and summed in bfloat16 or wider, within the bound.
No kernel may reach another device: no remote copies, remote signals or barrier semaphores. Data moves between devices by JAX's collectives and lax.ppermute only.
A program may use at most 128 MiB of HBM per device.

v0:
```python
import jax
import jax.numpy as jnp
from jax import lax
from jax.sharding import PartitionSpec as P

HIGHEST = lax.Precision.HIGHEST


def partner(array, axis, apart):
    return lax.ppermute(array, axis, [(i, i ^ 1 << apart) for i in range(lax.axis_size(axis))])


def cayley_many(gen_blocks, orderings):
    block_size = gen_blocks.shape[-1]
    identity = jnp.eye(block_size, dtype=gen_blocks.dtype)
    skewed = gen_blocks - jnp.swapaxes(gen_blocks, 1, 2)
    shifted = identity + skewed
    numerator = jnp.einsum("bij,bjk->bik", shifted, shifted, precision=HIGHEST)
    metric = identity - jnp.einsum("bij,bjk->bik", skewed, skewed, precision=HIGHEST)
    factor = jnp.linalg.cholesky(metric)
    target = jnp.swapaxes(numerator, 1, 2)
    partly = lax.linalg.triangular_solve(factor, target, left_side=True, lower=True)
    solved = lax.linalg.triangular_solve(
        factor, partly, left_side=True, lower=True, transpose_a=True
    )
    rotation = jnp.swapaxes(solved, 1, 2)
    picker = (
        orderings[:, :, None] == jnp.arange(block_size, dtype=jnp.int32)[None, None, :]
    ).astype(rotation.dtype)
    return jnp.einsum("bim,bmn,bjn->bij", picker, rotation, picker, precision=HIGHEST)


def local_blocks(gen_rows, distance, half_rows):
    row_count, block_size = gen_rows.shape
    grouped = gen_rows.reshape(
        row_count // (2 * distance), 2, distance // half_rows, half_rows, block_size
    )
    return jnp.transpose(grouped, (0, 2, 1, 3, 4)).reshape(-1, 2 * half_rows, block_size)


def local_rows(grad_blocks, row_count, distance, half_rows):
    block_size = grad_blocks.shape[-1]
    grouped = grad_blocks.reshape(
        row_count // (2 * distance), distance // half_rows, 2, half_rows, block_size
    )
    return jnp.transpose(grouped, (0, 2, 1, 3, 4)).reshape(row_count, block_size)


def cols_apply(values, rotation, distance, half_rows):
    tok_count, row_count = values.shape
    bunches = row_count // (2 * distance)
    spread = distance // half_rows
    grouped = values.reshape(tok_count, bunches, 2, spread, half_rows)
    shaped = rotation.reshape(bunches, spread, 2, half_rows, 2, half_rows)
    moved = jnp.einsum("tgasb,gsabcd->tgcsd", grouped, shaped, precision=HIGHEST)
    return moved.reshape(tok_count, row_count)


def cols_back(before, grad_after, rotation, distance, half_rows):
    tok_count, row_count = before.shape
    bunches = row_count // (2 * distance)
    spread = distance // half_rows
    grouped = before.reshape(tok_count, bunches, 2, spread, half_rows)
    grad_grouped = grad_after.reshape(tok_count, bunches, 2, spread, half_rows)
    shaped = rotation.reshape(bunches, spread, 2, half_rows, 2, half_rows)
    grad_rot = jnp.einsum("tgasb,tgcsd->gsabcd", grouped, grad_grouped, precision=HIGHEST)
    grad_before = jnp.einsum("tgcsd,gsabcd->tgasb", grad_grouped, shaped, precision=HIGHEST)
    return (grad_rot.reshape(rotation.shape), grad_before.reshape(tok_count, row_count))


def local(tokens, weight, generators, orders, cotangent):
    sections, row_count, block_size = generators.shape
    half_rows = block_size // 2
    blocks = row_count // half_rows
    tok_count = tokens.shape[0]
    pair_bit = lax.axis_size("tensor").bit_length() - 2
    is_low = jnp.bitwise_and(jnp.right_shift(lax.axis_index("tensor"), pair_bit), 1) == 0
    offset = jnp.where(is_low, 0, half_rows).astype(jnp.int32)

    def pair_up(own_part, other_part, along):
        first = jnp.where(is_low, own_part, other_part)
        second = jnp.where(is_low, other_part, own_part)
        return jnp.concatenate([first, second], axis=along)

    own_gen = generators[0]
    other_gen = partner(own_gen, "tensor", pair_bit)
    far_gen = pair_up(
        own_gen.reshape(blocks, half_rows, block_size),
        other_gen.reshape(blocks, half_rows, block_size),
        1,
    )
    every_gen = [far_gen]
    every_order = [jnp.broadcast_to(orders[0], (blocks, block_size))]
    starts = [0]
    counts = [blocks]
    for section in range(1, sections):
        distance = half_rows * 2 ** (section - 1)
        gen_blocks = local_blocks(generators[section], distance, half_rows)
        starts.append(starts[-1] + counts[-1])
        counts.append(gen_blocks.shape[0])
        every_gen.append(gen_blocks)
        every_order.append(jnp.broadcast_to(orders[section], (gen_blocks.shape[0], block_size)))
    all_gen = jnp.concatenate(every_gen, axis=0)
    all_order = jnp.concatenate(every_order, axis=0)

    def rotations_of(gen_blocks):
        return cayley_many(gen_blocks, all_order)

    all_rot, rot_pullback = jax.vjp(rotations_of, all_gen)
    far_rot = all_rot[0:blocks]
    near_rot = [
        all_rot[starts[section] : starts[section] + counts[section]]
        for section in range(1, sections)
    ]
    gathered = lax.all_gather(cotangent, "tensor", axis=1, tiled=True)
    grad_rots = [None] * sections
    current = tokens.astype(jnp.float32)
    inputs = [None] * sections
    for section in range(sections - 1, 0, -1):
        inputs[section] = current
        current = cols_apply(
            current, near_rot[section - 1], half_rows * 2 ** (section - 1), half_rows
        )
    other_cols = partner(current, "tensor", pair_bit)
    paired = pair_up(
        current.reshape(tok_count, blocks, half_rows),
        other_cols.reshape(tok_count, blocks, half_rows),
        2,
    )
    own_cols = lax.dynamic_slice_in_dim(far_rot, offset, half_rows, 2)
    rotated = jnp.einsum("tsj,sji->tsi", paired, own_cols, precision=HIGHEST).reshape(
        tok_count, row_count
    )
    partial_out = jnp.dot(rotated, weight, precision=HIGHEST)
    grad_cols = jnp.einsum("tc,rc->tr", gathered, weight, preferred_element_type=jnp.float32)
    other_grad = partner(grad_cols, "tensor", pair_bit)
    grad_paired = pair_up(
        grad_cols.reshape(tok_count, blocks, half_rows),
        other_grad.reshape(tok_count, blocks, half_rows),
        2,
    )
    grad_rots[0] = jnp.einsum("tsj,tsi->sji", paired, grad_paired, precision=HIGHEST)
    own_rows = lax.dynamic_slice_in_dim(far_rot, offset, half_rows, 1)
    current_grad = jnp.einsum("tsi,sji->tsj", grad_paired, own_rows, precision=HIGHEST).reshape(
        tok_count, row_count
    )
    for section in range(1, sections):
        distance = half_rows * 2 ** (section - 1)
        grad_rot, current_grad = cols_back(
            inputs[section], current_grad, near_rot[section - 1], distance, half_rows
        )
        grad_rots[section] = grad_rot
    all_grad_gen = rot_pullback(jnp.concatenate(grad_rots, axis=0))[0]
    grads = [None] * sections
    far_grad_gen = all_grad_gen[0:blocks]
    grads[0] = lax.dynamic_slice_in_dim(far_grad_gen, offset, half_rows, 1).reshape(
        row_count, block_size
    )
    for section in range(1, sections):
        distance = half_rows * 2 ** (section - 1)
        grad_blocks = all_grad_gen[starts[section] : starts[section] + counts[section]]
        grads[section] = local_rows(grad_blocks, row_count, distance, half_rows)
    outputs = lax.psum_scatter(partial_out, "tensor", scatter_dimension=1, tiled=True)
    return (outputs, current_grad, jnp.stack(grads))


def solution(mesh):
    placed = (
        P("groups", "tensor"),
        P("tensor", None),
        P("groups", "tensor", None),
        P(),
        P("groups", "tensor"),
    )
    return jax.shard_map(
        local,
        mesh=mesh,
        in_specs=placed,
        out_specs=(P("groups", "tensor"), P("groups", "tensor"), P("groups", "tensor", None)),
        check_vma=False,
    )
```

profile of v0, /device:TPU:8, one launch (start us, length us, event | category | flops | bytes accessed | tf_op | source)
XLA Modules:
  0.0 511.8 jit_solution(11508116756167954560)
XLA Ops:
  9.0 2.7 collective-permute-start
  15.1 12.2 %collective-permute-done = f32[512,32]{1,0:T(8,128)S(1)} collective-permute-done((f32[512,32]{1,0:T(8,128)S(1)}, f32[512,32]{1,0:T(8,128)S(1)}, u32[]{:S(2)}, u32[]{:S(2)}) %collective-permute-start) | collective-permute-done | bytes 65568 | tf_op jit(solution)/shard_map/ppermute | solution.py:10
  28.3 2.1 copy.390
  41.9 236.2 %custom-call.14 = f32[80,32,32]{2,1,0:T(8,128)} custom-call(f32[80,32,32]{2,1,0:T(8,128)} %copy.387), custom_call_target="Cholesky" | custom-call | tf_op jit(solution)/shard_map/jvp(jit(cholesky))/cholesky | solution.py:20
  282.3 12.5 %custom-call.22 = f32[80,1,32,32]{0,2,3,1:T(8,128)S(1)} custom-call(f32[80,1,32,32]{0,3,2,1:T(8,128)S(1)} %select_bitcast_fusion), custom_call_target="InvertDiagBlocksLowerTriangular" | custom-call | tf_op jit(solution)/shard_map/jvp()/triangular_solve/custom-call.0 | solution.py:23
  295.6 2.1 copy.392
  297.7 2.2 copy.393
  299.9 4.0 fusion.58
  312.0 2.1 reshape.132
  316.9 2.1 reshape.133
  318.9 2.1 convolution_bitcast_fusion.3
  322.8 4.2 collective-permute-start.1
  328.1 5.0 collective-permute-done.1
  335.4 12.7 %fusion.61 = f32[128,16384]{1,0:T(8,128)} fusion(f32[128,512]{0,1:T(8,128)S(1)} %bitcast.224, bf16[512,16384]{1,0:T(8,128)(2,1)} %param.10), kind=kOutput, calls=%fused_computation.106 | convolution fusion | flops 12884901888 | bytes 25427968 | tf_op jit(solution)/shard_map/dot_general | solution.py:134
  348.7 13.8 %fusion.62 = f32[128,512]{1,0:T(8,128)} fusion(bf16[128,16384]{1,0:T(8,128)(2,1)} %all-gather.2.cloned.1.call-done, bf16[512,16384]{1,0:T(8,128)(2,1)} %param.10), kind=kOutput, calls=%fused_computation.107 | convolution fusion | flops 2147483648 | bytes 21233664 | tf_op jit(solution)/shard_map/tc,rc->tr/dot_general | solution.py:135
  362.5 2.7 collective-permute-start.2
  367.3 3.2 copy.427
  370.5 13.8 %custom-call.26 = f32[80,1,32,32]{0,2,3,1:T(8,128)S(1)} custom-call(f32[80,1,32,32]{0,3,2,1:T(8,128)} %get-tuple-element.20), custom_call_target="InvertDiagBlocksLowerTriangular" | custom-call | tf_op jit(solution)/shard_map/transpose(jvp(jit(cholesky)))/triangular_solve/custom-call.0 | solution.py:20
  384.3 2.1 copy.432
  394.3 3.3 fusion.63
  398.6 2.1 reshape.142
  402.9 2.3 fusion.37
  406.3 2.1 reshape.143
  420.2 2.2 fusion.64
  422.5 2.5 fusion.65
  425.0 2.2 copy.423
  427.2 3.2 fusion.66
  430.4 2.2 fusion.67
  432.7 2.5 fusion.68
  435.2 2.8 copy.426
  438.0 2.1 fusion.21
  440.1 3.1 copy.428
  443.1 4.6 fusion.69
  450.9 3.1 copy.431
  454.0 4.0 fusion.70
  458.1 2.5 fusion.71
  460.6 2.8 copy.434
  463.4 3.0 copy.433
  467.9 2.8 fusion.74
  471.8 3.3 fusion.75
  475.1 2.4 copy.444
  477.5 4.7 fusion.76
  482.3 3.1 copy.447
  486.8 2.2 copy.437
  488.9 3.8 fusion.72
  492.8 2.9 copy.440
  495.7 3.3 fusion.73
  499.0 2.2 copy.441
  (178 shorter events, 75.8 us)
Async XLA Ops:
  7.2 5.8 %copy-start.38 = (bf16[128,512]{1,0:T(8,128)(2,1)S(1)}, bf16[128,512]{1,0:T(8,128)(2,1)}, u32[]{:S(2)}) copy-start(bf16[128,512]{1,0:T(8,128)(2,1)} %param.9) | copy-start | bytes 393220
  7.2 341.6 %all-gather.2.cloned.1.call-start = ((), (), s32[]{:S(2)}) async-start(), calls=%async_computation.2 | async-start | bytes 4456448 | tf_op jit(solution)/shard_map/all_gather | solution.py:115
  7.9 496.8 %reduce-scatter.2.cloned.1.call-start = ((), (), s32[]{:S(2)}) async-start(), calls=%async_computation.1 | async-start | bytes 8912896 | tf_op jit(solution)/shard_map/reduce_scatter | solution.py:163
  9.0 18.2 %collective-permute-start = (f32[512,32]{1,0:T(8,128)S(1)}, f32[512,32]{1,0:T(8,128)S(1)}, u32[]{:S(2)}, u32[]{:S(2)}) collective-permute-start(f32[512,32]{1,0:T(8,128)S(1)} %bitcast.229), channel_id=1, source_target_pairs={{0,8},{1,9},{2,10},{3,11},{4,12},{5,13},{6,14},{7,15},{8,0},{9,1},... | collective-permute-start | bytes 196616 | tf_op jit(solution)/shard_map/ppermute | solution.py:10
  13.0 295.4 %copy-start.33 = (s32[80,32]{1,0:T(8,128)}, s32[80,32]{1,0:T(8,128)S(1)}, u32[]{:S(2)}) copy-start(s32[80,32]{1,0:T(8,128)S(1)} %copy.394) | copy-start | bytes 30724
  281.3 0.8 copy-start.14
  294.8 0.8 copy-start.32
  299.9 4.0 copy-start
  305.4 1.5 copy-start.8
  306.9 1.5 copy-start.5
  310.1 1.1 copy-start.12
  318.9 2.1 copy-start.16
  321.1 1.7 copy-start.24
  322.8 10.3 %collective-permute-start.1 = (f32[128,512]{0,1:T(8,128)}, f32[128,512]{0,1:T(8,128)}, u32[]{:S(2)}, u32[]{:S(2)}) collective-permute-start(f32[128,512]{0,1:T(8,128)} %bitcast.38), channel_id=1, source_target_pairs={{0,8},{1,9},{2,10},{3,11},{4,12},{5,13},{6,14},{7,15},{8,0},{9,1},... | collective-permute-start | bytes 786440 | tf_op jit(solution)/shard_map/ppermute | solution.py:10
  328.1 6.1 %copy-start.18 = (f32[32,32,32]{2,1,0:T(8,128)}, f32[32,32,32]{2,1,0:T(8,128)S(1)}, u32[]{:S(2)}) copy-start(f32[32,32,32]{2,1,0:T(8,128)S(1)} %slice.80) | copy-start | bytes 393220
  334.2 1.2 copy-start.20
  334.2 1.2 copy-start.22
  362.5 23.9 %collective-permute-start.2 = (f32[128,512]{1,0:T(8,128)}, f32[128,512]{1,0:T(8,128)}, u32[]{:S(2)}, u32[]{:S(2)}) collective-permute-start(f32[128,512]{1,0:T(8,128)} %fusion.62), channel_id=1, source_target_pairs={{0,8},{1,9},{2,10},{3,11},{4,12},{5,13},{6,14},{7,15},{8,0},{9,1},... | collective-permute-start | bytes 786440 | tf_op jit(solution)/shard_map/ppermute | solution.py:10
  386.4 5.5 %copy-start.19 = (f32[32,32,32]{2,1,0:T(8,128)S(1)}, f32[32,32,32]{2,1,0:T(8,128)}, u32[]{:S(2)}) copy-start(f32[32,32,32]{2,1,0:T(8,128)} %copy-done.18) | copy-start | bytes 393220
  393.6 0.7 copy-start.27
  394.3 6.4 %copy-start.17 = (f32[16,2,16,2,16]{4,3,2,1,0:T(2,128)S(1)}, f32[16,2,16,2,16]{4,3,2,1,0:T(2,128)}, u32[]{:S(2)}) copy-start(f32[16,2,16,2,16]{4,3,2,1,0:T(2,128)} %reshape.132) | copy-start | bytes 196612
  402.2 0.7 copy-start.25
  402.9 5.4 %copy-start.15 = (f32[8,2,2,16,2,16]{5,4,3,2,1,0:T(2,128)S(1)}, f32[8,2,2,16,2,16]{5,4,3,2,1,0:T(2,128)}, u32[]{:S(2)}) copy-start(f32[8,2,2,16,2,16]{5,4,3,2,1,0:T(2,128)} %reshape.133) | copy-start | bytes 196612
  405.2 3.2 copy-start.26
  409.0 6.1 %copy-start.21 = (f32[128,32,16]{0,2,1:T(8,128)S(1)}, f32[128,32,16]{0,2,1:T(8,128)}, u32[]{:S(2)}) copy-start(f32[128,32,16]{0,2,1:T(8,128)} %copy-done.20) | copy-start | bytes 786436
  409.0 6.1 %copy-start.23 = (f32[128,32,16]{0,2,1:T(8,128)S(1)}, f32[128,32,16]{0,2,1:T(8,128)}, u32[]{:S(2)}) copy-start(f32[128,32,16]{0,2,1:T(8,128)} %copy-done.22) | copy-start | bytes 786436
  413.0 4.1 copy-start.34
  415.1 2.1 copy-start.35
  415.1 2.1 copy-start.36
  415.1 2.1 copy-start.37
  418.9 1.4 copy-start.6
  420.2 2.2 copy-start.7
  420.2 2.2 copy-start.1
  427.2 3.2 copy-start.9
  430.4 2.2 copy-start.10
  447.7 2.0 copy-start.39
  454.0 4.0 copy-start.4
  463.4 3.0 copy-start.13
  467.9 3.9 copy-start.3
  470.7 1.1 copy-start.11
  475.1 2.4 copy-start.2
  482.3 3.1 copy-start.28
  482.3 3.1 copy-start.29
  499.0 2.3 copy-start.30
  499.0 2.3 copy-start.31
Sparse Core Ops, SparseCore 0:
  10.2 54.1 all-gather.1
  348.3 106.2 reduce-scatter.1
where the time goes:
time: 520 us; the launch traced here: 512 us
  other arithmetic  276 us (53%)
  matrix products  103 us (20%)
  local copies, waits for them, and re-layouts  89.9 us (17%)
  waiting for transfers between devices  17.9 us (3%)
  between operations  15.1 us (3%)
  starting transfers between devices  9.62 us (2%)
    another operation x6, other arithmetic, cayley_many(): factor = jnp.linalg.cholesky(metric)  251 us
    ppermute x3, waiting for transfers between devices, partner(): lax.ppermute(array, axis, [(i, i ^ 1 << apart) for i in range(lax.axis_si...  17.2 us
    dot_general x1, matrix products, local(): jnp.einsum('tc,rc->tr', gathered, weight, preferred_element_type=jnp.floa...  13.8 us
    dot_general x1, matrix products, local(): partial_out = jnp.dot(rotated, weight, precision=HIGHEST)  12.7 us
    another operation x3, other arithmetic, cayley_many(): lax.linalg.triangular_solve(factor, partly, left_side=True, lower=True, t...  12.7 us
    dot_general x3, matrix products, cayley_many(): numerator = jnp.einsum('bij,bjk->bik', shifted, shifted, precision=HIGHEST)  12.1 us
  transfers between devices with their start and end apart: 5, of which 2 were waited for; matrix products, arithmetic and copies ran while one was open for 91% of the time, Pallas kernels for 0%

commit v1 on v0

v1 whole, which is shorter than its diff:
```python
import functools

import jax
import jax.numpy as jnp
import numpy as np
from jax import lax
from jax.experimental import pallas as pl
from jax.experimental.pallas import tpu as pltpu
from jax.sharding import PartitionSpec as P

HIGHEST = lax.Precision.HIGHEST
VMEM_LIMIT = 48 * 2**20
GROUP = 128
NN = (((1,), (0,)), ((), ()))
NT = (((1,), (1,)), ((), ()))
TN = (((0,), (0,)), ((), ()))
CHUNKS = 2


def exchange(array, bit):
    size = lax.axis_size("tensor")
    return lax.ppermute(array, "tensor", [(i, i ^ (1 << bit)) for i in range(size)])


def dot(a, b, dims=NN):
    return lax.dot_general(a, b, dims, precision=HIGHEST, preferred_element_type=jnp.float32)


def iota(shape, dim):
    return lax.broadcasted_iota(jnp.int32, shape, dim)


def split_halves(rows_ref, lo_ref, hi_ref, section, rows, half):
    step = half << (section - 1)
    base = section * rows
    for start in range(base, base + rows, 2 * step):
        low = rows_ref[start : start + step, :]
        high = rows_ref[start + step : start + 2 * step, :]
        lo_ref[start : start + step, :] = low
        lo_ref[start + step : start + 2 * step, :] = low
        hi_ref[start : start + step, :] = high
        hi_ref[start + step : start + 2 * step, :] = high


def to_lanes(lo_ref, hi_ref, out_ref, lanes, half, block):
    for a in range(half):
        out_ref[a * block : (a + 1) * block, :] = lo_ref[pl.ds(a, lanes, stride=half), :].T
        out_ref[(half + a) * block : (half + a + 1) * block, :] = hi_ref[
            pl.ds(a, lanes, stride=half), :
        ].T


def by_section(parts, section_of):
    out = parts[-1]
    for k in range(len(parts) - 2, -1, -1):
        out = jnp.where(section_of == k, parts[k], out)
    return out


def lane_facts(shape, per_section, high):
    lane = iota(shape, 1)
    section_of = lane // per_section
    part = lane % per_section
    upper = jnp.bitwise_and(jnp.right_shift(part, jnp.maximum(section_of - 1, 0)), 1)
    return section_of, jnp.where(section_of == 0, high, upper) == 1


def block_masks(section, half):
    row = iota((GROUP, GROUP), 0) // half
    col = iota((GROUP, GROUP), 1) // half
    bit = 1 << (section - 1)
    return col == jnp.bitwise_and(row, ~bit), col == jnp.bitwise_or(row, bit)


def same_mask(half):
    return iota((GROUP, GROUP), 0) // half == iota((GROUP, GROUP), 1) // half


def spreader(offset, block, half):
    return (iota((block, GROUP), 0) == offset + iota((block, GROUP), 1) % half).astype(jnp.float32)


def gatherer(offset, block, half):
    return (iota((GROUP, block), 1) == offset + iota((GROUP, block), 0) % half).astype(jnp.float32)


def rotate_kernel(
    orders_ref, high_ref, gen_ref, far_ref, tok_ref,
    inv_ref, near_ref, ffar_ref, bfar_ref, xs_ref,
    lo_ref, hi_ref, a_ref, b_ref, row_ref, rowt_ref,
):
    sections, block = orders_ref.shape
    half = block // 2
    rows = far_ref.shape[0]
    per_section = rows // half
    lanes = sections * per_section
    high = high_ref[0]
    own = gen_ref[0:rows, :]
    other = far_ref[...]
    lo_ref[0:rows, :] = jnp.where(high == 1, other, own)
    hi_ref[0:rows, :] = jnp.where(high == 1, own, other)
    for k in range(1, sections):
        split_halves(gen_ref, lo_ref, hi_ref, k, rows, half)
    to_lanes(lo_ref, hi_ref, a_ref, lanes, half, block)
    section_of, upper = lane_facts((block, lanes), per_section, high)

    def permute_rows(i, _):
        parts = [
            a_ref[pl.ds(pl.multiple_of(orders_ref[k, i] * block, block), block), :]
            for k in range(sections)
        ]
        b_ref[pl.ds(pl.multiple_of(i * block, block), block), :] = by_section(parts, section_of)
        return 0

    lax.fori_loop(0, block, permute_rows, 0, unroll=4)

    def permute_cols(j, _):
        parts = [
            b_ref[pl.ds(orders_ref[k, j], block, stride=block), :] for k in range(sections)
        ]
        a_ref[pl.ds(pl.multiple_of(j * block, block), block), :] = by_section(parts, section_of)
        return 0

    lax.fori_loop(0, block, permute_cols, 0, unroll=4)
    sub = iota((block, lanes), 0)
    for j in range(block):
        inv_ref[j * block : (j + 1) * block, :] = (
            a_ref[j * block : (j + 1) * block, :]
            - a_ref[pl.ds(j, block, stride=block), :]
            + (sub == j).astype(jnp.float32)
        )

    def eliminate(k, _):
        at = pl.multiple_of(k * block, block)
        here = sub == k
        inverse = 1.0 / inv_ref[pl.ds(at + k, 1), :]
        pivot = jnp.where(here, inverse, inv_ref[pl.ds(at, block), :] * inverse)
        for i in range(block):
            factor = inv_ref[pl.ds(i * block + k, 1), :]
            row = inv_ref[i * block : (i + 1) * block, :]
            inv_ref[i * block : (i + 1) * block, :] = jnp.where(here, 0.0, row) - factor * pivot
        inv_ref[pl.ds(at, block), :] = pivot
        return 0

    lax.fori_loop(0, block, eliminate, 0)

    for a in range(half):
        low = 2.0 * inv_ref[a * block : (a + 1) * block, :] - (sub == a).astype(jnp.float32)
        top = 2.0 * inv_ref[(half + a) * block : (half + a + 1) * block, :] - (
            sub == half + a
        ).astype(jnp.float32)
        row_ref[pl.ds(a, lanes, stride=half), :] = jnp.where(upper, top, low).T
        low = 2.0 * inv_ref[pl.ds(a, block, stride=block), :] - (sub == a).astype(jnp.float32)
        top = 2.0 * inv_ref[pl.ds(half + a, block, stride=block), :] - (sub == half + a).astype(
            jnp.float32
        )
        rowt_ref[pl.ds(a, lanes, stride=half), :] = jnp.where(upper, top, low).T
    spread_lo = spreader(0, block, half)
    spread_hi = spreader(half, block, half)
    spread_own = spreader(half * high, block, half)
    spread_oth = spreader(half * (1 - high), block, half)
    same = same_mask(half)
    for start in range(0, rows, GROUP):
        stop = start + GROUP
        part = rowt_ref[start:stop, :]
        ffar_ref[0, start:stop, :] = jnp.where(same, dot(part, spread_own), 0.0)
        ffar_ref[1, start:stop, :] = jnp.where(same, dot(part, spread_oth), 0.0)
        part = row_ref[start:stop, :]
        bfar_ref[0, start:stop, :] = jnp.where(same, dot(part, spread_own), 0.0)
        bfar_ref[1, start:stop, :] = jnp.where(same, dot(part, spread_oth), 0.0)
        value = tok_ref[:, start:stop].astype(jnp.float32)
        for k in range(sections - 1, 0, -1):
            lo_mask, hi_mask = block_masks(k, half)
            part = row_ref[k * rows + start : k * rows + stop, :]
            matrix = jnp.where(lo_mask, dot(part, spread_lo), 0.0) + jnp.where(
                hi_mask, dot(part, spread_hi), 0.0
            )
            near_ref[k - 1, start:stop, :] = matrix
            value = dot(value, matrix)
            xs_ref[k - 1, :, start:stop] = value


def far_kernel(own_ref, oth_ref, far_ref, out_ref):
    count, rows = own_ref.shape[1:]
    for start in range(0, rows, GROUP):
        stop = start + GROUP
        value = dot(own_ref[0, :, start:stop], far_ref[0, start:stop, :], NT) + dot(
            oth_ref[:, start:stop], far_ref[1, start:stop, :], NT
        )
        first = value.astype(jnp.bfloat16)
        out_ref[0:count, start:stop] = first
        out_ref[count : 2 * count, start:stop] = (value - first.astype(jnp.float32)).astype(
            jnp.bfloat16
        )


def project_kernel(places_ref, x_ref, w_ref, out_ref):
    count = out_ref.shape[1]
    both = jnp.dot(x_ref[...], w_ref[...], preferred_element_type=jnp.float32)
    out_ref[0] = both[:count] + both[count:]


def project(x_both, weight, places, chunk, chunks):
    pieces = places.shape[0]
    count2, rows = x_both.shape
    count = count2 // 2
    width = weight.shape[1] // lax.axis_size("tensor") // chunks
    return pl.pallas_call(
        project_kernel,
        out_shape=jax.ShapeDtypeStruct((pieces, count, width), jnp.float32),
        grid_spec=pltpu.PrefetchScalarGridSpec(
            num_scalar_prefetch=1,
            grid=(pieces,),
            in_specs=[
                pl.BlockSpec((count2, rows), lambda p, places: (0, 0)),
                pl.BlockSpec((rows, width), lambda p, places: (0, places[p] * chunks + chunk)),
            ],
            out_specs=pl.BlockSpec((1, count, width), lambda p, places: (p, 0, 0)),
        ),
        compiler_params=pltpu.CompilerParams(vmem_limit_bytes=VMEM_LIMIT),
        cost_estimate=pl.CostEstimate(
            flops=2 * count2 * rows * width * pieces,
            bytes_accessed=pieces * width * (2 * rows + 4 * count),
            transcendentals=0,
        ),
        name="project",
    )(places, x_both, weight)


def back_kernel(cot_ref, w_ref, out_ref):
    @pl.when(pl.program_id(0) == 0)
    def _():
        out_ref[...] = jnp.zeros_like(out_ref)

    out_ref[...] += lax.dot_general(
        cot_ref[0], w_ref[...], NT, preferred_element_type=jnp.float32
    )


def project_back(gathered, weight):
    pieces, count, width = gathered.shape
    rows = weight.shape[0]
    return pl.pallas_call(
        back_kernel,
        out_shape=jax.ShapeDtypeStruct((count, rows), jnp.float32),
        grid=(pieces,),
        in_specs=[
            pl.BlockSpec((1, count, width), lambda p: (p, 0, 0)),
            pl.BlockSpec((rows, width), lambda p: (0, p)),
        ],
        out_specs=pl.BlockSpec((count, rows), lambda p: (0, 0)),
        compiler_params=pltpu.CompilerParams(vmem_limit_bytes=VMEM_LIMIT),
        cost_estimate=pl.CostEstimate(
            flops=2 * count * rows * width * pieces,
            bytes_accessed=pieces * width * 2 * (rows + count),
            transcendentals=0,
        ),
        name="project_back",
    )(gathered, weight)


def lane_matmul(left_ref, right_ref, out_ref, block, lanes):
    step = 4

    def body(t, _):
        first = t * step
        totals = [jnp.zeros((block, lanes), jnp.float32) for _ in range(step)]
        for j in range(block):
            right = right_ref[j * block : (j + 1) * block, :]
            for s in range(step):
                totals[s] += left_ref[pl.ds((first + s) * block + j, 1), :] * right
        for s in range(step):
            out_ref[pl.ds(pl.multiple_of((first + s) * block, block), block), :] = totals[s]
        return 0

    lax.fori_loop(0, block // step, body, 0)


def grads_kernel(
    inverse_ref, high_ref, own_ref, oth_ref, x_oth_ref, tok_ref, xs_ref, near_ref, bfar_ref, inv_ref,
    gtok_ref, ggen_ref,
    row_ref, lo_ref, hi_ref, a_ref, b_ref, c_ref,
):
    sections, block = inverse_ref.shape
    half = block // 2
    count, rows = own_ref.shape
    per_section = rows // half
    lanes = sections * per_section
    high = high_ref[0]
    gather_lo = gatherer(0, block, half)
    gather_hi = gatherer(half, block, half)
    gather_own = gatherer(half * high, block, half)
    gather_oth = gatherer(half * (1 - high), block, half)
    same = same_mask(half)
    for start in range(0, rows, GROUP):
        stop = start + GROUP
        x_own = xs_ref[0, :, start:stop]
        x_oth = x_oth_ref[:, start:stop]
        g_own = own_ref[:, start:stop]
        g_oth = oth_ref[:, start:stop]

        def far_rows(x):
            return dot(jnp.where(same, dot(x, g_own, TN), 0.0), gather_own) + dot(
                jnp.where(same, dot(x, g_oth, TN), 0.0), gather_oth
            )

        mine, theirs = far_rows(x_own), far_rows(x_oth)
        lo_ref[start:stop, :] = jnp.where(high == 1, theirs, mine)
        hi_ref[start:stop, :] = jnp.where(high == 1, mine, theirs)
        grad = dot(g_own, bfar_ref[0, start:stop, :], NT) + dot(g_oth, bfar_ref[1, start:stop, :], NT)
        for k in range(1, sections):
            lo_mask, hi_mask = block_masks(k, half)
            if k < sections - 1:
                x = xs_ref[k, :, start:stop]
            else:
                x = tok_ref[:, start:stop].astype(jnp.float32)
            outer = dot(x, grad, TN)
            row_ref[k * rows + start : k * rows + stop, :] = dot(
                jnp.where(lo_mask, outer, 0.0), gather_lo
            ) + dot(jnp.where(hi_mask, outer, 0.0), gather_hi)
            grad = dot(grad, near_ref[k - 1, start:stop, :], NT)
        gtok_ref[:, start:stop] = grad
    for k in range(1, sections):
        split_halves(row_ref, lo_ref, hi_ref, k, rows, half)
    to_lanes(lo_ref, hi_ref, a_ref, lanes, half, block)
    for j in range(block):
        b_ref[j * block : (j + 1) * block, :] = inv_ref[pl.ds(j, block, stride=block), :]
    lane_matmul(a_ref, b_ref, c_ref, block, lanes)
    lane_matmul(b_ref, c_ref, a_ref, block, lanes)
    for j in range(block):
        c_ref[j * block : (j + 1) * block, :] = 2.0 * (
            a_ref[j * block : (j + 1) * block, :] - a_ref[pl.ds(j, block, stride=block), :]
        )
    section_of, upper = lane_facts((block, lanes), per_section, high)

    def permute_cols(j, _):
        parts = [
            c_ref[pl.ds(inverse_ref[k, j], block, stride=block), :] for k in range(sections)
        ]
        b_ref[pl.ds(pl.multiple_of(j * block, block), block), :] = by_section(parts, section_of)
        return 0

    lax.fori_loop(0, block, permute_cols, 0, unroll=4)
    for a in range(half):
        low, top = [
            by_section(
                [
                    b_ref[pl.ds(inverse_ref[k, at], block, stride=block), :]
                    for k in range(sections)
                ],
                section_of,
            )
            for at in (a, half + a)
        ]
        ggen_ref[pl.ds(a, lanes, stride=half), :] = jnp.where(upper, top, low).T


def local(tokens, weight, generators, orders, cotangent):
    sections, rows, block = generators.shape
    half = block // 2
    count = tokens.shape[0]
    size = lax.axis_size("tensor")
    bits = size.bit_length() - 1
    here = lax.axis_index("tensor")
    pair_bit = bits - 1
    high = jnp.bitwise_and(jnp.right_shift(here, pair_bit), 1).astype(jnp.int32).reshape(1)
    lanes = sections * (rows // half)
    f32 = jnp.float32
    full = pl.BlockSpec(memory_space=pltpu.VMEM)
    scalars = pl.BlockSpec(memory_space=pltpu.SMEM)
    params = pltpu.CompilerParams(vmem_limit_bytes=VMEM_LIMIT)

    far_gen = exchange(generators[0], pair_bit)
    gathered = lax.all_gather(cotangent, "tensor", axis=0, tiled=False)
    flat = generators.reshape(sections * rows, block)
    square = (block * block, lanes)
    inv, near, ffar, bfar, xs = pl.pallas_call(
        rotate_kernel,
        out_shape=(
            jax.ShapeDtypeStruct(square, f32),
            jax.ShapeDtypeStruct((sections - 1, rows, GROUP), f32),
            jax.ShapeDtypeStruct((2, rows, GROUP), f32),
            jax.ShapeDtypeStruct((2, rows, GROUP), f32),
            jax.ShapeDtypeStruct((sections - 1, count, rows), f32),
        ),
        in_specs=[scalars, scalars, full, full, full],
        out_specs=(full,) * 5,
        scratch_shapes=[
            pltpu.VMEM((sections * rows, block), f32),
            pltpu.VMEM((sections * rows, block), f32),
            pltpu.VMEM(square, f32),
            pltpu.VMEM(square, f32),
            pltpu.VMEM((sections * rows, block), f32),
            pltpu.VMEM((sections * rows, block), f32),
        ],
        compiler_params=params,
        name="rotations",
    )(orders, high, flat, far_gen, tokens)
    x_other = exchange(xs[0], pair_bit)
    x_both = pl.pallas_call(
        far_kernel,
        out_shape=jax.ShapeDtypeStruct((2 * count, rows), jnp.bfloat16),
        in_specs=[full] * 3,
        out_specs=full,
        compiler_params=params,
        name="far_apply",
    )(xs, x_other, ffar)

    reverse = np.array(
        [sum(((p >> b) & 1) << (bits - 1 - b) for b in range(bits)) for p in range(size)], np.int32
    )
    places = jnp.bitwise_xor(here.astype(jnp.int32), jnp.asarray(reverse))
    outs = []
    for chunk in range(CHUNKS):
        send = project(x_both, weight, places[size // 2 :], chunk, CHUNKS)
        keep = project(x_both, weight, places[: size // 2], chunk, CHUNKS)
        outs.append((send, keep))
    done = []
    for send, keep in outs:
        for bit in range(bits):
            got = exchange(send, bit)
            if bit < bits - 1:
                mid = keep.shape[0] // 2
                send, keep = keep[mid:] + got[mid:], keep[:mid] + got[:mid]
            else:
                keep = keep + got
        done.append(keep[0])
    outputs = jnp.concatenate(done, axis=1)

    grad_cols = project_back(gathered, weight)
    grad_other = exchange(grad_cols, pair_bit)
    numbers = jnp.arange(block, dtype=jnp.int32)
    inverse = jnp.sum(
        jnp.where(orders[:, :, None] == numbers[None, None, :], numbers[None, :, None], 0), axis=1
    ).astype(jnp.int32)
    grad_tokens, grad_gens = pl.pallas_call(
        grads_kernel,
        out_shape=(
            jax.ShapeDtypeStruct((count, rows), f32),
            jax.ShapeDtypeStruct((sections * rows, block), f32),
        ),
        in_specs=[scalars, scalars] + [full] * 8,
        out_specs=(full,) * 2,
        scratch_shapes=[
            pltpu.VMEM((sections * rows, block), f32),
            pltpu.VMEM((sections * rows, block), f32),
            pltpu.VMEM((sections * rows, block), f32),
            pltpu.VMEM(square, f32),
            pltpu.VMEM(square, f32),
            pltpu.VMEM(square, f32),
        ],
        compiler_params=params,
        name="gradients",
    )(inverse, high, grad_cols, grad_other, x_other, tokens, xs, near, bfar, inv)
    return outputs, grad_tokens, grad_gens.reshape(sections, rows, block)


def solution(mesh):
    placed = (
        P("groups", "tensor"),
        P("tensor", None),
        P("groups", "tensor", None),
        P(),
        P("groups", "tensor"),
    )
    return jax.shard_map(
        local,
        mesh=mesh,
        in_specs=placed,
        out_specs=(P("groups", "tensor"), P("groups", "tensor"), P("groups", "tensor", None)),
        check_vma=False,
    )
```

time: 520 us -> 217 us (0.42)
  the two profiles are of different devices: /device:TPU:8 before, /device:TPU:0 now
where the time goes in v1:
time: 217 us; the launch traced here: 216 us
  waiting for transfers between devices  105 us (48%)
  Pallas kernels  74.8 us (34%)
  between operations  14.3 us (7%)
  starting transfers between devices  12 us (6%)
  local copies, waits for them, and re-layouts  5.58 us (3%)
  other arithmetic  4.24 us (2%)
    ppermute x11, waiting for transfers between devices, exchange(): lax.ppermute(array, 'tensor', [(i, i ^ 1 << bit) for i in range(size)])  105 us
    pallas_call x4, Pallas kernels, project(): pl.pallas_call(project_kernel, out_shape=jax.ShapeDtypeStruct((pieces, co...  25.6 us
    pallas_call x1, Pallas kernels, local(): pl.pallas_call(grads_kernel, out_shape=(jax.ShapeDtypeStruct((count, rows...  18.4 us
    pallas_call x1, Pallas kernels, project_back(): pl.pallas_call(back_kernel, out_shape=jax.ShapeDtypeStruct((count, rows),...  15.1 us
    pallas_call x1, Pallas kernels, local(): pl.pallas_call(rotate_kernel, out_shape=(jax.ShapeDtypeStruct(square, f32...  14.6 us
    ppermute x11, starting transfers between devices, exchange(): lax.ppermute(array, 'tensor', [(i, i ^ 1 << bit) for i in range(size)])  12 us
    unnamed x22, local copies, waits for them, and re-layouts  5.47 us
  transfers between devices with their start and end apart: 12, of which 6 were waited for; matrix products, arithmetic and copies ran while one was open for 3% of the time, Pallas kernels for 26%

profile of v1, /device:TPU:0, one launch (start us, length us, event | category | flops | bytes accessed | tf_op | source)
XLA Modules:
  0.0 216.2 jit_solution(12297424401261780937)
XLA Ops:
  7.2 0.0 copy-start.9
  7.2 0.0 all-gather.3.cloned.1.call-start
  7.2 0.7 all-gather.3.cloned.1.call-update
  7.9 1.3 copy.12
  9.2 4.1 %collective-permute-start = (f32[512,32]{1,0:T(8,128)S(1)}, f32[512,32]{1,0:T(8,128)S(1)}, u32[]{:S(2)}, u32[]{:S(2)}) collective-permute-start(f32[512,32]{1,0:T(8,128)S(1)} %slice_bitcast_fusion), channel_id=1, source_target_pairs={{0,8},{1,9},{2,10},{3,11},{4,12},{5,13},{6,14},{7,15},{8,0},{9,1},... | collective-permute-start | bytes 196616 | tf_op jit(solution)/shard_map/ppermute | solution.py:22
  13.3 13.8 %collective-permute-done.far_ref = f32[512,32]{1,0:T(8,128)S(1)} collective-permute-done((f32[512,32]{1,0:T(8,128)S(1)}, f32[512,32]{1,0:T(8,128)S(1)}, u32[]{:S(2)}, u32[]{:S(2)}) %collective-permute-start) | collective-permute-done | bytes 65568 | tf_op jit(solution)/shard_map/ppermute | solution.py:22
  27.1 14.6 %rotations.1 = (f32[1024,128]{1,0:T(8,128)S(1)}, f32[3,512,128]{2,1,0:T(8,128)S(1)}, f32[2,512,128]{2,1,0:T(8,128)S(1)}, f32[2,512,128]{2,1,0:T(8,128)S(1)}, f32[3,128,512]{2,1,0:T(8,128)S(1)}) custom-call(s32[4,32]{1,0:T(4,128)S(1)} %copy-done.6, s32[1]{0:T(128)} %bitcast.high_ref, f32[2048,32]{1,0:T(8,128)S(1)} %bitcast.12, ...), custom_call_target="tpu_custom_call" | custom-call | tf_op jit(solution)/shard_map/rotations/pallas_call | solution.py:377
  41.8 0.9 copy-done.1
  42.7 0.1 collective-permute-start.1
  42.8 0.1 fusion.4
  42.9 27.0 %collective-permute-done.1.oth_ref.x_oth_ref = f32[128,512]{1,0:T(8,128)S(1)} collective-permute-done((f32[128,512]{1,0:T(8,128)S(1)}, f32[128,512]{1,0:T(8,128)S(1)}, u32[]{:S(2)}, u32[]{:S(2)}) %collective-permute-start.1) | collective-permute-done | bytes 262176 | tf_op jit(solution)/shard_map/ppermute | solution.py:22
  69.9 1.2 far_apply.1.x_ref
  71.1 6.4 %project.5 = f32[8,128,512]{2,1,0:T(8,128)S(1)} custom-call(s32[8]{0:T(128)S(1)} %get-tuple-element.32.places_ref, bf16[256,512]{1,0:T(8,128)(2,1)S(1)} %far_apply.1.x_ref, bf16[512,16384]{1,0:T(8,128)(2,1)} %w_ref.9), custom_call_target="tpu_custom_call" | custom-call | flops 1073741824 | bytes 6291456 | tf_op jit(solution)/shard_map/project/pallas_call | solution.py:208
  77.5 0.1 collective-permute-start.2
  77.6 6.4 %project.7 = f32[8,128,512]{2,1,0:T(8,128)S(1)} custom-call(s32[8]{0:T(128)S(1)} %get-tuple-element.32.places_ref, bf16[256,512]{1,0:T(8,128)(2,1)S(1)} %far_apply.1.x_ref, bf16[512,16384]{1,0:T(8,128)(2,1)} %w_ref.9), custom_call_target="tpu_custom_call" | custom-call | flops 1073741824 | bytes 6291456 | tf_op jit(solution)/shard_map/project/pallas_call | solution.py:208
  84.0 0.6 collective-permute-start.6
  84.6 6.4 %project.4 = f32[8,128,512]{2,1,0:T(8,128)S(1)} custom-call(s32[8]{0:T(128)S(1)} %get-tuple-element.31.places_ref, bf16[256,512]{1,0:T(8,128)(2,1)S(1)} %far_apply.1.x_ref, bf16[512,16384]{1,0:T(8,128)(2,1)} %w_ref.9), custom_call_target="tpu_custom_call" | custom-call | flops 1073741824 | bytes 6291456 | tf_op jit(solution)/shard_map/project/pallas_call | solution.py:208
  91.0 0.0 collective-permute-done.2
  91.0 0.5 slice_add_fusion.3
  91.5 1.4 collective-permute-start.3
  92.9 6.4 %project.6 = f32[8,128,512]{2,1,0:T(8,128)S(1)} custom-call(s32[8]{0:T(128)S(1)} %get-tuple-element.31.places_ref, bf16[256,512]{1,0:T(8,128)(2,1)S(1)} %far_apply.1.x_ref, bf16[512,16384]{1,0:T(8,128)(2,1)} %w_ref.9), custom_call_target="tpu_custom_call" | custom-call | flops 1073741824 | bytes 6291456 | tf_op jit(solution)/shard_map/project/pallas_call | solution.py:208
  99.3 0.0 collective-permute-done.6
  99.3 0.5 slice_add_fusion.1
  99.8 0.7 collective-permute-start.7
  100.5 17.0 %collective-permute-done.3 = f32[4,128,512]{2,1,0:T(8,128)S(1)} collective-permute-done((f32[4,128,512]{2,1,0:T(8,128)S(1)}, f32[4,128,512]{2,1,0:T(8,128)S(1)}, u32[]{:S(2)}, u32[]{:S(2)}) %collective-permute-start.3) | collective-permute-done | bytes 1048608 | tf_op jit(solution)/shard_map/ppermute | solution.py:22
  117.5 0.2 slice_add_fusion.7
  117.8 0.1 collective-permute-start.4
  117.8 21.2 %collective-permute-done.7 = f32[4,128,512]{2,1,0:T(8,128)S(1)} collective-permute-done((f32[4,128,512]{2,1,0:T(8,128)S(1)}, f32[4,128,512]{2,1,0:T(8,128)S(1)}, u32[]{:S(2)}, u32[]{:S(2)}) %collective-permute-start.7) | collective-permute-done | bytes 1048608 | tf_op jit(solution)/shard_map/ppermute | solution.py:22
  139.1 0.2 slice_add_fusion.5
  139.3 0.1 collective-permute-start.8
  139.4 0.0 collective-permute-done.4
  139.4 1.9 collective-permute-start.5
  141.4 0.1 select_reduce_fusion.inverse_ref
  141.5 16.5 %collective-permute-done.8 = f32[2,128,512]{2,1,0:T(8,128)S(1)} collective-permute-done((f32[2,128,512]{2,1,0:T(8,128)S(1)}, f32[2,128,512]{2,1,0:T(8,128)S(1)}, u32[]{:S(2)}, u32[]{:S(2)}) %collective-permute-start.8) | collective-permute-done | bytes 524320 | tf_op jit(solution)/shard_map/ppermute | solution.py:22
  158.0 0.8 slice_add_fusion.8
  158.8 0.0 collective-permute-start.9
  158.8 0.1 copy-done.7
  158.9 0.1 fusion.3
  158.9 0.0 all-gather.3.cloned.1.call-done
  159.0 2.2 %copy-done = bf16[2048,1024]{1,0:T(8,128)(2,1)S(1)} copy-done((bf16[2048,1024]{1,0:T(8,128)(2,1)S(1)}, bf16[2048,1024]{1,0:T(8,128)(2,1)}, u32[]{:S(2)}) %copy-start) | copy-done | bytes 4194328
  161.2 15.1 %project_back.1.own_ref = f32[128,512]{1,0:T(8,128)S(1)} custom-call(bf16[16,128,1024]{2,1,0:T(8,128)(2,1)S(1)} %bitcast.13, bf16[512,16384]{1,0:T(8,128)(2,1)} %w_ref.9), custom_call_target="tpu_custom_call" | custom-call | flops 2147483648 | bytes 20971520 | tf_op jit(solution)/shard_map/project_back/pallas_call | solution.py:243
  176.2 2.9 %collective-permute-start.10 = (f32[128,512]{1,0:T(8,128)S(1)}, f32[128,512]{1,0:T(8,128)S(1)}, u32[]{:S(2)}, u32[]{:S(2)}) collective-permute-start(f32[128,512]{1,0:T(8,128)S(1)} %project_back.1.own_ref), channel_id=1, source_target_pairs={{0,8},{1,9},{2,10},{3,11},{4,12},{5,13},{6,14},{7,15},{8,0},{9,1},... | collective-permute-start | bytes 786440 | tf_op jit(solution)/shard_map/ppermute | solution.py:22
  179.1 0.0 collective-permute-done.9
  179.1 1.0 fusion.1
  180.2 0.8 pad_maximum_fusion
  181.0 8.9 %collective-permute-done.10.oth_ref = f32[128,512]{1,0:T(8,128)S(1)} collective-permute-done((f32[128,512]{1,0:T(8,128)S(1)}, f32[128,512]{1,0:T(8,128)S(1)}, u32[]{:S(2)}, u32[]{:S(2)}) %collective-permute-start.10) | collective-permute-done | bytes 262176 | tf_op jit(solution)/shard_map/ppermute | solution.py:22
  189.9 18.4 %gradients.1 = (f32[128,512]{1,0:T(8,128)}, f32[2048,32]{1,0:T(8,128)S(1)}) custom-call(s32[4,32]{1,0:T(4,128)S(1)} %select_reduce_fusion.inverse_ref, s32[1]{0:T(128)} %bitcast.high_ref, f32[128,512]{1,0:T(8,128)S(1)} %project_back.1.own_ref, f32[128,512]{1,0:T(8,128)S(1)} %collective-permute-done.10.oth_ref, ...), custom_call_target="tpu_custom_call" | custom-call | tf_op jit(solution)/shard_map/gradients/pallas_call | solution.py:436
  208.3 1.0 copy.14
  (21 shorter events, 0.1 us)
Async XLA Ops:
  7.2 35.6 %copy-start.9 = (s32[16]{0:T(128)S(1)}, s32[16]{0:T(128)}, u32[]{:S(2)}) copy-start(s32[16]{0:T(128)} %constant.12.clone) | copy-start | bytes 196
  7.2 20.0 %copy-start.5 = (bf16[128,512]{1,0:T(8,128)(2,1)S(1)}, bf16[128,512]{1,0:T(8,128)(2,1)}, u32[]{:S(2)}) copy-start(bf16[128,512]{1,0:T(8,128)(2,1)} %tok_ref.3) | copy-start | bytes 393220
  7.2 20.0 %copy-start.6 = (s32[4,32]{1,0:T(4,128)S(1)}, s32[4,32]{1,0:T(4,128)}, u32[]{:S(2)}) copy-start(s32[4,32]{1,0:T(4,128)} %orders_ref.1) | copy-start | bytes 1540
  7.2 151.8 %all-gather.3.cloned.1.call-start = ((), (), s32[]{:S(2)}) async-start(), calls=%async_computation | async-start | bytes 4456448 | tf_op jit(solution)/shard_map/all_gather | solution.py:374
  9.2 17.9 %collective-permute-start = (f32[512,32]{1,0:T(8,128)S(1)}, f32[512,32]{1,0:T(8,128)S(1)}, u32[]{:S(2)}, u32[]{:S(2)}) collective-permute-start(f32[512,32]{1,0:T(8,128)S(1)} %slice_bitcast_fusion), channel_id=1, source_target_pairs={{0,8},{1,9},{2,10},{3,11},{4,12},{5,13},{6,14},{7,15},{8,0},{9,1},... | collective-permute-start | bytes 196616 | tf_op jit(solution)/shard_map/ppermute | solution.py:22
  41.8 0.9 copy-start.1
  42.7 34.8 %copy-start.3 = (f32[2,512,128]{2,1,0:T(8,128)}, f32[2,512,128]{2,1,0:T(8,128)S(1)}, u32[]{:S(2)}) copy-start(f32[2,512,128]{2,1,0:T(8,128)S(1)} %get-tuple-element.13.bfar_ref) | copy-start | bytes 1572868
  42.7 27.2 %collective-permute-start.1 = (f32[128,512]{1,0:T(8,128)S(1)}, f32[128,512]{1,0:T(8,128)S(1)}, u32[]{:S(2)}, u32[]{:S(2)}) collective-permute-start(f32[128,512]{1,0:T(8,128)S(1)} %slice_bitcast_fusion.1), channel_id=1, source_target_pairs={{0,8},{1,9},{2,10},{3,11},{4,12},{5,13},{6,14},{7,15},{8,0},{9,1},... | collective-permute-start | bytes 786440 | tf_op jit(solution)/shard_map/ppermute | solution.py:22
  77.5 13.4 %collective-permute-start.2 = (f32[8,128,512]{2,1,0:T(8,128)S(1)}, f32[8,128,512]{2,1,0:T(8,128)S(1)}, u32[]{:S(2)}, u32[]{:S(2)}) collective-permute-start(f32[8,128,512]{2,1,0:T(8,128)S(1)} %project.5), channel_id=1, source_target_pairs={{0,1},{1,0},{2,3},{3,2},{4,5},{5,4},{6,7},{7,6},{8,9},{9,8},{10,11... | collective-permute-start | bytes 6291464 | tf_op jit(solution)/shard_map/ppermute | solution.py:22
  84.0 15.3 %collective-permute-start.6 = (f32[8,128,512]{2,1,0:T(8,128)S(1)}, f32[8,128,512]{2,1,0:T(8,128)S(1)}, u32[]{:S(2)}, u32[]{:S(2)}) collective-permute-start(f32[8,128,512]{2,1,0:T(8,128)S(1)} %project.7), channel_id=1, source_target_pairs={{0,1},{1,0},{2,3},{3,2},{4,5},{5,4},{6,7},{7,6},{8,9},{9,8},{10,11... | collective-permute-start | bytes 6291464 | tf_op jit(solution)/shard_map/ppermute | solution.py:22
  91.5 26.1 %collective-permute-start.3 = (f32[4,128,512]{2,1,0:T(8,128)S(1)}, f32[4,128,512]{2,1,0:T(8,128)S(1)}, u32[]{:S(2)}, u32[]{:S(2)}) collective-permute-start(f32[4,128,512]{2,1,0:T(8,128)S(1)} %get-tuple-element.24), channel_id=1, source_target_pairs={{0,2},{1,3},{2,0},{3,1},{4,6},{5,7},{6,4},{7,5},{8,10},{9,11},{10,... | collective-permute-start | bytes 3145736 | tf_op jit(solution)/shard_map/ppermute | solution.py:22
  99.8 39.3 %collective-permute-start.7 = (f32[4,128,512]{2,1,0:T(8,128)S(1)}, f32[4,128,512]{2,1,0:T(8,128)S(1)}, u32[]{:S(2)}, u32[]{:S(2)}) collective-permute-start(f32[4,128,512]{2,1,0:T(8,128)S(1)} %get-tuple-element.26), channel_id=1, source_target_pairs={{0,2},{1,3},{2,0},{3,1},{4,6},{5,7},{6,4},{7,5},{8,10},{9,11},{10,... | collective-permute-start | bytes 3145736 | tf_op jit(solution)/shard_map/ppermute | solution.py:22
  117.8 21.6 %collective-permute-start.4 = (f32[2,128,512]{2,1,0:T(8,128)S(1)}, f32[2,128,512]{2,1,0:T(8,128)S(1)}, u32[]{:S(2)}, u32[]{:S(2)}) collective-permute-start(f32[2,128,512]{2,1,0:T(8,128)S(1)} %get-tuple-element.28), channel_id=1, source_target_pairs={{0,4},{1,5},{2,6},{3,7},{4,0},{5,1},{6,2},{7,3},{8,12},{9,13},{10,... | collective-permute-start | bytes 1572872 | tf_op jit(solution)/shard_map/ppermute | solution.py:22
  139.3 18.7 %collective-permute-start.8 = (f32[2,128,512]{2,1,0:T(8,128)S(1)}, f32[2,128,512]{2,1,0:T(8,128)S(1)}, u32[]{:S(2)}, u32[]{:S(2)}) collective-permute-start(f32[2,128,512]{2,1,0:T(8,128)S(1)} %get-tuple-element.30), channel_id=1, source_target_pairs={{0,4},{1,5},{2,6},{3,7},{4,0},{5,1},{6,2},{7,3},{8,12},{9,13},{10,... | collective-permute-start | bytes 1572872 | tf_op jit(solution)/shard_map/ppermute | solution.py:22
  139.4 19.4 %collective-permute-start.5 = (f32[1,128,512]{2,1,0:T(8,128)S(1)}, f32[1,128,512]{2,1,0:T(8,128)S(1)}, u32[]{:S(2)}, u32[]{:S(2)}) collective-permute-start(f32[1,128,512]{2,1,0:T(8,128)S(1)} %slice_add_fusion.10), channel_id=1, source_target_pairs={{0,8},{1,9},{2,10},{3,11},{4,12},{5,13},{6,14},{7,15},{8,0},{9,1},... | collective-permute-start | bytes 786440 | tf_op jit(solution)/shard_map/ppermute | solution.py:22
  158.0 0.9 copy-start.7
  158.8 20.4 %collective-permute-start.9 = (f32[1,128,512]{2,1,0:T(8,128)}, f32[1,128,512]{2,1,0:T(8,128)}, u32[]{:S(2)}, u32[]{:S(2)}) collective-permute-start(f32[1,128,512]{2,1,0:T(8,128)} %slice_add_fusion.8), channel_id=1, source_target_pairs={{0,8},{1,9},{2,10},{3,11},{4,12},{5,13},{6,14},{7,15},{8,0},{9,1},... | collective-permute-start | bytes 786440 | tf_op jit(solution)/shard_map/ppermute | solution.py:22
  159.0 2.2 %copy-start = (bf16[2048,1024]{1,0:T(8,128)(2,1)S(1)}, bf16[2048,1024]{1,0:T(8,128)(2,1)}, u32[]{:S(2)}) copy-start(bf16[2048,1024]{1,0:T(8,128)(2,1)} %all-gather.3.cloned.1.call-done) | copy-start | bytes 12582916
  161.1 18.0 %copy-start.8 = (f32[2,128,512]{2,1,0:T(8,128)S(1)}, f32[2,128,512]{2,1,0:T(8,128)}, u32[]{:S(2)}) copy-start(f32[2,128,512]{2,1,0:T(8,128)} %copy-done.7) | copy-start | bytes 1572868
  176.2 13.7 %copy-start.2 = (f32[3,512,128]{2,1,0:T(8,128)S(1)}, f32[3,512,128]{2,1,0:T(8,128)}, u32[]{:S(2)}) copy-start(f32[3,512,128]{2,1,0:T(8,128)} %copy-done.1) | copy-start | bytes 2359300
  176.2 13.7 %copy-start.4 = (f32[2,512,128]{2,1,0:T(8,128)S(1)}, f32[2,512,128]{2,1,0:T(8,128)}, u32[]{:S(2)}) copy-start(f32[2,512,128]{2,1,0:T(8,128)} %copy-done.3) | copy-start | bytes 1572868
  176.2 13.7 %collective-permute-start.10 = (f32[128,512]{1,0:T(8,128)S(1)}, f32[128,512]{1,0:T(8,128)S(1)}, u32[]{:S(2)}, u32[]{:S(2)}) collective-permute-start(f32[128,512]{1,0:T(8,128)S(1)} %project_back.1.own_ref), channel_id=1, source_target_pairs={{0,8},{1,9},{2,10},{3,11},{4,12},{5,13},{6,14},{7,15},{8,0},{9,1},... | collective-permute-start | bytes 786440 | tf_op jit(solution)/shard_map/ppermute | solution.py:22
Sparse Core Ops, SparseCore 0:
  10.2 63.2 all-gather.2

commit v2 on v1

--- a/solution.py
+++ b/solution.py
@@ -8,8 +8,8 @@
 from jax.experimental.pallas import tpu as pltpu
 from jax.sharding import PartitionSpec as P
 
-HIGHEST = lax.Precision.HIGHEST
-VMEM_LIMIT = 48 * 2**20
+VMEM_LIMIT = 16 * 2**20
+WIDE_LIMIT = 40 * 2**20
 GROUP = 128
 NN = (((1,), (0,)), ((), ()))
 NT = (((1,), (1,)), ((), ()))
@@ -22,8 +22,26 @@
     return lax.ppermute(array, "tensor", [(i, i ^ (1 << bit)) for i in range(size)])
 
 
+def parts_of(x):
+    first = x.astype(jnp.bfloat16)
+    return first, (x - first.astype(jnp.float32)).astype(jnp.bfloat16)
+
+
+def one_dot(a, b, dims=NN):
+    return lax.dot_general(a, b, dims, preferred_element_type=jnp.float32)
+
+
 def dot(a, b, dims=NN):
-    return lax.dot_general(a, b, dims, precision=HIGHEST, preferred_element_type=jnp.float32)
+    a_first, a_rest = parts_of(a)
+    b_first, b_rest = parts_of(b)
+    return (
+        one_dot(a_first, b_first, dims) + one_dot(a_rest, b_first, dims) + one_dot(a_first, b_rest, dims)
+    )
+
+
+def pick(a, chooser):
+    first, rest = parts_of(a)
+    return one_dot(first, chooser) + one_dot(rest, chooser)
 
 
 def iota(shape, dim):
@@ -76,33 +94,21 @@
     return iota((GROUP, GROUP), 0) // half == iota((GROUP, GROUP), 1) // half
 
 
-def spreader(offset, block, half):
-    return (iota((block, GROUP), 0) == offset + iota((block, GROUP), 1) % half).astype(jnp.float32)
+def spreader(offsets, block, half):
+    row, col = iota((block, GROUP), 0), iota((block, GROUP), 1) % half
+    return jnp.concatenate([(row == at + col).astype(jnp.bfloat16) for at in offsets], axis=1)
 
 
 def gatherer(offset, block, half):
-    return (iota((GROUP, block), 1) == offset + iota((GROUP, block), 0) % half).astype(jnp.float32)
-
-
-def rotate_kernel(
-    orders_ref, high_ref, gen_ref, far_ref, tok_ref,
-    inv_ref, near_ref, ffar_ref, bfar_ref, xs_ref,
-    lo_ref, hi_ref, a_ref, b_ref, row_ref, rowt_ref,
-):
+    row, col = iota((GROUP, block), 0) % half, iota((GROUP, block), 1)
+    return (col == offset + row).astype(jnp.bfloat16)
+
+
+def invert_blocks(orders_ref, lo_ref, hi_ref, inv_ref, a_ref, b_ref, section_of):
     sections, block = orders_ref.shape
     half = block // 2
-    rows = far_ref.shape[0]
-    per_section = rows // half
-    lanes = sections * per_section
-    high = high_ref[0]
-    own = gen_ref[0:rows, :]
-    other = far_ref[...]
-    lo_ref[0:rows, :] = jnp.where(high == 1, other, own)
-    hi_ref[0:rows, :] = jnp.where(high == 1, own, other)
-    for k in range(1, sections):
-        split_halves(gen_ref, lo_ref, hi_ref, k, rows, half)
+    lanes = inv_ref.shape[1]
     to_lanes(lo_ref, hi_ref, a_ref, lanes, half, block)
-    section_of, upper = lane_facts((block, lanes), per_section, high)
 
     def permute_rows(i, _):
         parts = [
@@ -134,50 +140,96 @@
         at = pl.multiple_of(k * block, block)
         here = sub == k
         inverse = 1.0 / inv_ref[pl.ds(at + k, 1), :]
+        factors = inv_ref[pl.ds(k, block, stride=block), :]
         pivot = jnp.where(here, inverse, inv_ref[pl.ds(at, block), :] * inverse)
         for i in range(block):
-            factor = inv_ref[pl.ds(i * block + k, 1), :]
             row = inv_ref[i * block : (i + 1) * block, :]
-            inv_ref[i * block : (i + 1) * block, :] = jnp.where(here, 0.0, row) - factor * pivot
+            inv_ref[i * block : (i + 1) * block, :] = (
+                jnp.where(here, 0.0, row) - factors[i : i + 1, :] * pivot
+            )
         inv_ref[pl.ds(at, block), :] = pivot
         return 0
 
     lax.fori_loop(0, block, eliminate, 0)
 
+
+def own_rows(inv_ref, out_ref, half, block, upper):
+    lanes = inv_ref.shape[1]
+    sub = iota((block, lanes), 0)
     for a in range(half):
         low = 2.0 * inv_ref[a * block : (a + 1) * block, :] - (sub == a).astype(jnp.float32)
         top = 2.0 * inv_ref[(half + a) * block : (half + a + 1) * block, :] - (
             sub == half + a
         ).astype(jnp.float32)
-        row_ref[pl.ds(a, lanes, stride=half), :] = jnp.where(upper, top, low).T
+        out_ref[pl.ds(a, lanes, stride=half), :] = jnp.where(upper, top, low).T
+
+
+def own_cols(inv_ref, out_ref, half, block, upper):
+    lanes = inv_ref.shape[1]
+    sub = iota((block, lanes), 0)
+    for a in range(half):
         low = 2.0 * inv_ref[pl.ds(a, block, stride=block), :] - (sub == a).astype(jnp.float32)
         top = 2.0 * inv_ref[pl.ds(half + a, block, stride=block), :] - (sub == half + a).astype(
             jnp.float32
         )
-        rowt_ref[pl.ds(a, lanes, stride=half), :] = jnp.where(upper, top, low).T
-    spread_lo = spreader(0, block, half)
-    spread_hi = spreader(half, block, half)
-    spread_own = spreader(half * high, block, half)
-    spread_oth = spreader(half * (1 - high), block, half)
-    same = same_mask(half)
+        out_ref[pl.ds(a, lanes, stride=half), :] = jnp.where(upper, top, low).T
+
+
+def near_kernel(
+    orders_ref, gen_ref, tok_ref, inv_ref, near_ref, xs_ref, lo_ref, hi_ref, a_ref, b_ref, row_ref
+):
+    sections, block = orders_ref.shape
+    half = block // 2
+    rows = tok_ref.shape[1]
+    lanes = sections * rows // half
+    lo_ref[0:rows, :] = gen_ref[0:rows, :]
+    hi_ref[0:rows, :] = gen_ref[0:rows, :]
+    for k in range(1, sections):
+        split_halves(gen_ref, lo_ref, hi_ref, k, rows, half)
+    section_of, upper = lane_facts((block, lanes), rows // half, 0)
+    invert_blocks(orders_ref, lo_ref, hi_ref, inv_ref, a_ref, b_ref, section_of)
+    own_rows(inv_ref, row_ref, half, block, upper)
+    spread = spreader((0, half), block, half)
+    for k in range(1, sections):
+        lo_mask, hi_mask = block_masks(k, half)
+        wide = pick(row_ref[k * rows : (k + 1) * rows, :], spread)
+        for start in range(0, rows, GROUP):
+            part = wide[start : start + GROUP]
+            near_ref[k - 1, start : start + GROUP, :] = jnp.where(
+                lo_mask, part[:, :GROUP], jnp.where(hi_mask, part[:, GROUP:], 0.0)
+            )
     for start in range(0, rows, GROUP):
         stop = start + GROUP
-        part = rowt_ref[start:stop, :]
-        ffar_ref[0, start:stop, :] = jnp.where(same, dot(part, spread_own), 0.0)
-        ffar_ref[1, start:stop, :] = jnp.where(same, dot(part, spread_oth), 0.0)
-        part = row_ref[start:stop, :]
-        bfar_ref[0, start:stop, :] = jnp.where(same, dot(part, spread_own), 0.0)
-        bfar_ref[1, start:stop, :] = jnp.where(same, dot(part, spread_oth), 0.0)
         value = tok_ref[:, start:stop].astype(jnp.float32)
         for k in range(sections - 1, 0, -1):
-            lo_mask, hi_mask = block_masks(k, half)
-            part = row_ref[k * rows + start : k * rows + stop, :]
-            matrix = jnp.where(lo_mask, dot(part, spread_lo), 0.0) + jnp.where(
-                hi_mask, dot(part, spread_hi), 0.0
-            )
-            near_ref[k - 1, start:stop, :] = matrix
-            value = dot(value, matrix)
+            value = dot(value, near_ref[k - 1, start:stop, :])
             xs_ref[k - 1, :, start:stop] = value
+
+
+def far_rotations_kernel(
+    orders_ref, high_ref, own_ref, far_ref, inv_ref, ffar_ref, bfar_ref,
+    lo_ref, hi_ref, a_ref, b_ref, row_ref, col_ref,
+):
+    block = orders_ref.shape[1]
+    half = block // 2
+    rows = far_ref.shape[0]
+    high = high_ref[0]
+    own = own_ref[...]
+    other = far_ref[...]
+    lo_ref[...] = jnp.where(high == 1, other, own)
+    hi_ref[...] = jnp.where(high == 1, own, other)
+    invert_blocks(orders_ref, lo_ref, hi_ref, inv_ref, a_ref, b_ref, None)
+    upper = high == 1
+    own_rows(inv_ref, row_ref, half, block, upper)
+    own_cols(inv_ref, col_ref, half, block, upper)
+    spread = spreader((half * high, half * (1 - high)), block, half)
+    same = same_mask(half)
+    for source, target in ((col_ref, ffar_ref), (row_ref, bfar_ref)):
+        wide = pick(source[...], spread)
+        for start in range(0, rows, GROUP):
+            part = wide[start : start + GROUP]
+            target[0, start : start + GROUP, :] = jnp.where(same, part[:, :GROUP], 0.0)
+            target[1, start : start + GROUP, :] = jnp.where(same, part[:, GROUP:], 0.0)
 
 
 def far_kernel(own_ref, oth_ref, far_ref, out_ref):
@@ -194,33 +246,32 @@
         )
 
 
-def project_kernel(places_ref, x_ref, w_ref, out_ref):
-    count = out_ref.shape[1]
-    both = jnp.dot(x_ref[...], w_ref[...], preferred_element_type=jnp.float32)
-    out_ref[0] = both[:count] + both[count:]
-
-
-def project(x_both, weight, places, chunk, chunks):
+def project_kernel(chunk, places_ref, x_ref, w_ref, out_ref):
+    pieces, count, width = out_ref.shape
+
+    def body(p, _):
+        at = pl.multiple_of((places_ref[p] * CHUNKS + chunk) * width, width)
+        both = one_dot(x_ref[...], w_ref[:, pl.ds(at, width)])
+        out_ref[p] = both[:count] + both[count:]
+        return 0
+
+    lax.fori_loop(0, pieces, body, 0)
+
+
+def project(x_both, weight, places, chunk):
     pieces = places.shape[0]
     count2, rows = x_both.shape
     count = count2 // 2
-    width = weight.shape[1] // lax.axis_size("tensor") // chunks
+    width = weight.shape[1] // lax.axis_size("tensor") // CHUNKS
     return pl.pallas_call(
-        project_kernel,
+        functools.partial(project_kernel, chunk),
         out_shape=jax.ShapeDtypeStruct((pieces, count, width), jnp.float32),
-        grid_spec=pltpu.PrefetchScalarGridSpec(
-            num_scalar_prefetch=1,
-            grid=(pieces,),
-            in_specs=[
-                pl.BlockSpec((count2, rows), lambda p, places: (0, 0)),
-                pl.BlockSpec((rows, width), lambda p, places: (0, places[p] * chunks + chunk)),
-            ],
-            out_specs=pl.BlockSpec((1, count, width), lambda p, places: (p, 0, 0)),
-        ),
-        compiler_params=pltpu.CompilerParams(vmem_limit_bytes=VMEM_LIMIT),
+        in_specs=[pl.BlockSpec(memory_space=pltpu.SMEM)] + [pl.BlockSpec(memory_space=pltpu.VMEM)] * 2,
+        out_specs=pl.BlockSpec(memory_space=pltpu.VMEM),
+        compiler_params=pltpu.CompilerParams(vmem_limit_bytes=WIDE_LIMIT),
         cost_estimate=pl.CostEstimate(
             flops=2 * count2 * rows * width * pieces,
-            bytes_accessed=pieces * width * (2 * rows + 4 * count),
+            bytes_accessed=pieces * width * 4 * count,
             transcendentals=0,
         ),
         name="project",
@@ -228,13 +279,11 @@
 
 
 def back_kernel(cot_ref, w_ref, out_ref):
-    @pl.when(pl.program_id(0) == 0)
-    def _():
-        out_ref[...] = jnp.zeros_like(out_ref)
-
-    out_ref[...] += lax.dot_general(
-        cot_ref[0], w_ref[...], NT, preferred_element_type=jnp.float32
-    )
+    pieces, count, width = cot_ref.shape
+    total = jnp.zeros(out_ref.shape, jnp.float32)
+    for p in range(pieces):
+        total += one_dot(cot_ref[p], w_ref[:, p * width : (p + 1) * width], NT)
+    out_ref[...] = total
 
 
 def project_back(gathered, weight):
@@ -243,13 +292,9 @@
     return pl.pallas_call(
         back_kernel,
         out_shape=jax.ShapeDtypeStruct((count, rows), jnp.float32),
-        grid=(pieces,),
-        in_specs=[
-            pl.BlockSpec((1, count, width), lambda p: (p, 0, 0)),
-            pl.BlockSpec((rows, width), lambda p: (0, p)),
-        ],
-        out_specs=pl.BlockSpec((count, rows), lambda p: (0, 0)),
-        compiler_params=pltpu.CompilerParams(vmem_limit_bytes=VMEM_LIMIT),
+        in_specs=[pl.BlockSpec(memory_space=pltpu.VMEM)] * 2,
+        out_specs=pl.BlockSpec(memory_space=pltpu.VMEM),
+        compiler_params=pltpu.CompilerParams(vmem_limit_bytes=WIDE_LIMIT),
         cost_estimate=pl.CostEstimate(
             flops=2 * count * rows * width * pieces,
             bytes_accessed=pieces * width * 2 * (rows + count),
@@ -277,7 +322,7 @@
 
 
 def grads_kernel(
-    inverse_ref, high_ref, own_ref, oth_ref, x_oth_ref, tok_ref, xs_ref, near_ref, bfar_ref, inv_ref,
+    inverse_ref, high_ref, own_ref, oth_ref, x_oth_ref, tok_ref, xs_ref, near_ref, bfar_ref, inv_far_ref, inv_ref,
     gtok_ref, ggen_ref,
     row_ref, lo_ref, hi_ref, a_ref, b_ref, c_ref,
 ):
@@ -300,7 +345,7 @@
         g_oth = oth_ref[:, start:stop]
 
         def far_rows(x):
-            return dot(jnp.where(same, dot(x, g_own, TN), 0.0), gather_own) + dot(
+            return pick(jnp.where(same, dot(x, g_own, TN), 0.0), gather_own) + pick(
                 jnp.where(same, dot(x, g_oth, TN), 0.0), gather_oth
             )
 
@@ -315,9 +360,9 @@
             else:
                 x = tok_ref[:, start:stop].astype(jnp.float32)
             outer = dot(x, grad, TN)
-            row_ref[k * rows + start : k * rows + stop, :] = dot(
+            row_ref[k * rows + start : k * rows + stop, :] = pick(
                 jnp.where(lo_mask, outer, 0.0), gather_lo
-            ) + dot(jnp.where(hi_mask, outer, 0.0), gather_hi)
+            ) + pick(jnp.where(hi_mask, outer, 0.0), gather_hi)
             grad = dot(grad, near_ref[k - 1, start:stop, :], NT)
         gtok_ref[:, start:stop] = grad
     for k in range(1, sections):
@@ -325,6 +370,9 @@
     to_lanes(lo_ref, hi_ref, a_ref, lanes, half, block)
     for j in range(block):
         b_ref[j * block : (j + 1) * block, :] = inv_ref[pl.ds(j, block, stride=block), :]
+        b_ref[j * block : (j + 1) * block, 0:per_section] = inv_far_ref[
+            pl.ds(j, block, stride=block), :
+        ]
     lane_matmul(a_ref, b_ref, c_ref, block, lanes)
     lane_matmul(b_ref, c_ref, a_ref, block, lanes)
     for j in range(block):
@@ -374,29 +422,48 @@
     gathered = lax.all_gather(cotangent, "tensor", axis=0, tiled=False)
     flat = generators.reshape(sections * rows, block)
     square = (block * block, lanes)
-    inv, near, ffar, bfar, xs = pl.pallas_call(
-        rotate_kernel,
+    far_square = (block * block, lanes // sections)
+    inv, near, xs = pl.pallas_call(
+        near_kernel,
         out_shape=(
             jax.ShapeDtypeStruct(square, f32),
             jax.ShapeDtypeStruct((sections - 1, rows, GROUP), f32),
-            jax.ShapeDtypeStruct((2, rows, GROUP), f32),
-            jax.ShapeDtypeStruct((2, rows, GROUP), f32),
             jax.ShapeDtypeStruct((sections - 1, count, rows), f32),
         ),
-        in_specs=[scalars, scalars, full, full, full],
-        out_specs=(full,) * 5,
+        in_specs=[scalars, full, full],
+        out_specs=(full,) * 3,
         scratch_shapes=[
             pltpu.VMEM((sections * rows, block), f32),
             pltpu.VMEM((sections * rows, block), f32),
             pltpu.VMEM(square, f32),
             pltpu.VMEM(square, f32),
             pltpu.VMEM((sections * rows, block), f32),
-            pltpu.VMEM((sections * rows, block), f32),
         ],
         compiler_params=params,
-        name="rotations",
-    )(orders, high, flat, far_gen, tokens)
+        name="near_rotations",
+    )(orders, flat, tokens)
     x_other = exchange(xs[0], pair_bit)
+    inv_far, ffar, bfar = pl.pallas_call(
+        far_rotations_kernel,
+        out_shape=(
+            jax.ShapeDtypeStruct(far_square, f32),
+            jax.ShapeDtypeStruct((2, rows, GROUP), f32),
+            jax.ShapeDtypeStruct((2, rows, GROUP), f32),
+        ),
+        in_specs=[scalars, scalars, full, full],
+        out_specs=(full,) * 3,
+        scratch_shapes=[
+            pltpu.VMEM((rows, block), f32),
+            pltpu.VMEM((rows, block), f32),
+            pltpu.VMEM(far_square, f32),
+            pltpu.VMEM(far_square, f32),
+            pltpu.VMEM((rows, block), f32),
+            pltpu.VMEM((rows, block), f32),
+        ],
+        compiler_params=params,
+        cost_estimate=pl.CostEstimate(flops=10**7, bytes_accessed=10**7, transcendentals=0),
+        name="far_rotations",
+    )(orders[:1], high, generators[0], far_gen)
     x_both = pl.pallas_call(
         far_kernel,
         out_shape=jax.ShapeDtypeStruct((2 * count, rows), jnp.bfloat16),
@@ -412,23 +479,25 @@
     places = jnp.bitwise_xor(here.astype(jnp.int32), jnp.asarray(reverse))
     outs = []
     for chunk in range(CHUNKS):
-        send = project(x_both, weight, places[size // 2 :], chunk, CHUNKS)
-        keep = project(x_both, weight, places[: size // 2], chunk, CHUNKS)
+        send = project(x_both, weight, places[size // 2 :], chunk)
+        keep = project(x_both, weight, places[: size // 2], chunk)
         outs.append((send, keep))
-    done = []
-    for send, keep in outs:
-        for bit in range(bits):
-            got = exchange(send, bit)
-            if bit < bits - 1:
-                mid = keep.shape[0] // 2
-                send, keep = keep[mid:] + got[mid:], keep[:mid] + got[:mid]
-            else:
-                keep = keep + got
-        done.append(keep[0])
-    outputs = jnp.concatenate(done, axis=1)
-
-    grad_cols = project_back(gathered, weight)
-    grad_other = exchange(grad_cols, pair_bit)
+    def stage(pair, got):
+        send, keep = pair
+        if keep.shape[0] == 1:
+            return None, keep + got
+        mid = keep.shape[0] // 2
+        return keep[mid:] + got[mid:], keep[:mid] + got[:mid]
+
+    for bit in range(bits):
+        gots = [exchange(send, bit) for send, _ in outs]
+        if bit == min(1, bits - 1):
+            grad_cols = project_back(gathered, weight)
+            grad_cols, *gots = lax.optimization_barrier([grad_cols] + gots)
+            grad_other = exchange(grad_cols, pair_bit)
+        outs = [stage(pair, got) for pair, got in zip(outs, gots)]
+    outputs = jnp.concatenate([keep[0] for _, keep in outs], axis=1)
+
     numbers = jnp.arange(block, dtype=jnp.int32)
     inverse = jnp.sum(
         jnp.where(orders[:, :, None] == numbers[None, None, :], numbers[None, :, None], 0), axis=1
@@ -439,7 +508,7 @@
             jax.ShapeDtypeStruct((count, rows), f32),
             jax.ShapeDtypeStruct((sections * rows, block), f32),
         ),
-        in_specs=[scalars, scalars] + [full] * 8,
+        in_specs=[scalars, scalars] + [full] * 9,
         out_specs=(full,) * 2,
         scratch_shapes=[
             pltpu.VMEM((sections * rows, block), f32),
@@ -451,7 +520,7 @@
         ],
         compiler_params=params,
         name="gradients",
-    )(inverse, high, grad_cols, grad_other, x_other, tokens, xs, near, bfar, inv)
+    )(inverse, high, grad_cols, grad_other, x_other, tokens, xs, near, bfar, inv_far, inv)
     return outputs, grad_tokens, grad_gens.reshape(sections, rows, block)
 
 

time: 217 us -> 194 us (0.89)
  waiting for transfers between devices: 105 us -> 72.6 us
  other arithmetic: 4.24 us -> 11.1 us
  Pallas kernels: 74.8 us -> 77.2 us
    ppermute x11, waiting for transfers between devices: 105 us -> 71.9 us  [exchange(): lax.ppermute(array, 'tensor', [(i, i ^ 1 << bit) for i in range(size)])]
    pallas_call x5 -> x6, Pallas kernels: 40.2 us -> 48.4 us  [the longest x4 33.8 us: project(): pl.pallas_call(functools.partial(project_kernel, chunk), out_shape=jax.Sh...]
    add x6, other arithmetic: 2.23 us -> 8.09 us  [stage(): return (keep[mid:] + got[mid:], keep[:mid] + got[:mid])]
    pallas_call x1, Pallas kernels: 15.1 us -> 11.4 us  [project_back(): pl.pallas_call(back_kernel, out_shape=jax.ShapeDtypeStruct((count, rows),...]
    unnamed x22 -> x34, local copies, waits for them, and re-layouts: 5.47 us -> 5.39 us
  transfers between devices with their start and end apart: 12 -> 12, of which waited for: 6 -> 6; matrix products, arithmetic and copies ran while one was open for 3% -> 5% of each run, Pallas kernels for 26% -> 40%
where the time goes in v2:
time: 194 us
  Pallas kernels  77.2 us (40%)
  waiting for transfers between devices  72.6 us (37%)
  between operations  14.3 us (7%)
  starting transfers between devices  12.9 us (7%)
  other arithmetic  11.1 us (6%)
  local copies, waits for them, and re-layouts  5.5 us (3%)
    ppermute x11, waiting for transfers between devices, exchange(): lax.ppermute(array, 'tensor', [(i, i ^ 1 << bit) for i in range(size)])  71.9 us
    pallas_call x4, Pallas kernels, project(): pl.pallas_call(functools.partial(project_kernel, chunk), out_shape=jax.Sh...  33.8 us
    pallas_call x1, Pallas kernels, local(): pl.pallas_call(grads_kernel, out_shape=(jax.ShapeDtypeStruct((count, rows...  16.8 us
    ppermute x11, starting transfers between devices, exchange(): lax.ppermute(array, 'tensor', [(i, i ^ 1 << bit) for i in range(size)])  12.9 us
    pallas_call x1, Pallas kernels, project_back(): pl.pallas_call(back_kernel, out_shape=jax.ShapeDtypeStruct((count, rows),...  11.4 us
    pallas_call x1, Pallas kernels, local(): pl.pallas_call(near_kernel, out_shape=(jax.ShapeDtypeStruct(square, f32),...  9.2 us
    add x6, other arithmetic, stage(): return (keep[mid:] + got[mid:], keep[:mid] + got[:mid])  8.09 us
    unnamed x34, local copies, waits for them, and re-layouts  5.39 us
  transfers between devices with their start and end apart: 12, of which 6 were waited for; matrix products, arithmetic and copies ran while one was open for 5% of the time, Pallas kernels for 40%

profile of v2, /device:TPU:0, one launch (start us, length us, event | category | flops | bytes accessed | tf_op | source)
XLA Modules:
  0.0 193.6 jit_solution(13534415621209383126)
XLA Ops:
  7.2 0.0 copy-start.15
  7.2 0.0 all-gather.3.cloned.1.call-start
  7.2 0.7 all-gather.3.cloned.1.call-update
  7.9 1.3 copy.12
  9.2 4.1 %collective-permute-start.1 = (f32[512,32]{1,0:T(8,128)S(1)}, f32[512,32]{1,0:T(8,128)S(1)}, u32[]{:S(2)}, u32[]{:S(2)}) collective-permute-start(f32[512,32]{1,0:T(8,128)S(1)} %slice_bitcast_fusion.own_ref), channel_id=1, source_target_pairs={{0,8},{1,9},{2,10},{3,11},{4,12},{5,13},{6,14},{7,15},{8,0},{9,1},... | collective-permute-start | bytes 196616 | tf_op jit(solution)/shard_map/ppermute | solution.py:22
  13.4 9.2 %near_rotations.1 = (f32[1024,128]{1,0:T(8,128)S(1)}, f32[3,512,128]{2,1,0:T(8,128)S(1)}, f32[3,128,512]{2,1,0:T(8,128)S(1)}) custom-call(s32[4,32]{1,0:T(4,128)S(1)} %copy-done.8, f32[2048,32]{1,0:T(8,128)S(1)} %bitcast.12, bf16[128,512]{1,0:T(8,128)(2,1)S(1)} %copy-done.1), custom_call_target="tpu_custom_call" | custom-call | tf_op jit(solution)/shard_map/near_rotations/pallas_call | solution.py:426
  22.6 0.8 copy-done.2
  23.4 0.1 collective-permute-start
  23.5 0.1 fusion.4
  23.6 3.8 %collective-permute-done.1.far_ref = f32[512,32]{1,0:T(8,128)S(1)} collective-permute-done((f32[512,32]{1,0:T(8,128)S(1)}, f32[512,32]{1,0:T(8,128)S(1)}, u32[]{:S(2)}, u32[]{:S(2)}) %collective-permute-start.1) | collective-permute-done | bytes 65568 | tf_op jit(solution)/shard_map/ppermute | solution.py:22
  27.4 5.3 %far_rotations.1 = (f32[1024,32]{1,0:T(8,128)S(1)}, f32[2,512,128]{2,1,0:T(8,128)S(1)}, f32[2,512,128]{2,1,0:T(8,128)S(1)}) custom-call(s32[1,32]{1,0:T(1,128)S(1)} %slice.92.orders_ref, s32[1]{0:T(128)} %bitcast.2.high_ref, f32[512,32]{1,0:T(8,128)S(1)} %slice_bitcast_fusion.own_ref, f32[512,32]{1,0:T(8,128)S(1)} %collective-permute-done.1.far_ref), custom_call_target="tpu_custom_call" | custom-call | flops 10000000 | bytes 10000000 | tf_op jit(solution)/shard_map/far_rotations/pallas_call | solution.py:446
  32.7 12.2 %collective-permute-done.oth_ref.x_oth_ref = f32[128,512]{1,0:T(8,128)S(1)} collective-permute-done((f32[128,512]{1,0:T(8,128)S(1)}, f32[128,512]{1,0:T(8,128)S(1)}, u32[]{:S(2)}, u32[]{:S(2)}) %collective-permute-start) | collective-permute-done | bytes 262176 | tf_op jit(solution)/shard_map/ppermute | solution.py:22
  45.0 0.7 far_apply.1.x_ref
  45.7 8.8 %project.5 = f32[8,128,512]{2,1,0:T(8,128)S(1)} custom-call(s32[8]{0:T(128)S(1)} %get-tuple-element.40.places_ref, bf16[256,512]{1,0:T(8,128)(2,1)S(1)} %far_apply.1.x_ref, bf16[512,16384]{1,0:T(8,128)(2,1)} %w_ref.9), custom_call_target="tpu_custom_call" | custom-call | flops 1073741824 | bytes 2097152 | tf_op jit(solution)/shard_map/project/pallas_call | solution.py:266
  54.4 0.1 collective-permute-start.2
  54.5 8.3 %project.7 = f32[8,128,512]{2,1,0:T(8,128)S(1)} custom-call(s32[8]{0:T(128)S(1)} %get-tuple-element.40.places_ref, bf16[256,512]{1,0:T(8,128)(2,1)S(1)} %far_apply.1.x_ref, bf16[512,16384]{1,0:T(8,128)(2,1)} %w_ref.9), custom_call_target="tpu_custom_call" | custom-call | flops 1073741824 | bytes 2097152 | tf_op jit(solution)/shard_map/project/pallas_call | solution.py:266
  62.8 0.6 collective-permute-start.4
  63.4 8.3 %project.4 = f32[8,128,512]{2,1,0:T(8,128)S(1)} custom-call(s32[8]{0:T(128)S(1)} %get-tuple-element.39.places_ref, bf16[256,512]{1,0:T(8,128)(2,1)S(1)} %far_apply.1.x_ref, bf16[512,16384]{1,0:T(8,128)(2,1)} %w_ref.9), custom_call_target="tpu_custom_call" | custom-call | flops 1073741824 | bytes 2097152 | tf_op jit(solution)/shard_map/project/pallas_call | solution.py:266
  71.7 8.4 %project.6 = f32[8,128,512]{2,1,0:T(8,128)S(1)} custom-call(s32[8]{0:T(128)S(1)} %get-tuple-element.39.places_ref, bf16[256,512]{1,0:T(8,128)(2,1)S(1)} %far_apply.1.x_ref, bf16[512,16384]{1,0:T(8,128)(2,1)} %w_ref.9), custom_call_target="tpu_custom_call" | custom-call | flops 1073741824 | bytes 2097152 | tf_op jit(solution)/shard_map/project/pallas_call | solution.py:266
  80.2 0.0 collective-permute-done.2
  80.2 1.7 slice_add_fusion.3
  81.8 1.6 collective-permute-start.3
  83.4 0.0 collective-permute-done.4
  83.4 1.8 slice_add_fusion.1
  85.2 0.4 collective-permute-start.5
  85.7 2.2 %copy-done = bf16[2048,1024]{1,0:T(8,128)(2,1)S(1)} copy-done((bf16[2048,1024]{1,0:T(8,128)(2,1)S(1)}, bf16[2048,1024]{1,0:T(8,128)(2,1)}, u32[]{:S(2)}) %copy-start) | copy-done | bytes 4194328
  87.9 11.4 %project_back.1.own_ref = f32[128,512]{1,0:T(8,128)S(1)} custom-call(bf16[16,128,1024]{2,1,0:T(8,128)(2,1)S(1)} %bitcast.13, bf16[512,16384]{1,0:T(8,128)(2,1)} %w_ref.9), custom_call_target="tpu_custom_call" | custom-call | flops 2147483648 | bytes 20971520 | tf_op jit(solution)/shard_map/project_back/pallas_call | solution.py:292
  99.3 8.8 %collective-permute-done.3 = f32[4,128,512]{2,1,0:T(8,128)} collective-permute-done((f32[4,128,512]{2,1,0:T(8,128)}, f32[4,128,512]{2,1,0:T(8,128)}, u32[]{:S(2)}, u32[]{:S(2)}) %collective-permute-start.3) | collective-permute-done | bytes 1048608 | tf_op jit(solution)/shard_map/ppermute | solution.py:22
  108.2 21.6 %collective-permute-done.5 = f32[4,128,512]{2,1,0:T(8,128)} collective-permute-done((f32[4,128,512]{2,1,0:T(8,128)}, f32[4,128,512]{2,1,0:T(8,128)}, u32[]{:S(2)}, u32[]{:S(2)}) %collective-permute-start.5) | collective-permute-done | bytes 1048608 | tf_op jit(solution)/shard_map/ppermute | solution.py:22
  129.8 1.4 slice_add_fusion.7
  131.2 0.7 collective-permute-start.6
  132.0 1.6 slice_add_fusion.5
  133.6 1.4 collective-permute-start.8
  135.0 2.2 %collective-permute-start.10 = (f32[128,512]{1,0:T(8,128)S(1)}, f32[128,512]{1,0:T(8,128)S(1)}, u32[]{:S(2)}, u32[]{:S(2)}) collective-permute-start(f32[128,512]{1,0:T(8,128)S(1)} %project_back.1.own_ref), channel_id=1, source_target_pairs={{0,8},{1,9},{2,10},{3,11},{4,12},{5,13},{6,14},{7,15},{8,0},{9,1},... | collective-permute-start | bytes 786440 | tf_op jit(solution)/shard_map/ppermute | solution.py:22
  137.2 14.6 %collective-permute-done.6 = f32[2,128,512]{2,1,0:T(8,128)S(1)} collective-permute-done((f32[2,128,512]{2,1,0:T(8,128)S(1)}, f32[2,128,512]{2,1,0:T(8,128)S(1)}, u32[]{:S(2)}, u32[]{:S(2)}) %collective-permute-start.6) | collective-permute-done | bytes 524320 | tf_op jit(solution)/shard_map/ppermute | solution.py:22
  151.8 0.8 slice_add_fusion.10
  152.6 1.7 collective-permute-start.7
  154.3 10.8 %collective-permute-done.8 = f32[2,128,512]{2,1,0:T(8,128)S(1)} collective-permute-done((f32[2,128,512]{2,1,0:T(8,128)S(1)}, f32[2,128,512]{2,1,0:T(8,128)S(1)}, u32[]{:S(2)}, u32[]{:S(2)}) %collective-permute-start.8) | collective-permute-done | bytes 524320 | tf_op jit(solution)/shard_map/ppermute | solution.py:22
  165.0 0.8 slice_add_fusion.8
  165.8 0.1 copy-done.13
  165.9 0.1 select_reduce_fusion.inverse_ref
  166.0 0.0 collective-permute-done.10.oth_ref
  166.1 16.8 %gradients.1 = (f32[128,512]{1,0:T(8,128)}, f32[2048,32]{1,0:T(8,128)S(1)}) custom-call(s32[4,32]{1,0:T(4,128)S(1)} %select_reduce_fusion.inverse_ref, s32[1]{0:T(128)} %bitcast.2.high_ref, f32[128,512]{1,0:T(8,128)S(1)} %project_back.1.own_ref, f32[128,512]{1,0:T(8,128)S(1)} %collective-permute-done.10.oth_ref, ...), custom_call_target="tpu_custom_call" | custom-call | tf_op jit(solution)/shard_map/gradients/pallas_call | solution.py:505
  182.8 1.0 copy.14
  183.8 1.1 fusion.3
  184.9 0.0 collective-permute-done.9
  185.0 1.0 fusion.1
  186.0 0.8 pad_maximum_fusion
  (35 shorter events, 0.1 us)
Async XLA Ops:
  7.2 16.3 %copy-start.15 = (s32[16]{0:T(128)S(1)}, s32[16]{0:T(128)}, u32[]{:S(2)}) copy-start(s32[16]{0:T(128)} %constant.12.clone) | copy-start | bytes 196
  7.2 6.2 %copy-start.8 = (s32[4,32]{1,0:T(4,128)S(1)}, s32[4,32]{1,0:T(4,128)}, u32[]{:S(2)}) copy-start(s32[4,32]{1,0:T(4,128)} %orders_ref.1) | copy-start | bytes 1540
  7.2 6.2 %copy-start.1 = (bf16[128,512]{1,0:T(8,128)(2,1)S(1)}, bf16[128,512]{1,0:T(8,128)(2,1)}, u32[]{:S(2)}) copy-start(bf16[128,512]{1,0:T(8,128)(2,1)} %tok_ref.3) | copy-start | bytes 393220
  7.2 78.5 %all-gather.3.cloned.1.call-start = ((), (), s32[]{:S(2)}) async-start(), calls=%async_computation | async-start | bytes 4456448 | tf_op jit(solution)/shard_map/all_gather | solution.py:422
  9.2 18.1 %collective-permute-start.1 = (f32[512,32]{1,0:T(8,128)S(1)}, f32[512,32]{1,0:T(8,128)S(1)}, u32[]{:S(2)}, u32[]{:S(2)}) collective-permute-start(f32[512,32]{1,0:T(8,128)S(1)} %slice_bitcast_fusion.own_ref), channel_id=1, source_target_pairs={{0,8},{1,9},{2,10},{3,11},{4,12},{5,13},{6,14},{7,15},{8,0},{9,1},... | collective-permute-start | bytes 196616 | tf_op jit(solution)/shard_map/ppermute | solution.py:22
  22.6 0.8 copy-start.2
  23.4 21.6 %collective-permute-start = (f32[128,512]{1,0:T(8,128)S(1)}, f32[128,512]{1,0:T(8,128)S(1)}, u32[]{:S(2)}, u32[]{:S(2)}) collective-permute-start(f32[128,512]{1,0:T(8,128)S(1)} %slice_bitcast_fusion.1), channel_id=1, source_target_pairs={{0,8},{1,9},{2,10},{3,11},{4,12},{5,13},{6,14},{7,15},{8,0},{9,1},... | collective-permute-start | bytes 786440 | tf_op jit(solution)/shard_map/ppermute | solution.py:22
  32.7 12.9 %copy-start.4 = (f32[1024,32]{1,0:T(8,128)}, f32[1024,32]{1,0:T(8,128)S(1)}, u32[]{:S(2)}) copy-start(f32[1024,32]{1,0:T(8,128)S(1)} %get-tuple-element.21.inv_far_ref) | copy-start | bytes 393220
  32.7 12.9 %copy-start.6 = (f32[2,512,128]{2,1,0:T(8,128)}, f32[2,512,128]{2,1,0:T(8,128)S(1)}, u32[]{:S(2)}) copy-start(f32[2,512,128]{2,1,0:T(8,128)S(1)} %get-tuple-element.20.bfar_ref) | copy-start | bytes 1572868
  54.4 25.7 %collective-permute-start.2 = (f32[8,128,512]{2,1,0:T(8,128)S(1)}, f32[8,128,512]{2,1,0:T(8,128)S(1)}, u32[]{:S(2)}, u32[]{:S(2)}) collective-permute-start(f32[8,128,512]{2,1,0:T(8,128)S(1)} %project.5), channel_id=1, source_target_pairs={{0,1},{1,0},{2,3},{3,2},{4,5},{5,4},{6,7},{7,6},{8,9},{9,8},{10,11... | collective-permute-start | bytes 6291464 | tf_op jit(solution)/shard_map/ppermute | solution.py:22
  62.8 20.6 %collective-permute-start.4 = (f32[8,128,512]{2,1,0:T(8,128)S(1)}, f32[8,128,512]{2,1,0:T(8,128)S(1)}, u32[]{:S(2)}, u32[]{:S(2)}) collective-permute-start(f32[8,128,512]{2,1,0:T(8,128)S(1)} %project.7), channel_id=1, source_target_pairs={{0,1},{1,0},{2,3},{3,2},{4,5},{5,4},{6,7},{7,6},{8,9},{9,8},{10,11... | collective-permute-start | bytes 6291464 | tf_op jit(solution)/shard_map/ppermute | solution.py:22
  81.8 26.3 %collective-permute-start.3 = (f32[4,128,512]{2,1,0:T(8,128)}, f32[4,128,512]{2,1,0:T(8,128)}, u32[]{:S(2)}, u32[]{:S(2)}) collective-permute-start(f32[4,128,512]{2,1,0:T(8,128)} %get-tuple-element.32), channel_id=1, source_target_pairs={{0,2},{1,3},{2,0},{3,1},{4,6},{5,7},{6,4},{7,5},{8,10},{9,11},{10,... | collective-permute-start | bytes 3145736 | tf_op jit(solution)/shard_map/ppermute | solution.py:22
  85.2 44.6 %collective-permute-start.5 = (f32[4,128,512]{2,1,0:T(8,128)}, f32[4,128,512]{2,1,0:T(8,128)}, u32[]{:S(2)}, u32[]{:S(2)}) collective-permute-start(f32[4,128,512]{2,1,0:T(8,128)} %get-tuple-element.33), channel_id=1, source_target_pairs={{0,2},{1,3},{2,0},{3,1},{4,6},{5,7},{6,4},{7,5},{8,10},{9,11},{10,... | collective-permute-start | bytes 3145736 | tf_op jit(solution)/shard_map/ppermute | solution.py:22
  85.7 2.2 %copy-start = (bf16[2048,1024]{1,0:T(8,128)(2,1)S(1)}, bf16[2048,1024]{1,0:T(8,128)(2,1)}, u32[]{:S(2)}) copy-start(bf16[2048,1024]{1,0:T(8,128)(2,1)} %all-gather.3.cloned.1.call-done) | copy-start | bytes 12582916
  99.3 32.7 %copy-start.9 = (f32[4,128,512]{2,1,0:T(8,128)S(1)}, f32[4,128,512]{2,1,0:T(8,128)}, u32[]{:S(2)}) copy-start(f32[4,128,512]{2,1,0:T(8,128)} %get-tuple-element.34) | copy-start | bytes 3145732
  131.2 20.5 %collective-permute-start.6 = (f32[2,128,512]{2,1,0:T(8,128)S(1)}, f32[2,128,512]{2,1,0:T(8,128)S(1)}, u32[]{:S(2)}, u32[]{:S(2)}) collective-permute-start(f32[2,128,512]{2,1,0:T(8,128)S(1)} %get-tuple-element.36), channel_id=1, source_target_pairs={{0,4},{1,5},{2,6},{3,7},{4,0},{5,1},{6,2},{7,3},{8,12},{9,13},{10,... | collective-permute-start | bytes 1572872 | tf_op jit(solution)/shard_map/ppermute | solution.py:22
  132.0 34.0 %copy-start.3 = (f32[1024,128]{1,0:T(8,128)S(1)}, f32[1024,128]{1,0:T(8,128)}, u32[]{:S(2)}) copy-start(f32[1024,128]{1,0:T(8,128)} %copy-done.2) | copy-start | bytes 1572868
  132.0 34.1 %copy-start.5 = (f32[1024,32]{1,0:T(8,128)S(1)}, f32[1024,32]{1,0:T(8,128)}, u32[]{:S(2)}) copy-start(f32[1024,32]{1,0:T(8,128)} %copy-done.4) | copy-start | bytes 393220
  132.0 34.1 %copy-start.7 = (f32[2,512,128]{2,1,0:T(8,128)S(1)}, f32[2,512,128]{2,1,0:T(8,128)}, u32[]{:S(2)}) copy-start(f32[2,512,128]{2,1,0:T(8,128)} %copy-done.6) | copy-start | bytes 1572868
  133.6 32.5 %copy-start.10 = (f32[2,128,512]{2,1,0:T(8,128)}, f32[2,128,512]{2,1,0:T(8,128)S(1)}, u32[]{:S(2)}) copy-start(f32[2,128,512]{2,1,0:T(8,128)S(1)} %get-tuple-element.37) | copy-start | bytes 1572868
  133.6 31.5 %collective-permute-start.8 = (f32[2,128,512]{2,1,0:T(8,128)S(1)}, f32[2,128,512]{2,1,0:T(8,128)S(1)}, u32[]{:S(2)}, u32[]{:S(2)}) collective-permute-start(f32[2,128,512]{2,1,0:T(8,128)S(1)} %get-tuple-element.38), channel_id=1, source_target_pairs={{0,4},{1,5},{2,6},{3,7},{4,0},{5,1},{6,2},{7,3},{8,12},{9,13},{10,... | collective-permute-start | bytes 1572872 | tf_op jit(solution)/shard_map/ppermute | solution.py:22
  135.0 31.0 %collective-permute-start.10 = (f32[128,512]{1,0:T(8,128)S(1)}, f32[128,512]{1,0:T(8,128)S(1)}, u32[]{:S(2)}, u32[]{:S(2)}) collective-permute-start(f32[128,512]{1,0:T(8,128)S(1)} %project_back.1.own_ref), channel_id=1, source_target_pairs={{0,8},{1,9},{2,10},{3,11},{4,12},{5,13},{6,14},{7,15},{8,0},{9,1},... | collective-permute-start | bytes 786440 | tf_op jit(solution)/shard_map/ppermute | solution.py:22
  151.8 31.0 %copy-start.12 = (f32[2,128,512]{2,1,0:T(8,128)}, f32[2,128,512]{2,1,0:T(8,128)S(1)}, u32[]{:S(2)}) copy-start(f32[2,128,512]{2,1,0:T(8,128)S(1)} %collective-permute-done.6) | copy-start | bytes 1572868
  152.6 31.2 %collective-permute-start.7 = (f32[1,128,512]{2,1,0:T(8,128)}, f32[1,128,512]{2,1,0:T(8,128)}, u32[]{:S(2)}, u32[]{:S(2)}) collective-permute-start(f32[1,128,512]{2,1,0:T(8,128)} %slice_add_fusion.10), channel_id=1, source_target_pairs={{0,8},{1,9},{2,10},{3,11},{4,12},{5,13},{6,14},{7,15},{8,0},{9,1},... | collective-permute-start | bytes 786440 | tf_op jit(solution)/shard_map/ppermute | solution.py:22
  165.0 0.9 copy-start.13
  165.9 19.0 %collective-permute-start.9 = (f32[1,128,512]{2,1,0:T(8,128)}, f32[1,128,512]{2,1,0:T(8,128)}, u32[]{:S(2)}, u32[]{:S(2)}) collective-permute-start(f32[1,128,512]{2,1,0:T(8,128)} %slice_add_fusion.8), channel_id=1, source_target_pairs={{0,8},{1,9},{2,10},{3,11},{4,12},{5,13},{6,14},{7,15},{8,0},{9,1},... | collective-permute-start | bytes 786440 | tf_op jit(solution)/shard_map/ppermute | solution.py:22
  182.8 2.1 %copy-start.11 = (f32[2,128,512]{2,1,0:T(8,128)S(1)}, f32[2,128,512]{2,1,0:T(8,128)}, u32[]{:S(2)}) copy-start(f32[2,128,512]{2,1,0:T(8,128)} %copy-done.10) | copy-start | bytes 1572868
  182.8 2.1 %copy-start.14 = (f32[2,128,512]{2,1,0:T(8,128)S(1)}, f32[2,128,512]{2,1,0:T(8,128)}, u32[]{:S(2)}) copy-start(f32[2,128,512]{2,1,0:T(8,128)} %copy-done.13) | copy-start | bytes 1572868
Sparse Core Ops, SparseCore 0:
  10.2 61.0 all-gather.2

commit v3 on v2

--- a/solution.py
+++ b/solution.py
@@ -9,7 +9,7 @@
 from jax.sharding import PartitionSpec as P
 
 VMEM_LIMIT = 16 * 2**20
-WIDE_LIMIT = 40 * 2**20
+WIDE_LIMIT = 50 * 2**20
 GROUP = 128
 NN = (((1,), (0,)), ((), ()))
 NT = (((1,), (1,)), ((), ()))
@@ -246,16 +246,19 @@
         )
 
 
-def project_kernel(chunk, places_ref, x_ref, w_ref, out_ref):
+def project_kernel(chunk, places_ref, x_ref, w_ref, out_ref, held_ref, sems):
     pieces, count, width = out_ref.shape
 
-    def body(p, _):
+    def fetch(p):
         at = pl.multiple_of((places_ref[p] * CHUNKS + chunk) * width, width)
-        both = one_dot(x_ref[...], w_ref[:, pl.ds(at, width)])
+        return pltpu.make_async_copy(w_ref.at[:, pl.ds(at, width)], held_ref.at[p], sems.at[p])
+
+    for p in range(pieces):
+        fetch(p).start()
+    for p in range(pieces):
+        fetch(p).wait()
+        both = one_dot(x_ref[...], held_ref[p])
         out_ref[p] = both[:count] + both[count:]
-        return 0
-
-    lax.fori_loop(0, pieces, body, 0)
 
 
 def project(x_both, weight, places, chunk):
@@ -266,23 +269,45 @@
     return pl.pallas_call(
         functools.partial(project_kernel, chunk),
         out_shape=jax.ShapeDtypeStruct((pieces, count, width), jnp.float32),
-        in_specs=[pl.BlockSpec(memory_space=pltpu.SMEM)] + [pl.BlockSpec(memory_space=pltpu.VMEM)] * 2,
+        in_specs=[
+            pl.BlockSpec(memory_space=pltpu.SMEM),
+            pl.BlockSpec(memory_space=pltpu.VMEM),
+            pl.BlockSpec(memory_space=pl.ANY),
+        ],
         out_specs=pl.BlockSpec(memory_space=pltpu.VMEM),
+        scratch_shapes=[
+            pltpu.VMEM((pieces, rows, width), weight.dtype),
+            pltpu.SemaphoreType.DMA((pieces,)),
+        ],
         compiler_params=pltpu.CompilerParams(vmem_limit_bytes=WIDE_LIMIT),
         cost_estimate=pl.CostEstimate(
             flops=2 * count2 * rows * width * pieces,
-            bytes_accessed=pieces * width * 4 * count,
+            bytes_accessed=pieces * width * (2 * rows + 4 * count),
             transcendentals=0,
         ),
         name="project",
     )(places, x_both, weight)
 
 
-def back_kernel(cot_ref, w_ref, out_ref):
-    pieces, count, width = cot_ref.shape
+def back_kernel(cot_ref, w_ref, out_ref, cots_ref, held_ref, cot_sems, sems):
+    pieces, _, width = cot_ref.shape
+
+    def fetches(p):
+        return (
+            pltpu.make_async_copy(cot_ref.at[p], cots_ref.at[p], cot_sems.at[p]),
+            pltpu.make_async_copy(
+                w_ref.at[:, pl.ds(p * width, width)], held_ref.at[p], sems.at[p]
+            ),
+        )
+
+    for p in range(pieces):
+        for copy in fetches(p):
+            copy.start()
     total = jnp.zeros(out_ref.shape, jnp.float32)
     for p in range(pieces):
-        total += one_dot(cot_ref[p], w_ref[:, p * width : (p + 1) * width], NT)
+        for copy in fetches(p):
+            copy.wait()
+        total += one_dot(cots_ref[p], held_ref[p], NT)
     out_ref[...] = total
 
 
@@ -292,8 +317,14 @@
     return pl.pallas_call(
         back_kernel,
         out_shape=jax.ShapeDtypeStruct((count, rows), jnp.float32),
-        in_specs=[pl.BlockSpec(memory_space=pltpu.VMEM)] * 2,
+        in_specs=[pl.BlockSpec(memory_space=pl.ANY)] * 2,
         out_specs=pl.BlockSpec(memory_space=pltpu.VMEM),
+        scratch_shapes=[
+            pltpu.VMEM((pieces, count, width), gathered.dtype),
+            pltpu.VMEM((pieces, rows, width), weight.dtype),
+            pltpu.SemaphoreType.DMA((pieces,)),
+            pltpu.SemaphoreType.DMA((pieces,)),
+        ],
         compiler_params=pltpu.CompilerParams(vmem_limit_bytes=WIDE_LIMIT),
         cost_estimate=pl.CostEstimate(
             flops=2 * count * rows * width * pieces,
@@ -489,38 +520,40 @@
         mid = keep.shape[0] // 2
         return keep[mid:] + got[mid:], keep[:mid] + got[:mid]
 
+    numbers = jnp.arange(block, dtype=jnp.int32)
+    inverse = jnp.sum(
+        jnp.where(orders[:, :, None] == numbers[None, None, :], numbers[None, :, None], 0), axis=1
+    ).astype(jnp.int32)
     for bit in range(bits):
         gots = [exchange(send, bit) for send, _ in outs]
         if bit == min(1, bits - 1):
             grad_cols = project_back(gathered, weight)
-            grad_cols, *gots = lax.optimization_barrier([grad_cols] + gots)
+            grad_cols, gots[0] = lax.optimization_barrier((grad_cols, gots[0]))
             grad_other = exchange(grad_cols, pair_bit)
+            grad_tokens, grad_gens = pl.pallas_call(
+                grads_kernel,
+                out_shape=(
+                    jax.ShapeDtypeStruct((count, rows), f32),
+                    jax.ShapeDtypeStruct((sections * rows, block), f32),
+                ),
+                in_specs=[scalars, scalars] + [full] * 9,
+                out_specs=(full,) * 2,
+                scratch_shapes=[
+                    pltpu.VMEM((sections * rows, block), f32),
+                    pltpu.VMEM((sections * rows, block), f32),
+                    pltpu.VMEM((sections * rows, block), f32),
+                    pltpu.VMEM(square, f32),
+                    pltpu.VMEM(square, f32),
+                    pltpu.VMEM(square, f32),
+                ],
+                compiler_params=params,
+                name="gradients",
+            )(inverse, high, grad_cols, grad_other, x_other, tokens, xs, near, bfar, inv_far, inv)
+            grad_tokens, grad_gens, gots[-1] = lax.optimization_barrier(
+                (grad_tokens, grad_gens, gots[-1])
+            )
         outs = [stage(pair, got) for pair, got in zip(outs, gots)]
     outputs = jnp.concatenate([keep[0] for _, keep in outs], axis=1)
-
-    numbers = jnp.arange(block, dtype=jnp.int32)
-    inverse = jnp.sum(
-        jnp.where(orders[:, :, None] == numbers[None, None, :], numbers[None, :, None], 0), axis=1
-    ).astype(jnp.int32)
-    grad_tokens, grad_gens = pl.pallas_call(
-        grads_kernel,
-        out_shape=(
-            jax.ShapeDtypeStruct((count, rows), f32),
-            jax.ShapeDtypeStruct((sections * rows, block), f32),
-        ),
-        in_specs=[scalars, scalars] + [full] * 9,
-        out_specs=(full,) * 2,
-        scratch_shapes=[
-            pltpu.VMEM((sections * rows, block), f32),
-            pltpu.VMEM((sections * rows, block), f32),
-            pltpu.VMEM((sections * rows, block), f32),
-            pltpu.VMEM(square, f32),
-            pltpu.VMEM(square, f32),
-            pltpu.VMEM(square, f32),
-        ],
-        compiler_params=params,
-        name="gradients",
-    )(inverse, high, grad_cols, grad_other, x_other, tokens, xs, near, bfar, inv_far, inv)
     return outputs, grad_tokens, grad_gens.reshape(sections, rows, block)
 
 

time: 194 us -> 165 us (0.85)
  Pallas kernels: 77.2 us -> 56.3 us
  waiting for transfers between devices: 72.6 us -> 65 us
    pallas_call x4, Pallas kernels: 33.8 us -> 16.4 us  [project(): pl.pallas_call(functools.partial(project_kernel, chunk), out_shape=jax.Sh...]
    ppermute x11, waiting for transfers between devices: 71.9 us -> 62.8 us  [exchange(): lax.ppermute(array, 'tensor', [(i, i ^ 1 << bit) for i in range(size)])]
    pallas_call x1, Pallas kernels: 11.4 us -> 8.11 us  [project_back(): pl.pallas_call(back_kernel, out_shape=jax.ShapeDtypeStruct((count, rows),...]
    unnamed x34 -> x30, local copies, waits for them, and re-layouts: 5.39 us -> 3.89 us
  transfers between devices with their start and end apart: 12 -> 12, of which waited for: 6 -> 7; matrix products, arithmetic and copies ran while one was open for 5% -> 7% of each run, Pallas kernels for 40% -> 34%
where the time goes in v3:
time: 165 us; the launch traced here: 164 us
  waiting for transfers between devices  65 us (39%)
  Pallas kernels  56.3 us (34%)
  between operations  14.3 us (9%)
  starting transfers between devices  13.1 us (8%)
  other arithmetic  11.5 us (7%)
  local copies, waits for them, and re-layouts  4 us (2%)
    ppermute x11, waiting for transfers between devices, exchange(): lax.ppermute(array, 'tensor', [(i, i ^ 1 << bit) for i in range(size)])  62.8 us
    pallas_call x1, Pallas kernels, local(): pl.pallas_call(grads_kernel, out_shape=(jax.ShapeDtypeStruct((count, rows...  16.5 us
    pallas_call x4, Pallas kernels, project(): pl.pallas_call(functools.partial(project_kernel, chunk), out_shape=jax.Sh...  16.4 us
    ppermute x11, starting transfers between devices, exchange(): lax.ppermute(array, 'tensor', [(i, i ^ 1 << bit) for i in range(size)])  13 us
    pallas_call x1, Pallas kernels, local(): pl.pallas_call(near_kernel, out_shape=(jax.ShapeDtypeStruct(square, f32),...  9.18 us
    add x6, other arithmetic, stage(): return (keep[mid:] + got[mid:], keep[:mid] + got[:mid])  8.56 us
    pallas_call x1, Pallas kernels, project_back(): pl.pallas_call(back_kernel, out_shape=jax.ShapeDtypeStruct((count, rows),...  8.11 us
    pallas_call x1, Pallas kernels, local(): pl.pallas_call(far_rotations_kernel, out_shape=(jax.ShapeDtypeStruct(far_...  5.51 us
  transfers between devices with their start and end apart: 12, of which 7 were waited for; matrix products, arithmetic and copies ran while one was open for 7% of the time, Pallas kernels for 34%

profile of v3, /device:TPU:0, one launch (start us, length us, event | category | flops | bytes accessed | tf_op | source)
XLA Modules:
  0.0 164.2 jit_solution(6505515609389752840)
XLA Ops:
  7.2 0.0 copy-start.13
  7.2 0.0 all-gather.3.cloned.1.call-start
  7.2 0.7 all-gather.3.cloned.1.call-update
  7.9 1.3 copy.12
  9.2 4.1 %collective-permute-start.1 = (f32[512,32]{1,0:T(8,128)S(1)}, f32[512,32]{1,0:T(8,128)S(1)}, u32[]{:S(2)}, u32[]{:S(2)}) collective-permute-start(f32[512,32]{1,0:T(8,128)S(1)} %slice_bitcast_fusion.own_ref), channel_id=1, source_target_pairs={{0,8},{1,9},{2,10},{3,11},{4,12},{5,13},{6,14},{7,15},{8,0},{9,1},... | collective-permute-start | bytes 196616 | tf_op jit(solution)/shard_map/ppermute | solution.py:22
  13.4 9.2 %near_rotations.1 = (f32[1024,128]{1,0:T(8,128)S(1)}, f32[3,512,128]{2,1,0:T(8,128)S(1)}, f32[3,128,512]{2,1,0:T(8,128)S(1)}) custom-call(s32[4,32]{1,0:T(4,128)S(1)} %copy-done.7, f32[2048,32]{1,0:T(8,128)S(1)} %bitcast.12, bf16[128,512]{1,0:T(8,128)(2,1)S(1)} %copy-done), custom_call_target="tpu_custom_call" | custom-call | tf_op jit(solution)/shard_map/near_rotations/pallas_call | solution.py:457
  22.5 0.8 copy-done.1
  23.4 0.1 collective-permute-start
  23.5 0.1 fusion.4
  23.6 3.8 %collective-permute-done.1.far_ref = f32[512,32]{1,0:T(8,128)S(1)} collective-permute-done((f32[512,32]{1,0:T(8,128)S(1)}, f32[512,32]{1,0:T(8,128)S(1)}, u32[]{:S(2)}, u32[]{:S(2)}) %collective-permute-start.1) | collective-permute-done | bytes 65568 | tf_op jit(solution)/shard_map/ppermute | solution.py:22
  27.4 5.5 %far_rotations.1 = (f32[1024,32]{1,0:T(8,128)S(1)}, f32[2,512,128]{2,1,0:T(8,128)S(1)}, f32[2,512,128]{2,1,0:T(8,128)S(1)}) custom-call(s32[1,32]{1,0:T(1,128)S(1)} %slice.92.orders_ref, s32[1]{0:T(128)} %bitcast.2.high_ref, f32[512,32]{1,0:T(8,128)S(1)} %slice_bitcast_fusion.own_ref, f32[512,32]{1,0:T(8,128)S(1)} %collective-permute-done.1.far_ref), custom_call_target="tpu_custom_call" | custom-call | flops 10000000 | bytes 10000000 | tf_op jit(solution)/shard_map/far_rotations/pallas_call | solution.py:477
  32.9 0.0 copy-start.5
  32.9 12.1 %collective-permute-done.oth_ref.x_oth_ref = f32[128,512]{1,0:T(8,128)S(1)} collective-permute-done((f32[128,512]{1,0:T(8,128)S(1)}, f32[128,512]{1,0:T(8,128)S(1)}, u32[]{:S(2)}, u32[]{:S(2)}) %collective-permute-start) | collective-permute-done | bytes 262176 | tf_op jit(solution)/shard_map/ppermute | solution.py:22
  45.0 0.7 far_apply.1.x_ref
  45.7 4.1 %project.5 = f32[8,128,512]{2,1,0:T(8,128)S(1)} custom-call(s32[8]{0:T(128)S(1)} %get-tuple-element.44.places_ref, bf16[256,512]{1,0:T(8,128)(2,1)S(1)} %far_apply.1.x_ref, bf16[512,16384]{1,0:T(8,128)(2,1)} %w_ref.9), custom_call_target="tpu_custom_call" | custom-call | flops 1073741824 | bytes 6291456 | tf_op jit(solution)/shard_map/project/pallas_call | solution.py:269
  49.7 0.1 collective-permute-start.2
  49.8 4.1 %project.7 = f32[8,128,512]{2,1,0:T(8,128)S(1)} custom-call(s32[8]{0:T(128)S(1)} %get-tuple-element.44.places_ref, bf16[256,512]{1,0:T(8,128)(2,1)S(1)} %far_apply.1.x_ref, bf16[512,16384]{1,0:T(8,128)(2,1)} %w_ref.9), custom_call_target="tpu_custom_call" | custom-call | flops 1073741824 | bytes 6291456 | tf_op jit(solution)/shard_map/project/pallas_call | solution.py:269
  53.9 0.6 collective-permute-start.6
  54.5 4.1 %project.4 = f32[8,128,512]{2,1,0:T(8,128)S(1)} custom-call(s32[8]{0:T(128)S(1)} %get-tuple-element.43.places_ref, bf16[256,512]{1,0:T(8,128)(2,1)S(1)} %far_apply.1.x_ref, bf16[512,16384]{1,0:T(8,128)(2,1)} %w_ref.9), custom_call_target="tpu_custom_call" | custom-call | flops 1073741824 | bytes 6291456 | tf_op jit(solution)/shard_map/project/pallas_call | solution.py:269
  58.6 4.1 %project.6 = f32[8,128,512]{2,1,0:T(8,128)S(1)} custom-call(s32[8]{0:T(128)S(1)} %get-tuple-element.43.places_ref, bf16[256,512]{1,0:T(8,128)(2,1)S(1)} %far_apply.1.x_ref, bf16[512,16384]{1,0:T(8,128)(2,1)} %w_ref.9), custom_call_target="tpu_custom_call" | custom-call | flops 1073741824 | bytes 6291456 | tf_op jit(solution)/shard_map/project/pallas_call | solution.py:269
  62.7 0.0 collective-permute-done.2
  62.7 3.1 %slice_add_fusion.3 = (f32[4,128,512]{2,1,0:T(8,128)S(1)}, f32[4,128,512]{2,1,0:T(8,128)}) fusion(f32[8,128,512]{2,1,0:T(8,128)} %collective-permute-done.2, f32[8,128,512]{2,1,0:T(8,128)S(1)} %project.4), kind=kLoop, calls=%fused_computation.3 | loop fusion | flops 524288 | bytes 6291456 | tf_op jit(solution)/shard_map/add | solution.py:521
  65.8 1.6 collective-permute-start.3
  67.4 0.0 collective-permute-done.6
  67.4 1.9 %slice_add_fusion = (f32[4,128,512]{2,1,0:T(8,128)}, f32[4,128,512]{2,1,0:T(8,128)}) fusion(f32[8,128,512]{2,1,0:T(8,128)S(1)} %collective-permute-done.6, f32[8,128,512]{2,1,0:T(8,128)S(1)} %project.6), kind=kLoop, calls=%fused_computation | loop fusion | flops 524288 | bytes 6291456 | tf_op jit(solution)/shard_map/add | solution.py:521
  69.2 0.5 collective-permute-start.8
  69.7 0.1 select_reduce_fusion.inverse_ref
  69.8 1.6 all-gather.3.cloned.1.call-done
  71.4 8.1 %project_back.1.own_ref = f32[128,512]{1,0:T(8,128)S(1)} custom-call(bf16[16,128,1024]{2,1,0:T(8,128)(2,1)} %bitcast.14, bf16[512,16384]{1,0:T(8,128)(2,1)} %w_ref.9), custom_call_target="tpu_custom_call" | custom-call | flops 2147483648 | bytes 20971520 | tf_op jit(solution)/shard_map/project_back/pallas_call | solution.py:317
  79.5 0.0 copy-start.6
  79.5 12.6 %collective-permute-done.3 = f32[4,128,512]{2,1,0:T(8,128)} collective-permute-done((f32[4,128,512]{2,1,0:T(8,128)}, f32[4,128,512]{2,1,0:T(8,128)}, u32[]{:S(2)}, u32[]{:S(2)}) %collective-permute-start.3) | collective-permute-done | bytes 1048608 | tf_op jit(solution)/shard_map/ppermute | solution.py:22
  92.2 1.4 slice_add_fusion.7
  93.6 4.1 %collective-permute-start.4 = (f32[2,128,512]{2,1,0:T(8,128)S(1)}, f32[2,128,512]{2,1,0:T(8,128)S(1)}, u32[]{:S(2)}, u32[]{:S(2)}) collective-permute-start(f32[2,128,512]{2,1,0:T(8,128)S(1)} %get-tuple-element.40), channel_id=1, source_target_pairs={{0,4},{1,5},{2,6},{3,7},{4,0},{5,1},{6,2},{7,3},{8,12},{9,13},{10,... | collective-permute-start | bytes 1572872 | tf_op jit(solution)/shard_map/ppermute | solution.py:22
  97.7 7.4 %collective-permute-done.7.oth_ref = f32[128,512]{1,0:T(8,128)S(1)} collective-permute-done((f32[128,512]{1,0:T(8,128)S(1)}, f32[128,512]{1,0:T(8,128)S(1)}, u32[]{:S(2)}, u32[]{:S(2)}) %collective-permute-start.7) | collective-permute-done | bytes 262176 | tf_op jit(solution)/shard_map/ppermute | solution.py:22
  105.2 16.5 %gradients.1 = (f32[128,512]{1,0:T(8,128)}, f32[2048,32]{1,0:T(8,128)S(1)}) custom-call(s32[4,32]{1,0:T(4,128)S(1)} %select_reduce_fusion.inverse_ref, s32[1]{0:T(128)} %bitcast.2.high_ref, f32[128,512]{1,0:T(8,128)S(1)} %project_back.1.own_ref, f32[128,512]{1,0:T(8,128)S(1)} %collective-permute-done.7.oth_ref, ...), custom_call_target="tpu_custom_call" | custom-call | tf_op jit(solution)/shard_map/gradients/pallas_call | solution.py:533
  121.7 1.4 slice_add_fusion.5
  123.1 0.1 collective-permute-start.9
  123.2 0.0 copy-start.11
  123.2 0.7 copy-done.11
  124.0 1.7 %collective-permute-start.5 = (f32[1,128,512]{2,1,0:T(8,128)S(1)}, f32[1,128,512]{2,1,0:T(8,128)}, u32[]{:S(2)}, u32[]{:S(2)}) collective-permute-start(f32[1,128,512]{2,1,0:T(8,128)S(1)} %slice_add_fusion.10), channel_id=1, source_target_pairs={{0,8},{1,9},{2,10},{3,11},{4,12},{5,13},{6,14},{7,15},{8,0},{9,1},... | collective-permute-start | bytes 786440 | tf_op jit(solution)/shard_map/ppermute | solution.py:22
  125.7 15.9 %collective-permute-done.9 = f32[2,128,512]{2,1,0:T(8,128)S(1)} collective-permute-done((f32[2,128,512]{2,1,0:T(8,128)S(1)}, f32[2,128,512]{2,1,0:T(8,128)S(1)}, u32[]{:S(2)}, u32[]{:S(2)}) %collective-permute-start.9) | collective-permute-done | bytes 524320 | tf_op jit(solution)/shard_map/ppermute | solution.py:22
  141.6 0.7 slice_add_fusion.8
  142.3 0.2 collective-permute-start.10
  142.5 1.0 copy.14
  143.6 1.0 fusion.3
  144.6 11.0 %collective-permute-done.10 = f32[1,128,512]{2,1,0:T(8,128)} collective-permute-done((f32[1,128,512]{2,1,0:T(8,128)}, f32[1,128,512]{2,1,0:T(8,128)}, u32[]{:S(2)}, u32[]{:S(2)}) %collective-permute-start.10) | collective-permute-done | bytes 262176 | tf_op jit(solution)/shard_map/ppermute | solution.py:22
  155.6 1.0 fusion.1
  156.6 0.8 pad_maximum_fusion
  (31 shorter events, 0.1 us)
Async XLA Ops:
  7.2 16.3 %copy-start.13 = (s32[16]{0:T(128)S(1)}, s32[16]{0:T(128)}, u32[]{:S(2)}) copy-start(s32[16]{0:T(128)} %constant.12.clone) | copy-start | bytes 196
  7.2 6.2 %copy-start.7 = (s32[4,32]{1,0:T(4,128)S(1)}, s32[4,32]{1,0:T(4,128)}, u32[]{:S(2)}) copy-start(s32[4,32]{1,0:T(4,128)} %orders_ref.1) | copy-start | bytes 1540
  7.2 6.2 %copy-start = (bf16[128,512]{1,0:T(8,128)(2,1)S(1)}, bf16[128,512]{1,0:T(8,128)(2,1)}, u32[]{:S(2)}) copy-start(bf16[128,512]{1,0:T(8,128)(2,1)} %tok_ref.3) | copy-start | bytes 393220
  7.2 64.2 %all-gather.3.cloned.1.call-start = ((), (), s32[]{:S(2)}) async-start(), calls=%async_computation | async-start | bytes 4456448 | tf_op jit(solution)/shard_map/all_gather | solution.py:453
  9.2 18.1 %collective-permute-start.1 = (f32[512,32]{1,0:T(8,128)S(1)}, f32[512,32]{1,0:T(8,128)S(1)}, u32[]{:S(2)}, u32[]{:S(2)}) collective-permute-start(f32[512,32]{1,0:T(8,128)S(1)} %slice_bitcast_fusion.own_ref), channel_id=1, source_target_pairs={{0,8},{1,9},{2,10},{3,11},{4,12},{5,13},{6,14},{7,15},{8,0},{9,1},... | collective-permute-start | bytes 196616 | tf_op jit(solution)/shard_map/ppermute | solution.py:22
  22.5 0.8 copy-start.1
  23.4 21.6 %collective-permute-start = (f32[128,512]{1,0:T(8,128)S(1)}, f32[128,512]{1,0:T(8,128)S(1)}, u32[]{:S(2)}, u32[]{:S(2)}) collective-permute-start(f32[128,512]{1,0:T(8,128)S(1)} %slice_bitcast_fusion.1), channel_id=1, source_target_pairs={{0,8},{1,9},{2,10},{3,11},{4,12},{5,13},{6,14},{7,15},{8,0},{9,1},... | collective-permute-start | bytes 786440 | tf_op jit(solution)/shard_map/ppermute | solution.py:22
  32.9 12.8 %copy-start.3 = (f32[1024,32]{1,0:T(8,128)}, f32[1024,32]{1,0:T(8,128)S(1)}, u32[]{:S(2)}) copy-start(f32[1024,32]{1,0:T(8,128)S(1)} %get-tuple-element.22.inv_far_ref) | copy-start | bytes 393220
  32.9 12.8 %copy-start.5 = (f32[2,512,128]{2,1,0:T(8,128)}, f32[2,512,128]{2,1,0:T(8,128)S(1)}, u32[]{:S(2)}) copy-start(f32[2,512,128]{2,1,0:T(8,128)S(1)} %get-tuple-element.21.bfar_ref) | copy-start | bytes 1572868
  49.7 12.9 %collective-permute-start.2 = (f32[8,128,512]{2,1,0:T(8,128)S(1)}, f32[8,128,512]{2,1,0:T(8,128)}, u32[]{:S(2)}, u32[]{:S(2)}) collective-permute-start(f32[8,128,512]{2,1,0:T(8,128)S(1)} %project.5), channel_id=1, source_target_pairs={{0,1},{1,0},{2,3},{3,2},{4,5},{5,4},{6,7},{7,6},{8,9},{9,8},{10,11... | collective-permute-start | bytes 6291464 | tf_op jit(solution)/shard_map/ppermute | solution.py:22
  53.9 13.5 %collective-permute-start.6 = (f32[8,128,512]{2,1,0:T(8,128)S(1)}, f32[8,128,512]{2,1,0:T(8,128)S(1)}, u32[]{:S(2)}, u32[]{:S(2)}) collective-permute-start(f32[8,128,512]{2,1,0:T(8,128)S(1)} %project.7), channel_id=1, source_target_pairs={{0,1},{1,0},{2,3},{3,2},{4,5},{5,4},{6,7},{7,6},{8,9},{9,8},{10,11... | collective-permute-start | bytes 6291464 | tf_op jit(solution)/shard_map/ppermute | solution.py:22
  65.8 26.3 %collective-permute-start.3 = (f32[4,128,512]{2,1,0:T(8,128)}, f32[4,128,512]{2,1,0:T(8,128)}, u32[]{:S(2)}, u32[]{:S(2)}) collective-permute-start(f32[4,128,512]{2,1,0:T(8,128)} %get-tuple-element.36), channel_id=1, source_target_pairs={{0,2},{1,3},{2,0},{3,1},{4,6},{5,7},{6,4},{7,5},{8,10},{9,11},{10,... | collective-permute-start | bytes 3145736 | tf_op jit(solution)/shard_map/ppermute | solution.py:22
  69.2 52.4 %collective-permute-start.8 = (f32[4,128,512]{2,1,0:T(8,128)}, f32[4,128,512]{2,1,0:T(8,128)}, u32[]{:S(2)}, u32[]{:S(2)}) collective-permute-start(f32[4,128,512]{2,1,0:T(8,128)} %get-tuple-element.37), channel_id=1, source_target_pairs={{0,2},{1,3},{2,0},{3,1},{4,6},{5,7},{6,4},{7,5},{8,10},{9,11},{10,... | collective-permute-start | bytes 3145736 | tf_op jit(solution)/shard_map/ppermute | solution.py:22
  79.5 25.7 %copy-start.2 = (f32[1024,128]{1,0:T(8,128)S(1)}, f32[1024,128]{1,0:T(8,128)}, u32[]{:S(2)}) copy-start(f32[1024,128]{1,0:T(8,128)} %copy-done.1) | copy-start | bytes 1572868
  79.5 25.6 %copy-start.4 = (f32[1024,32]{1,0:T(8,128)S(1)}, f32[1024,32]{1,0:T(8,128)}, u32[]{:S(2)}) copy-start(f32[1024,32]{1,0:T(8,128)} %copy-done.3) | copy-start | bytes 393220
  79.5 25.6 %copy-start.6 = (f32[2,512,128]{2,1,0:T(8,128)S(1)}, f32[2,512,128]{2,1,0:T(8,128)}, u32[]{:S(2)}) copy-start(f32[2,512,128]{2,1,0:T(8,128)} %copy-done.5) | copy-start | bytes 1572868
  92.2 13.0 %collective-permute-start.7 = (f32[128,512]{1,0:T(8,128)S(1)}, f32[128,512]{1,0:T(8,128)S(1)}, u32[]{:S(2)}, u32[]{:S(2)}) collective-permute-start(f32[128,512]{1,0:T(8,128)S(1)} %project_back.1.own_ref), channel_id=1, source_target_pairs={{0,8},{1,9},{2,10},{3,11},{4,12},{5,13},{6,14},{7,15},{8,0},{9,1},... | collective-permute-start | bytes 786440 | tf_op jit(solution)/shard_map/ppermute | solution.py:22
  93.6 29.6 %copy-start.9 = (f32[2,128,512]{2,1,0:T(8,128)}, f32[2,128,512]{2,1,0:T(8,128)S(1)}, u32[]{:S(2)}) copy-start(f32[2,128,512]{2,1,0:T(8,128)S(1)} %get-tuple-element.39) | copy-start | bytes 1572868
  93.6 28.1 %copy-start.8 = (f32[4,128,512]{2,1,0:T(8,128)S(1)}, f32[4,128,512]{2,1,0:T(8,128)}, u32[]{:S(2)}) copy-start(f32[4,128,512]{2,1,0:T(8,128)} %get-tuple-element.38) | copy-start | bytes 3145732
  93.6 29.6 %collective-permute-start.4 = (f32[2,128,512]{2,1,0:T(8,128)S(1)}, f32[2,128,512]{2,1,0:T(8,128)S(1)}, u32[]{:S(2)}, u32[]{:S(2)}) collective-permute-start(f32[2,128,512]{2,1,0:T(8,128)S(1)} %get-tuple-element.40), channel_id=1, source_target_pairs={{0,4},{1,5},{2,6},{3,7},{4,0},{5,1},{6,2},{7,3},{8,12},{9,13},{10,... | collective-permute-start | bytes 1572872 | tf_op jit(solution)/shard_map/ppermute | solution.py:22
  123.1 18.5 %collective-permute-start.9 = (f32[2,128,512]{2,1,0:T(8,128)S(1)}, f32[2,128,512]{2,1,0:T(8,128)S(1)}, u32[]{:S(2)}, u32[]{:S(2)}) collective-permute-start(f32[2,128,512]{2,1,0:T(8,128)S(1)} %get-tuple-element.42), channel_id=1, source_target_pairs={{0,4},{1,5},{2,6},{3,7},{4,0},{5,1},{6,2},{7,3},{8,12},{9,13},{10,... | collective-permute-start | bytes 1572872 | tf_op jit(solution)/shard_map/ppermute | solution.py:22
  123.2 0.8 copy-start.11
  124.0 19.6 %copy-start.10 = (f32[2,128,512]{2,1,0:T(8,128)S(1)}, f32[2,128,512]{2,1,0:T(8,128)}, u32[]{:S(2)}) copy-start(f32[2,128,512]{2,1,0:T(8,128)} %copy-done.9) | copy-start | bytes 1572868
  124.0 19.6 %collective-permute-start.5 = (f32[1,128,512]{2,1,0:T(8,128)S(1)}, f32[1,128,512]{2,1,0:T(8,128)}, u32[]{:S(2)}, u32[]{:S(2)}) collective-permute-start(f32[1,128,512]{2,1,0:T(8,128)S(1)} %slice_add_fusion.10), channel_id=1, source_target_pairs={{0,8},{1,9},{2,10},{3,11},{4,12},{5,13},{6,14},{7,15},{8,0},{9,1},... | collective-permute-start | bytes 786440 | tf_op jit(solution)/shard_map/ppermute | solution.py:22
  125.7 17.9 %copy-start.12 = (f32[2,128,512]{2,1,0:T(8,128)S(1)}, f32[2,128,512]{2,1,0:T(8,128)}, u32[]{:S(2)}) copy-start(f32[2,128,512]{2,1,0:T(8,128)} %copy-done.11) | copy-start | bytes 1572868
  142.3 13.3 %collective-permute-start.10 = (f32[1,128,512]{2,1,0:T(8,128)}, f32[1,128,512]{2,1,0:T(8,128)}, u32[]{:S(2)}, u32[]{:S(2)}) collective-permute-start(f32[1,128,512]{2,1,0:T(8,128)} %slice_add_fusion.8), channel_id=1, source_target_pairs={{0,8},{1,9},{2,10},{3,11},{4,12},{5,13},{6,14},{7,15},{8,0},{9,1},... | collective-permute-start | bytes 786440 | tf_op jit(solution)/shard_map/ppermute | solution.py:22
Sparse Core Ops, SparseCore 0:
  10.2 61.1 all-gather.2

commit v4 on v3

--- a/solution.py
+++ b/solution.py
@@ -233,10 +233,10 @@
 
 
 def far_kernel(own_ref, oth_ref, far_ref, out_ref):
-    count, rows = own_ref.shape[1:]
+    count, rows = own_ref.shape
     for start in range(0, rows, GROUP):
         stop = start + GROUP
-        value = dot(own_ref[0, :, start:stop], far_ref[0, start:stop, :], NT) + dot(
+        value = dot(own_ref[:, start:stop], far_ref[0, start:stop, :], NT) + dot(
             oth_ref[:, start:stop], far_ref[1, start:stop, :], NT
         )
         first = value.astype(jnp.bfloat16)
@@ -246,19 +246,20 @@
         )
 
 
-def project_kernel(chunk, places_ref, x_ref, w_ref, out_ref, held_ref, sems):
-    pieces, count, width = out_ref.shape
+def project_kernel(chunk, places_ref, x_ref, w_ref, send_ref, keep_ref, held_ref, sems):
+    pieces, count, width = send_ref.shape
 
     def fetch(p):
         at = pl.multiple_of((places_ref[p] * CHUNKS + chunk) * width, width)
         return pltpu.make_async_copy(w_ref.at[:, pl.ds(at, width)], held_ref.at[p], sems.at[p])
 
-    for p in range(pieces):
+    for p in range(2 * pieces):
         fetch(p).start()
-    for p in range(pieces):
+    for p in range(2 * pieces):
         fetch(p).wait()
         both = one_dot(x_ref[...], held_ref[p])
-        out_ref[p] = both[:count] + both[count:]
+        target = send_ref if p < pieces else keep_ref
+        target[p % pieces] = both[:count] + both[count:]
 
 
 def project(x_both, weight, places, chunk):
@@ -268,13 +269,13 @@
     width = weight.shape[1] // lax.axis_size("tensor") // CHUNKS
     return pl.pallas_call(
         functools.partial(project_kernel, chunk),
-        out_shape=jax.ShapeDtypeStruct((pieces, count, width), jnp.float32),
+        out_shape=(jax.ShapeDtypeStruct((pieces // 2, count, width), jnp.float32),) * 2,
         in_specs=[
             pl.BlockSpec(memory_space=pltpu.SMEM),
             pl.BlockSpec(memory_space=pltpu.VMEM),
             pl.BlockSpec(memory_space=pl.ANY),
         ],
-        out_specs=pl.BlockSpec(memory_space=pltpu.VMEM),
+        out_specs=(pl.BlockSpec(memory_space=pltpu.VMEM),) * 2,
         scratch_shapes=[
             pltpu.VMEM((pieces, rows, width), weight.dtype),
             pltpu.SemaphoreType.DMA((pieces,)),
@@ -289,50 +290,70 @@
     )(places, x_both, weight)
 
 
-def back_kernel(cot_ref, w_ref, out_ref, cots_ref, held_ref, cot_sems, sems):
-    pieces, _, width = cot_ref.shape
-
-    def fetches(p):
+def back_kernel(orders, places_ref, *refs):
+    cots = refs[: 2 * len(orders)]
+    w_ref, out_ref, cots_ref, held_ref, cot_sems, sems = refs[2 * len(orders) :]
+    half, _, width = cots[0].shape
+    todo = []
+    for part, order in enumerate(orders):
+        for n, offset in enumerate(order):
+            todo.append((len(todo), cots[2 * part + n // half].at[n % half], offset, part))
+
+    def fetches(slot, cot, offset, part):
+        at = pl.multiple_of((places_ref[offset] * len(orders) + part) * width, width)
         return (
-            pltpu.make_async_copy(cot_ref.at[p], cots_ref.at[p], cot_sems.at[p]),
+            pltpu.make_async_copy(cot, cots_ref.at[slot], cot_sems.at[slot]),
             pltpu.make_async_copy(
-                w_ref.at[:, pl.ds(p * width, width)], held_ref.at[p], sems.at[p]
+                w_ref.at[:, pl.ds(at, width)], held_ref.at[slot], sems.at[slot]
             ),
         )
 
-    for p in range(pieces):
-        for copy in fetches(p):
+    for item in todo:
+        for copy in fetches(*item):
             copy.start()
     total = jnp.zeros(out_ref.shape, jnp.float32)
-    for p in range(pieces):
-        for copy in fetches(p):
+    for item in todo:
+        for copy in fetches(*item):
             copy.wait()
-        total += one_dot(cots_ref[p], held_ref[p], NT)
+        total += one_dot(cots_ref[item[0]], held_ref[item[0]], NT)
     out_ref[...] = total
 
 
-def project_back(gathered, weight):
-    pieces, count, width = gathered.shape
+def project_back(places, gathered, orders, weight):
+    half, count, width = gathered[0].shape
+    steps = half * len(gathered)
     rows = weight.shape[0]
     return pl.pallas_call(
-        back_kernel,
+        functools.partial(back_kernel, orders),
         out_shape=jax.ShapeDtypeStruct((count, rows), jnp.float32),
-        in_specs=[pl.BlockSpec(memory_space=pl.ANY)] * 2,
+        in_specs=[pl.BlockSpec(memory_space=pltpu.SMEM)]
+        + [pl.BlockSpec(memory_space=pl.ANY)] * (len(gathered) + 1),
         out_specs=pl.BlockSpec(memory_space=pltpu.VMEM),
         scratch_shapes=[
-            pltpu.VMEM((pieces, count, width), gathered.dtype),
-            pltpu.VMEM((pieces, rows, width), weight.dtype),
-            pltpu.SemaphoreType.DMA((pieces,)),
-            pltpu.SemaphoreType.DMA((pieces,)),
+            pltpu.VMEM((steps, count, width), weight.dtype),
+            pltpu.VMEM((steps, rows, width), weight.dtype),
+            pltpu.SemaphoreType.DMA((steps,)),
+            pltpu.SemaphoreType.DMA((steps,)),
         ],
         compiler_params=pltpu.CompilerParams(vmem_limit_bytes=WIDE_LIMIT),
         cost_estimate=pl.CostEstimate(
-            flops=2 * count * rows * width * pieces,
-            bytes_accessed=pieces * width * 2 * (rows + count),
+            flops=2 * count * rows * width * steps,
+            bytes_accessed=steps * width * 2 * (rows + count),
             transcendentals=0,
         ),
         name="project_back",
-    )(gathered, weight)
+    )(places, *gathered, weight)
+
+
+def grow(array, bit):
+    return jnp.concatenate([array, exchange(array, bit)], axis=0)
+
+
+def gather_order(stages):
+    order = [0]
+    for bit in stages:
+        order = order + [n ^ (1 << bit) for n in order]
+    return tuple(order)
 
 
 def lane_matmul(left_ref, right_ref, out_ref, block, lanes):
@@ -450,7 +471,12 @@
     params = pltpu.CompilerParams(vmem_limit_bytes=VMEM_LIMIT)
 
     far_gen = exchange(generators[0], pair_bit)
-    gathered = lax.all_gather(cotangent, "tensor", axis=0, tiled=False)
+    wide = cotangent.shape[1] // 2
+    first, second = cotangent[None, :, :wide], cotangent[None, :, wide:]
+    order_first = list(range(bits - 1, -1, -1))
+    order_second = [1] + list(range(bits - 1, 1, -1)) + [0]
+    first = grow(first, order_first[0])
+    second = grow(second, order_second[0])
     flat = generators.reshape(sections * rows, block)
     square = (block * block, lanes)
     far_square = (block * block, lanes // sections)
@@ -473,7 +499,10 @@
         compiler_params=params,
         name="near_rotations",
     )(orders, flat, tokens)
-    x_other = exchange(xs[0], pair_bit)
+    x_last, first, second, far_gen = lax.optimization_barrier((xs[0], first, second, far_gen))
+    for bit in order_first[1:-2]:
+        first = grow(first, bit)
+    x_other = exchange(x_last, pair_bit)
     inv_far, ffar, bfar = pl.pallas_call(
         far_rotations_kernel,
         out_shape=(
@@ -495,6 +524,10 @@
         cost_estimate=pl.CostEstimate(flops=10**7, bytes_accessed=10**7, transcendentals=0),
         name="far_rotations",
     )(orders[:1], high, generators[0], far_gen)
+    ffar, first = lax.optimization_barrier((ffar, first))
+    first = grow(first, order_first[-2])
+    x_other, second = lax.optimization_barrier((x_other, second))
+    second = grow(second, order_second[1])
     x_both = pl.pallas_call(
         far_kernel,
         out_shape=jax.ShapeDtypeStruct((2 * count, rows), jnp.bfloat16),
@@ -502,17 +535,22 @@
         out_specs=full,
         compiler_params=params,
         name="far_apply",
-    )(xs, x_other, ffar)
+    )(x_last, x_other, ffar)
 
     reverse = np.array(
         [sum(((p >> b) & 1) << (bits - 1 - b) for b in range(bits)) for p in range(size)], np.int32
     )
-    places = jnp.bitwise_xor(here.astype(jnp.int32), jnp.asarray(reverse))
-    outs = []
-    for chunk in range(CHUNKS):
-        send = project(x_both, weight, places[size // 2 :], chunk)
-        keep = project(x_both, weight, places[: size // 2], chunk)
-        outs.append((send, keep))
+    fixed = here.astype(jnp.int32)
+    places = jnp.bitwise_xor(fixed, jnp.asarray(np.roll(reverse, size // 2)))
+    back_places = jnp.bitwise_xor(fixed, jnp.arange(size, dtype=jnp.int32))
+    outs = [project(x_both, weight, places, chunk) for chunk in range(CHUNKS)]
+    keep, first, second = lax.optimization_barrier((outs[-1][1], first, second))
+    outs[-1] = (outs[-1][0], keep)
+    for bit in order_second[2:-1]:
+        second = grow(second, bit)
+    gathered = [first, exchange(first, 0), second, exchange(second, 0)]
+    gather_orders = (gather_order(order_first), gather_order(order_second))
+
     def stage(pair, got):
         send, keep = pair
         if keep.shape[0] == 1:
@@ -527,7 +565,7 @@
     for bit in range(bits):
         gots = [exchange(send, bit) for send, _ in outs]
         if bit == min(1, bits - 1):
-            grad_cols = project_back(gathered, weight)
+            grad_cols = project_back(back_places, gathered, gather_orders, weight)
             grad_cols, gots[0] = lax.optimization_barrier((grad_cols, gots[0]))
             grad_other = exchange(grad_cols, pair_bit)
             grad_tokens, grad_gens = pl.pallas_call(

time: 165 us -> 181 us (1.097)
  starting transfers between devices: 13.1 us -> 28.2 us
  between operations: 14.3 us -> 0.9 us
  waiting for transfers between devices: 65 us -> 77 us
  Pallas kernels: 56.3 us -> 59.5 us
    ppermute x11 -> x19, starting transfers between devices: 13 us -> 28.2 us  [exchange(): lax.ppermute(array, 'tensor', [(i, i ^ 1 << bit) for i in range(size)])]
    ppermute x11 -> x19, waiting for transfers between devices: 62.8 us -> 77 us  [exchange(): lax.ppermute(array, 'tensor', [(i, i ^ 1 << bit) for i in range(size)])]
    add x6, other arithmetic: 8.56 us -> 4.85 us  [stage(): return (keep[mid:] + got[mid:], keep[:mid] + got[:mid])]
    pallas_call x5 -> x3, Pallas kernels: 24.5 us -> 27.9 us  [the longest x2 15.9 us: project(): pl.pallas_call(functools.partial(project_kernel, chunk), out_shape=(jax.S...]
    concatenate x0 -> x5, other arithmetic: none -> 3.02 us  [grow(): return jnp.concatenate([array, exchange(array, bit)], axis=0)]
    unnamed x30 -> x25, local copies, waits for them, and re-layouts: 3.89 us -> 3.12 us
  transfers between devices with their start and end apart: 12 -> 19, of which waited for: 7 -> 10; matrix products, arithmetic and copies ran while one was open for 7% -> 6% of each run, Pallas kernels for 34% -> 28%
where the time goes in v4:
time: 181 us
  waiting for transfers between devices  77 us (43%)
  Pallas kernels  59.5 us (33%)
  starting transfers between devices  28.2 us (16%)
  other arithmetic  10.8 us (6%)
  local copies, waits for them, and re-layouts  4.22 us (2%)
    ppermute x19, waiting for transfers between devices, exchange(): lax.ppermute(array, 'tensor', [(i, i ^ 1 << bit) for i in range(size)])  77 us
    ppermute x19, starting transfers between devices, exchange(): lax.ppermute(array, 'tensor', [(i, i ^ 1 << bit) for i in range(size)])  28.2 us
    pallas_call x1, Pallas kernels, local(): pl.pallas_call(grads_kernel, out_shape=(jax.ShapeDtypeStruct((count, rows...  16.5 us
    pallas_call x2, Pallas kernels, project(): pl.pallas_call(functools.partial(project_kernel, chunk), out_shape=(jax.S...  15.9 us
    pallas_call x1, Pallas kernels, project_back(): pl.pallas_call(functools.partial(back_kernel, orders), out_shape=jax.Shap...  12 us
    pallas_call x1, Pallas kernels, local(): pl.pallas_call(near_kernel, out_shape=(jax.ShapeDtypeStruct(square, f32),...  9.18 us
    pallas_call x1, Pallas kernels, local(): pl.pallas_call(far_rotations_kernel, out_shape=(jax.ShapeDtypeStruct(far_...  5.31 us
    add x6, other arithmetic, stage(): return (keep[mid:] + got[mid:], keep[:mid] + got[:mid])  4.85 us
  transfers between devices with their start and end apart: 19, of which 10 were waited for; matrix products, arithmetic and copies ran while one was open for 6% of the time, Pallas kernels for 28%

profile of v4, /device:TPU:0, one launch (start us, length us, event | category | flops | bytes accessed | tf_op | source)
XLA Modules:
  0.0 180.6 jit_solution(13515612722001145849)
XLA Ops:
  0.7 1.0 slice_bitcast_fusion.2
  1.7 4.1 %collective-permute-start = (bf16[1,128,512]{2,1,0:T(8,128)(2,1)S(1)}, bf16[1,128,512]{2,1,0:T(8,128)(2,1)}, u32[]{:S(2)}, u32[]{:S(2)}) collective-permute-start(bf16[1,128,512]{2,1,0:T(8,128)(2,1)S(1)} %get-tuple-element.74), channel_id=1, source_target_pairs={{0,8},{1,9},{2,10},{3,11},{4,12},{5,13},{6,14},{7,15},{8,0},{9,1},... | collective-permute-start | bytes 393224 | tf_op jit(solution)/shard_map/ppermute | solution.py:22
  5.8 1.5 collective-permute-start.1
  7.3 1.3 copy.12
  8.6 0.4 collective-permute-start.2
  9.0 9.2 %near_rotations.1 = (f32[1024,128]{1,0:T(8,128)S(1)}, f32[3,512,128]{2,1,0:T(8,128)S(1)}, f32[3,128,512]{2,1,0:T(8,128)S(1)}) custom-call(s32[4,32]{1,0:T(4,128)S(1)} %copy-done.3, f32[2048,32]{1,0:T(8,128)S(1)} %bitcast.15, bf16[128,512]{1,0:T(8,128)(2,1)S(1)} %copy-done), custom_call_target="tpu_custom_call" | custom-call | tf_op jit(solution)/shard_map/near_rotations/pallas_call | solution.py:483
  18.2 0.1 collective-permute-done
  18.4 1.0 pad_maximum_fusion.4
  19.3 0.9 pad_maximum_fusion.5
  20.3 3.0 %collective-permute-done.2.far_ref = f32[512,32]{1,0:T(8,128)S(1)} collective-permute-done((f32[512,32]{1,0:T(8,128)S(1)}, f32[512,32]{1,0:T(8,128)S(1)}, u32[]{:S(2)}, u32[]{:S(2)}) %collective-permute-start.2) | collective-permute-done | bytes 65568 | tf_op jit(solution)/shard_map/ppermute | solution.py:22
  23.3 4.1 %collective-permute-start.4 = (bf16[2,128,512]{2,1,0:T(8,128)(2,1)S(1)}, bf16[2,128,512]{2,1,0:T(8,128)(2,1)}, u32[]{:S(2)}, u32[]{:S(2)}) collective-permute-start(bf16[2,128,512]{2,1,0:T(8,128)(2,1)S(1)} %pad_maximum_fusion.4), channel_id=1, source_target_pairs={{0,4},{1,5},{2,6},{3,7},{4,0},{5,1},{6,2},{7,3},{8,12},{9,13},{10,... | collective-permute-start | bytes 786440 | tf_op jit(solution)/shard_map/ppermute | solution.py:22
  27.4 5.3 %far_rotations.1 = (f32[1024,32]{1,0:T(8,128)S(1)}, f32[2,512,128]{2,1,0:T(8,128)S(1)}, f32[2,512,128]{2,1,0:T(8,128)S(1)}) custom-call(s32[1,32]{1,0:T(1,128)S(1)} %slice.92.orders_ref, s32[1]{0:T(128)} %bitcast.5.high_ref, f32[512,32]{1,0:T(8,128)S(1)} %slice_bitcast_fusion.own_ref, f32[512,32]{1,0:T(8,128)S(1)} %collective-permute-done.2.far_ref), custom_call_target="tpu_custom_call" | custom-call | flops 10000000 | bytes 10000000 | tf_op jit(solution)/shard_map/far_rotations/pallas_call | solution.py:506
  32.8 4.9 %collective-permute-done.3.oth_ref.x_oth_ref = f32[128,512]{1,0:T(8,128)S(1)} collective-permute-done((f32[128,512]{1,0:T(8,128)S(1)}, f32[128,512]{1,0:T(8,128)S(1)}, u32[]{:S(2)}, u32[]{:S(2)}) %collective-permute-start.3) | collective-permute-done | bytes 262176 | tf_op jit(solution)/shard_map/ppermute | solution.py:22
  37.7 0.2 collective-permute-done.4
  37.9 1.0 pad_maximum_fusion.1
  38.9 0.7 far_apply.1.x_ref
  39.6 8.0 %project.2 = (f32[8,128,512]{2,1,0:T(8,128)S(1)}, f32[8,128,512]{2,1,0:T(8,128)}) custom-call(s32[16]{0:T(128)S(1)} %broadcast_xor_fusion.places_ref, bf16[256,512]{1,0:T(8,128)(2,1)S(1)} %far_apply.1.x_ref, bf16[512,16384]{1,0:T(8,128)(2,1)} %refs_4_.1), custom_call_target="tpu_custom_call" | custom-call | flops 2147483648 | bytes 12582912 | tf_op jit(solution)/shard_map/project/pallas_call | solution.py:270
  47.6 7.9 %project.3 = (f32[8,128,512]{2,1,0:T(8,128)S(1)}, f32[8,128,512]{2,1,0:T(8,128)}) custom-call(s32[16]{0:T(128)S(1)} %broadcast_xor_fusion.places_ref, bf16[256,512]{1,0:T(8,128)(2,1)S(1)} %far_apply.1.x_ref, bf16[512,16384]{1,0:T(8,128)(2,1)} %refs_4_.1), custom_call_target="tpu_custom_call" | custom-call | flops 2147483648 | bytes 12582912 | tf_op jit(solution)/shard_map/project/pallas_call | solution.py:270
  55.5 0.6 collective-permute-start.14
  56.1 1.0 collective-permute-start.6
  57.1 2.3 %collective-permute-start.7 = (bf16[2,128,512]{2,1,0:T(8,128)(2,1)S(1)}, bf16[2,128,512]{2,1,0:T(8,128)(2,1)S(1)}, u32[]{:S(2)}, u32[]{:S(2)}) collective-permute-start(bf16[2,128,512]{2,1,0:T(8,128)(2,1)S(1)} %pad_maximum_fusion.5), channel_id=1, source_target_pairs={{0,8},{1,9},{2,10},{3,11},{4,12},{5,13},{6,14},{7,15},{8,0},{9,1},... | collective-permute-start | bytes 786440 | tf_op jit(solution)/shard_map/ppermute | solution.py:22
  59.4 12.2 %collective-permute-done.7 = bf16[2,128,512]{2,1,0:T(8,128)(2,1)S(1)} collective-permute-done((bf16[2,128,512]{2,1,0:T(8,128)(2,1)S(1)}, bf16[2,128,512]{2,1,0:T(8,128)(2,1)S(1)}, u32[]{:S(2)}, u32[]{:S(2)}) %collective-permute-start.7) | collective-permute-done | bytes 262176 | tf_op jit(solution)/shard_map/ppermute | solution.py:22
  71.8 0.5 collective-permute-start.9
  72.3 12.6 %collective-permute-done.9 = bf16[4,128,512]{2,1,0:T(8,128)(2,1)S(1)} collective-permute-done((bf16[4,128,512]{2,1,0:T(8,128)(2,1)S(1)}, bf16[4,128,512]{2,1,0:T(8,128)(2,1)S(1)}, u32[]{:S(2)}, u32[]{:S(2)}) %collective-permute-start.9) | collective-permute-done | bytes 524320 | tf_op jit(solution)/shard_map/ppermute | solution.py:22
  85.0 3.2 %slice_add_fusion.3 = (f32[4,128,512]{2,1,0:T(8,128)S(1)}, f32[4,128,512]{2,1,0:T(8,128)}) fusion(f32[8,128,512]{2,1,0:T(8,128)} %collective-permute-done.5, f32[8,128,512]{2,1,0:T(8,128)S(1)} %copy-done.5), kind=kLoop, calls=%fused_computation.3 | loop fusion | flops 524288 | bytes 6291456 | tf_op jit(solution)/shard_map/add | solution.py:559
  88.2 1.5 collective-permute-start.11
  89.8 0.5 slice_add_fusion
  90.2 0.6 collective-permute-start.16
  90.8 0.1 select_reduce_fusion.inverse_ref
  90.9 12.0 %project_back.1.own_ref = f32[128,512]{1,0:T(8,128)S(1)} custom-call(s32[16]{0:T(128)S(1)} %iota_xor_fusion.places_ref, bf16[8,128,512]{2,1,0:T(8,128)(2,1)S(1)} %pad_maximum_fusion.refs_0_, bf16[8,128,512]{2,1,0:T(8,128)(2,1)S(1)} %collective-permute-done.8.refs_1_, bf16[8,128,512]{2,1,0:T(8,128)(2,1)S(1)} %constant_dynamic-update-slice_fusion.refs_2_, ...), custom_call_target="tpu_custom_call" | custom-call | flops 2147483648 | bytes 20971520 | tf_op jit(solution)/shard_map/project_back/pallas_call | solution.py:326
  103.0 11.5 %collective-permute-done.11 = f32[4,128,512]{2,1,0:T(8,128)S(1)} collective-permute-done((f32[4,128,512]{2,1,0:T(8,128)}, f32[4,128,512]{2,1,0:T(8,128)S(1)}, u32[]{:S(2)}, u32[]{:S(2)}) %collective-permute-start.11) | collective-permute-done | bytes 1048608 | tf_op jit(solution)/shard_map/ppermute | solution.py:22
  114.4 2.9 %collective-permute-start.15 = (f32[128,512]{1,0:T(8,128)S(1)}, f32[128,512]{1,0:T(8,128)S(1)}, u32[]{:S(2)}, u32[]{:S(2)}) collective-permute-start(f32[128,512]{1,0:T(8,128)S(1)} %project_back.1.own_ref), channel_id=1, source_target_pairs={{0,8},{1,9},{2,10},{3,11},{4,12},{5,13},{6,14},{7,15},{8,0},{9,1},... | collective-permute-start | bytes 786440 | tf_op jit(solution)/shard_map/ppermute | solution.py:22
  117.3 0.2 slice_add_fusion.7
  117.5 1.8 collective-permute-start.12
  119.3 9.4 %collective-permute-done.15.oth_ref = f32[128,512]{1,0:T(8,128)S(1)} collective-permute-done((f32[128,512]{1,0:T(8,128)S(1)}, f32[128,512]{1,0:T(8,128)S(1)}, u32[]{:S(2)}, u32[]{:S(2)}) %collective-permute-start.15) | collective-permute-done | bytes 262176 | tf_op jit(solution)/shard_map/ppermute | solution.py:22
  128.7 16.5 %gradients.1 = (f32[128,512]{1,0:T(8,128)}, f32[2048,32]{1,0:T(8,128)S(1)}) custom-call(s32[4,32]{1,0:T(4,128)S(1)} %select_reduce_fusion.inverse_ref, s32[1]{0:T(128)} %bitcast.5.high_ref, f32[128,512]{1,0:T(8,128)S(1)} %project_back.1.own_ref, f32[128,512]{1,0:T(8,128)S(1)} %collective-permute-done.15.oth_ref, ...), custom_call_target="tpu_custom_call" | custom-call | tf_op jit(solution)/shard_map/gradients/pallas_call | solution.py:571
  145.2 0.2 slice_add_fusion.5
  145.4 0.7 collective-permute-start.17
  146.2 0.7 copy-done.8
  147.0 3.4 %collective-permute-start.13 = (f32[1,128,512]{2,1,0:T(8,128)S(1)}, f32[1,128,512]{2,1,0:T(8,128)}, u32[]{:S(2)}, u32[]{:S(2)}) collective-permute-start(f32[1,128,512]{2,1,0:T(8,128)S(1)} %slice_add_fusion.10), channel_id=1, source_target_pairs={{0,8},{1,9},{2,10},{3,11},{4,12},{5,13},{6,14},{7,15},{8,0},{9,1},... | collective-permute-start | bytes 786440 | tf_op jit(solution)/shard_map/ppermute | solution.py:22
  150.4 13.5 %collective-permute-done.17 = f32[2,128,512]{2,1,0:T(8,128)S(1)} collective-permute-done((f32[2,128,512]{2,1,0:T(8,128)S(1)}, f32[2,128,512]{2,1,0:T(8,128)S(1)}, u32[]{:S(2)}, u32[]{:S(2)}) %collective-permute-start.17) | collective-permute-done | bytes 524320 | tf_op jit(solution)/shard_map/ppermute | solution.py:22
  163.9 0.7 slice_add_fusion.8
  164.6 2.6 %collective-permute-start.18 = (f32[1,128,512]{2,1,0:T(8,128)}, f32[1,128,512]{2,1,0:T(8,128)}, u32[]{:S(2)}, u32[]{:S(2)}) collective-permute-start(f32[1,128,512]{2,1,0:T(8,128)} %slice_add_fusion.8), channel_id=1, source_target_pairs={{0,8},{1,9},{2,10},{3,11},{4,12},{5,13},{6,14},{7,15},{8,0},{9,1},... | collective-permute-start | bytes 786440 | tf_op jit(solution)/shard_map/ppermute | solution.py:22
  167.3 1.0 copy.14
  168.3 1.0 fusion.3
  169.3 9.5 %collective-permute-done.18 = f32[1,128,512]{2,1,0:T(8,128)} collective-permute-done((f32[1,128,512]{2,1,0:T(8,128)}, f32[1,128,512]{2,1,0:T(8,128)}, u32[]{:S(2)}, u32[]{:S(2)}) %collective-permute-start.18) | collective-permute-done | bytes 262176 | tf_op jit(solution)/shard_map/ppermute | solution.py:22
  178.8 1.0 fusion.1
  179.8 0.8 pad_maximum_fusion.3
  (44 shorter events, 0.5 us)
Async XLA Ops:
  0.6 8.4 %copy-start.3 = (s32[4,32]{1,0:T(4,128)S(1)}, s32[4,32]{1,0:T(4,128)}, u32[]{:S(2)}) copy-start(s32[4,32]{1,0:T(4,128)} %orders_ref.1) | copy-start | bytes 1540
  0.6 8.4 %copy-start = (bf16[128,512]{1,0:T(8,128)(2,1)S(1)}, bf16[128,512]{1,0:T(8,128)(2,1)}, u32[]{:S(2)}) copy-start(bf16[128,512]{1,0:T(8,128)(2,1)} %tok_ref.3) | copy-start | bytes 393220
  1.7 16.7 %collective-permute-start = (bf16[1,128,512]{2,1,0:T(8,128)(2,1)S(1)}, bf16[1,128,512]{2,1,0:T(8,128)(2,1)}, u32[]{:S(2)}, u32[]{:S(2)}) collective-permute-start(bf16[1,128,512]{2,1,0:T(8,128)(2,1)S(1)} %get-tuple-element.74), channel_id=1, source_target_pairs={{0,8},{1,9},{2,10},{3,11},{4,12},{5,13},{6,14},{7,15},{8,0},{9,1},... | collective-permute-start | bytes 393224 | tf_op jit(solution)/shard_map/ppermute | solution.py:22
  5.8 21.7 %copy-start.10 = (s32[16]{0:T(128)S(1)}, s32[16]{0:T(128)}, u32[]{:S(2)}) copy-start(s32[16]{0:T(128)} %constant.12.clone) | copy-start | bytes 196
  5.8 13.6 %collective-permute-start.1 = (bf16[1,128,512]{2,1,0:T(8,128)(2,1)S(1)}, bf16[1,128,512]{2,1,0:T(8,128)(2,1)}, u32[]{:S(2)}, u32[]{:S(2)}) collective-permute-start(bf16[1,128,512]{2,1,0:T(8,128)(2,1)S(1)} %get-tuple-element.73), channel_id=1, source_target_pairs={{0,2},{1,3},{2,0},{3,1},{4,6},{5,7},{6,4},{7,5},{8,10},{9,11},{10,... | collective-permute-start | bytes 393224 | tf_op jit(solution)/shard_map/ppermute | solution.py:22
  8.6 14.7 %collective-permute-start.2 = (f32[512,32]{1,0:T(8,128)S(1)}, f32[512,32]{1,0:T(8,128)S(1)}, u32[]{:S(2)}, u32[]{:S(2)}) collective-permute-start(f32[512,32]{1,0:T(8,128)S(1)} %slice_bitcast_fusion.own_ref), channel_id=1, source_target_pairs={{0,8},{1,9},{2,10},{3,11},{4,12},{5,13},{6,14},{7,15},{8,0},{9,1},... | collective-permute-start | bytes 196616 | tf_op jit(solution)/shard_map/ppermute | solution.py:22
  18.2 5.1 %copy-start.1 = (f32[1024,128]{1,0:T(8,128)}, f32[1024,128]{1,0:T(8,128)S(1)}, u32[]{:S(2)}) copy-start(f32[1024,128]{1,0:T(8,128)S(1)} %get-tuple-element.53.inv_ref) | copy-start | bytes 1572868
  23.3 14.4 %collective-permute-start.3 = (f32[128,512]{1,0:T(8,128)S(1)}, f32[128,512]{1,0:T(8,128)S(1)}, u32[]{:S(2)}, u32[]{:S(2)}) collective-permute-start(f32[128,512]{1,0:T(8,128)S(1)} %slice_bitcast_fusion.1.own_ref), channel_id=1, source_target_pairs={{0,8},{1,9},{2,10},{3,11},{4,12},{5,13},{6,14},{7,15},{8,0},{9,1},... | collective-permute-start | bytes 786440 | tf_op jit(solution)/shard_map/ppermute | solution.py:22
  23.3 14.6 %collective-permute-start.4 = (bf16[2,128,512]{2,1,0:T(8,128)(2,1)S(1)}, bf16[2,128,512]{2,1,0:T(8,128)(2,1)}, u32[]{:S(2)}, u32[]{:S(2)}) collective-permute-start(bf16[2,128,512]{2,1,0:T(8,128)(2,1)S(1)} %pad_maximum_fusion.4), channel_id=1, source_target_pairs={{0,4},{1,5},{2,6},{3,7},{4,0},{5,1},{6,2},{7,3},{8,12},{9,13},{10,... | collective-permute-start | bytes 786440 | tf_op jit(solution)/shard_map/ppermute | solution.py:22
  47.5 37.5 %collective-permute-start.5 = (f32[8,128,512]{2,1,0:T(8,128)S(1)}, f32[8,128,512]{2,1,0:T(8,128)}, u32[]{:S(2)}, u32[]{:S(2)}) collective-permute-start(f32[8,128,512]{2,1,0:T(8,128)S(1)} %get-tuple-element.40), channel_id=1, source_target_pairs={{0,1},{1,0},{2,3},{3,2},{4,5},{5,4},{6,7},{7,6},{8,9},{9,8},{10,11... | collective-permute-start | bytes 6291464 | tf_op jit(solution)/shard_map/ppermute | solution.py:22
  55.5 34.2 %collective-permute-start.14 = (f32[8,128,512]{2,1,0:T(8,128)S(1)}, f32[8,128,512]{2,1,0:T(8,128)S(1)}, u32[]{:S(2)}, u32[]{:S(2)}) collective-permute-start(f32[8,128,512]{2,1,0:T(8,128)S(1)} %get-tuple-element.48), channel_id=1, source_target_pairs={{0,1},{1,0},{2,3},{3,2},{4,5},{5,4},{6,7},{7,6},{8,9},{9,8},{10,11... | collective-permute-start | bytes 6291464 | tf_op jit(solution)/shard_map/ppermute | solution.py:22
  56.1 15.6 %collective-permute-start.6 = (bf16[4,128,512]{2,1,0:T(8,128)(2,1)S(1)}, bf16[4,128,512]{2,1,0:T(8,128)(2,1)S(1)}, u32[]{:S(2)}, u32[]{:S(2)}) collective-permute-start(bf16[4,128,512]{2,1,0:T(8,128)(2,1)S(1)} %pad_maximum_fusion.1), channel_id=1, source_target_pairs={{0,2},{1,3},{2,0},{3,1},{4,6},{5,7},{6,4},{7,5},{8,10},{9,11},{10,... | collective-permute-start | bytes 1572872 | tf_op jit(solution)/shard_map/ppermute | solution.py:22
  57.1 14.5 %collective-permute-start.7 = (bf16[2,128,512]{2,1,0:T(8,128)(2,1)S(1)}, bf16[2,128,512]{2,1,0:T(8,128)(2,1)S(1)}, u32[]{:S(2)}, u32[]{:S(2)}) collective-permute-start(bf16[2,128,512]{2,1,0:T(8,128)(2,1)S(1)} %pad_maximum_fusion.5), channel_id=1, source_target_pairs={{0,8},{1,9},{2,10},{3,11},{4,12},{5,13},{6,14},{7,15},{8,0},{9,1},... | collective-permute-start | bytes 786440 | tf_op jit(solution)/shard_map/ppermute | solution.py:22
  71.7 13.3 %copy-start.5 = (f32[8,128,512]{2,1,0:T(8,128)S(1)}, f32[8,128,512]{2,1,0:T(8,128)}, u32[]{:S(2)}) copy-start(f32[8,128,512]{2,1,0:T(8,128)} %get-tuple-element.39) | copy-start | bytes 6291460
  71.8 13.1 %collective-permute-start.9 = (bf16[4,128,512]{2,1,0:T(8,128)(2,1)S(1)}, bf16[4,128,512]{2,1,0:T(8,128)(2,1)S(1)}, u32[]{:S(2)}, u32[]{:S(2)}) collective-permute-start(bf16[4,128,512]{2,1,0:T(8,128)(2,1)S(1)} %pad_maximum_fusion.2), channel_id=1, source_target_pairs={{0,4},{1,5},{2,6},{3,7},{4,0},{5,1},{6,2},{7,3},{8,12},{9,13},{10,... | collective-permute-start | bytes 1572872 | tf_op jit(solution)/shard_map/ppermute | solution.py:22
  72.3 18.6 %collective-permute-start.8 = (bf16[8,128,512]{2,1,0:T(8,128)(2,1)S(1)}, bf16[8,128,512]{2,1,0:T(8,128)(2,1)S(1)}, u32[]{:S(2)}, u32[]{:S(2)}) collective-permute-start(bf16[8,128,512]{2,1,0:T(8,128)(2,1)S(1)} %pad_maximum_fusion.refs_0_), channel_id=1, source_target_pairs={{0,1},{1,0},{2,3},{3,2},{4,5},{5,4},{6,7},{7,6},{8,9},{9,8},{10,11... | collective-permute-start | bytes 3145736 | tf_op jit(solution)/shard_map/ppermute | solution.py:22
  84.9 6.0 %collective-permute-start.10 = (bf16[8,128,512]{2,1,0:T(8,128)(2,1)S(1)}, bf16[8,128,512]{2,1,0:T(8,128)(2,1)}, u32[]{:S(2)}, u32[]{:S(2)}) collective-permute-start(bf16[8,128,512]{2,1,0:T(8,128)(2,1)S(1)} %constant_dynamic-update-slice_fusion.refs_2_), channel_id=1, source_target_pairs={{0,1},{1,0},{2,3},{3,2},{4,5},{5,4},{6,7},{7,6},{8,9},{9,8},{10,11... | collective-permute-start | bytes 3145736 | tf_op jit(solution)/shard_map/ppermute | solution.py:22
  85.0 4.7 %copy-start.4 = (f32[8,128,512]{2,1,0:T(8,128)S(1)}, f32[8,128,512]{2,1,0:T(8,128)}, u32[]{:S(2)}) copy-start(f32[8,128,512]{2,1,0:T(8,128)} %get-tuple-element.47) | copy-start | bytes 6291460
  88.2 26.2 %collective-permute-start.11 = (f32[4,128,512]{2,1,0:T(8,128)}, f32[4,128,512]{2,1,0:T(8,128)S(1)}, u32[]{:S(2)}, u32[]{:S(2)}) collective-permute-start(f32[4,128,512]{2,1,0:T(8,128)} %get-tuple-element.66), channel_id=1, source_target_pairs={{0,2},{1,3},{2,0},{3,1},{4,6},{5,7},{6,4},{7,5},{8,10},{9,11},{10,... | collective-permute-start | bytes 3145736 | tf_op jit(solution)/shard_map/ppermute | solution.py:22
  90.2 55.0 %collective-permute-start.16 = (f32[4,128,512]{2,1,0:T(8,128)S(1)}, f32[4,128,512]{2,1,0:T(8,128)S(1)}, u32[]{:S(2)}, u32[]{:S(2)}) collective-permute-start(f32[4,128,512]{2,1,0:T(8,128)S(1)} %get-tuple-element.67), channel_id=1, source_target_pairs={{0,2},{1,3},{2,0},{3,1},{4,6},{5,7},{6,4},{7,5},{8,10},{9,11},{10,... | collective-permute-start | bytes 3145736 | tf_op jit(solution)/shard_map/ppermute | solution.py:22
  102.9 25.8 %copy-start.2 = (f32[1024,128]{1,0:T(8,128)S(1)}, f32[1024,128]{1,0:T(8,128)}, u32[]{:S(2)}) copy-start(f32[1024,128]{1,0:T(8,128)} %copy-done.1) | copy-start | bytes 1572868
  114.4 14.3 %collective-permute-start.15 = (f32[128,512]{1,0:T(8,128)S(1)}, f32[128,512]{1,0:T(8,128)S(1)}, u32[]{:S(2)}, u32[]{:S(2)}) collective-permute-start(f32[128,512]{1,0:T(8,128)S(1)} %project_back.1.own_ref), channel_id=1, source_target_pairs={{0,8},{1,9},{2,10},{3,11},{4,12},{5,13},{6,14},{7,15},{8,0},{9,1},... | collective-permute-start | bytes 786440 | tf_op jit(solution)/shard_map/ppermute | solution.py:22
  117.5 28.7 %copy-start.6 = (f32[2,128,512]{2,1,0:T(8,128)}, f32[2,128,512]{2,1,0:T(8,128)S(1)}, u32[]{:S(2)}) copy-start(f32[2,128,512]{2,1,0:T(8,128)S(1)} %get-tuple-element.69) | copy-start | bytes 1572868
  117.5 28.7 %collective-permute-start.12 = (f32[2,128,512]{2,1,0:T(8,128)S(1)}, f32[2,128,512]{2,1,0:T(8,128)S(1)}, u32[]{:S(2)}, u32[]{:S(2)}) collective-permute-start(f32[2,128,512]{2,1,0:T(8,128)S(1)} %get-tuple-element.70), channel_id=1, source_target_pairs={{0,4},{1,5},{2,6},{3,7},{4,0},{5,1},{6,2},{7,3},{8,12},{9,13},{10,... | collective-permute-start | bytes 1572872 | tf_op jit(solution)/shard_map/ppermute | solution.py:22
  145.4 18.5 %collective-permute-start.17 = (f32[2,128,512]{2,1,0:T(8,128)S(1)}, f32[2,128,512]{2,1,0:T(8,128)S(1)}, u32[]{:S(2)}, u32[]{:S(2)}) collective-permute-start(f32[2,128,512]{2,1,0:T(8,128)S(1)} %get-tuple-element.72), channel_id=1, source_target_pairs={{0,4},{1,5},{2,6},{3,7},{4,0},{5,1},{6,2},{7,3},{8,12},{9,13},{10,... | collective-permute-start | bytes 1572872 | tf_op jit(solution)/shard_map/ppermute | solution.py:22
  146.2 0.8 copy-start.8
  147.0 21.3 %copy-start.7 = (f32[2,128,512]{2,1,0:T(8,128)S(1)}, f32[2,128,512]{2,1,0:T(8,128)}, u32[]{:S(2)}) copy-start(f32[2,128,512]{2,1,0:T(8,128)} %copy-done.6) | copy-start | bytes 1572868
  147.0 21.3 %collective-permute-start.13 = (f32[1,128,512]{2,1,0:T(8,128)S(1)}, f32[1,128,512]{2,1,0:T(8,128)}, u32[]{:S(2)}, u32[]{:S(2)}) collective-permute-start(f32[1,128,512]{2,1,0:T(8,128)S(1)} %slice_add_fusion.10), channel_id=1, source_target_pairs={{0,8},{1,9},{2,10},{3,11},{4,12},{5,13},{6,14},{7,15},{8,0},{9,1},... | collective-permute-start | bytes 786440 | tf_op jit(solution)/shard_map/ppermute | solution.py:22
  150.4 17.9 %copy-start.9 = (f32[2,128,512]{2,1,0:T(8,128)S(1)}, f32[2,128,512]{2,1,0:T(8,128)}, u32[]{:S(2)}) copy-start(f32[2,128,512]{2,1,0:T(8,128)} %copy-done.8) | copy-start | bytes 1572868
  164.6 14.1 %collective-permute-start.18 = (f32[1,128,512]{2,1,0:T(8,128)}, f32[1,128,512]{2,1,0:T(8,128)}, u32[]{:S(2)}, u32[]{:S(2)}) collective-permute-start(f32[1,128,512]{2,1,0:T(8,128)} %slice_add_fusion.8), channel_id=1, source_target_pairs={{0,8},{1,9},{2,10},{3,11},{4,12},{5,13},{6,14},{7,15},{8,0},{9,1},... | collective-permute-start | bytes 786440 | tf_op jit(solution)/shard_map/ppermute | solution.py:22

commit v5 on v4

--- a/solution.py
+++ b/solution.py
@@ -29,6 +29,10 @@
 
 def one_dot(a, b, dims=NN):
     return lax.dot_general(a, b, dims, preferred_element_type=jnp.float32)
+
+
+def after(value, *earlier):
+    return lax.optimization_barrier((value, *earlier))[0]
 
 
 def dot(a, b, dims=NN):
@@ -246,8 +250,14 @@
         )
 
 
-def project_kernel(chunk, places_ref, x_ref, w_ref, send_ref, keep_ref, held_ref, sems):
+def project_kernel(
+    chunk, places_ref, x_ref, w_ref, send_ref, keep_ref, held_ref, made_ref, sems, out_sems
+):
     pieces, count, width = send_ref.shape
+
+    def leave(p):
+        target = send_ref if p < pieces else keep_ref
+        return pltpu.make_async_copy(made_ref.at[p], target.at[p % pieces], out_sems.at[p])
 
     def fetch(p):
         at = pl.multiple_of((places_ref[p] * CHUNKS + chunk) * width, width)
@@ -258,8 +268,10 @@
     for p in range(2 * pieces):
         fetch(p).wait()
         both = one_dot(x_ref[...], held_ref[p])
-        target = send_ref if p < pieces else keep_ref
-        target[p % pieces] = both[:count] + both[count:]
+        made_ref[p] = both[:count] + both[count:]
+        leave(p).start()
+    for p in range(2 * pieces):
+        leave(p).wait()
 
 
 def project(x_both, weight, places, chunk):
@@ -275,9 +287,11 @@
             pl.BlockSpec(memory_space=pltpu.VMEM),
             pl.BlockSpec(memory_space=pl.ANY),
         ],
-        out_specs=(pl.BlockSpec(memory_space=pltpu.VMEM),) * 2,
+        out_specs=(pl.BlockSpec(memory_space=pl.ANY),) * 2,
         scratch_shapes=[
             pltpu.VMEM((pieces, rows, width), weight.dtype),
+            pltpu.VMEM((pieces, count, width), jnp.float32),
+            pltpu.SemaphoreType.DMA((pieces,)),
             pltpu.SemaphoreType.DMA((pieces,)),
         ],
         compiler_params=pltpu.CompilerParams(vmem_limit_bytes=WIDE_LIMIT),
@@ -301,22 +315,25 @@
 
     def fetches(slot, cot, offset, part):
         at = pl.multiple_of((places_ref[offset] * len(orders) + part) * width, width)
+        here = pl.ds(slot * width, width)
         return (
-            pltpu.make_async_copy(cot, cots_ref.at[slot], cot_sems.at[slot]),
-            pltpu.make_async_copy(
-                w_ref.at[:, pl.ds(at, width)], held_ref.at[slot], sems.at[slot]
-            ),
+            pltpu.make_async_copy(cot, cots_ref.at[:, here], cot_sems.at[slot]),
+            pltpu.make_async_copy(w_ref.at[:, pl.ds(at, width)], held_ref.at[:, here], sems.at[slot]),
         )
 
     for item in todo:
         for copy in fetches(*item):
             copy.start()
-    total = jnp.zeros(out_ref.shape, jnp.float32)
-    for item in todo:
-        for copy in fetches(*item):
-            copy.wait()
-        total += one_dot(cots_ref[item[0]], held_ref[item[0]], NT)
-    out_ref[...] = total
+    for first in range(0, len(todo), 2):
+        for item in todo[first : first + 2]:
+            for copy in fetches(*item):
+                copy.wait()
+        here = slice(first * width, (first + 2) * width)
+        product = one_dot(cots_ref[:, here], held_ref[:, here], NT)
+        if first == 0:
+            out_ref[...] = product
+        else:
+            out_ref[...] += product
 
 
 def project_back(places, gathered, orders, weight):
@@ -330,8 +347,8 @@
         + [pl.BlockSpec(memory_space=pl.ANY)] * (len(gathered) + 1),
         out_specs=pl.BlockSpec(memory_space=pltpu.VMEM),
         scratch_shapes=[
-            pltpu.VMEM((steps, count, width), weight.dtype),
-            pltpu.VMEM((steps, rows, width), weight.dtype),
+            pltpu.VMEM((count, steps * width), weight.dtype),
+            pltpu.VMEM((rows, steps * width), weight.dtype),
             pltpu.SemaphoreType.DMA((steps,)),
             pltpu.SemaphoreType.DMA((steps,)),
         ],
@@ -347,6 +364,18 @@
 
 def grow(array, bit):
     return jnp.concatenate([array, exchange(array, bit)], axis=0)
+
+
+def narrow(values):
+    rows = values.reshape(-1, values.shape[-1])
+    exponent = jnp.ceil(jnp.log2(jnp.maximum(jnp.max(jnp.abs(rows)), 1e-30))) - 15.0
+    tag = jnp.full((16, rows.shape[1]), exponent)
+    return jnp.concatenate([rows * jnp.exp2(-exponent), tag], axis=0).astype(jnp.float16)
+
+
+def widen(packed, shape):
+    rows = packed.astype(jnp.float32)
+    return (rows[:-16] * jnp.exp2(rows[-16, 0])).reshape(shape)
 
 
 def gather_order(stages):
@@ -543,13 +572,11 @@
     fixed = here.astype(jnp.int32)
     places = jnp.bitwise_xor(fixed, jnp.asarray(np.roll(reverse, size // 2)))
     back_places = jnp.bitwise_xor(fixed, jnp.arange(size, dtype=jnp.int32))
-    outs = [project(x_both, weight, places, chunk) for chunk in range(CHUNKS)]
-    keep, first, second = lax.optimization_barrier((outs[-1][1], first, second))
-    outs[-1] = (outs[-1][0], keep)
-    for bit in order_second[2:-1]:
-        second = grow(second, bit)
-    gathered = [first, exchange(first, 0), second, exchange(second, 0)]
-    gather_orders = (gather_order(order_first), gather_order(order_second))
+    outs = []
+    for chunk in range(CHUNKS):
+        outs.append(project(x_both, weight, places, chunk))
+        if chunk == 0:
+            x_both = after(x_both, outs[0][0], first, second)
 
     def stage(pair, got):
         send, keep = pair
@@ -558,39 +585,49 @@
         mid = keep.shape[0] // 2
         return keep[mid:] + got[mid:], keep[:mid] + got[:mid]
 
+    def advance(outs, gots):
+        return [stage(pair, got) for pair, got in zip(outs, gots)]
+
+    outs = advance(outs, [exchange(send, 0) for send, _ in outs])
+    shapes = [send.shape for send, _ in outs]
+    sends = [narrow(send) for send, _ in outs]
+    gots = [exchange(send, 1) for send in sends]
+    for bit in order_second[2:-1]:
+        second = jnp.concatenate([second, after(exchange(second, bit), *sends)], axis=0)
+    gathered = [first, exchange(first, 0), second, exchange(second, 0)]
+    gather_orders = (gather_order(order_first), gather_order(order_second))
     numbers = jnp.arange(block, dtype=jnp.int32)
     inverse = jnp.sum(
         jnp.where(orders[:, :, None] == numbers[None, None, :], numbers[None, :, None], 0), axis=1
     ).astype(jnp.int32)
-    for bit in range(bits):
+    grad_cols = project_back(back_places, gathered, gather_orders, weight)
+    gots[-1] = after(gots[-1], grad_cols)
+    grad_other = exchange(grad_cols, pair_bit)
+    grad_tokens, grad_gens = pl.pallas_call(
+        grads_kernel,
+        out_shape=(
+            jax.ShapeDtypeStruct((count, rows), f32),
+            jax.ShapeDtypeStruct((sections * rows, block), f32),
+        ),
+        in_specs=[scalars, scalars] + [full] * 9,
+        out_specs=(full,) * 2,
+        scratch_shapes=[
+            pltpu.VMEM((sections * rows, block), f32),
+            pltpu.VMEM((sections * rows, block), f32),
+            pltpu.VMEM((sections * rows, block), f32),
+            pltpu.VMEM(square, f32),
+            pltpu.VMEM(square, f32),
+            pltpu.VMEM(square, f32),
+        ],
+        compiler_params=params,
+        name="gradients",
+    )(inverse, high, grad_cols, grad_other, x_other, tokens, xs, near, bfar, inv_far, inv)
+    outs = advance(outs, [widen(got, shape) for got, shape in zip(gots, shapes)])
+    for bit in range(2, bits):
         gots = [exchange(send, bit) for send, _ in outs]
-        if bit == min(1, bits - 1):
-            grad_cols = project_back(back_places, gathered, gather_orders, weight)
-            grad_cols, gots[0] = lax.optimization_barrier((grad_cols, gots[0]))
-            grad_other = exchange(grad_cols, pair_bit)
-            grad_tokens, grad_gens = pl.pallas_call(
-                grads_kernel,
-                out_shape=(
-                    jax.ShapeDtypeStruct((count, rows), f32),
-                    jax.ShapeDtypeStruct((sections * rows, block), f32),
-                ),
-                in_specs=[scalars, scalars] + [full] * 9,
-                out_specs=(full,) * 2,
-                scratch_shapes=[
-                    pltpu.VMEM((sections * rows, block), f32),
-                    pltpu.VMEM((sections * rows, block), f32),
-                    pltpu.VMEM((sections * rows, block), f32),
-                    pltpu.VMEM(square, f32),
-                    pltpu.VMEM(square, f32),
-                    pltpu.VMEM(square, f32),
-                ],
-                compiler_params=params,
-                name="gradients",
-            )(inverse, high, grad_cols, grad_other, x_other, tokens, xs, near, bfar, inv_far, inv)
-            grad_tokens, grad_gens, gots[-1] = lax.optimization_barrier(
-                (grad_tokens, grad_gens, gots[-1])
-            )
-        outs = [stage(pair, got) for pair, got in zip(outs, gots)]
+        if bit == 2:
+            gots[-1] = after(gots[-1], grad_tokens, grad_gens)
+        outs = advance(outs, gots)
     outputs = jnp.concatenate([keep[0] for _, keep in outs], axis=1)
     return outputs, grad_tokens, grad_gens.reshape(sections, rows, block)
 

time: 181 us -> 152 us (0.84)
  waiting for transfers between devices: 77 us -> 37.3 us
  other arithmetic: 10.8 us -> 19.4 us
  local copies, waits for them, and re-layouts: 4.22 us -> 11.3 us
  Pallas kernels: 59.5 us -> 55.3 us
  starting transfers between devices: 28.2 us -> 24.1 us
  between operations: 0.9 us -> 3.89 us
    ppermute x19, waiting for transfers between devices: 77 us -> 37.3 us  [exchange(): lax.ppermute(array, 'tensor', [(i, i ^ 1 << bit) for i in range(size)])]
    reduce_max x0 -> x2, other arithmetic: none -> 4.43 us  [narrow(): jnp.max(jnp.abs(rows))]
    ppermute x19, starting transfers between devices: 28.2 us -> 24.1 us  [exchange(): lax.ppermute(array, 'tensor', [(i, i ^ 1 << bit) for i in range(size)])]
    pallas_call x1, Pallas kernels: 12 us -> 8.53 us  [project_back(): pl.pallas_call(functools.partial(back_kernel, orders), out_shape=jax.Shap...]
    concatenate x0 -> x3, local copies, waits for them, and re-layouts: none -> 3.12 us  [the longest x2 2.04 us: narrow(): jnp.concatenate([rows * jnp.exp2(-exponent), tag], axis=0)]
    unnamed x25 -> x41, local copies, waits for them, and re-layouts: 3.12 us -> 5.93 us
    add x6, other arithmetic: 4.85 us -> 7.01 us  [stage(): return (keep[mid:] + got[mid:], keep[:mid] + got[:mid])]
    concatenate x5 -> x3, other arithmetic: 3.02 us -> 4.49 us  [grow(): return jnp.concatenate([array, exchange(array, bit)], axis=0)]
  transfers between devices with their start and end apart: 19 -> 19, of which waited for: 10 -> 8; matrix products, arithmetic and copies ran while one was open for 6% -> 17% of each run, Pallas kernels for 28% -> 37%
where the time goes in v5:
time: 152 us; the launch traced here: 151 us
  Pallas kernels  55.3 us (36%)
  waiting for transfers between devices  37.3 us (25%)
  starting transfers between devices  24.1 us (16%)
  other arithmetic  19.4 us (13%)
  local copies, waits for them, and re-layouts  11.3 us (7%)
  between operations  3.89 us (3%)
    ppermute x19, waiting for transfers between devices, exchange(): lax.ppermute(array, 'tensor', [(i, i ^ 1 << bit) for i in range(size)])  37.3 us
    ppermute x19, starting transfers between devices, exchange(): lax.ppermute(array, 'tensor', [(i, i ^ 1 << bit) for i in range(size)])  24.1 us
    pallas_call x1, Pallas kernels, local(): pl.pallas_call(grads_kernel, out_shape=(jax.ShapeDtypeStruct((count, rows...  16.5 us
    pallas_call x2, Pallas kernels, project(): pl.pallas_call(functools.partial(project_kernel, chunk), out_shape=(jax.S...  15.1 us
    pallas_call x1, Pallas kernels, local(): pl.pallas_call(near_kernel, out_shape=(jax.ShapeDtypeStruct(square, f32),...  9.18 us
    pallas_call x1, Pallas kernels, project_back(): pl.pallas_call(functools.partial(back_kernel, orders), out_shape=jax.Shap...  8.53 us
    add x6, other arithmetic, stage(): return (keep[mid:] + got[mid:], keep[:mid] + got[:mid])  7.01 us
    unnamed x41, local copies, waits for them, and re-layouts  5.93 us
  transfers between devices with their start and end apart: 19, of which 8 were waited for; matrix products, arithmetic and copies ran while one was open for 17% of the time, Pallas kernels for 37%

profile of v5, /device:TPU:0, one launch (start us, length us, event | category | flops | bytes accessed | tf_op | source)
XLA Modules:
  0.0 151.3 jit_solution(7428254879891906678)
XLA Ops:
  0.7 1.0 slice_bitcast_fusion.2
  1.7 4.1 %collective-permute-start = (bf16[1,128,512]{2,1,0:T(8,128)(2,1)S(1)}, bf16[1,128,512]{2,1,0:T(8,128)(2,1)}, u32[]{:S(2)}, u32[]{:S(2)}) collective-permute-start(bf16[1,128,512]{2,1,0:T(8,128)(2,1)S(1)} %get-tuple-element.74), channel_id=1, source_target_pairs={{0,8},{1,9},{2,10},{3,11},{4,12},{5,13},{6,14},{7,15},{8,0},{9,1},... | collective-permute-start | bytes 393224 | tf_op jit(solution)/shard_map/ppermute | solution.py:22
  5.8 1.5 %collective-permute-start.1 = (bf16[1,128,512]{2,1,0:T(8,128)(2,1)S(1)}, bf16[1,128,512]{2,1,0:T(8,128)(2,1)}, u32[]{:S(2)}, u32[]{:S(2)}) collective-permute-start(bf16[1,128,512]{2,1,0:T(8,128)(2,1)S(1)} %get-tuple-element.73), channel_id=1, source_target_pairs={{0,2},{1,3},{2,0},{3,1},{4,6},{5,7},{6,4},{7,5},{8,10},{9,11},{10,... | collective-permute-start | bytes 393224 | tf_op jit(solution)/shard_map/ppermute | solution.py:22
  7.3 1.3 copy.12
  8.6 0.4 collective-permute-start.2
  9.0 9.2 %near_rotations.1 = (f32[1024,128]{1,0:T(8,128)S(1)}, f32[3,512,128]{2,1,0:T(8,128)S(1)}, f32[3,128,512]{2,1,0:T(8,128)S(1)}) custom-call(s32[4,32]{1,0:T(4,128)S(1)} %copy-done.9, f32[2048,32]{1,0:T(8,128)S(1)} %bitcast.23, bf16[128,512]{1,0:T(8,128)(2,1)S(1)} %copy-done.2), custom_call_target="tpu_custom_call" | custom-call | tf_op jit(solution)/shard_map/near_rotations/pallas_call | solution.py:512
  18.4 1.8 %pad_maximum_fusion.2 = bf16[2,128,512]{2,1,0:T(8,128)(2,1)} fusion(bf16[1,128,512]{2,1,0:T(8,128)(2,1)} %collective-permute-done, bf16[1,128,512]{2,1,0:T(8,128)(2,1)S(1)} %get-tuple-element.74), kind=kLoop, calls=%fused_computation.25 | loop fusion | flops 131072 | bytes 524288 | tf_op jit(solution)/shard_map/concatenate | solution.py:366
  20.2 1.6 %pad_maximum_fusion.3 = bf16[2,128,512]{2,1,0:T(8,128)(2,1)} fusion(bf16[1,128,512]{2,1,0:T(8,128)(2,1)} %collective-permute-done.1, bf16[1,128,512]{2,1,0:T(8,128)(2,1)S(1)} %get-tuple-element.73), kind=kLoop, calls=%fused_computation.26 | loop fusion | flops 131072 | bytes 524288 | tf_op jit(solution)/shard_map/concatenate | solution.py:366
  21.8 1.5 %collective-permute-done.2.far_ref = f32[512,32]{1,0:T(8,128)S(1)} collective-permute-done((f32[512,32]{1,0:T(8,128)S(1)}, f32[512,32]{1,0:T(8,128)S(1)}, u32[]{:S(2)}, u32[]{:S(2)}) %collective-permute-start.2) | collective-permute-done | bytes 65568 | tf_op jit(solution)/shard_map/ppermute | solution.py:22
  23.3 0.7 collective-permute-start.4
  24.0 3.4 %collective-permute-start.3 = (f32[128,512]{1,0:T(8,128)S(1)}, f32[128,512]{1,0:T(8,128)S(1)}, u32[]{:S(2)}, u32[]{:S(2)}) collective-permute-start(f32[128,512]{1,0:T(8,128)S(1)} %slice_bitcast_fusion.1.own_ref), channel_id=1, source_target_pairs={{0,8},{1,9},{2,10},{3,11},{4,12},{5,13},{6,14},{7,15},{8,0},{9,1},... | collective-permute-start | bytes 786440 | tf_op jit(solution)/shard_map/ppermute | solution.py:22
  27.4 5.3 %far_rotations.1 = (f32[1024,32]{1,0:T(8,128)S(1)}, f32[2,512,128]{2,1,0:T(8,128)S(1)}, f32[2,512,128]{2,1,0:T(8,128)S(1)}) custom-call(s32[1,32]{1,0:T(1,128)S(1)} %slice.116.orders_ref, s32[1]{0:T(128)} %bitcast.5.high_ref, f32[512,32]{1,0:T(8,128)S(1)} %slice_bitcast_fusion.own_ref, f32[512,32]{1,0:T(8,128)S(1)} %collective-permute-done.2.far_ref), custom_call_target="tpu_custom_call" | custom-call | flops 10000000 | bytes 10000000 | tf_op jit(solution)/shard_map/far_rotations/pallas_call | solution.py:535
  32.8 4.2 %collective-permute-done.4 = bf16[2,128,512]{2,1,0:T(8,128)(2,1)} collective-permute-done((bf16[2,128,512]{2,1,0:T(8,128)(2,1)}, bf16[2,128,512]{2,1,0:T(8,128)(2,1)}, u32[]{:S(2)}, u32[]{:S(2)}) %collective-permute-start.4) | collective-permute-done | bytes 262176 | tf_op jit(solution)/shard_map/ppermute | solution.py:22
  37.0 1.1 pad_maximum_fusion
  38.1 1.2 collective-permute-done.3.oth_ref.x_oth_ref
  39.3 1.5 %collective-permute-start.9 = (bf16[4,128,512]{2,1,0:T(8,128)(2,1)S(1)}, bf16[4,128,512]{2,1,0:T(8,128)(2,1)S(1)}, u32[]{:S(2)}, u32[]{:S(2)}) collective-permute-start(bf16[4,128,512]{2,1,0:T(8,128)(2,1)S(1)} %pad_maximum_fusion), channel_id=1, source_target_pairs={{0,2},{1,3},{2,0},{3,1},{4,6},{5,7},{6,4},{7,5},{8,10},{9,11},{10,... | collective-permute-start | bytes 1572872 | tf_op jit(solution)/shard_map/ppermute | solution.py:22
  40.8 0.7 far_apply.1.x_ref
  41.5 7.6 %project.2 = (f32[8,128,512]{2,1,0:T(8,128)S(1)}, f32[8,128,512]{2,1,0:T(8,128)}) custom-call(s32[16]{0:T(128)S(1)} %broadcast_xor_fusion.places_ref, bf16[256,512]{1,0:T(8,128)(2,1)S(1)} %far_apply.1.x_ref, bf16[512,16384]{1,0:T(8,128)(2,1)} %refs_4_.1), custom_call_target="tpu_custom_call" | custom-call | flops 2147483648 | bytes 12582912 | tf_op jit(solution)/shard_map/project/pallas_call | solution.py:282
  49.2 0.8 constant_dynamic-update-slice_fusion.6
  50.0 2.1 %collective-permute-done.10 = bf16[2,128,512]{2,1,0:T(8,128)(2,1)S(1)} collective-permute-done((bf16[2,128,512]{2,1,0:T(8,128)(2,1)}, bf16[2,128,512]{2,1,0:T(8,128)(2,1)S(1)}, u32[]{:S(2)}, u32[]{:S(2)}) %collective-permute-start.10) | collective-permute-done | bytes 262176 | tf_op jit(solution)/shard_map/ppermute | solution.py:22
  52.1 0.7 constant_dynamic-update-slice_fusion.5
  52.9 7.5 %project.3 = (f32[8,128,512]{2,1,0:T(8,128)}, f32[8,128,512]{2,1,0:T(8,128)}) custom-call(s32[16]{0:T(128)S(1)} %broadcast_xor_fusion.places_ref, bf16[256,512]{1,0:T(8,128)(2,1)S(1)} %far_apply.1.x_ref, bf16[512,16384]{1,0:T(8,128)(2,1)} %refs_4_.1), custom_call_target="tpu_custom_call" | custom-call | flops 2147483648 | bytes 12582912 | tf_op jit(solution)/shard_map/project/pallas_call | solution.py:282
  60.5 1.4 collective-permute-start.14
  61.9 2.1 %abs_reduce_fusion.1 = f32[]{:T(128)} fusion(f32[8,128,512]{2,1,0:T(8,128)} %collective-permute-done.5, f32[8,128,512]{2,1,0:T(8,128)S(1)} %copy-done.10), kind=kLoop, calls=%fused_computation.9 | loop fusion | flops 786431 | bytes 2097156 | tf_op jit(solution)/shard_map/reduce_max | solution.py:371
  64.7 3.8 %slice_add_fusion.3 = (f32[4,128,512]{2,1,0:T(8,128)}, f16[4,128,512]{2,1,0:T(8,128)(2,1)}) fusion(f32[8,128,512]{2,1,0:T(8,128)} %collective-permute-done.5, f32[8,128,512]{2,1,0:T(8,128)} %get-tuple-element.35, f32[]{:T(128)S(6)} %exp2.33), kind=kLoop, calls=%fused_computation.5 | loop fusion | flops 1048576 | bytes 5767172 | tf_op jit(solution)/shard_map/add | solution.py:586
  68.5 1.9 %concatenate.31 = f16[528,512]{1,0:T(8,128)(2,1)} pad(f16[512,512]{1,0:T(8,128)(2,1)} %bitcast.25, f16[]{:T(256)S(6)} %convert.15), padding=0_16x0_0 | pad | bytes 1064962 | tf_op jit(solution)/shard_map/concatenate | solution.py:373
  70.5 0.7 collective-permute-start.6
  71.1 2.4 %abs_reduce_fusion = f32[]{:T(128)} fusion(f32[8,128,512]{2,1,0:T(8,128)} %collective-permute-done.11, f32[8,128,512]{2,1,0:T(8,128)} %get-tuple-element.40), kind=kLoop, calls=%fused_computation.7 | loop fusion | flops 786431 | bytes 2097156 | tf_op jit(solution)/shard_map/reduce_max | solution.py:371
  74.2 2.7 %slice_add_fusion.1 = (f32[4,128,512]{2,1,0:T(8,128)S(1)}, f16[4,128,512]{2,1,0:T(8,128)(2,1)S(1)}) fusion(f32[8,128,512]{2,1,0:T(8,128)} %collective-permute-done.11, f32[8,128,512]{2,1,0:T(8,128)} %get-tuple-element.40, f32[]{:T(128)S(6)} %exp2.38), kind=kLoop, calls=%fused_computation.2 | loop fusion | flops 1048576 | bytes 5767172 | tf_op jit(solution)/shard_map/add | solution.py:586
  77.0 1.1 constant_dynamic-update-slice_fusion.4.refs_2_
  78.3 1.5 %collective-permute-start.12 = (f16[528,512]{1,0:T(8,128)(2,1)S(1)}, f16[528,512]{1,0:T(8,128)(2,1)S(1)}, u32[]{:S(2)}, u32[]{:S(2)}) collective-permute-start(f16[528,512]{1,0:T(8,128)(2,1)S(1)} %concatenate.34), channel_id=1, source_target_pairs={{0,2},{1,3},{2,0},{3,1},{4,6},{5,7},{6,4},{7,5},{8,10},{9,11},{10,... | collective-permute-start | bytes 1622024 | tf_op jit(solution)/shard_map/ppermute | solution.py:22
  79.8 6.1 %collective-permute-done.6 = f16[528,512]{1,0:T(8,128)(2,1)} collective-permute-done((f16[528,512]{1,0:T(8,128)(2,1)}, f16[528,512]{1,0:T(8,128)(2,1)}, u32[]{:S(2)}, u32[]{:S(2)}) %collective-permute-start.6) | collective-permute-done | bytes 540704 | tf_op jit(solution)/shard_map/ppermute | solution.py:22
  85.8 1.2 convert_element_type.8
  87.0 0.5 slice.154
  88.4 1.0 copy-done.11
  89.7 0.9 collective-permute-start.7
  90.6 1.0 copy-done.14
  91.6 8.5 %project_back.1.own_ref = f32[128,512]{1,0:T(8,128)S(1)} custom-call(s32[16]{0:T(128)S(1)} %iota_xor_fusion.places_ref, bf16[8,128,512]{2,1,0:T(8,128)(2,1)S(1)} %constant_dynamic-update-slice_fusion.refs_0_, bf16[8,128,512]{2,1,0:T(8,128)(2,1)} %collective-permute-done.13.refs_1_, bf16[8,128,512]{2,1,0:T(8,128)(2,1)S(1)} %constant_dynamic-update-slice_fusion.4.refs_2_, ...), custom_call_target="tpu_custom_call" | custom-call | flops 2147483648 | bytes 20971520 | tf_op jit(solution)/shard_map/project_back/pallas_call | solution.py:343
  100.3 0.5 slice.166
  102.0 1.2 collective-permute-start.16
  103.2 2.6 %collective-permute-start.17 = (f32[128,512]{1,0:T(8,128)S(1)}, f32[128,512]{1,0:T(8,128)S(1)}, u32[]{:S(2)}, u32[]{:S(2)}) collective-permute-start(f32[128,512]{1,0:T(8,128)S(1)} %project_back.1.own_ref), channel_id=1, source_target_pairs={{0,8},{1,9},{2,10},{3,11},{4,12},{5,13},{6,14},{7,15},{8,0},{9,1},... | collective-permute-start | bytes 786440 | tf_op jit(solution)/shard_map/ppermute | solution.py:22
  106.3 14.9 %collective-permute-done.17.oth_ref = f32[128,512]{1,0:T(8,128)S(1)} collective-permute-done((f32[128,512]{1,0:T(8,128)S(1)}, f32[128,512]{1,0:T(8,128)S(1)}, u32[]{:S(2)}, u32[]{:S(2)}) %collective-permute-start.17) | collective-permute-done | bytes 262176 | tf_op jit(solution)/shard_map/ppermute | solution.py:22
  121.2 16.5 %gradients.1 = (f32[128,512]{1,0:T(8,128)}, f32[2048,32]{1,0:T(8,128)S(1)}) custom-call(s32[4,32]{1,0:T(4,128)S(1)} %select_reduce_fusion.inverse_ref, s32[1]{0:T(128)} %bitcast.5.high_ref, f32[128,512]{1,0:T(8,128)S(1)} %project_back.1.own_ref, f32[128,512]{1,0:T(8,128)S(1)} %collective-permute-done.17.oth_ref, ...), custom_call_target="tpu_custom_call" | custom-call | tf_op jit(solution)/shard_map/gradients/pallas_call | solution.py:606
  137.8 3.5 %collective-permute-start.18 = (f32[1,128,512]{2,1,0:T(8,128)S(1)}, f32[1,128,512]{2,1,0:T(8,128)S(1)}, u32[]{:S(2)}, u32[]{:S(2)}) collective-permute-start(f32[1,128,512]{2,1,0:T(8,128)S(1)} %slice_add_fusion.8), channel_id=1, source_target_pairs={{0,8},{1,9},{2,10},{3,11},{4,12},{5,13},{6,14},{7,15},{8,0},{9,1},... | collective-permute-start | bytes 786440 | tf_op jit(solution)/shard_map/ppermute | solution.py:22
  141.4 1.0 copy.14
  142.4 7.1 %collective-permute-done.18 = f32[1,128,512]{2,1,0:T(8,128)S(1)} collective-permute-done((f32[1,128,512]{2,1,0:T(8,128)S(1)}, f32[1,128,512]{2,1,0:T(8,128)S(1)}, u32[]{:S(2)}, u32[]{:S(2)}) %collective-permute-start.18) | collective-permute-done | bytes 262176 | tf_op jit(solution)/shard_map/ppermute | solution.py:22
  149.5 1.0 fusion.1
  150.5 0.8 pad_maximum_fusion.1
  (71 shorter events, 2.2 us)
Async XLA Ops:
  0.6 8.4 %copy-start.2 = (bf16[128,512]{1,0:T(8,128)(2,1)S(1)}, bf16[128,512]{1,0:T(8,128)(2,1)}, u32[]{:S(2)}) copy-start(bf16[128,512]{1,0:T(8,128)(2,1)} %tok_ref.3) | copy-start | bytes 393220
  0.6 8.4 %copy-start.9 = (s32[4,32]{1,0:T(4,128)S(1)}, s32[4,32]{1,0:T(4,128)}, u32[]{:S(2)}) copy-start(s32[4,32]{1,0:T(4,128)} %orders_ref.1) | copy-start | bytes 1540
  1.7 16.7 %collective-permute-start = (bf16[1,128,512]{2,1,0:T(8,128)(2,1)S(1)}, bf16[1,128,512]{2,1,0:T(8,128)(2,1)}, u32[]{:S(2)}, u32[]{:S(2)}) collective-permute-start(bf16[1,128,512]{2,1,0:T(8,128)(2,1)S(1)} %get-tuple-element.74), channel_id=1, source_target_pairs={{0,8},{1,9},{2,10},{3,11},{4,12},{5,13},{6,14},{7,15},{8,0},{9,1},... | collective-permute-start | bytes 393224 | tf_op jit(solution)/shard_map/ppermute | solution.py:22
  5.8 21.7 %copy-start.17 = (s32[16]{0:T(128)S(1)}, s32[16]{0:T(128)}, u32[]{:S(2)}) copy-start(s32[16]{0:T(128)} %constant.27.clone) | copy-start | bytes 196
  5.8 14.4 %collective-permute-start.1 = (bf16[1,128,512]{2,1,0:T(8,128)(2,1)S(1)}, bf16[1,128,512]{2,1,0:T(8,128)(2,1)}, u32[]{:S(2)}, u32[]{:S(2)}) collective-permute-start(bf16[1,128,512]{2,1,0:T(8,128)(2,1)S(1)} %get-tuple-element.73), channel_id=1, source_target_pairs={{0,2},{1,3},{2,0},{3,1},{4,6},{5,7},{6,4},{7,5},{8,10},{9,11},{10,... | collective-permute-start | bytes 393224 | tf_op jit(solution)/shard_map/ppermute | solution.py:22
  8.6 14.7 %collective-permute-start.2 = (f32[512,32]{1,0:T(8,128)S(1)}, f32[512,32]{1,0:T(8,128)S(1)}, u32[]{:S(2)}, u32[]{:S(2)}) collective-permute-start(f32[512,32]{1,0:T(8,128)S(1)} %slice_bitcast_fusion.own_ref), channel_id=1, source_target_pairs={{0,8},{1,9},{2,10},{3,11},{4,12},{5,13},{6,14},{7,15},{8,0},{9,1},... | collective-permute-start | bytes 196616 | tf_op jit(solution)/shard_map/ppermute | solution.py:22
  18.2 5.1 %copy-start.3 = (f32[1024,128]{1,0:T(8,128)}, f32[1024,128]{1,0:T(8,128)S(1)}, u32[]{:S(2)}) copy-start(f32[1024,128]{1,0:T(8,128)S(1)} %get-tuple-element.47.inv_ref) | copy-start | bytes 1572868
  18.2 23.3 %copy-start = (f32[3,512,128]{2,1,0:T(8,128)}, f32[3,512,128]{2,1,0:T(8,128)S(1)}, u32[]{:S(2)}) copy-start(f32[3,512,128]{2,1,0:T(8,128)S(1)} %get-tuple-element.44.near_ref) | copy-start | bytes 2359300
  23.3 13.7 %collective-permute-start.4 = (bf16[2,128,512]{2,1,0:T(8,128)(2,1)}, bf16[2,128,512]{2,1,0:T(8,128)(2,1)}, u32[]{:S(2)}, u32[]{:S(2)}) collective-permute-start(bf16[2,128,512]{2,1,0:T(8,128)(2,1)} %pad_maximum_fusion.2), channel_id=1, source_target_pairs={{0,4},{1,5},{2,6},{3,7},{4,0},{5,1},{6,2},{7,3},{8,12},{9,13},{10,... | collective-permute-start | bytes 786440 | tf_op jit(solution)/shard_map/ppermute | solution.py:22
  24.0 15.2 %collective-permute-start.3 = (f32[128,512]{1,0:T(8,128)S(1)}, f32[128,512]{1,0:T(8,128)S(1)}, u32[]{:S(2)}, u32[]{:S(2)}) collective-permute-start(f32[128,512]{1,0:T(8,128)S(1)} %slice_bitcast_fusion.1.own_ref), channel_id=1, source_target_pairs={{0,8},{1,9},{2,10},{3,11},{4,12},{5,13},{6,14},{7,15},{8,0},{9,1},... | collective-permute-start | bytes 786440 | tf_op jit(solution)/shard_map/ppermute | solution.py:22
  32.8 8.0 %copy-start.5 = (f32[1024,32]{1,0:T(8,128)}, f32[1024,32]{1,0:T(8,128)S(1)}, u32[]{:S(2)}) copy-start(f32[1024,32]{1,0:T(8,128)S(1)} %get-tuple-element.46.inv_far_ref) | copy-start | bytes 393220
  32.8 16.3 %copy-start.7 = (f32[2,512,128]{2,1,0:T(8,128)}, f32[2,512,128]{2,1,0:T(8,128)S(1)}, u32[]{:S(2)}) copy-start(f32[2,512,128]{2,1,0:T(8,128)S(1)} %get-tuple-element.45.bfar_ref) | copy-start | bytes 1572868
  39.3 13.5 %collective-permute-start.9 = (bf16[4,128,512]{2,1,0:T(8,128)(2,1)S(1)}, bf16[4,128,512]{2,1,0:T(8,128)(2,1)S(1)}, u32[]{:S(2)}, u32[]{:S(2)}) collective-permute-start(bf16[4,128,512]{2,1,0:T(8,128)(2,1)S(1)} %pad_maximum_fusion), channel_id=1, source_target_pairs={{0,2},{1,3},{2,0},{3,1},{4,6},{5,7},{6,4},{7,5},{8,10},{9,11},{10,... | collective-permute-start | bytes 1572872 | tf_op jit(solution)/shard_map/ppermute | solution.py:22
  40.8 11.3 %collective-permute-start.10 = (bf16[2,128,512]{2,1,0:T(8,128)(2,1)}, bf16[2,128,512]{2,1,0:T(8,128)(2,1)S(1)}, u32[]{:S(2)}, u32[]{:S(2)}) collective-permute-start(bf16[2,128,512]{2,1,0:T(8,128)(2,1)} %pad_maximum_fusion.3), channel_id=1, source_target_pairs={{0,8},{1,9},{2,10},{3,11},{4,12},{5,13},{6,14},{7,15},{8,0},{9,1},... | collective-permute-start | bytes 786440 | tf_op jit(solution)/shard_map/ppermute | solution.py:22
  41.5 7.7 %copy-start.15 = (bf16[2,128,512]{2,1,0:T(8,128)(2,1)S(1)}, bf16[2,128,512]{2,1,0:T(8,128)(2,1)}, u32[]{:S(2)}) copy-start(bf16[2,128,512]{2,1,0:T(8,128)(2,1)} %pad_maximum_fusion.3) | copy-start | bytes 786436
  49.1 12.8 %collective-permute-start.5 = (f32[8,128,512]{2,1,0:T(8,128)S(1)}, f32[8,128,512]{2,1,0:T(8,128)}, u32[]{:S(2)}, u32[]{:S(2)}) collective-permute-start(f32[8,128,512]{2,1,0:T(8,128)S(1)} %get-tuple-element.36), channel_id=1, source_target_pairs={{0,1},{1,0},{2,3},{3,2},{4,5},{5,4},{6,7},{7,6},{8,9},{9,8},{10,11... | collective-permute-start | bytes 6291464 | tf_op jit(solution)/shard_map/ppermute | solution.py:22
  52.9 9.0 %copy-start.10 = (f32[8,128,512]{2,1,0:T(8,128)S(1)}, f32[8,128,512]{2,1,0:T(8,128)}, u32[]{:S(2)}) copy-start(f32[8,128,512]{2,1,0:T(8,128)} %get-tuple-element.35) | copy-start | bytes 6291460
  60.4 10.7 %collective-permute-start.11 = (f32[8,128,512]{2,1,0:T(8,128)}, f32[8,128,512]{2,1,0:T(8,128)}, u32[]{:S(2)}, u32[]{:S(2)}) collective-permute-start(f32[8,128,512]{2,1,0:T(8,128)} %get-tuple-element.41), channel_id=1, source_target_pairs={{0,1},{1,0},{2,3},{3,2},{4,5},{5,4},{6,7},{7,6},{8,9},{9,8},{10,11... | collective-permute-start | bytes 6291464 | tf_op jit(solution)/shard_map/ppermute | solution.py:22
  60.5 16.5 %collective-permute-start.14 = (bf16[4,128,512]{2,1,0:T(8,128)(2,1)}, bf16[4,128,512]{2,1,0:T(8,128)(2,1)}, u32[]{:S(2)}, u32[]{:S(2)}) collective-permute-start(bf16[4,128,512]{2,1,0:T(8,128)(2,1)} %get-tuple-element.70), channel_id=1, source_target_pairs={{0,4},{1,5},{2,6},{3,7},{4,0},{5,1},{6,2},{7,3},{8,12},{9,13},{10,... | collective-permute-start | bytes 1572872 | tf_op jit(solution)/shard_map/ppermute | solution.py:22
  61.9 28.8 %collective-permute-start.13 = (bf16[8,128,512]{2,1,0:T(8,128)(2,1)S(1)}, bf16[8,128,512]{2,1,0:T(8,128)(2,1)}, u32[]{:S(2)}, u32[]{:S(2)}) collective-permute-start(bf16[8,128,512]{2,1,0:T(8,128)(2,1)S(1)} %constant_dynamic-update-slice_fusion.refs_0_), channel_id=1, source_target_pairs={{0,1},{1,0},{2,3},{3,2},{4,5},{5,4},{6,7},{7,6},{8,9},{9,8},{10,11... | collective-permute-start | bytes 3145736 | tf_op jit(solution)/shard_map/ppermute | solution.py:22
  70.5 15.4 %collective-permute-start.6 = (f16[528,512]{1,0:T(8,128)(2,1)}, f16[528,512]{1,0:T(8,128)(2,1)}, u32[]{:S(2)}, u32[]{:S(2)}) collective-permute-start(f16[528,512]{1,0:T(8,128)(2,1)} %concatenate.31), channel_id=1, source_target_pairs={{0,2},{1,3},{2,0},{3,1},{4,6},{5,7},{6,4},{7,5},{8,10},{9,11},{10,... | collective-permute-start | bytes 1622024 | tf_op jit(solution)/shard_map/ppermute | solution.py:22
  78.1 12.5 %collective-permute-start.15 = (bf16[8,128,512]{2,1,0:T(8,128)(2,1)S(1)}, bf16[8,128,512]{2,1,0:T(8,128)(2,1)S(1)}, u32[]{:S(2)}, u32[]{:S(2)}) collective-permute-start(bf16[8,128,512]{2,1,0:T(8,128)(2,1)S(1)} %constant_dynamic-update-slice_fusion.4.refs_2_), channel_id=1, source_target_pairs={{0,1},{1,0},{2,3},{3,2},{4,5},{5,4},{6,7},{7,6},{8,9},{9,8},{10,11... | collective-permute-start | bytes 3145736 | tf_op jit(solution)/shard_map/ppermute | solution.py:22
  78.3 21.9 %collective-permute-start.12 = (f16[528,512]{1,0:T(8,128)(2,1)S(1)}, f16[528,512]{1,0:T(8,128)(2,1)S(1)}, u32[]{:S(2)}, u32[]{:S(2)}) collective-permute-start(f16[528,512]{1,0:T(8,128)(2,1)S(1)} %concatenate.34), channel_id=1, source_target_pairs={{0,2},{1,3},{2,0},{3,1},{4,6},{5,7},{6,4},{7,5},{8,10},{9,11},{10,... | collective-permute-start | bytes 1622024 | tf_op jit(solution)/shard_map/ppermute | solution.py:22
  88.2 1.2 copy-start.11
  89.7 16.1 %collective-permute-start.7 = (f32[2,128,512]{2,1,0:T(8,128)S(1)}, f32[2,128,512]{2,1,0:T(8,128)S(1)}, u32[]{:S(2)}, u32[]{:S(2)}) collective-permute-start(f32[2,128,512]{2,1,0:T(8,128)S(1)} %get-tuple-element.62), channel_id=1, source_target_pairs={{0,4},{1,5},{2,6},{3,7},{4,0},{5,1},{6,2},{7,3},{8,12},{9,13},{10,... | collective-permute-start | bytes 1572872 | tf_op jit(solution)/shard_map/ppermute | solution.py:22
  90.6 1.0 copy-start.14
  101.7 19.5 %copy-start.1 = (f32[3,512,128]{2,1,0:T(8,128)S(1)}, f32[3,512,128]{2,1,0:T(8,128)}, u32[]{:S(2)}) copy-start(f32[3,512,128]{2,1,0:T(8,128)} %copy-done) | copy-start | bytes 2359300
  101.7 19.5 %copy-start.4 = (f32[1024,128]{1,0:T(8,128)S(1)}, f32[1024,128]{1,0:T(8,128)}, u32[]{:S(2)}) copy-start(f32[1024,128]{1,0:T(8,128)} %copy-done.3) | copy-start | bytes 1572868
  101.7 19.5 %copy-start.6 = (f32[1024,32]{1,0:T(8,128)S(1)}, f32[1024,32]{1,0:T(8,128)}, u32[]{:S(2)}) copy-start(f32[1024,32]{1,0:T(8,128)} %copy-done.5) | copy-start | bytes 393220
  101.7 19.5 %copy-start.8 = (f32[2,512,128]{2,1,0:T(8,128)S(1)}, f32[2,512,128]{2,1,0:T(8,128)}, u32[]{:S(2)}) copy-start(f32[2,512,128]{2,1,0:T(8,128)} %copy-done.7) | copy-start | bytes 1572868
  102.0 35.8 %copy-start.12 = (f32[2,128,512]{2,1,0:T(8,128)}, f32[2,128,512]{2,1,0:T(8,128)S(1)}, u32[]{:S(2)}) copy-start(f32[2,128,512]{2,1,0:T(8,128)S(1)} %get-tuple-element.66) | copy-start | bytes 1572868
  102.0 35.8 %collective-permute-start.16 = (f32[2,128,512]{2,1,0:T(8,128)S(1)}, f32[2,128,512]{2,1,0:T(8,128)S(1)}, u32[]{:S(2)}, u32[]{:S(2)}) collective-permute-start(f32[2,128,512]{2,1,0:T(8,128)S(1)} %get-tuple-element.65), channel_id=1, source_target_pairs={{0,4},{1,5},{2,6},{3,7},{4,0},{5,1},{6,2},{7,3},{8,12},{9,13},{10,... | collective-permute-start | bytes 1572872 | tf_op jit(solution)/shard_map/ppermute | solution.py:22
  103.2 18.0 %collective-permute-start.17 = (f32[128,512]{1,0:T(8,128)S(1)}, f32[128,512]{1,0:T(8,128)S(1)}, u32[]{:S(2)}, u32[]{:S(2)}) collective-permute-start(f32[128,512]{1,0:T(8,128)S(1)} %project_back.1.own_ref), channel_id=1, source_target_pairs={{0,8},{1,9},{2,10},{3,11},{4,12},{5,13},{6,14},{7,15},{8,0},{9,1},... | collective-permute-start | bytes 786440 | tf_op jit(solution)/shard_map/ppermute | solution.py:22
  105.9 35.5 %collective-permute-start.8 = (f32[1,128,512]{2,1,0:T(8,128)S(1)}, f32[1,128,512]{2,1,0:T(8,128)S(1)}, u32[]{:S(2)}, u32[]{:S(2)}) collective-permute-start(f32[1,128,512]{2,1,0:T(8,128)S(1)} %slice_add_fusion.10), channel_id=1, source_target_pairs={{0,8},{1,9},{2,10},{3,11},{4,12},{5,13},{6,14},{7,15},{8,0},{9,1},... | collective-permute-start | bytes 786440 | tf_op jit(solution)/shard_map/ppermute | solution.py:22
  137.8 3.6 %copy-start.16 = (f32[2,128,512]{2,1,0:T(8,128)}, f32[2,128,512]{2,1,0:T(8,128)S(1)}, u32[]{:S(2)}) copy-start(f32[2,128,512]{2,1,0:T(8,128)S(1)} %collective-permute-done.16) | copy-start | bytes 1572868
  137.8 11.7 %copy-start.13 = (f32[2,128,512]{2,1,0:T(8,128)S(1)}, f32[2,128,512]{2,1,0:T(8,128)}, u32[]{:S(2)}) copy-start(f32[2,128,512]{2,1,0:T(8,128)} %copy-done.12) | copy-start | bytes 1572868
  137.8 11.7 %collective-permute-start.18 = (f32[1,128,512]{2,1,0:T(8,128)S(1)}, f32[1,128,512]{2,1,0:T(8,128)S(1)}, u32[]{:S(2)}, u32[]{:S(2)}) collective-permute-start(f32[1,128,512]{2,1,0:T(8,128)S(1)} %slice_add_fusion.8), channel_id=1, source_target_pairs={{0,8},{1,9},{2,10},{3,11},{4,12},{5,13},{6,14},{7,15},{8,0},{9,1},... | collective-permute-start | bytes 786440 | tf_op jit(solution)/shard_map/ppermute | solution.py:22

commit v6 on v5

--- a/solution.py
+++ b/solution.py
@@ -108,37 +108,41 @@
     return (col == offset + row).astype(jnp.bfloat16)
 
 
+def transpose_to(out_ref, in_ref, block, change=lambda j, t: t):
+    for j in range(block):
+        out_ref[j * block : (j + 1) * block, :] = change(j, in_ref[pl.ds(j, block, stride=block), :])
+
+
+def permuted_row(orders_ref, in_ref, i, section_of):
+    sections, block = orders_ref.shape
+    return by_section(
+        [
+            in_ref[pl.ds(pl.multiple_of(orders_ref[k, i] * block, block), block), :]
+            for k in range(sections)
+        ],
+        section_of,
+    )
+
+
+def permute_rows(orders_ref, in_ref, out_ref, section_of):
+    block = orders_ref.shape[1]
+    for i in range(block):
+        out_ref[i * block : (i + 1) * block, :] = permuted_row(orders_ref, in_ref, i, section_of)
+
+
 def invert_blocks(orders_ref, lo_ref, hi_ref, inv_ref, a_ref, b_ref, section_of):
     sections, block = orders_ref.shape
     half = block // 2
     lanes = inv_ref.shape[1]
     to_lanes(lo_ref, hi_ref, a_ref, lanes, half, block)
 
-    def permute_rows(i, _):
-        parts = [
-            a_ref[pl.ds(pl.multiple_of(orders_ref[k, i] * block, block), block), :]
-            for k in range(sections)
-        ]
-        b_ref[pl.ds(pl.multiple_of(i * block, block), block), :] = by_section(parts, section_of)
-        return 0
-
-    lax.fori_loop(0, block, permute_rows, 0, unroll=4)
-
-    def permute_cols(j, _):
-        parts = [
-            b_ref[pl.ds(orders_ref[k, j], block, stride=block), :] for k in range(sections)
-        ]
-        a_ref[pl.ds(pl.multiple_of(j * block, block), block), :] = by_section(parts, section_of)
-        return 0
-
-    lax.fori_loop(0, block, permute_cols, 0, unroll=4)
+    transpose_to(b_ref, a_ref, block, lambda j, t: a_ref[j * block : (j + 1) * block, :] - t)
+    permute_rows(orders_ref, b_ref, a_ref, section_of)
+    transpose_to(b_ref, a_ref, block)
+    permute_rows(orders_ref, b_ref, inv_ref, section_of)
     sub = iota((block, lanes), 0)
     for j in range(block):
-        inv_ref[j * block : (j + 1) * block, :] = (
-            a_ref[j * block : (j + 1) * block, :]
-            - a_ref[pl.ds(j, block, stride=block), :]
-            + (sub == j).astype(jnp.float32)
-        )
+        inv_ref[j * block : (j + 1) * block, :] += (sub == j).astype(jnp.float32)
 
     def eliminate(k, _):
         at = pl.multiple_of(k * block, block)
@@ -186,10 +190,12 @@
     half = block // 2
     rows = tok_ref.shape[1]
     lanes = sections * rows // half
-    lo_ref[0:rows, :] = gen_ref[0:rows, :]
-    hi_ref[0:rows, :] = gen_ref[0:rows, :]
+    for k in range(sections):
+        row_ref[k * rows : (k + 1) * rows, :] = gen_ref[k * block : (k + 1) * block, :].T
+    lo_ref[0:rows, :] = row_ref[0:rows, :]
+    hi_ref[0:rows, :] = row_ref[0:rows, :]
     for k in range(1, sections):
-        split_halves(gen_ref, lo_ref, hi_ref, k, rows, half)
+        split_halves(row_ref, lo_ref, hi_ref, k, rows, half)
     section_of, upper = lane_facts((block, lanes), rows // half, 0)
     invert_blocks(orders_ref, lo_ref, hi_ref, inv_ref, a_ref, b_ref, section_of)
     own_rows(inv_ref, row_ref, half, block, upper)
@@ -216,10 +222,10 @@
 ):
     block = orders_ref.shape[1]
     half = block // 2
-    rows = far_ref.shape[0]
+    rows = far_ref.shape[1]
     high = high_ref[0]
-    own = own_ref[...]
-    other = far_ref[...]
+    own = own_ref[...].T
+    other = far_ref[...].T
     lo_ref[...] = jnp.where(high == 1, other, own)
     hi_ref[...] = jnp.where(high == 1, own, other)
     invert_blocks(orders_ref, lo_ref, hi_ref, inv_ref, a_ref, b_ref, None)
@@ -236,12 +242,18 @@
             target[1, start : start + GROUP, :] = jnp.where(same, part[:, GROUP:], 0.0)
 
 
+def beside(a, b):
+    return jnp.concatenate([a, b], axis=1)
+
+
 def far_kernel(own_ref, oth_ref, far_ref, out_ref):
     count, rows = own_ref.shape
     for start in range(0, rows, GROUP):
         stop = start + GROUP
-        value = dot(own_ref[:, start:stop], far_ref[0, start:stop, :], NT) + dot(
-            oth_ref[:, start:stop], far_ref[1, start:stop, :], NT
+        value = dot(
+            beside(own_ref[:, start:stop], oth_ref[:, start:stop]),
+            beside(far_ref[0, start:stop, :], far_ref[1, start:stop, :]),
+            NT,
         )
         first = value.astype(jnp.bfloat16)
         out_ref[0:count, start:stop] = first
@@ -304,44 +316,38 @@
     )(places, x_both, weight)
 
 
-def back_kernel(orders, places_ref, *refs):
-    cots = refs[: 2 * len(orders)]
-    w_ref, out_ref, cots_ref, held_ref, cot_sems, sems = refs[2 * len(orders) :]
-    half, _, width = cots[0].shape
-    todo = []
-    for part, order in enumerate(orders):
-        for n, offset in enumerate(order):
-            todo.append((len(todo), cots[2 * part + n // half].at[n % half], offset, part))
-
-    def fetches(slot, cot, offset, part):
-        at = pl.multiple_of((places_ref[offset] * len(orders) + part) * width, width)
+def back_kernel(order, places_ref, low_ref, high_ref, w_ref, out_ref, cots_ref, held_ref, cot_sems, sems):
+    half, _, width = low_ref.shape
+
+    def fetches(slot):
+        at = pl.multiple_of(places_ref[order[slot]] * width, width)
         here = pl.ds(slot * width, width)
+        cot = (low_ref if slot < half else high_ref).at[slot % half]
         return (
             pltpu.make_async_copy(cot, cots_ref.at[:, here], cot_sems.at[slot]),
             pltpu.make_async_copy(w_ref.at[:, pl.ds(at, width)], held_ref.at[:, here], sems.at[slot]),
         )
 
-    for item in todo:
-        for copy in fetches(*item):
+    for slot in range(2 * half):
+        for copy in fetches(slot):
             copy.start()
-    for first in range(0, len(todo), 2):
-        for item in todo[first : first + 2]:
-            for copy in fetches(*item):
-                copy.wait()
-        here = slice(first * width, (first + 2) * width)
+    for slot in range(2 * half):
+        for copy in fetches(slot):
+            copy.wait()
+        here = slice(slot * width, (slot + 1) * width)
         product = one_dot(cots_ref[:, here], held_ref[:, here], NT)
-        if first == 0:
+        if slot == 0:
             out_ref[...] = product
         else:
             out_ref[...] += product
 
 
-def project_back(places, gathered, orders, weight):
+def project_back(places, gathered, order, weight):
     half, count, width = gathered[0].shape
     steps = half * len(gathered)
     rows = weight.shape[0]
     return pl.pallas_call(
-        functools.partial(back_kernel, orders),
+        functools.partial(back_kernel, order),
         out_shape=jax.ShapeDtypeStruct((count, rows), jnp.float32),
         in_specs=[pl.BlockSpec(memory_space=pltpu.SMEM)]
         + [pl.BlockSpec(memory_space=pl.ANY)] * (len(gathered) + 1),
@@ -364,18 +370,6 @@
 
 def grow(array, bit):
     return jnp.concatenate([array, exchange(array, bit)], axis=0)
-
-
-def narrow(values):
-    rows = values.reshape(-1, values.shape[-1])
-    exponent = jnp.ceil(jnp.log2(jnp.maximum(jnp.max(jnp.abs(rows)), 1e-30))) - 15.0
-    tag = jnp.full((16, rows.shape[1]), exponent)
-    return jnp.concatenate([rows * jnp.exp2(-exponent), tag], axis=0).astype(jnp.float16)
-
-
-def widen(packed, shape):
-    rows = packed.astype(jnp.float32)
-    return (rows[:-16] * jnp.exp2(rows[-16, 0])).reshape(shape)
 
 
 def gather_order(stages):
@@ -456,32 +450,67 @@
         ]
     lane_matmul(a_ref, b_ref, c_ref, block, lanes)
     lane_matmul(b_ref, c_ref, a_ref, block, lanes)
-    for j in range(block):
-        c_ref[j * block : (j + 1) * block, :] = 2.0 * (
-            a_ref[j * block : (j + 1) * block, :] - a_ref[pl.ds(j, block, stride=block), :]
-        )
     section_of, upper = lane_facts((block, lanes), per_section, high)
-
-    def permute_cols(j, _):
-        parts = [
-            c_ref[pl.ds(inverse_ref[k, j], block, stride=block), :] for k in range(sections)
-        ]
-        b_ref[pl.ds(pl.multiple_of(j * block, block), block), :] = by_section(parts, section_of)
-        return 0
-
-    lax.fori_loop(0, block, permute_cols, 0, unroll=4)
+    transpose_to(c_ref, a_ref, block, lambda j, t: 2.0 * (t - a_ref[j * block : (j + 1) * block, :]))
+    permute_rows(inverse_ref, c_ref, b_ref, section_of)
+    transpose_to(a_ref, b_ref, block)
     for a in range(half):
-        low, top = [
-            by_section(
-                [
-                    b_ref[pl.ds(inverse_ref[k, at], block, stride=block), :]
-                    for k in range(sections)
-                ],
-                section_of,
-            )
-            for at in (a, half + a)
-        ]
-        ggen_ref[pl.ds(a, lanes, stride=half), :] = jnp.where(upper, top, low).T
+        low = permuted_row(inverse_ref, a_ref, a, section_of)
+        top = permuted_row(inverse_ref, a_ref, half + a, section_of)
+        row_ref[pl.ds(a, lanes, stride=half), :] = jnp.where(upper, top, low).T
+    for k in range(sections):
+        ggen_ref[k * block : (k + 1) * block, :] = row_ref[k * rows : (k + 1) * rows, :].T
+
+
+def pack_kernel(keep_ref, got_ref, packed_ref, out_ref):
+    half, count, width = out_ref.shape
+    largest = jnp.zeros((count, width), jnp.float32)
+    for p in range(half):
+        total = keep_ref[half + p] + got_ref[half + p]
+        packed_ref[p * count : (p + 1) * count, :] = total
+        largest = jnp.maximum(largest, jnp.abs(total))
+        out_ref[p] = keep_ref[p] + got_ref[p]
+    peak = jnp.max(largest, axis=(0, 1), keepdims=True)
+    exponent = jnp.ceil(jnp.log2(jnp.maximum(peak, 1e-30))) - 15.0
+    scale = jnp.exp2(-exponent)
+    for p in range(half):
+        packed_ref[p * count : (p + 1) * count, :] *= scale
+    packed_ref[half * count :, :] = jnp.broadcast_to(exponent, (16, width))
+
+
+def unpack_kernel(keep_ref, got_ref, send_ref, out_ref):
+    half, count, width = out_ref.shape
+    scale = jnp.exp2(got_ref[2 * half * count : 2 * half * count + 1, 0:1])
+    for p in range(half):
+        low, top = p * count, (half + p) * count
+        out_ref[p] = keep_ref[p] + got_ref[low : low + count, :] * scale
+        send_ref[p] = keep_ref[half + p] + got_ref[top : top + count, :] * scale
+
+
+def summed(kernel, name, keep, got, first):
+    pieces, count, width = keep.shape
+    full = pl.BlockSpec(memory_space=pltpu.VMEM)
+    return pl.pallas_call(
+        kernel,
+        out_shape=(first, jax.ShapeDtypeStruct((pieces // 2, count, width), jnp.float32)),
+        in_specs=[full] * 2,
+        out_specs=(full,) * 2,
+        compiler_params=pltpu.CompilerParams(vmem_limit_bytes=VMEM_LIMIT),
+        name=name,
+    )(keep, got)
+
+
+def pack(keep, got):
+    pieces, count, width = keep.shape
+    first = jax.ShapeDtypeStruct((pieces // 2 * count + 16, width), jnp.float32)
+    packed, keep = summed(pack_kernel, "sum_pack", keep, got, first)
+    return packed.astype(jnp.float16), keep
+
+
+def unpack(keep, got):
+    pieces, count, width = keep.shape
+    first = jax.ShapeDtypeStruct((pieces // 2, count, width), jnp.float32)
+    return summed(unpack_kernel, "sum_unpack", keep, got.astype(jnp.float32), first)
 
 
 def local(tokens, weight, generators, orders, cotangent):
@@ -499,14 +528,11 @@
     scalars = pl.BlockSpec(memory_space=pltpu.SMEM)
     params = pltpu.CompilerParams(vmem_limit_bytes=VMEM_LIMIT)
 
-    far_gen = exchange(generators[0], pair_bit)
-    wide = cotangent.shape[1] // 2
-    first, second = cotangent[None, :, :wide], cotangent[None, :, wide:]
-    order_first = list(range(bits - 1, -1, -1))
-    order_second = [1] + list(range(bits - 1, 1, -1)) + [0]
-    first = grow(first, order_first[0])
-    second = grow(second, order_second[0])
-    flat = generators.reshape(sections * rows, block)
+    stored = jnp.swapaxes(generators, 1, 2)
+    far_gen = exchange(stored[0], pair_bit)
+    order = list(range(bits - 1, -1, -1))
+    pieces = grow(cotangent[None], order[0])
+    flat = stored.reshape(sections * block, rows)
     square = (block * block, lanes)
     far_square = (block * block, lanes // sections)
     inv, near, xs = pl.pallas_call(
@@ -528,9 +554,8 @@
         compiler_params=params,
         name="near_rotations",
     )(orders, flat, tokens)
-    x_last, first, second, far_gen = lax.optimization_barrier((xs[0], first, second, far_gen))
-    for bit in order_first[1:-2]:
-        first = grow(first, bit)
+    x_last, pieces, far_gen = lax.optimization_barrier((xs[0], pieces, far_gen))
+    news = exchange(pieces, order[1])
     x_other = exchange(x_last, pair_bit)
     inv_far, ffar, bfar = pl.pallas_call(
         far_rotations_kernel,
@@ -552,11 +577,10 @@
         compiler_params=params,
         cost_estimate=pl.CostEstimate(flops=10**7, bytes_accessed=10**7, transcendentals=0),
         name="far_rotations",
-    )(orders[:1], high, generators[0], far_gen)
-    ffar, first = lax.optimization_barrier((ffar, first))
-    first = grow(first, order_first[-2])
-    x_other, second = lax.optimization_barrier((x_other, second))
-    second = grow(second, order_second[1])
+    )(orders[:1], high, stored[0], far_gen)
+    pieces = jnp.concatenate([pieces, after(news, ffar)], axis=0)
+    for bit in order[2:-1]:
+        pieces = grow(pieces, bit)
     x_both = pl.pallas_call(
         far_kernel,
         out_shape=jax.ShapeDtypeStruct((2 * count, rows), jnp.bfloat16),
@@ -575,8 +599,7 @@
     outs = []
     for chunk in range(CHUNKS):
         outs.append(project(x_both, weight, places, chunk))
-        if chunk == 0:
-            x_both = after(x_both, outs[0][0], first, second)
+        x_both = after(x_both, outs[-1][0])
 
     def stage(pair, got):
         send, keep = pair
@@ -585,29 +608,22 @@
         mid = keep.shape[0] // 2
         return keep[mid:] + got[mid:], keep[:mid] + got[:mid]
 
-    def advance(outs, gots):
-        return [stage(pair, got) for pair, got in zip(outs, gots)]
-
-    outs = advance(outs, [exchange(send, 0) for send, _ in outs])
-    shapes = [send.shape for send, _ in outs]
-    sends = [narrow(send) for send, _ in outs]
-    gots = [exchange(send, 1) for send in sends]
-    for bit in order_second[2:-1]:
-        second = jnp.concatenate([second, after(exchange(second, bit), *sends)], axis=0)
-    gathered = [first, exchange(first, 0), second, exchange(second, 0)]
-    gather_orders = (gather_order(order_first), gather_order(order_second))
+    outs = [pack(keep, exchange(send, 0)) for send, keep in outs]
+    gots = [exchange(send, 1) for send, _ in outs]
+    gathered = [after(pieces, *[send for send, _ in outs]), exchange(pieces, 0)]
     numbers = jnp.arange(block, dtype=jnp.int32)
     inverse = jnp.sum(
         jnp.where(orders[:, :, None] == numbers[None, None, :], numbers[None, :, None], 0), axis=1
     ).astype(jnp.int32)
-    grad_cols = project_back(back_places, gathered, gather_orders, weight)
-    gots[-1] = after(gots[-1], grad_cols)
+    grad_cols = project_back(back_places, gathered, gather_order(order), weight)
     grad_other = exchange(grad_cols, pair_bit)
+    gots[0] = after(gots[0], grad_cols)
+    gots[-1] = after(gots[-1], grad_other)
     grad_tokens, grad_gens = pl.pallas_call(
         grads_kernel,
         out_shape=(
             jax.ShapeDtypeStruct((count, rows), f32),
-            jax.ShapeDtypeStruct((sections * rows, block), f32),
+            jax.ShapeDtypeStruct((sections * block, rows), f32),
         ),
         in_specs=[scalars, scalars] + [full] * 9,
         out_specs=(full,) * 2,
@@ -622,14 +638,14 @@
         compiler_params=params,
         name="gradients",
     )(inverse, high, grad_cols, grad_other, x_other, tokens, xs, near, bfar, inv_far, inv)
-    outs = advance(outs, [widen(got, shape) for got, shape in zip(gots, shapes)])
+    outs = [unpack(keep, got) for (_, keep), got in zip(outs, gots)]
     for bit in range(2, bits):
         gots = [exchange(send, bit) for send, _ in outs]
-        if bit == 2:
+        if bit == bits - 1:
             gots[-1] = after(gots[-1], grad_tokens, grad_gens)
-        outs = advance(outs, gots)
+        outs = [stage(pair, got) for pair, got in zip(outs, gots)]
     outputs = jnp.concatenate([keep[0] for _, keep in outs], axis=1)
-    return outputs, grad_tokens, grad_gens.reshape(sections, rows, block)
+    return outputs, grad_tokens, jnp.swapaxes(grad_gens.reshape(sections, block, rows), 1, 2)
 
 
 def solution(mesh):

time: 152 us -> 135 us (0.89)
  waiting for transfers between devices: 37.3 us -> 57.3 us
  other arithmetic: 19.4 us -> 3.72 us
  starting transfers between devices: 24.1 us -> 17.4 us
  local copies, waits for them, and re-layouts: 11.3 us -> 4.82 us
  Pallas kernels: 55.3 us -> 51.1 us
  between operations: 3.89 us -> 0.87 us
    ppermute x19 -> x15, waiting for transfers between devices: 37.3 us -> 57.3 us  [exchange(): lax.ppermute(array, 'tensor', [(i, i ^ 1 << bit) for i in range(size)])]
    add x6 -> x2, other arithmetic: 7.01 us -> 0.08 us  [stage(): return (keep[mid:] + got[mid:], keep[:mid] + got[:mid])]
    ppermute x19 -> x15, starting transfers between devices: 24.1 us -> 17.4 us  [exchange(): lax.ppermute(array, 'tensor', [(i, i ^ 1 << bit) for i in range(size)])]
    reduce_max x2 -> x0, other arithmetic: 4.43 us -> none  [narrow(): jnp.max(jnp.abs(rows))]
    concatenate x3 -> x1, other arithmetic: 4.49 us -> 1 us  [grow(): return jnp.concatenate([array, exchange(array, bit)], axis=0)]
    pallas_call x1, Pallas kernels: 16.5 us -> 13.1 us  [local(): pl.pallas_call(grads_kernel, out_shape=(jax.ShapeDtypeStruct((count, rows...]
    unnamed x41 -> x18, local copies, waits for them, and re-layouts: 5.93 us -> 2.63 us
    concatenate x3 -> x0, local copies, waits for them, and re-layouts: 3.12 us -> none  [the longest x2 2.04 us: narrow(): jnp.concatenate([rows * jnp.exp2(-exponent), tag], axis=0)]
  transfers between devices with their start and end apart: 19 -> 15, of which waited for: 8 -> 10; matrix products, arithmetic and copies ran while one was open for 17% -> 3% of each run, Pallas kernels for 37% -> 38%
where the time goes in v6:
time: 135 us
  waiting for transfers between devices  57.3 us (42%)
  Pallas kernels  51.1 us (38%)
  starting transfers between devices  17.4 us (13%)
  local copies, waits for them, and re-layouts  4.82 us (4%)
  other arithmetic  3.72 us (3%)
    ppermute x15, waiting for transfers between devices, exchange(): lax.ppermute(array, 'tensor', [(i, i ^ 1 << bit) for i in range(size)])  57.3 us
    ppermute x15, starting transfers between devices, exchange(): lax.ppermute(array, 'tensor', [(i, i ^ 1 << bit) for i in range(size)])  17.4 us
    pallas_call x2, Pallas kernels, project(): pl.pallas_call(functools.partial(project_kernel, chunk), out_shape=(jax.S...  15.1 us
    pallas_call x1, Pallas kernels, local(): pl.pallas_call(grads_kernel, out_shape=(jax.ShapeDtypeStruct((count, rows...  13.1 us
    pallas_call x1, Pallas kernels, project_back(): pl.pallas_call(functools.partial(back_kernel, order), out_shape=jax.Shape...  8.23 us
    pallas_call x1, Pallas kernels, local(): pl.pallas_call(near_kernel, out_shape=(jax.ShapeDtypeStruct(square, f32),...  7.41 us
    pallas_call x1, Pallas kernels, local(): pl.pallas_call(far_rotations_kernel, out_shape=(jax.ShapeDtypeStruct(far_...  5.28 us
  transfers between devices with their start and end apart: 15, of which 10 were waited for; matrix products, arithmetic and copies ran while one was open for 3% of the time, Pallas kernels for 38%

profile of v6, /device:TPU:0, one launch (start us, length us, event | category | flops | bytes accessed | tf_op | source)
XLA Modules:
  0.0 135.1 jit_solution(13617565320240155994)
XLA Ops:
  0.6 4.1 %collective-permute-start = (bf16[1,128,1024]{2,1,0:T(8,128)(2,1)}, bf16[1,128,1024]{2,1,0:T(8,128)(2,1)S(1)}, u32[]{:S(2)}, u32[]{:S(2)}) collective-permute-start(bf16[1,128,1024]{2,1,0:T(8,128)(2,1)} %bitcast.18), channel_id=1, source_target_pairs={{0,8},{1,9},{2,10},{3,11},{4,12},{5,13},{6,14},{7,15},{8,0},{9,1},... | collective-permute-start | bytes 786440 | tf_op jit(solution)/shard_map/ppermute | solution.py:22
  4.7 0.8 slice_bitcast_fusion.1.own_ref
  5.6 0.9 copy-done.2
  6.5 0.9 copy-done.4
  7.5 0.7 copy-done.5
  8.1 7.4 %near_rotations.1 = (f32[1024,128]{1,0:T(8,128)S(1)}, f32[3,512,128]{2,1,0:T(8,128)S(1)}, f32[3,128,512]{2,1,0:T(8,128)S(1)}) custom-call(s32[4,32]{1,0:T(4,128)S(1)} %copy-done.5, f32[128,512]{1,0:T(8,128)S(1)} %bitcast.17, bf16[128,512]{1,0:T(8,128)(2,1)S(1)} %copy-done.2), custom_call_target="tpu_custom_call" | custom-call | tf_op jit(solution)/shard_map/near_rotations/pallas_call | solution.py:538
  15.6 3.4 %collective-permute-done = bf16[1,128,1024]{2,1,0:T(8,128)(2,1)S(1)} collective-permute-done((bf16[1,128,1024]{2,1,0:T(8,128)(2,1)}, bf16[1,128,1024]{2,1,0:T(8,128)(2,1)S(1)}, u32[]{:S(2)}, u32[]{:S(2)}) %collective-permute-start) | collective-permute-done | bytes 262176 | tf_op jit(solution)/shard_map/ppermute | solution.py:22
  19.0 1.0 pad_maximum_fusion.1
  20.0 0.4 collective-permute-start.5
  20.4 5.3 %far_rotations.1 = (f32[1024,32]{1,0:T(8,128)S(1)}, f32[2,512,128]{2,1,0:T(8,128)S(1)}, f32[2,512,128]{2,1,0:T(8,128)S(1)}) custom-call(s32[1,32]{1,0:T(1,128)S(1)} %slice.36.orders_ref, s32[1]{0:T(128)} %bitcast.5.high_ref, f32[32,512]{1,0:T(8,128)S(1)} %slice_bitcast_fusion.1.own_ref, f32[32,512]{1,0:T(8,128)S(1)} %collective-permute-done.1.far_ref), custom_call_target="tpu_custom_call" | custom-call | flops 10000000 | bytes 10000000 | tf_op jit(solution)/shard_map/far_rotations/pallas_call | solution.py:560
  25.7 7.1 %collective-permute-done.5 = bf16[2,128,1024]{2,1,0:T(8,128)(2,1)S(1)} collective-permute-done((bf16[2,128,1024]{2,1,0:T(8,128)(2,1)S(1)}, bf16[2,128,1024]{2,1,0:T(8,128)(2,1)S(1)}, u32[]{:S(2)}, u32[]{:S(2)}) %collective-permute-start.5) | collective-permute-done | bytes 524320 | tf_op jit(solution)/shard_map/ppermute | solution.py:22
  32.8 1.1 pad_maximum_fusion
  33.9 1.3 collective-permute-start.6
  35.2 3.3 %collective-permute-start.2 = (f32[128,512]{1,0:T(8,128)S(1)}, f32[128,512]{1,0:T(8,128)S(1)}, u32[]{:S(2)}, u32[]{:S(2)}) collective-permute-start(f32[128,512]{1,0:T(8,128)S(1)} %slice_bitcast_fusion.own_ref), channel_id=1, source_target_pairs={{0,8},{1,9},{2,10},{3,11},{4,12},{5,13},{6,14},{7,15},{8,0},{9,1},... | collective-permute-start | bytes 786440 | tf_op jit(solution)/shard_map/ppermute | solution.py:22
  38.5 11.3 %collective-permute-done.2.oth_ref.x_oth_ref = f32[128,512]{1,0:T(8,128)S(1)} collective-permute-done((f32[128,512]{1,0:T(8,128)S(1)}, f32[128,512]{1,0:T(8,128)S(1)}, u32[]{:S(2)}, u32[]{:S(2)}) %collective-permute-start.2) | collective-permute-done | bytes 262176 | tf_op jit(solution)/shard_map/ppermute | solution.py:22
  49.8 0.4 far_apply.1.x_ref
  50.2 7.6 %project.2 = (f32[8,128,512]{2,1,0:T(8,128)S(1)}, f32[8,128,512]{2,1,0:T(8,128)}) custom-call(s32[16]{0:T(128)S(1)} %broadcast_xor_fusion.places_ref, bf16[256,512]{1,0:T(8,128)(2,1)S(1)} %far_apply.1.x_ref, bf16[512,16384]{1,0:T(8,128)(2,1)} %w_ref.5), custom_call_target="tpu_custom_call" | custom-call | flops 2147483648 | bytes 12582912 | tf_op jit(solution)/shard_map/project/pallas_call | solution.py:294
  57.8 0.1 collective-permute-start.3
  57.8 7.6 %project.3 = (f32[8,128,512]{2,1,0:T(8,128)S(1)}, f32[8,128,512]{2,1,0:T(8,128)}) custom-call(s32[16]{0:T(128)S(1)} %broadcast_xor_fusion.places_ref, bf16[256,512]{1,0:T(8,128)(2,1)S(1)} %far_apply.1.x_ref, bf16[512,16384]{1,0:T(8,128)(2,1)} %w_ref.5), custom_call_target="tpu_custom_call" | custom-call | flops 2147483648 | bytes 12582912 | tf_op jit(solution)/shard_map/project/pallas_call | solution.py:294
  65.4 0.6 collective-permute-start.7
  66.0 1.3 constant_dynamic-update-slice_fusion.low_ref
  67.4 0.2 collective-permute-start.8
  67.6 0.6 sum_pack.2
  68.2 0.1 convert_element_type.12
  68.3 0.6 collective-permute-start.4
  68.8 0.9 collective-permute-done.7.got_ref
  69.8 0.5 sum_pack.3
  70.3 0.1 convert_element_type.13
  70.4 0.7 collective-permute-start.11
  71.1 1.8 %collective-permute-done.8.high_ref = bf16[8,128,1024]{2,1,0:T(8,128)(2,1)} collective-permute-done((bf16[8,128,1024]{2,1,0:T(8,128)(2,1)S(1)}, bf16[8,128,1024]{2,1,0:T(8,128)(2,1)}, u32[]{:S(2)}, u32[]{:S(2)}) %collective-permute-start.8) | collective-permute-done | bytes 2097184 | tf_op jit(solution)/shard_map/ppermute | solution.py:22
  72.9 8.2 %project_back.1.own_ref = f32[128,512]{1,0:T(8,128)S(1)} custom-call(s32[16]{0:T(128)S(1)} %iota_xor_fusion.places_ref, bf16[8,128,1024]{2,1,0:T(8,128)(2,1)S(1)} %constant_dynamic-update-slice_fusion.low_ref, bf16[8,128,1024]{2,1,0:T(8,128)(2,1)} %collective-permute-done.8.high_ref, bf16[512,16384]{1,0:T(8,128)(2,1)} %w_ref.5), custom_call_target="tpu_custom_call" | custom-call | flops 2147483648 | bytes 20971520 | tf_op jit(solution)/shard_map/project_back/pallas_call | solution.py:349
  81.1 0.1 collective-permute-start.12
  81.2 2.2 %collective-permute-done.4 = f16[528,512]{1,0:T(8,128)(2,1)S(1)} collective-permute-done((f16[528,512]{1,0:T(8,128)(2,1)S(1)}, f16[528,512]{1,0:T(8,128)(2,1)S(1)}, u32[]{:S(2)}, u32[]{:S(2)}) %collective-permute-start.4) | collective-permute-done | bytes 540704 | tf_op jit(solution)/shard_map/ppermute | solution.py:22
  83.4 0.1 convert_element_type.14.got_ref
  83.6 0.2 sum_unpack.2
  83.8 1.9 %collective-permute-start.9 = (f32[2,128,512]{2,1,0:T(8,128)S(1)}, f32[2,128,512]{2,1,0:T(8,128)S(1)}, u32[]{:S(2)}, u32[]{:S(2)}) collective-permute-start(f32[2,128,512]{2,1,0:T(8,128)S(1)} %get-tuple-element.49), channel_id=1, source_target_pairs={{0,4},{1,5},{2,6},{3,7},{4,0},{5,1},{6,2},{7,3},{8,12},{9,13},{10,... | collective-permute-start | bytes 1572872 | tf_op jit(solution)/shard_map/ppermute | solution.py:22
  85.7 8.8 %collective-permute-done.11 = f16[528,512]{1,0:T(8,128)(2,1)S(1)} collective-permute-done((f16[528,512]{1,0:T(8,128)(2,1)S(1)}, f16[528,512]{1,0:T(8,128)(2,1)S(1)}, u32[]{:S(2)}, u32[]{:S(2)}) %collective-permute-start.11) | collective-permute-done | bytes 540704 | tf_op jit(solution)/shard_map/ppermute | solution.py:22
  94.5 1.9 %collective-permute-done.12.oth_ref = f32[128,512]{1,0:T(8,128)S(1)} collective-permute-done((f32[128,512]{1,0:T(8,128)S(1)}, f32[128,512]{1,0:T(8,128)S(1)}, u32[]{:S(2)}, u32[]{:S(2)}) %collective-permute-start.12) | collective-permute-done | bytes 262176 | tf_op jit(solution)/shard_map/ppermute | solution.py:22
  96.4 0.1 convert_element_type.15.got_ref
  96.6 0.2 sum_unpack.3
  96.8 0.1 collective-permute-start.13
  96.9 6.4 %collective-permute-done.9 = f32[2,128,512]{2,1,0:T(8,128)S(1)} collective-permute-done((f32[2,128,512]{2,1,0:T(8,128)S(1)}, f32[2,128,512]{2,1,0:T(8,128)S(1)}, u32[]{:S(2)}, u32[]{:S(2)}) %collective-permute-start.9) | collective-permute-done | bytes 524320 | tf_op jit(solution)/shard_map/ppermute | solution.py:22
  103.3 2.6 %collective-permute-start.10 = (f32[1,128,512]{2,1,0:T(8,128)S(1)}, f32[1,128,512]{2,1,0:T(8,128)S(1)}, u32[]{:S(2)}, u32[]{:S(2)}) collective-permute-start(f32[1,128,512]{2,1,0:T(8,128)S(1)} %slice_add_fusion.2), channel_id=1, source_target_pairs={{0,8},{1,9},{2,10},{3,11},{4,12},{5,13},{6,14},{7,15},{8,0},{9,1},... | collective-permute-start | bytes 786440 | tf_op jit(solution)/shard_map/ppermute | solution.py:22
  105.9 13.5 %collective-permute-done.13 = f32[2,128,512]{2,1,0:T(8,128)S(1)} collective-permute-done((f32[2,128,512]{2,1,0:T(8,128)S(1)}, f32[2,128,512]{2,1,0:T(8,128)S(1)}, u32[]{:S(2)}, u32[]{:S(2)}) %collective-permute-start.13) | collective-permute-done | bytes 524320 | tf_op jit(solution)/shard_map/ppermute | solution.py:22
  119.4 1.5 %collective-permute-start.14 = (f32[1,128,512]{2,1,0:T(8,128)S(1)}, f32[1,128,512]{2,1,0:T(8,128)S(1)}, u32[]{:S(2)}, u32[]{:S(2)}) collective-permute-start(f32[1,128,512]{2,1,0:T(8,128)S(1)} %slice_add_fusion), channel_id=1, source_target_pairs={{0,8},{1,9},{2,10},{3,11},{4,12},{5,13},{6,14},{7,15},{8,0},{9,1},... | collective-permute-start | bytes 786440 | tf_op jit(solution)/shard_map/ppermute | solution.py:22
  121.0 0.1 select_reduce_fusion.inverse_ref
  121.1 13.1 %gradients.1 = (f32[128,512]{1,0:T(8,128)}, f32[128,512]{1,0:T(8,128)}) custom-call(s32[4,32]{1,0:T(4,128)S(1)} %select_reduce_fusion.inverse_ref, s32[1]{0:T(128)} %bitcast.5.high_ref, f32[128,512]{1,0:T(8,128)S(1)} %project_back.1.own_ref, f32[128,512]{1,0:T(8,128)S(1)} %collective-permute-done.12.oth_ref, ...), custom_call_target="tpu_custom_call" | custom-call | tf_op jit(solution)/shard_map/gradients/pallas_call | solution.py:622
  134.3 0.8 pad_maximum_fusion.2
  (29 shorter events, 0.4 us)
Async XLA Ops:
  0.6 18.3 %collective-permute-start = (bf16[1,128,1024]{2,1,0:T(8,128)(2,1)}, bf16[1,128,1024]{2,1,0:T(8,128)(2,1)S(1)}, u32[]{:S(2)}, u32[]{:S(2)}) collective-permute-start(bf16[1,128,1024]{2,1,0:T(8,128)(2,1)} %bitcast.18), channel_id=1, source_target_pairs={{0,8},{1,9},{2,10},{3,11},{4,12},{5,13},{6,14},{7,15},{8,0},{9,1},... | collective-permute-start | bytes 786440 | tf_op jit(solution)/shard_map/ppermute | solution.py:22
  5.6 14.4 %collective-permute-start.1 = (f32[32,512]{1,0:T(8,128)S(1)}, f32[32,512]{1,0:T(8,128)S(1)}, u32[]{:S(2)}, u32[]{:S(2)}) collective-permute-start(f32[32,512]{1,0:T(8,128)S(1)} %slice_bitcast_fusion.1.own_ref), channel_id=1, source_target_pairs={{0,8},{1,9},{2,10},{3,11},{4,12},{5,13},{6,14},{7,15},{8,0},{9,1},... | collective-permute-start | bytes 196616 | tf_op jit(solution)/shard_map/ppermute | solution.py:22
  5.6 0.9 copy-start.2
  6.5 0.9 copy-start.4
  7.5 0.7 copy-start.5
  8.1 30.4 %copy-start.7 = (s32[16]{0:T(128)S(1)}, s32[16]{0:T(128)}, u32[]{:S(2)}) copy-start(s32[16]{0:T(128)} %constant.12.clone) | copy-start | bytes 196
  20.0 12.8 %collective-permute-start.5 = (bf16[2,128,1024]{2,1,0:T(8,128)(2,1)S(1)}, bf16[2,128,1024]{2,1,0:T(8,128)(2,1)S(1)}, u32[]{:S(2)}, u32[]{:S(2)}) collective-permute-start(bf16[2,128,1024]{2,1,0:T(8,128)(2,1)S(1)} %pad_maximum_fusion.1), channel_id=1, source_target_pairs={{0,4},{1,5},{2,6},{3,7},{4,0},{5,1},{6,2},{7,3},{8,12},{9,13},{10,... | collective-permute-start | bytes 1572872 | tf_op jit(solution)/shard_map/ppermute | solution.py:22
  33.9 32.1 %collective-permute-start.6 = (bf16[4,128,1024]{2,1,0:T(8,128)(2,1)}, bf16[4,128,1024]{2,1,0:T(8,128)(2,1)}, u32[]{:S(2)}, u32[]{:S(2)}) collective-permute-start(bf16[4,128,1024]{2,1,0:T(8,128)(2,1)} %pad_maximum_fusion), channel_id=1, source_target_pairs={{0,2},{1,3},{2,0},{3,1},{4,6},{5,7},{6,4},{7,5},{8,10},{9,11},{10,... | collective-permute-start | bytes 3145736 | tf_op jit(solution)/shard_map/ppermute | solution.py:22
  35.2 14.6 %collective-permute-start.2 = (f32[128,512]{1,0:T(8,128)S(1)}, f32[128,512]{1,0:T(8,128)S(1)}, u32[]{:S(2)}, u32[]{:S(2)}) collective-permute-start(f32[128,512]{1,0:T(8,128)S(1)} %slice_bitcast_fusion.own_ref), channel_id=1, source_target_pairs={{0,8},{1,9},{2,10},{3,11},{4,12},{5,13},{6,14},{7,15},{8,0},{9,1},... | collective-permute-start | bytes 786440 | tf_op jit(solution)/shard_map/ppermute | solution.py:22
  57.8 9.8 %collective-permute-start.3 = (f32[8,128,512]{2,1,0:T(8,128)S(1)}, f32[8,128,512]{2,1,0:T(8,128)S(1)}, u32[]{:S(2)}, u32[]{:S(2)}) collective-permute-start(f32[8,128,512]{2,1,0:T(8,128)S(1)} %get-tuple-element.37), channel_id=1, source_target_pairs={{0,1},{1,0},{2,3},{3,2},{4,5},{5,4},{6,7},{7,6},{8,9},{9,8},{10,11... | collective-permute-start | bytes 6291464 | tf_op jit(solution)/shard_map/ppermute | solution.py:22
  65.4 2.1 %copy-start.1 = (f32[8,128,512]{2,1,0:T(8,128)S(1)}, f32[8,128,512]{2,1,0:T(8,128)}, u32[]{:S(2)}) copy-start(f32[8,128,512]{2,1,0:T(8,128)} %get-tuple-element.36.keep_ref) | copy-start | bytes 6291460
  65.4 4.3 %collective-permute-start.7 = (f32[8,128,512]{2,1,0:T(8,128)S(1)}, f32[8,128,512]{2,1,0:T(8,128)S(1)}, u32[]{:S(2)}, u32[]{:S(2)}) collective-permute-start(f32[8,128,512]{2,1,0:T(8,128)S(1)} %get-tuple-element.44), channel_id=1, source_target_pairs={{0,1},{1,0},{2,3},{3,2},{4,5},{5,4},{6,7},{7,6},{8,9},{9,8},{10,11... | collective-permute-start | bytes 6291464 | tf_op jit(solution)/shard_map/ppermute | solution.py:22
  67.4 5.5 %collective-permute-start.8 = (bf16[8,128,1024]{2,1,0:T(8,128)(2,1)S(1)}, bf16[8,128,1024]{2,1,0:T(8,128)(2,1)}, u32[]{:S(2)}, u32[]{:S(2)}) collective-permute-start(bf16[8,128,1024]{2,1,0:T(8,128)(2,1)S(1)} %constant_dynamic-update-slice_fusion.low_ref), channel_id=1, source_target_pairs={{0,1},{1,0},{2,3},{3,2},{4,5},{5,4},{6,7},{7,6},{8,9},{9,8},{10,11... | collective-permute-start | bytes 6291464 | tf_op jit(solution)/shard_map/ppermute | solution.py:22
  67.6 2.2 %copy-start = (f32[8,128,512]{2,1,0:T(8,128)S(1)}, f32[8,128,512]{2,1,0:T(8,128)}, u32[]{:S(2)}) copy-start(f32[8,128,512]{2,1,0:T(8,128)} %get-tuple-element.43.keep_ref) | copy-start | bytes 6291460
  68.3 15.1 %collective-permute-start.4 = (f16[528,512]{1,0:T(8,128)(2,1)S(1)}, f16[528,512]{1,0:T(8,128)(2,1)S(1)}, u32[]{:S(2)}, u32[]{:S(2)}) collective-permute-start(f16[528,512]{1,0:T(8,128)(2,1)S(1)} %convert_element_type.12), channel_id=1, source_target_pairs={{0,2},{1,3},{2,0},{3,1},{4,6},{5,7},{6,4},{7,5},{8,10},{9,11},{10,... | collective-permute-start | bytes 1622024 | tf_op jit(solution)/shard_map/ppermute | solution.py:22
  70.4 24.1 %collective-permute-start.11 = (f16[528,512]{1,0:T(8,128)(2,1)S(1)}, f16[528,512]{1,0:T(8,128)(2,1)S(1)}, u32[]{:S(2)}, u32[]{:S(2)}) collective-permute-start(f16[528,512]{1,0:T(8,128)(2,1)S(1)} %convert_element_type.13), channel_id=1, source_target_pairs={{0,2},{1,3},{2,0},{3,1},{4,6},{5,7},{6,4},{7,5},{8,10},{9,11},{10,... | collective-permute-start | bytes 1622024 | tf_op jit(solution)/shard_map/ppermute | solution.py:22
  81.1 15.3 %collective-permute-start.12 = (f32[128,512]{1,0:T(8,128)S(1)}, f32[128,512]{1,0:T(8,128)S(1)}, u32[]{:S(2)}, u32[]{:S(2)}) collective-permute-start(f32[128,512]{1,0:T(8,128)S(1)} %project_back.1.own_ref), channel_id=1, source_target_pairs={{0,8},{1,9},{2,10},{3,11},{4,12},{5,13},{6,14},{7,15},{8,0},{9,1},... | collective-permute-start | bytes 786440 | tf_op jit(solution)/shard_map/ppermute | solution.py:22
  83.8 19.5 %collective-permute-start.9 = (f32[2,128,512]{2,1,0:T(8,128)S(1)}, f32[2,128,512]{2,1,0:T(8,128)S(1)}, u32[]{:S(2)}, u32[]{:S(2)}) collective-permute-start(f32[2,128,512]{2,1,0:T(8,128)S(1)} %get-tuple-element.49), channel_id=1, source_target_pairs={{0,4},{1,5},{2,6},{3,7},{4,0},{5,1},{6,2},{7,3},{8,12},{9,13},{10,... | collective-permute-start | bytes 1572872 | tf_op jit(solution)/shard_map/ppermute | solution.py:22
  96.6 24.4 %copy-start.6 = (s32[4,32]{1,0:T(4,128)S(1)}, s32[4,32]{1,0:T(4,128)}, u32[]{:S(2)}) copy-start(s32[4,32]{1,0:T(4,128)} %orders_ref.1) | copy-start | bytes 1540
  96.6 24.5 %copy-start.3 = (bf16[128,512]{1,0:T(8,128)(2,1)S(1)}, bf16[128,512]{1,0:T(8,128)(2,1)}, u32[]{:S(2)}) copy-start(bf16[128,512]{1,0:T(8,128)(2,1)} %tok_ref.3) | copy-start | bytes 393220
  96.8 22.6 %collective-permute-start.13 = (f32[2,128,512]{2,1,0:T(8,128)S(1)}, f32[2,128,512]{2,1,0:T(8,128)S(1)}, u32[]{:S(2)}, u32[]{:S(2)}) collective-permute-start(f32[2,128,512]{2,1,0:T(8,128)S(1)} %get-tuple-element.53), channel_id=1, source_target_pairs={{0,4},{1,5},{2,6},{3,7},{4,0},{5,1},{6,2},{7,3},{8,12},{9,13},{10,... | collective-permute-start | bytes 1572872 | tf_op jit(solution)/shard_map/ppermute | solution.py:22
  103.3 30.8 %collective-permute-start.10 = (f32[1,128,512]{2,1,0:T(8,128)S(1)}, f32[1,128,512]{2,1,0:T(8,128)S(1)}, u32[]{:S(2)}, u32[]{:S(2)}) collective-permute-start(f32[1,128,512]{2,1,0:T(8,128)S(1)} %slice_add_fusion.2), channel_id=1, source_target_pairs={{0,8},{1,9},{2,10},{3,11},{4,12},{5,13},{6,14},{7,15},{8,0},{9,1},... | collective-permute-start | bytes 786440 | tf_op jit(solution)/shard_map/ppermute | solution.py:22
  119.4 14.8 %collective-permute-start.14 = (f32[1,128,512]{2,1,0:T(8,128)S(1)}, f32[1,128,512]{2,1,0:T(8,128)S(1)}, u32[]{:S(2)}, u32[]{:S(2)}) collective-permute-start(f32[1,128,512]{2,1,0:T(8,128)S(1)} %slice_add_fusion), channel_id=1, source_target_pairs={{0,8},{1,9},{2,10},{3,11},{4,12},{5,13},{6,14},{7,15},{8,0},{9,1},... | collective-permute-start | bytes 786440 | tf_op jit(solution)/shard_map/ppermute | solution.py:22

commit v7 on v6

--- a/solution.py
+++ b/solution.py
@@ -262,49 +262,56 @@
         )
 
 
-def project_kernel(
-    chunk, places_ref, x_ref, w_ref, send_ref, keep_ref, held_ref, made_ref, sems, out_sems
-):
-    pieces, count, width = send_ref.shape
-
-    def leave(p):
-        target = send_ref if p < pieces else keep_ref
-        return pltpu.make_async_copy(made_ref.at[p], target.at[p % pieces], out_sems.at[p])
+def project_kernel(places_ref, x_ref, w_ref, *refs):
+    *out_refs, held_ref, made_ref, sems, out_sems = refs
+    pieces, count, width = made_ref.shape
+    half = pieces // 2
+    part = width // CHUNKS
 
     def fetch(p):
-        at = pl.multiple_of((places_ref[p] * CHUNKS + chunk) * width, width)
+        at = pl.multiple_of(places_ref[p] * width, width)
         return pltpu.make_async_copy(w_ref.at[:, pl.ds(at, width)], held_ref.at[p], sems.at[p])
 
-    for p in range(2 * pieces):
+    def leave(p, chunk):
+        return pltpu.make_async_copy(
+            made_ref.at[p, :, pl.ds(chunk * part, part)],
+            out_refs[2 * chunk + p // half].at[p % half],
+            out_sems.at[chunk, p],
+        )
+
+    for p in range(pieces):
         fetch(p).start()
-    for p in range(2 * pieces):
+    for p in range(pieces):
         fetch(p).wait()
         both = one_dot(x_ref[...], held_ref[p])
         made_ref[p] = both[:count] + both[count:]
-        leave(p).start()
-    for p in range(2 * pieces):
-        leave(p).wait()
-
-
-def project(x_both, weight, places, chunk):
+        for chunk in range(CHUNKS):
+            leave(p, chunk).start()
+    for p in range(pieces):
+        for chunk in range(CHUNKS):
+            leave(p, chunk).wait()
+
+
+def project(x_both, weight, places):
     pieces = places.shape[0]
     count2, rows = x_both.shape
     count = count2 // 2
-    width = weight.shape[1] // lax.axis_size("tensor") // CHUNKS
-    return pl.pallas_call(
-        functools.partial(project_kernel, chunk),
-        out_shape=(jax.ShapeDtypeStruct((pieces // 2, count, width), jnp.float32),) * 2,
+    width = weight.shape[1] // lax.axis_size("tensor")
+    outs = pl.pallas_call(
+        project_kernel,
+        out_shape=(jax.ShapeDtypeStruct((pieces // 2, count, width // CHUNKS), jnp.float32),)
+        * (2 * CHUNKS),
         in_specs=[
             pl.BlockSpec(memory_space=pltpu.SMEM),
             pl.BlockSpec(memory_space=pltpu.VMEM),
             pl.BlockSpec(memory_space=pl.ANY),
         ],
-        out_specs=(pl.BlockSpec(memory_space=pl.ANY),) * 2,
+        out_specs=(pl.BlockSpec(memory_space=pl.ANY),) * (2 * CHUNKS),
         scratch_shapes=[
             pltpu.VMEM((pieces, rows, width), weight.dtype),
             pltpu.VMEM((pieces, count, width), jnp.float32),
             pltpu.SemaphoreType.DMA((pieces,)),
-            pltpu.SemaphoreType.DMA((pieces,)),
+            pltpu.SemaphoreType.DMA((CHUNKS, pieces)),
         ],
         compiler_params=pltpu.CompilerParams(vmem_limit_bytes=WIDE_LIMIT),
         cost_estimate=pl.CostEstimate(
@@ -314,6 +321,7 @@
         ),
         name="project",
     )(places, x_both, weight)
+    return [outs[2 * chunk : 2 * chunk + 2] for chunk in range(CHUNKS)]
 
 
 def back_kernel(order, places_ref, low_ref, high_ref, w_ref, out_ref, cots_ref, held_ref, cot_sems, sems):
@@ -578,7 +586,7 @@
         cost_estimate=pl.CostEstimate(flops=10**7, bytes_accessed=10**7, transcendentals=0),
         name="far_rotations",
     )(orders[:1], high, stored[0], far_gen)
-    pieces = jnp.concatenate([pieces, after(news, ffar)], axis=0)
+    pieces = jnp.concatenate([pieces, after(news, ffar, x_other)], axis=0)
     for bit in order[2:-1]:
         pieces = grow(pieces, bit)
     x_both = pl.pallas_call(
@@ -596,10 +604,7 @@
     fixed = here.astype(jnp.int32)
     places = jnp.bitwise_xor(fixed, jnp.asarray(np.roll(reverse, size // 2)))
     back_places = jnp.bitwise_xor(fixed, jnp.arange(size, dtype=jnp.int32))
-    outs = []
-    for chunk in range(CHUNKS):
-        outs.append(project(x_both, weight, places, chunk))
-        x_both = after(x_both, outs[-1][0])
+    outs = project(x_both, weight, places)
 
     def stage(pair, got):
         send, keep = pair
@@ -641,7 +646,7 @@
     outs = [unpack(keep, got) for (_, keep), got in zip(outs, gots)]
     for bit in range(2, bits):
         gots = [exchange(send, bit) for send, _ in outs]
-        if bit == bits - 1:
+        if bit == 2:
             gots[-1] = after(gots[-1], grad_tokens, grad_gens)
         outs = [stage(pair, got) for pair, got in zip(outs, gots)]
     outputs = jnp.concatenate([keep[0] for _, keep in outs], axis=1)

time: 135 us -> 133 us (0.985)
  Pallas kernels: 51.1 us -> 46.1 us
  starting transfers between devices: 17.4 us -> 22.4 us
  waiting for transfers between devices: 57.3 us -> 54.1 us
    ppermute x15, starting transfers between devices: 17.4 us -> 22.4 us  [exchange(): lax.ppermute(array, 'tensor', [(i, i ^ 1 << bit) for i in range(size)])]
    pallas_call x2 -> x1, Pallas kernels: 15.1 us -> 10.2 us  [project(): pl.pallas_call(project_kernel, out_shape=(jax.ShapeDtypeStruct((pieces //...]
    ppermute x15, waiting for transfers between devices: 57.3 us -> 54.1 us  [exchange(): lax.ppermute(array, 'tensor', [(i, i ^ 1 << bit) for i in range(size)])]
    unnamed x18 -> x20, local copies, waits for them, and re-layouts: 2.63 us -> 5.01 us
  transfers between devices with their start and end apart: 15 -> 15, of which waited for: 10 -> 10; matrix products, arithmetic and copies ran while one was open for 3% -> 3% of each run, Pallas kernels for 38% -> 35%
where the time goes in v7:
time: 133 us
  waiting for transfers between devices  54.1 us (41%)
  Pallas kernels  46.1 us (35%)
  starting transfers between devices  22.4 us (17%)
  local copies, waits for them, and re-layouts  5.94 us (4%)
  other arithmetic  3.73 us (3%)
    ppermute x15, waiting for transfers between devices, exchange(): lax.ppermute(array, 'tensor', [(i, i ^ 1 << bit) for i in range(size)])  54.1 us
    ppermute x15, starting transfers between devices, exchange(): lax.ppermute(array, 'tensor', [(i, i ^ 1 << bit) for i in range(size)])  22.4 us
    pallas_call x1, Pallas kernels, local(): pl.pallas_call(grads_kernel, out_shape=(jax.ShapeDtypeStruct((count, rows...  13.1 us
    pallas_call x1, Pallas kernels, project(): pl.pallas_call(project_kernel, out_shape=(jax.ShapeDtypeStruct((pieces //...  10.2 us
    pallas_call x1, Pallas kernels, project_back(): pl.pallas_call(functools.partial(back_kernel, order), out_shape=jax.Shape...  8.24 us
    pallas_call x1, Pallas kernels, local(): pl.pallas_call(near_kernel, out_shape=(jax.ShapeDtypeStruct(square, f32),...  7.41 us
    pallas_call x1, Pallas kernels, local(): pl.pallas_call(far_rotations_kernel, out_shape=(jax.ShapeDtypeStruct(far_...  5.28 us
    unnamed x20, local copies, waits for them, and re-layouts  5.01 us
  transfers between devices with their start and end apart: 15, of which 10 were waited for; matrix products, arithmetic and copies ran while one was open for 3% of the time, Pallas kernels for 35%

profile of v7, /device:TPU:0, one launch (start us, length us, event | category | flops | bytes accessed | tf_op | source)
XLA Modules:
  0.0 133.1 jit_solution(3677733653883778585)
XLA Ops:
  0.6 4.1 %collective-permute-start = (bf16[1,128,1024]{2,1,0:T(8,128)(2,1)}, bf16[1,128,1024]{2,1,0:T(8,128)(2,1)S(1)}, u32[]{:S(2)}, u32[]{:S(2)}) collective-permute-start(bf16[1,128,1024]{2,1,0:T(8,128)(2,1)} %bitcast.18), channel_id=1, source_target_pairs={{0,8},{1,9},{2,10},{3,11},{4,12},{5,13},{6,14},{7,15},{8,0},{9,1},... | collective-permute-start | bytes 786440 | tf_op jit(solution)/shard_map/ppermute | solution.py:22
  4.7 0.8 slice_bitcast_fusion.1.own_ref
  5.6 0.9 copy-done.2
  6.5 0.9 copy-done.4
  7.5 0.7 copy-done.5
  8.1 7.4 %near_rotations.1 = (f32[1024,128]{1,0:T(8,128)S(1)}, f32[3,512,128]{2,1,0:T(8,128)S(1)}, f32[3,128,512]{2,1,0:T(8,128)S(1)}) custom-call(s32[4,32]{1,0:T(4,128)S(1)} %copy-done.5, f32[128,512]{1,0:T(8,128)S(1)} %bitcast.17, bf16[128,512]{1,0:T(8,128)(2,1)S(1)} %copy-done.2), custom_call_target="tpu_custom_call" | custom-call | tf_op jit(solution)/shard_map/near_rotations/pallas_call | solution.py:546
  15.6 3.4 %collective-permute-done = bf16[1,128,1024]{2,1,0:T(8,128)(2,1)S(1)} collective-permute-done((bf16[1,128,1024]{2,1,0:T(8,128)(2,1)}, bf16[1,128,1024]{2,1,0:T(8,128)(2,1)S(1)}, u32[]{:S(2)}, u32[]{:S(2)}) %collective-permute-start) | collective-permute-done | bytes 262176 | tf_op jit(solution)/shard_map/ppermute | solution.py:22
  19.0 1.0 pad_maximum_fusion.1
  20.0 0.4 collective-permute-start.5
  20.4 3.4 %collective-permute-start.2 = (f32[128,512]{1,0:T(8,128)S(1)}, f32[128,512]{1,0:T(8,128)S(1)}, u32[]{:S(2)}, u32[]{:S(2)}) collective-permute-start(f32[128,512]{1,0:T(8,128)S(1)} %slice_bitcast_fusion.own_ref), channel_id=1, source_target_pairs={{0,8},{1,9},{2,10},{3,11},{4,12},{5,13},{6,14},{7,15},{8,0},{9,1},... | collective-permute-start | bytes 786440 | tf_op jit(solution)/shard_map/ppermute | solution.py:22
  23.8 5.3 %far_rotations.1 = (f32[1024,32]{1,0:T(8,128)S(1)}, f32[2,512,128]{2,1,0:T(8,128)S(1)}, f32[2,512,128]{2,1,0:T(8,128)S(1)}) custom-call(s32[1,32]{1,0:T(1,128)S(1)} %slice.36.orders_ref, s32[1]{0:T(128)} %bitcast.5.high_ref, f32[32,512]{1,0:T(8,128)S(1)} %slice_bitcast_fusion.1.own_ref, f32[32,512]{1,0:T(8,128)S(1)} %collective-permute-done.1.far_ref), custom_call_target="tpu_custom_call" | custom-call | flops 10000000 | bytes 10000000 | tf_op jit(solution)/shard_map/far_rotations/pallas_call | solution.py:568
  29.1 8.3 %collective-permute-done.2.oth_ref.x_oth_ref = f32[128,512]{1,0:T(8,128)S(1)} collective-permute-done((f32[128,512]{1,0:T(8,128)S(1)}, f32[128,512]{1,0:T(8,128)S(1)}, u32[]{:S(2)}, u32[]{:S(2)}) %collective-permute-start.2) | collective-permute-done | bytes 262176 | tf_op jit(solution)/shard_map/ppermute | solution.py:22
  37.4 1.1 collective-permute-done.5
  38.5 1.1 pad_maximum_fusion
  39.6 1.3 %collective-permute-start.6 = (bf16[4,128,1024]{2,1,0:T(8,128)(2,1)S(1)}, bf16[4,128,1024]{2,1,0:T(8,128)(2,1)S(1)}, u32[]{:S(2)}, u32[]{:S(2)}) collective-permute-start(bf16[4,128,1024]{2,1,0:T(8,128)(2,1)S(1)} %pad_maximum_fusion), channel_id=1, source_target_pairs={{0,2},{1,3},{2,0},{3,1},{4,6},{5,7},{6,4},{7,5},{8,10},{9,11},{10,... | collective-permute-start | bytes 3145736 | tf_op jit(solution)/shard_map/ppermute | solution.py:22
  41.0 0.4 far_apply.1.x_ref
  41.4 10.2 %project.1 = (f32[8,128,512]{2,1,0:T(8,128)S(1)}, f32[8,128,512]{2,1,0:T(8,128)}, f32[8,128,512]{2,1,0:T(8,128)}, f32[8,128,512]{2,1,0:T(8,128)}) custom-call(s32[16]{0:T(128)S(1)} %broadcast_xor_fusion.places_ref, bf16[256,512]{1,0:T(8,128)(2,1)S(1)} %far_apply.1.x_ref, bf16[512,16384]{1,0:T(8,128)(2,1)} %w_ref.3), custom_call_target="tpu_custom_call" | custom-call | flops 4294967296 | bytes 25165824 | tf_op jit(solution)/shard_map/project/pallas_call | solution.py:300
  51.6 0.1 collective-permute-start.3
  51.7 0.6 collective-permute-start.7
  52.3 1.1 constant_dynamic-update-slice_fusion.1
  53.3 9.5 %collective-permute-done.6 = bf16[4,128,1024]{2,1,0:T(8,128)(2,1)S(1)} collective-permute-done((bf16[4,128,1024]{2,1,0:T(8,128)(2,1)S(1)}, bf16[4,128,1024]{2,1,0:T(8,128)(2,1)S(1)}, u32[]{:S(2)}, u32[]{:S(2)}) %collective-permute-start.6) | collective-permute-done | bytes 1048608 | tf_op jit(solution)/shard_map/ppermute | solution.py:22
  62.9 0.1 collective-permute-start.8
  63.0 0.5 sum_pack.2
  63.5 0.1 convert_element_type.12
  63.7 1.6 %collective-permute-start.4 = (f16[528,512]{1,0:T(8,128)(2,1)S(1)}, f16[528,512]{1,0:T(8,128)(2,1)S(1)}, u32[]{:S(2)}, u32[]{:S(2)}) collective-permute-start(f16[528,512]{1,0:T(8,128)(2,1)S(1)} %convert_element_type.12), channel_id=1, source_target_pairs={{0,2},{1,3},{2,0},{3,1},{4,6},{5,7},{6,4},{7,5},{8,10},{9,11},{10,... | collective-permute-start | bytes 1622024 | tf_op jit(solution)/shard_map/ppermute | solution.py:22
  65.3 0.5 sum_pack.3
  65.8 0.1 convert_element_type.13
  65.9 0.9 collective-permute-start.11
  66.8 0.3 collective-permute-done.8.high_ref
  67.1 1.3 %copy-done.7 = bf16[8,128,1024]{2,1,0:T(8,128)(2,1)} copy-done((bf16[8,128,1024]{2,1,0:T(8,128)(2,1)}, bf16[8,128,1024]{2,1,0:T(8,128)(2,1)S(1)}, u32[]{:S(2)}) %copy-start.7) | copy-done | bytes 2097176
  68.5 8.2 %project_back.1.own_ref = f32[128,512]{1,0:T(8,128)S(1)} custom-call(s32[16]{0:T(128)S(1)} %iota_xor_fusion.places_ref, bf16[8,128,1024]{2,1,0:T(8,128)(2,1)S(1)} %constant_dynamic-update-slice_fusion.low_ref, bf16[8,128,1024]{2,1,0:T(8,128)(2,1)} %copy-done.7, bf16[512,16384]{1,0:T(8,128)(2,1)} %w_ref.3), custom_call_target="tpu_custom_call" | custom-call | flops 2147483648 | bytes 20971520 | tf_op jit(solution)/shard_map/project_back/pallas_call | solution.py:357
  76.7 2.1 %collective-permute-done.4 = f16[528,512]{1,0:T(8,128)(2,1)S(1)} collective-permute-done((f16[528,512]{1,0:T(8,128)(2,1)S(1)}, f16[528,512]{1,0:T(8,128)(2,1)S(1)}, u32[]{:S(2)}, u32[]{:S(2)}) %collective-permute-start.4) | collective-permute-done | bytes 540704 | tf_op jit(solution)/shard_map/ppermute | solution.py:22
  78.8 0.1 convert_element_type.14.got_ref
  78.9 0.2 sum_unpack.2
  79.2 4.5 %collective-permute-start.9 = (f32[2,128,512]{2,1,0:T(8,128)S(1)}, f32[2,128,512]{2,1,0:T(8,128)S(1)}, u32[]{:S(2)}, u32[]{:S(2)}) collective-permute-start(f32[2,128,512]{2,1,0:T(8,128)S(1)} %get-tuple-element.47), channel_id=1, source_target_pairs={{0,4},{1,5},{2,6},{3,7},{4,0},{5,1},{6,2},{7,3},{8,12},{9,13},{10,... | collective-permute-start | bytes 1572872 | tf_op jit(solution)/shard_map/ppermute | solution.py:22
  83.7 1.5 %collective-permute-start.12 = (f32[128,512]{1,0:T(8,128)S(1)}, f32[128,512]{1,0:T(8,128)S(1)}, u32[]{:S(2)}, u32[]{:S(2)}) collective-permute-start(f32[128,512]{1,0:T(8,128)S(1)} %project_back.1.own_ref), channel_id=1, source_target_pairs={{0,8},{1,9},{2,10},{3,11},{4,12},{5,13},{6,14},{7,15},{8,0},{9,1},... | collective-permute-start | bytes 786440 | tf_op jit(solution)/shard_map/ppermute | solution.py:22
  85.2 4.7 %collective-permute-done.11 = f16[528,512]{1,0:T(8,128)(2,1)S(1)} collective-permute-done((f16[528,512]{1,0:T(8,128)(2,1)S(1)}, f16[528,512]{1,0:T(8,128)(2,1)S(1)}, u32[]{:S(2)}, u32[]{:S(2)}) %collective-permute-start.11) | collective-permute-done | bytes 540704 | tf_op jit(solution)/shard_map/ppermute | solution.py:22
  90.0 10.0 %collective-permute-done.12.oth_ref = f32[128,512]{1,0:T(8,128)S(1)} collective-permute-done((f32[128,512]{1,0:T(8,128)S(1)}, f32[128,512]{1,0:T(8,128)S(1)}, u32[]{:S(2)}, u32[]{:S(2)}) %collective-permute-start.12) | collective-permute-done | bytes 262176 | tf_op jit(solution)/shard_map/ppermute | solution.py:22
  99.9 0.1 convert_element_type.15.got_ref
  100.1 0.2 sum_unpack.3
  100.3 2.3 %collective-permute-start.13 = (f32[2,128,512]{2,1,0:T(8,128)S(1)}, f32[2,128,512]{2,1,0:T(8,128)S(1)}, u32[]{:S(2)}, u32[]{:S(2)}) collective-permute-start(f32[2,128,512]{2,1,0:T(8,128)S(1)} %get-tuple-element.51), channel_id=1, source_target_pairs={{0,4},{1,5},{2,6},{3,7},{4,0},{5,1},{6,2},{7,3},{8,12},{9,13},{10,... | collective-permute-start | bytes 1572872 | tf_op jit(solution)/shard_map/ppermute | solution.py:22
  102.7 1.2 collective-permute-start.10
  103.9 0.1 select_reduce_fusion.inverse_ref
  104.0 13.1 %gradients.1 = (f32[128,512]{1,0:T(8,128)}, f32[128,512]{1,0:T(8,128)}) custom-call(s32[4,32]{1,0:T(4,128)S(1)} %select_reduce_fusion.inverse_ref, s32[1]{0:T(128)} %bitcast.5.high_ref, f32[128,512]{1,0:T(8,128)S(1)} %project_back.1.own_ref, f32[128,512]{1,0:T(8,128)S(1)} %collective-permute-done.12.oth_ref, ...), custom_call_target="tpu_custom_call" | custom-call | tf_op jit(solution)/shard_map/gradients/pallas_call | solution.py:627
  117.0 1.9 %collective-permute-done.13 = f32[2,128,512]{2,1,0:T(8,128)S(1)} collective-permute-done((f32[2,128,512]{2,1,0:T(8,128)S(1)}, f32[2,128,512]{2,1,0:T(8,128)S(1)}, u32[]{:S(2)}, u32[]{:S(2)}) %collective-permute-start.13) | collective-permute-done | bytes 524320 | tf_op jit(solution)/shard_map/ppermute | solution.py:22
  119.0 0.4 collective-permute-start.14
  119.5 12.7 %collective-permute-done.14 = f32[1,128,512]{2,1,0:T(8,128)S(1)} collective-permute-done((f32[1,128,512]{2,1,0:T(8,128)S(1)}, f32[1,128,512]{2,1,0:T(8,128)S(1)}, u32[]{:S(2)}, u32[]{:S(2)}) %collective-permute-start.14) | collective-permute-done | bytes 262176 | tf_op jit(solution)/shard_map/ppermute | solution.py:22
  132.3 0.8 pad_maximum_fusion.2
  (30 shorter events, 0.4 us)
Async XLA Ops:
  0.6 18.3 %collective-permute-start = (bf16[1,128,1024]{2,1,0:T(8,128)(2,1)}, bf16[1,128,1024]{2,1,0:T(8,128)(2,1)S(1)}, u32[]{:S(2)}, u32[]{:S(2)}) collective-permute-start(bf16[1,128,1024]{2,1,0:T(8,128)(2,1)} %bitcast.18), channel_id=1, source_target_pairs={{0,8},{1,9},{2,10},{3,11},{4,12},{5,13},{6,14},{7,15},{8,0},{9,1},... | collective-permute-start | bytes 786440 | tf_op jit(solution)/shard_map/ppermute | solution.py:22
  5.6 14.4 %collective-permute-start.1 = (f32[32,512]{1,0:T(8,128)S(1)}, f32[32,512]{1,0:T(8,128)S(1)}, u32[]{:S(2)}, u32[]{:S(2)}) collective-permute-start(f32[32,512]{1,0:T(8,128)S(1)} %slice_bitcast_fusion.1.own_ref), channel_id=1, source_target_pairs={{0,8},{1,9},{2,10},{3,11},{4,12},{5,13},{6,14},{7,15},{8,0},{9,1},... | collective-permute-start | bytes 196616 | tf_op jit(solution)/shard_map/ppermute | solution.py:22
  5.6 0.9 copy-start.2
  6.5 0.9 copy-start.4
  7.5 0.7 copy-start.5
  8.1 32.9 %copy-start.8 = (s32[16]{0:T(128)S(1)}, s32[16]{0:T(128)}, u32[]{:S(2)}) copy-start(s32[16]{0:T(128)} %constant.12.clone) | copy-start | bytes 196
  20.0 18.5 %collective-permute-start.5 = (bf16[2,128,1024]{2,1,0:T(8,128)(2,1)S(1)}, bf16[2,128,1024]{2,1,0:T(8,128)(2,1)}, u32[]{:S(2)}, u32[]{:S(2)}) collective-permute-start(bf16[2,128,1024]{2,1,0:T(8,128)(2,1)S(1)} %pad_maximum_fusion.1), channel_id=1, source_target_pairs={{0,4},{1,5},{2,6},{3,7},{4,0},{5,1},{6,2},{7,3},{8,12},{9,13},{10,... | collective-permute-start | bytes 1572872 | tf_op jit(solution)/shard_map/ppermute | solution.py:22
  20.4 17.0 %collective-permute-start.2 = (f32[128,512]{1,0:T(8,128)S(1)}, f32[128,512]{1,0:T(8,128)S(1)}, u32[]{:S(2)}, u32[]{:S(2)}) collective-permute-start(f32[128,512]{1,0:T(8,128)S(1)} %slice_bitcast_fusion.own_ref), channel_id=1, source_target_pairs={{0,8},{1,9},{2,10},{3,11},{4,12},{5,13},{6,14},{7,15},{8,0},{9,1},... | collective-permute-start | bytes 786440 | tf_op jit(solution)/shard_map/ppermute | solution.py:22
  39.6 23.2 %collective-permute-start.6 = (bf16[4,128,1024]{2,1,0:T(8,128)(2,1)S(1)}, bf16[4,128,1024]{2,1,0:T(8,128)(2,1)S(1)}, u32[]{:S(2)}, u32[]{:S(2)}) collective-permute-start(bf16[4,128,1024]{2,1,0:T(8,128)(2,1)S(1)} %pad_maximum_fusion), channel_id=1, source_target_pairs={{0,2},{1,3},{2,0},{3,1},{4,6},{5,7},{6,4},{7,5},{8,10},{9,11},{10,... | collective-permute-start | bytes 3145736 | tf_op jit(solution)/shard_map/ppermute | solution.py:22
  51.6 11.4 %copy-start.1 = (f32[8,128,512]{2,1,0:T(8,128)S(1)}, f32[8,128,512]{2,1,0:T(8,128)}, u32[]{:S(2)}) copy-start(f32[8,128,512]{2,1,0:T(8,128)} %get-tuple-element.35.keep_ref) | copy-start | bytes 6291460
  51.6 11.4 %collective-permute-start.3 = (f32[8,128,512]{2,1,0:T(8,128)S(1)}, f32[8,128,512]{2,1,0:T(8,128)S(1)}, u32[]{:S(2)}, u32[]{:S(2)}) collective-permute-start(f32[8,128,512]{2,1,0:T(8,128)S(1)} %get-tuple-element.36), channel_id=1, source_target_pairs={{0,1},{1,0},{2,3},{3,2},{4,5},{5,4},{6,7},{7,6},{8,9},{9,8},{10,11... | collective-permute-start | bytes 6291464 | tf_op jit(solution)/shard_map/ppermute | solution.py:22
  51.7 13.5 %collective-permute-start.7 = (f32[8,128,512]{2,1,0:T(8,128)}, f32[8,128,512]{2,1,0:T(8,128)S(1)}, u32[]{:S(2)}, u32[]{:S(2)}) collective-permute-start(f32[8,128,512]{2,1,0:T(8,128)} %get-tuple-element.42), channel_id=1, source_target_pairs={{0,1},{1,0},{2,3},{3,2},{4,5},{5,4},{6,7},{7,6},{8,9},{9,8},{10,11... | collective-permute-start | bytes 6291464 | tf_op jit(solution)/shard_map/ppermute | solution.py:22
  62.9 4.2 %collective-permute-start.8 = (bf16[8,128,1024]{2,1,0:T(8,128)(2,1)S(1)}, bf16[8,128,1024]{2,1,0:T(8,128)(2,1)S(1)}, u32[]{:S(2)}, u32[]{:S(2)}) collective-permute-start(bf16[8,128,1024]{2,1,0:T(8,128)(2,1)S(1)} %constant_dynamic-update-slice_fusion.low_ref), channel_id=1, source_target_pairs={{0,1},{1,0},{2,3},{3,2},{4,5},{5,4},{6,7},{7,6},{8,9},{9,8},{10,11... | collective-permute-start | bytes 6291464 | tf_op jit(solution)/shard_map/ppermute | solution.py:22
  63.0 2.3 %copy-start = (f32[8,128,512]{2,1,0:T(8,128)S(1)}, f32[8,128,512]{2,1,0:T(8,128)}, u32[]{:S(2)}) copy-start(f32[8,128,512]{2,1,0:T(8,128)} %get-tuple-element.41.keep_ref) | copy-start | bytes 6291460
  63.7 15.1 %collective-permute-start.4 = (f16[528,512]{1,0:T(8,128)(2,1)S(1)}, f16[528,512]{1,0:T(8,128)(2,1)S(1)}, u32[]{:S(2)}, u32[]{:S(2)}) collective-permute-start(f16[528,512]{1,0:T(8,128)(2,1)S(1)} %convert_element_type.12), channel_id=1, source_target_pairs={{0,2},{1,3},{2,0},{3,1},{4,6},{5,7},{6,4},{7,5},{8,10},{9,11},{10,... | collective-permute-start | bytes 1622024 | tf_op jit(solution)/shard_map/ppermute | solution.py:22
  65.9 24.1 %collective-permute-start.11 = (f16[528,512]{1,0:T(8,128)(2,1)S(1)}, f16[528,512]{1,0:T(8,128)(2,1)S(1)}, u32[]{:S(2)}, u32[]{:S(2)}) collective-permute-start(f16[528,512]{1,0:T(8,128)(2,1)S(1)} %convert_element_type.13), channel_id=1, source_target_pairs={{0,2},{1,3},{2,0},{3,1},{4,6},{5,7},{6,4},{7,5},{8,10},{9,11},{10,... | collective-permute-start | bytes 1622024 | tf_op jit(solution)/shard_map/ppermute | solution.py:22
  67.1 1.3 %copy-start.7 = (bf16[8,128,1024]{2,1,0:T(8,128)(2,1)}, bf16[8,128,1024]{2,1,0:T(8,128)(2,1)S(1)}, u32[]{:S(2)}) copy-start(bf16[8,128,1024]{2,1,0:T(8,128)(2,1)S(1)} %collective-permute-done.8.high_ref) | copy-start | bytes 6291460
  79.2 24.7 %copy-start.6 = (s32[4,32]{1,0:T(4,128)S(1)}, s32[4,32]{1,0:T(4,128)}, u32[]{:S(2)}) copy-start(s32[4,32]{1,0:T(4,128)} %orders_ref.1) | copy-start | bytes 1540
  79.2 24.8 %copy-start.3 = (bf16[128,512]{1,0:T(8,128)(2,1)S(1)}, bf16[128,512]{1,0:T(8,128)(2,1)}, u32[]{:S(2)}) copy-start(bf16[128,512]{1,0:T(8,128)(2,1)} %tok_ref.3) | copy-start | bytes 393220
  79.2 23.4 %collective-permute-start.9 = (f32[2,128,512]{2,1,0:T(8,128)S(1)}, f32[2,128,512]{2,1,0:T(8,128)S(1)}, u32[]{:S(2)}, u32[]{:S(2)}) collective-permute-start(f32[2,128,512]{2,1,0:T(8,128)S(1)} %get-tuple-element.47), channel_id=1, source_target_pairs={{0,4},{1,5},{2,6},{3,7},{4,0},{5,1},{6,2},{7,3},{8,12},{9,13},{10,... | collective-permute-start | bytes 1572872 | tf_op jit(solution)/shard_map/ppermute | solution.py:22
  83.7 16.2 %collective-permute-start.12 = (f32[128,512]{1,0:T(8,128)S(1)}, f32[128,512]{1,0:T(8,128)S(1)}, u32[]{:S(2)}, u32[]{:S(2)}) collective-permute-start(f32[128,512]{1,0:T(8,128)S(1)} %project_back.1.own_ref), channel_id=1, source_target_pairs={{0,8},{1,9},{2,10},{3,11},{4,12},{5,13},{6,14},{7,15},{8,0},{9,1},... | collective-permute-start | bytes 786440 | tf_op jit(solution)/shard_map/ppermute | solution.py:22
  100.3 18.7 %collective-permute-start.13 = (f32[2,128,512]{2,1,0:T(8,128)S(1)}, f32[2,128,512]{2,1,0:T(8,128)S(1)}, u32[]{:S(2)}, u32[]{:S(2)}) collective-permute-start(f32[2,128,512]{2,1,0:T(8,128)S(1)} %get-tuple-element.51), channel_id=1, source_target_pairs={{0,4},{1,5},{2,6},{3,7},{4,0},{5,1},{6,2},{7,3},{8,12},{9,13},{10,... | collective-permute-start | bytes 1572872 | tf_op jit(solution)/shard_map/ppermute | solution.py:22
  102.7 16.8 %collective-permute-start.10 = (f32[1,128,512]{2,1,0:T(8,128)S(1)}, f32[1,128,512]{2,1,0:T(8,128)S(1)}, u32[]{:S(2)}, u32[]{:S(2)}) collective-permute-start(f32[1,128,512]{2,1,0:T(8,128)S(1)} %slice_add_fusion), channel_id=1, source_target_pairs={{0,8},{1,9},{2,10},{3,11},{4,12},{5,13},{6,14},{7,15},{8,0},{9,1},... | collective-permute-start | bytes 786440 | tf_op jit(solution)/shard_map/ppermute | solution.py:22
  119.0 13.2 %collective-permute-start.14 = (f32[1,128,512]{2,1,0:T(8,128)S(1)}, f32[1,128,512]{2,1,0:T(8,128)S(1)}, u32[]{:S(2)}, u32[]{:S(2)}) collective-permute-start(f32[1,128,512]{2,1,0:T(8,128)S(1)} %slice_add_fusion.2), channel_id=1, source_target_pairs={{0,8},{1,9},{2,10},{3,11},{4,12},{5,13},{6,14},{7,15},{8,0},{9,1},... | collective-permute-start | bytes 786440 | tf_op jit(solution)/shard_map/ppermute | solution.py:22

commit v8 on v7

--- a/solution.py
+++ b/solution.py
@@ -184,7 +184,8 @@
 
 
 def near_kernel(
-    orders_ref, gen_ref, tok_ref, inv_ref, near_ref, xs_ref, lo_ref, hi_ref, a_ref, b_ref, row_ref
+    orders_ref, gen_ref, tok_ref, inv_ref, near_ref, xs_ref, packed_ref,
+    lo_ref, hi_ref, a_ref, b_ref, row_ref,
 ):
     sections, block = orders_ref.shape
     half = block // 2
@@ -214,6 +215,7 @@
         for k in range(sections - 1, 0, -1):
             value = dot(value, near_ref[k - 1, start:stop, :])
             xs_ref[k - 1, :, start:stop] = value
+    write_packed(packed_ref, xs_ref[0])
 
 
 def far_rotations_kernel(
@@ -242,16 +244,33 @@
             target[1, start : start + GROUP, :] = jnp.where(same, part[:, GROUP:], 0.0)
 
 
+def write_packed(packed_ref, value):
+    count, width = value.shape
+    peak = jnp.max(jnp.abs(value), axis=(0, 1), keepdims=True)
+    exponent = jnp.ceil(jnp.log2(jnp.maximum(peak, 1e-30))) - 15.0
+    packed_ref[0:count, :] = value * jnp.exp2(-exponent)
+    packed_ref[count:, :] = jnp.broadcast_to(exponent, (16, width))
+
+
+def read_packed(packed_ref, start, stop):
+    count = packed_ref.shape[0] - 16
+    return packed_ref[0:count, start:stop] * jnp.exp2(packed_ref[count : count + 1, 0:1])
+
+
+def exchange_packed(packed, bit):
+    return exchange(packed.astype(jnp.float16), bit).astype(jnp.float32)
+
+
 def beside(a, b):
     return jnp.concatenate([a, b], axis=1)
 
 
 def far_kernel(own_ref, oth_ref, far_ref, out_ref):
-    count, rows = own_ref.shape
+    count, rows = own_ref.shape[1:]
     for start in range(0, rows, GROUP):
         stop = start + GROUP
         value = dot(
-            beside(own_ref[:, start:stop], oth_ref[:, start:stop]),
+            beside(own_ref[0, :, start:stop], read_packed(oth_ref, start, stop)),
             beside(far_ref[0, start:stop, :], far_ref[1, start:stop, :]),
             NT,
         )
@@ -324,7 +343,7 @@
     return [outs[2 * chunk : 2 * chunk + 2] for chunk in range(CHUNKS)]
 
 
-def back_kernel(order, places_ref, low_ref, high_ref, w_ref, out_ref, cots_ref, held_ref, cot_sems, sems):
+def back_kernel(order, places_ref, low_ref, high_ref, w_ref, out_ref, packed_ref, cots_ref, held_ref, cot_sems, sems):
     half, _, width = low_ref.shape
 
     def fetches(slot):
@@ -348,6 +367,7 @@
             out_ref[...] = product
         else:
             out_ref[...] += product
+    write_packed(packed_ref, out_ref[...])
 
 
 def project_back(places, gathered, order, weight):
@@ -356,10 +376,13 @@
     rows = weight.shape[0]
     return pl.pallas_call(
         functools.partial(back_kernel, order),
-        out_shape=jax.ShapeDtypeStruct((count, rows), jnp.float32),
+        out_shape=(
+            jax.ShapeDtypeStruct((count, rows), jnp.float32),
+            jax.ShapeDtypeStruct((count + 16, rows), jnp.float32),
+        ),
         in_specs=[pl.BlockSpec(memory_space=pltpu.SMEM)]
         + [pl.BlockSpec(memory_space=pl.ANY)] * (len(gathered) + 1),
-        out_specs=pl.BlockSpec(memory_space=pltpu.VMEM),
+        out_specs=(pl.BlockSpec(memory_space=pltpu.VMEM),) * 2,
         scratch_shapes=[
             pltpu.VMEM((count, steps * width), weight.dtype),
             pltpu.VMEM((rows, steps * width), weight.dtype),
@@ -415,27 +438,21 @@
     per_section = rows // half
     lanes = sections * per_section
     high = high_ref[0]
-    gather_lo = gatherer(0, block, half)
-    gather_hi = gatherer(half, block, half)
-    gather_own = gatherer(half * high, block, half)
-    gather_oth = gatherer(half * (1 - high), block, half)
+    chooser = jnp.concatenate([gatherer(0, block, half), gatherer(half, block, half)], axis=0)
+    far_chooser = jnp.concatenate(
+        [gatherer(half * high, block, half), gatherer(half * (1 - high), block, half)], axis=0
+    )
     same = same_mask(half)
+    same = jnp.concatenate([beside(same, same)] * 2, axis=0)
     for start in range(0, rows, GROUP):
         stop = start + GROUP
-        x_own = xs_ref[0, :, start:stop]
-        x_oth = x_oth_ref[:, start:stop]
-        g_own = own_ref[:, start:stop]
-        g_oth = oth_ref[:, start:stop]
-
-        def far_rows(x):
-            return pick(jnp.where(same, dot(x, g_own, TN), 0.0), gather_own) + pick(
-                jnp.where(same, dot(x, g_oth, TN), 0.0), gather_oth
-            )
-
-        mine, theirs = far_rows(x_own), far_rows(x_oth)
+        x_pair = beside(xs_ref[0, :, start:stop], read_packed(x_oth_ref, start, stop))
+        g_pair = beside(own_ref[:, start:stop], read_packed(oth_ref, start, stop))
+        both = pick(jnp.where(same, dot(x_pair, g_pair, TN), 0.0), far_chooser)
+        mine, theirs = both[:GROUP], both[GROUP:]
         lo_ref[start:stop, :] = jnp.where(high == 1, theirs, mine)
         hi_ref[start:stop, :] = jnp.where(high == 1, mine, theirs)
-        grad = dot(g_own, bfar_ref[0, start:stop, :], NT) + dot(g_oth, bfar_ref[1, start:stop, :], NT)
+        grad = dot(g_pair, beside(bfar_ref[0, start:stop, :], bfar_ref[1, start:stop, :]), NT)
         for k in range(1, sections):
             lo_mask, hi_mask = block_masks(k, half)
             if k < sections - 1:
@@ -444,8 +461,8 @@
                 x = tok_ref[:, start:stop].astype(jnp.float32)
             outer = dot(x, grad, TN)
             row_ref[k * rows + start : k * rows + stop, :] = pick(
-                jnp.where(lo_mask, outer, 0.0), gather_lo
-            ) + pick(jnp.where(hi_mask, outer, 0.0), gather_hi)
+                beside(jnp.where(lo_mask, outer, 0.0), jnp.where(hi_mask, outer, 0.0)), chooser
+            )
             grad = dot(grad, near_ref[k - 1, start:stop, :], NT)
         gtok_ref[:, start:stop] = grad
     for k in range(1, sections):
@@ -539,19 +556,22 @@
     stored = jnp.swapaxes(generators, 1, 2)
     far_gen = exchange(stored[0], pair_bit)
     order = list(range(bits - 1, -1, -1))
-    pieces = grow(cotangent[None], order[0])
+    pieces = cotangent[None]
+    for bit in order[:-3]:
+        pieces = grow(pieces, bit)
     flat = stored.reshape(sections * block, rows)
     square = (block * block, lanes)
     far_square = (block * block, lanes // sections)
-    inv, near, xs = pl.pallas_call(
+    inv, near, xs, x_packed = pl.pallas_call(
         near_kernel,
         out_shape=(
             jax.ShapeDtypeStruct(square, f32),
             jax.ShapeDtypeStruct((sections - 1, rows, GROUP), f32),
             jax.ShapeDtypeStruct((sections - 1, count, rows), f32),
+            jax.ShapeDtypeStruct((count + 16, rows), f32),
         ),
         in_specs=[scalars, full, full],
-        out_specs=(full,) * 3,
+        out_specs=(full,) * 4,
         scratch_shapes=[
             pltpu.VMEM((sections * rows, block), f32),
             pltpu.VMEM((sections * rows, block), f32),
@@ -562,9 +582,9 @@
         compiler_params=params,
         name="near_rotations",
     )(orders, flat, tokens)
-    x_last, pieces, far_gen = lax.optimization_barrier((xs[0], pieces, far_gen))
-    news = exchange(pieces, order[1])
-    x_other = exchange(x_last, pair_bit)
+    x_packed, pieces, far_gen = lax.optimization_barrier((x_packed, pieces, far_gen))
+    near_news, side_news = exchange(pieces, order[-3]), exchange(pieces, order[-2])
+    x_other = exchange_packed(x_packed, pair_bit)
     inv_far, ffar, bfar = pl.pallas_call(
         far_rotations_kernel,
         out_shape=(
@@ -586,9 +606,8 @@
         cost_estimate=pl.CostEstimate(flops=10**7, bytes_accessed=10**7, transcendentals=0),
         name="far_rotations",
     )(orders[:1], high, stored[0], far_gen)
-    pieces = jnp.concatenate([pieces, after(news, ffar, x_other)], axis=0)
-    for bit in order[2:-1]:
-        pieces = grow(pieces, bit)
+    near_news = after(near_news, ffar, x_other)
+    last_news = exchange(near_news, order[-2])
     x_both = pl.pallas_call(
         far_kernel,
         out_shape=jax.ShapeDtypeStruct((2 * count, rows), jnp.bfloat16),
@@ -596,7 +615,7 @@
         out_specs=full,
         compiler_params=params,
         name="far_apply",
-    )(x_last, x_other, ffar)
+    )(xs, x_other, ffar)
 
     reverse = np.array(
         [sum(((p >> b) & 1) << (bits - 1 - b) for b in range(bits)) for p in range(size)], np.int32
@@ -604,7 +623,7 @@
     fixed = here.astype(jnp.int32)
     places = jnp.bitwise_xor(fixed, jnp.asarray(np.roll(reverse, size // 2)))
     back_places = jnp.bitwise_xor(fixed, jnp.arange(size, dtype=jnp.int32))
-    outs = project(x_both, weight, places)
+    outs = project(after(x_both, near_news, side_news), weight, places)
 
     def stage(pair, got):
         send, keep = pair
@@ -615,13 +634,15 @@
 
     outs = [pack(keep, exchange(send, 0)) for send, keep in outs]
     gots = [exchange(send, 1) for send, _ in outs]
-    gathered = [after(pieces, *[send for send, _ in outs]), exchange(pieces, 0)]
+    last_news = after(last_news, *[send for send, _ in outs])
+    pieces = jnp.concatenate([pieces, near_news, side_news, last_news], axis=0)
+    gathered = [pieces, exchange(pieces, 0)]
     numbers = jnp.arange(block, dtype=jnp.int32)
     inverse = jnp.sum(
         jnp.where(orders[:, :, None] == numbers[None, None, :], numbers[None, :, None], 0), axis=1
     ).astype(jnp.int32)
-    grad_cols = project_back(back_places, gathered, gather_order(order), weight)
-    grad_other = exchange(grad_cols, pair_bit)
+    grad_cols, grad_packed = project_back(back_places, gathered, gather_order(order), weight)
+    grad_other = exchange_packed(grad_packed, pair_bit)
     gots[0] = after(gots[0], grad_cols)
     gots[-1] = after(gots[-1], grad_other)
     grad_tokens, grad_gens = pl.pallas_call(

time: 133 us -> 127 us (0.955)
  waiting for transfers between devices: 54.1 us -> 46.4 us
  local copies, waits for them, and re-layouts: 5.94 us -> 7.6 us
    ppermute x15 -> x16, waiting for transfers between devices: 54.1 us -> 46.4 us  [exchange(): lax.ppermute(array, 'tensor', [(i, i ^ 1 << bit) for i in range(size)])]
    unnamed x20 -> x19, local copies, waits for them, and re-layouts: 5.01 us -> 6.72 us
    ppermute x15 -> x16, starting transfers between devices: 22.4 us -> 22.3 us  [exchange(): lax.ppermute(array, 'tensor', [(i, i ^ 1 << bit) for i in range(size)])]
  transfers between devices with their start and end apart: 15 -> 16, of which waited for: 10 -> 11; matrix products, arithmetic and copies ran while one was open for 3% -> 4% of each run, Pallas kernels for 35% -> 28%
where the time goes in v8:
time: 127 us
  waiting for transfers between devices  46.4 us (37%)
  Pallas kernels  46.2 us (36%)
  starting transfers between devices  22.3 us (18%)
  local copies, waits for them, and re-layouts  7.6 us (6%)
  other arithmetic  3.35 us (3%)
    ppermute x16, waiting for transfers between devices, exchange(): lax.ppermute(array, 'tensor', [(i, i ^ 1 << bit) for i in range(size)])  46.4 us
    ppermute x16, starting transfers between devices, exchange(): lax.ppermute(array, 'tensor', [(i, i ^ 1 << bit) for i in range(size)])  22.3 us
    pallas_call x1, Pallas kernels, local(): pl.pallas_call(grads_kernel, out_shape=(jax.ShapeDtypeStruct((count, rows...  12.8 us
    pallas_call x1, Pallas kernels, project(): pl.pallas_call(project_kernel, out_shape=(jax.ShapeDtypeStruct((pieces //...  10.2 us
    pallas_call x1, Pallas kernels, project_back(): pl.pallas_call(functools.partial(back_kernel, order), out_shape=(jax.Shap...  8.39 us
    pallas_call x1, Pallas kernels, local(): pl.pallas_call(near_kernel, out_shape=(jax.ShapeDtypeStruct(square, f32),...  7.57 us
    unnamed x19, local copies, waits for them, and re-layouts  6.72 us
    pallas_call x1, Pallas kernels, local(): pl.pallas_call(far_rotations_kernel, out_shape=(jax.ShapeDtypeStruct(far_...  5.28 us
  transfers between devices with their start and end apart: 16, of which 11 were waited for; matrix products, arithmetic and copies ran while one was open for 4% of the time, Pallas kernels for 28%

profile of v8, /device:TPU:0, one launch (start us, length us, event | category | flops | bytes accessed | tf_op | source)
XLA Modules:
  0.0 126.7 jit_solution(376612821652802949)
XLA Ops:
  0.6 4.1 %collective-permute-start = (bf16[1,128,1024]{2,1,0:T(8,128)(2,1)}, bf16[1,128,1024]{2,1,0:T(8,128)(2,1)S(1)}, u32[]{:S(2)}, u32[]{:S(2)}) collective-permute-start(bf16[1,128,1024]{2,1,0:T(8,128)(2,1)} %bitcast.16), channel_id=1, source_target_pairs={{0,8},{1,9},{2,10},{3,11},{4,12},{5,13},{6,14},{7,15},{8,0},{9,1},... | collective-permute-start | bytes 786440 | tf_op jit(solution)/shard_map/ppermute | solution.py:22
  4.7 0.8 slice_bitcast_fusion.own_ref
  5.6 0.9 copy-done.2
  6.5 0.9 copy-done.4
  7.5 0.7 copy-done.5
  8.1 7.6 %near_rotations.1 = (f32[1024,128]{1,0:T(8,128)S(1)}, f32[3,512,128]{2,1,0:T(8,128)S(1)}, f32[3,128,512]{2,1,0:T(8,128)S(1)}, f32[144,512]{1,0:T(8,128)S(1)}) custom-call(s32[4,32]{1,0:T(4,128)S(1)} %copy-done.5, f32[128,512]{1,0:T(8,128)S(1)} %bitcast.15, bf16[128,512]{1,0:T(8,128)(2,1)S(1)} %copy-done.2), custom_call_target="tpu_custom_call" | custom-call | tf_op jit(solution)/shard_map/near_rotations/pallas_call | solution.py:565
  15.7 3.3 %collective-permute-done = bf16[1,128,1024]{2,1,0:T(8,128)(2,1)S(1)} collective-permute-done((bf16[1,128,1024]{2,1,0:T(8,128)(2,1)}, bf16[1,128,1024]{2,1,0:T(8,128)(2,1)S(1)}, u32[]{:S(2)}, u32[]{:S(2)}) %collective-permute-start) | collective-permute-done | bytes 262176 | tf_op jit(solution)/shard_map/ppermute | solution.py:22
  19.0 1.0 pad_maximum_fusion
  20.0 0.4 collective-permute-start.3
  20.4 1.5 %collective-permute-start.4 = (bf16[2,128,1024]{2,1,0:T(8,128)(2,1)S(1)}, bf16[2,128,1024]{2,1,0:T(8,128)(2,1)}, u32[]{:S(2)}, u32[]{:S(2)}) collective-permute-start(bf16[2,128,1024]{2,1,0:T(8,128)(2,1)S(1)} %pad_maximum_fusion), channel_id=1, source_target_pairs={{0,2},{1,3},{2,0},{3,1},{4,6},{5,7},{6,4},{7,5},{8,10},{9,11},{10,... | collective-permute-start | bytes 1572872 | tf_op jit(solution)/shard_map/ppermute | solution.py:22
  21.9 3.4 %collective-permute-start.2 = (f16[144,512]{1,0:T(8,128)(2,1)S(1)}, f16[144,512]{1,0:T(8,128)(2,1)S(1)}, u32[]{:S(2)}, u32[]{:S(2)}) collective-permute-start(f16[144,512]{1,0:T(8,128)(2,1)S(1)} %convert_element_type.24), channel_id=1, source_target_pairs={{0,8},{1,9},{2,10},{3,11},{4,12},{5,13},{6,14},{7,15},{8,0},{9,1},... | collective-permute-start | bytes 442376 | tf_op jit(solution)/shard_map/ppermute | solution.py:22
  25.4 0.7 broadcast_xor_fusion.places_ref
  26.0 5.3 %far_rotations.1 = (f32[1024,32]{1,0:T(8,128)S(1)}, f32[2,512,128]{2,1,0:T(8,128)S(1)}, f32[2,512,128]{2,1,0:T(8,128)S(1)}) custom-call(s32[1,32]{1,0:T(1,128)S(1)} %slice.32.orders_ref, s32[1]{0:T(128)} %bitcast.4.high_ref, f32[32,512]{1,0:T(8,128)S(1)} %slice_bitcast_fusion.own_ref, f32[32,512]{1,0:T(8,128)S(1)} %collective-permute-done.1.far_ref), custom_call_target="tpu_custom_call" | custom-call | flops 10000000 | bytes 10000000 | tf_op jit(solution)/shard_map/far_rotations/pallas_call | solution.py:588
  31.3 3.6 %collective-permute-done.2 = f16[144,512]{1,0:T(8,128)(2,1)S(1)} collective-permute-done((f16[144,512]{1,0:T(8,128)(2,1)S(1)}, f16[144,512]{1,0:T(8,128)(2,1)S(1)}, u32[]{:S(2)}, u32[]{:S(2)}) %collective-permute-start.2) | collective-permute-done | bytes 147488 | tf_op jit(solution)/shard_map/ppermute | solution.py:22
  35.0 0.4 far_apply.1.x_ref
  35.4 0.7 collective-permute-done.3
  36.1 10.2 %project.1 = (f32[8,128,512]{2,1,0:T(8,128)S(1)}, f32[8,128,512]{2,1,0:T(8,128)}, f32[8,128,512]{2,1,0:T(8,128)}, f32[8,128,512]{2,1,0:T(8,128)}) custom-call(s32[16]{0:T(128)S(1)} %broadcast_xor_fusion.places_ref, bf16[256,512]{1,0:T(8,128)(2,1)S(1)} %far_apply.1.x_ref, bf16[512,16384]{1,0:T(8,128)(2,1)} %w_ref.3), custom_call_target="tpu_custom_call" | custom-call | flops 4294967296 | bytes 25165824 | tf_op jit(solution)/shard_map/project/pallas_call | solution.py:319
  46.3 0.5 collective-permute-start.8
  46.8 1.3 %collective-permute-start.7 = (bf16[2,128,1024]{2,1,0:T(8,128)(2,1)}, bf16[2,128,1024]{2,1,0:T(8,128)(2,1)S(1)}, u32[]{:S(2)}, u32[]{:S(2)}) collective-permute-start(bf16[2,128,1024]{2,1,0:T(8,128)(2,1)} %collective-permute-done.3), channel_id=1, source_target_pairs={{0,2},{1,3},{2,0},{3,1},{4,6},{5,7},{6,4},{7,5},{8,10},{9,11},{10,... | collective-permute-start | bytes 1572872 | tf_op jit(solution)/shard_map/ppermute | solution.py:22
  48.1 1.1 constant_dynamic-update-slice_fusion.2
  49.3 1.1 constant_dynamic-update-slice_fusion.1
  50.3 2.4 %collective-permute-done.5.got_ref = f32[8,128,512]{2,1,0:T(8,128)S(1)} collective-permute-done((f32[8,128,512]{2,1,0:T(8,128)S(1)}, f32[8,128,512]{2,1,0:T(8,128)S(1)}, u32[]{:S(2)}, u32[]{:S(2)}) %collective-permute-start.5) | collective-permute-done | bytes 2097184 | tf_op jit(solution)/shard_map/ppermute | solution.py:22
  52.7 0.5 sum_pack.2
  53.2 0.1 convert_element_type.26
  53.4 0.3 collective-permute-done.8.got_ref
  53.7 0.6 copy-done
  54.3 0.5 sum_pack.3
  54.9 6.0 %collective-permute-done.7 = bf16[2,128,1024]{2,1,0:T(8,128)(2,1)S(1)} collective-permute-done((bf16[2,128,1024]{2,1,0:T(8,128)(2,1)}, bf16[2,128,1024]{2,1,0:T(8,128)(2,1)S(1)}, u32[]{:S(2)}, u32[]{:S(2)}) %collective-permute-start.7) | collective-permute-done | bytes 524320 | tf_op jit(solution)/shard_map/ppermute | solution.py:22
  61.1 1.3 %collective-permute-start.6 = (f16[528,512]{1,0:T(8,128)(2,1)S(1)}, f16[528,512]{1,0:T(8,128)(2,1)S(1)}, u32[]{:S(2)}, u32[]{:S(2)}) collective-permute-start(f16[528,512]{1,0:T(8,128)(2,1)S(1)} %convert_element_type.26), channel_id=1, source_target_pairs={{0,2},{1,3},{2,0},{3,1},{4,6},{5,7},{6,4},{7,5},{8,10},{9,11},{10,... | collective-permute-start | bytes 1622024 | tf_op jit(solution)/shard_map/ppermute | solution.py:22
  62.4 0.8 collective-permute-start.12
  63.2 2.1 %collective-permute-done.9.high_ref = bf16[8,128,1024]{2,1,0:T(8,128)(2,1)S(1)} collective-permute-done((bf16[8,128,1024]{2,1,0:T(8,128)(2,1)S(1)}, bf16[8,128,1024]{2,1,0:T(8,128)(2,1)S(1)}, u32[]{:S(2)}, u32[]{:S(2)}) %collective-permute-start.9) | collective-permute-done | bytes 2097184 | tf_op jit(solution)/shard_map/ppermute | solution.py:22
  65.2 1.4 %copy-done.7 = bf16[8,128,1024]{2,1,0:T(8,128)(2,1)} copy-done((bf16[8,128,1024]{2,1,0:T(8,128)(2,1)}, bf16[8,128,1024]{2,1,0:T(8,128)(2,1)S(1)}, u32[]{:S(2)}) %copy-start.7) | copy-done | bytes 2097176
  66.6 8.4 %project_back.1 = (f32[128,512]{1,0:T(8,128)S(1)}, f32[144,512]{1,0:T(8,128)S(1)}) custom-call(s32[16]{0:T(128)S(1)} %iota_xor_fusion.places_ref, bf16[8,128,1024]{2,1,0:T(8,128)(2,1)S(1)} %constant_dynamic-update-slice_fusion.low_ref, bf16[8,128,1024]{2,1,0:T(8,128)(2,1)} %copy-done.7, bf16[512,16384]{1,0:T(8,128)(2,1)} %w_ref.3), custom_call_target="tpu_custom_call" | custom-call | flops 2147483648 | bytes 20971520 | tf_op jit(solution)/shard_map/project_back/pallas_call | solution.py:377
  75.0 1.2 collective-permute-done.6
  76.2 0.1 convert_element_type.28.got_ref
  76.4 0.2 sum_unpack.2
  76.6 3.5 %collective-permute-start.10 = (f32[2,128,512]{2,1,0:T(8,128)S(1)}, f32[2,128,512]{2,1,0:T(8,128)S(1)}, u32[]{:S(2)}, u32[]{:S(2)}) collective-permute-start(f32[2,128,512]{2,1,0:T(8,128)S(1)} %get-tuple-element.54), channel_id=1, source_target_pairs={{0,4},{1,5},{2,6},{3,7},{4,0},{5,1},{6,2},{7,3},{8,12},{9,13},{10,... | collective-permute-start | bytes 1572872 | tf_op jit(solution)/shard_map/ppermute | solution.py:22
  80.1 1.4 %collective-permute-start.13 = (f16[144,512]{1,0:T(8,128)(2,1)S(1)}, f16[144,512]{1,0:T(8,128)(2,1)S(1)}, u32[]{:S(2)}, u32[]{:S(2)}) collective-permute-start(f16[144,512]{1,0:T(8,128)(2,1)S(1)} %convert_element_type.29), channel_id=1, source_target_pairs={{0,8},{1,9},{2,10},{3,11},{4,12},{5,13},{6,14},{7,15},{8,0},{9,1},... | collective-permute-start | bytes 442376 | tf_op jit(solution)/shard_map/ppermute | solution.py:22
  81.6 12.3 %collective-permute-done.13 = f16[144,512]{1,0:T(8,128)(2,1)S(1)} collective-permute-done((f16[144,512]{1,0:T(8,128)(2,1)S(1)}, f16[144,512]{1,0:T(8,128)(2,1)S(1)}, u32[]{:S(2)}, u32[]{:S(2)}) %collective-permute-start.13) | collective-permute-done | bytes 147488 | tf_op jit(solution)/shard_map/ppermute | solution.py:22
  93.9 0.1 convert_element_type.31.got_ref
  94.0 0.2 sum_unpack.3
  94.3 2.2 %collective-permute-start.14 = (f32[2,128,512]{2,1,0:T(8,128)S(1)}, f32[2,128,512]{2,1,0:T(8,128)S(1)}, u32[]{:S(2)}, u32[]{:S(2)}) collective-permute-start(f32[2,128,512]{2,1,0:T(8,128)S(1)} %get-tuple-element.59), channel_id=1, source_target_pairs={{0,4},{1,5},{2,6},{3,7},{4,0},{5,1},{6,2},{7,3},{8,12},{9,13},{10,... | collective-permute-start | bytes 1572872 | tf_op jit(solution)/shard_map/ppermute | solution.py:22
  96.5 1.4 %collective-permute-start.11 = (f32[1,128,512]{2,1,0:T(8,128)S(1)}, f32[1,128,512]{2,1,0:T(8,128)S(1)}, u32[]{:S(2)}, u32[]{:S(2)}) collective-permute-start(f32[1,128,512]{2,1,0:T(8,128)S(1)} %slice_add_fusion), channel_id=1, source_target_pairs={{0,8},{1,9},{2,10},{3,11},{4,12},{5,13},{6,14},{7,15},{8,0},{9,1},... | collective-permute-start | bytes 786440 | tf_op jit(solution)/shard_map/ppermute | solution.py:22
  98.0 12.8 %gradients.1 = (f32[128,512]{1,0:T(8,128)}, f32[128,512]{1,0:T(8,128)}) custom-call(s32[4,32]{1,0:T(4,128)S(1)} %select_reduce_fusion.inverse_ref, s32[1]{0:T(128)} %bitcast.4.high_ref, f32[128,512]{1,0:T(8,128)S(1)} %get-tuple-element.51.own_ref, f32[144,512]{1,0:T(8,128)S(1)} %convert_element_type.30.oth_ref, ...), custom_call_target="tpu_custom_call" | custom-call | tf_op jit(solution)/shard_map/gradients/pallas_call | solution.py:648
  110.8 1.9 %collective-permute-done.14 = f32[2,128,512]{2,1,0:T(8,128)S(1)} collective-permute-done((f32[2,128,512]{2,1,0:T(8,128)S(1)}, f32[2,128,512]{2,1,0:T(8,128)S(1)}, u32[]{:S(2)}, u32[]{:S(2)}) %collective-permute-start.14) | collective-permute-done | bytes 524320 | tf_op jit(solution)/shard_map/ppermute | solution.py:22
  112.8 0.3 collective-permute-start.15
  113.1 12.7 %collective-permute-done.15 = f32[1,128,512]{2,1,0:T(8,128)S(1)} collective-permute-done((f32[1,128,512]{2,1,0:T(8,128)S(1)}, f32[1,128,512]{2,1,0:T(8,128)S(1)}, u32[]{:S(2)}, u32[]{:S(2)}) %collective-permute-start.15) | collective-permute-done | bytes 262176 | tf_op jit(solution)/shard_map/ppermute | solution.py:22
  125.9 0.8 pad_maximum_fusion.1
  (33 shorter events, 0.8 us)
Async XLA Ops:
  0.6 18.3 %collective-permute-start = (bf16[1,128,1024]{2,1,0:T(8,128)(2,1)}, bf16[1,128,1024]{2,1,0:T(8,128)(2,1)S(1)}, u32[]{:S(2)}, u32[]{:S(2)}) collective-permute-start(bf16[1,128,1024]{2,1,0:T(8,128)(2,1)} %bitcast.16), channel_id=1, source_target_pairs={{0,8},{1,9},{2,10},{3,11},{4,12},{5,13},{6,14},{7,15},{8,0},{9,1},... | collective-permute-start | bytes 786440 | tf_op jit(solution)/shard_map/ppermute | solution.py:22
  5.6 14.4 %collective-permute-start.1 = (f32[32,512]{1,0:T(8,128)S(1)}, f32[32,512]{1,0:T(8,128)S(1)}, u32[]{:S(2)}, u32[]{:S(2)}) collective-permute-start(f32[32,512]{1,0:T(8,128)S(1)} %slice_bitcast_fusion.own_ref), channel_id=1, source_target_pairs={{0,8},{1,9},{2,10},{3,11},{4,12},{5,13},{6,14},{7,15},{8,0},{9,1},... | collective-permute-start | bytes 196616 | tf_op jit(solution)/shard_map/ppermute | solution.py:22
  5.6 0.9 copy-start.2
  6.5 0.9 copy-start.4
  7.5 0.7 copy-start.5
  20.0 16.1 %collective-permute-start.3 = (bf16[2,128,1024]{2,1,0:T(8,128)(2,1)S(1)}, bf16[2,128,1024]{2,1,0:T(8,128)(2,1)}, u32[]{:S(2)}, u32[]{:S(2)}) collective-permute-start(bf16[2,128,1024]{2,1,0:T(8,128)(2,1)S(1)} %pad_maximum_fusion), channel_id=1, source_target_pairs={{0,4},{1,5},{2,6},{3,7},{4,0},{5,1},{6,2},{7,3},{8,12},{9,13},{10,... | collective-permute-start | bytes 1572872 | tf_op jit(solution)/shard_map/ppermute | solution.py:22
  20.4 15.7 %collective-permute-start.4 = (bf16[2,128,1024]{2,1,0:T(8,128)(2,1)S(1)}, bf16[2,128,1024]{2,1,0:T(8,128)(2,1)}, u32[]{:S(2)}, u32[]{:S(2)}) collective-permute-start(bf16[2,128,1024]{2,1,0:T(8,128)(2,1)S(1)} %pad_maximum_fusion), channel_id=1, source_target_pairs={{0,2},{1,3},{2,0},{3,1},{4,6},{5,7},{6,4},{7,5},{8,10},{9,11},{10,... | collective-permute-start | bytes 1572872 | tf_op jit(solution)/shard_map/ppermute | solution.py:22
  21.9 13.0 %collective-permute-start.2 = (f16[144,512]{1,0:T(8,128)(2,1)S(1)}, f16[144,512]{1,0:T(8,128)(2,1)S(1)}, u32[]{:S(2)}, u32[]{:S(2)}) collective-permute-start(f16[144,512]{1,0:T(8,128)(2,1)S(1)} %convert_element_type.24), channel_id=1, source_target_pairs={{0,8},{1,9},{2,10},{3,11},{4,12},{5,13},{6,14},{7,15},{8,0},{9,1},... | collective-permute-start | bytes 442376 | tf_op jit(solution)/shard_map/ppermute | solution.py:22
  46.2 6.4 %copy-start.1 = (f32[8,128,512]{2,1,0:T(8,128)S(1)}, f32[8,128,512]{2,1,0:T(8,128)}, u32[]{:S(2)}) copy-start(f32[8,128,512]{2,1,0:T(8,128)} %get-tuple-element.43.keep_ref) | copy-start | bytes 6291460
  46.3 6.4 %collective-permute-start.5 = (f32[8,128,512]{2,1,0:T(8,128)S(1)}, f32[8,128,512]{2,1,0:T(8,128)S(1)}, u32[]{:S(2)}, u32[]{:S(2)}) collective-permute-start(f32[8,128,512]{2,1,0:T(8,128)S(1)} %get-tuple-element.44), channel_id=1, source_target_pairs={{0,1},{1,0},{2,3},{3,2},{4,5},{5,4},{6,7},{7,6},{8,9},{9,8},{10,11... | collective-permute-start | bytes 6291464 | tf_op jit(solution)/shard_map/ppermute | solution.py:22
  46.3 7.4 %collective-permute-start.8 = (f32[8,128,512]{2,1,0:T(8,128)}, f32[8,128,512]{2,1,0:T(8,128)S(1)}, u32[]{:S(2)}, u32[]{:S(2)}) collective-permute-start(f32[8,128,512]{2,1,0:T(8,128)} %get-tuple-element.48), channel_id=1, source_target_pairs={{0,1},{1,0},{2,3},{3,2},{4,5},{5,4},{6,7},{7,6},{8,9},{9,8},{10,11... | collective-permute-start | bytes 6291464 | tf_op jit(solution)/shard_map/ppermute | solution.py:22
  46.8 14.1 %collective-permute-start.7 = (bf16[2,128,1024]{2,1,0:T(8,128)(2,1)}, bf16[2,128,1024]{2,1,0:T(8,128)(2,1)S(1)}, u32[]{:S(2)}, u32[]{:S(2)}) collective-permute-start(bf16[2,128,1024]{2,1,0:T(8,128)(2,1)} %collective-permute-done.3), channel_id=1, source_target_pairs={{0,2},{1,3},{2,0},{3,1},{4,6},{5,7},{6,4},{7,5},{8,10},{9,11},{10,... | collective-permute-start | bytes 1572872 | tf_op jit(solution)/shard_map/ppermute | solution.py:22
  52.7 1.6 %copy-start = (f32[8,128,512]{2,1,0:T(8,128)S(1)}, f32[8,128,512]{2,1,0:T(8,128)}, u32[]{:S(2)}) copy-start(f32[8,128,512]{2,1,0:T(8,128)} %get-tuple-element.47.keep_ref) | copy-start | bytes 6291460
  61.0 4.2 %collective-permute-start.9 = (bf16[8,128,1024]{2,1,0:T(8,128)(2,1)S(1)}, bf16[8,128,1024]{2,1,0:T(8,128)(2,1)S(1)}, u32[]{:S(2)}, u32[]{:S(2)}) collective-permute-start(bf16[8,128,1024]{2,1,0:T(8,128)(2,1)S(1)} %constant_dynamic-update-slice_fusion.low_ref), channel_id=1, source_target_pairs={{0,1},{1,0},{2,3},{3,2},{4,5},{5,4},{6,7},{7,6},{8,9},{9,8},{10,11... | collective-permute-start | bytes 6291464 | tf_op jit(solution)/shard_map/ppermute | solution.py:22
  61.1 15.1 %collective-permute-start.6 = (f16[528,512]{1,0:T(8,128)(2,1)S(1)}, f16[528,512]{1,0:T(8,128)(2,1)S(1)}, u32[]{:S(2)}, u32[]{:S(2)}) collective-permute-start(f16[528,512]{1,0:T(8,128)(2,1)S(1)} %convert_element_type.26), channel_id=1, source_target_pairs={{0,2},{1,3},{2,0},{3,1},{4,6},{5,7},{6,4},{7,5},{8,10},{9,11},{10,... | collective-permute-start | bytes 1622024 | tf_op jit(solution)/shard_map/ppermute | solution.py:22
  62.4 31.5 %collective-permute-start.12 = (f16[528,512]{1,0:T(8,128)(2,1)S(1)}, f16[528,512]{1,0:T(8,128)(2,1)S(1)}, u32[]{:S(2)}, u32[]{:S(2)}) collective-permute-start(f16[528,512]{1,0:T(8,128)(2,1)S(1)} %convert_element_type.27), channel_id=1, source_target_pairs={{0,2},{1,3},{2,0},{3,1},{4,6},{5,7},{6,4},{7,5},{8,10},{9,11},{10,... | collective-permute-start | bytes 1622024 | tf_op jit(solution)/shard_map/ppermute | solution.py:22
  65.2 1.4 %copy-start.7 = (bf16[8,128,1024]{2,1,0:T(8,128)(2,1)}, bf16[8,128,1024]{2,1,0:T(8,128)(2,1)S(1)}, u32[]{:S(2)}) copy-start(bf16[8,128,1024]{2,1,0:T(8,128)(2,1)S(1)} %collective-permute-done.9.high_ref) | copy-start | bytes 6291460
  76.6 19.9 %collective-permute-start.10 = (f32[2,128,512]{2,1,0:T(8,128)S(1)}, f32[2,128,512]{2,1,0:T(8,128)S(1)}, u32[]{:S(2)}, u32[]{:S(2)}) collective-permute-start(f32[2,128,512]{2,1,0:T(8,128)S(1)} %get-tuple-element.54), channel_id=1, source_target_pairs={{0,4},{1,5},{2,6},{3,7},{4,0},{5,1},{6,2},{7,3},{8,12},{9,13},{10,... | collective-permute-start | bytes 1572872 | tf_op jit(solution)/shard_map/ppermute | solution.py:22
  80.1 13.7 %collective-permute-start.13 = (f16[144,512]{1,0:T(8,128)(2,1)S(1)}, f16[144,512]{1,0:T(8,128)(2,1)S(1)}, u32[]{:S(2)}, u32[]{:S(2)}) collective-permute-start(f16[144,512]{1,0:T(8,128)(2,1)S(1)} %convert_element_type.29), channel_id=1, source_target_pairs={{0,8},{1,9},{2,10},{3,11},{4,12},{5,13},{6,14},{7,15},{8,0},{9,1},... | collective-permute-start | bytes 442376 | tf_op jit(solution)/shard_map/ppermute | solution.py:22
  93.9 4.0 %copy-start.6 = (s32[4,32]{1,0:T(4,128)S(1)}, s32[4,32]{1,0:T(4,128)}, u32[]{:S(2)}) copy-start(s32[4,32]{1,0:T(4,128)} %orders_ref.1) | copy-start | bytes 1540
  93.9 4.1 %copy-start.3 = (bf16[128,512]{1,0:T(8,128)(2,1)S(1)}, bf16[128,512]{1,0:T(8,128)(2,1)}, u32[]{:S(2)}) copy-start(bf16[128,512]{1,0:T(8,128)(2,1)} %tok_ref.3) | copy-start | bytes 393220
  94.3 18.4 %collective-permute-start.14 = (f32[2,128,512]{2,1,0:T(8,128)S(1)}, f32[2,128,512]{2,1,0:T(8,128)S(1)}, u32[]{:S(2)}, u32[]{:S(2)}) collective-permute-start(f32[2,128,512]{2,1,0:T(8,128)S(1)} %get-tuple-element.59), channel_id=1, source_target_pairs={{0,4},{1,5},{2,6},{3,7},{4,0},{5,1},{6,2},{7,3},{8,12},{9,13},{10,... | collective-permute-start | bytes 1572872 | tf_op jit(solution)/shard_map/ppermute | solution.py:22
  96.5 16.6 %collective-permute-start.11 = (f32[1,128,512]{2,1,0:T(8,128)S(1)}, f32[1,128,512]{2,1,0:T(8,128)S(1)}, u32[]{:S(2)}, u32[]{:S(2)}) collective-permute-start(f32[1,128,512]{2,1,0:T(8,128)S(1)} %slice_add_fusion), channel_id=1, source_target_pairs={{0,8},{1,9},{2,10},{3,11},{4,12},{5,13},{6,14},{7,15},{8,0},{9,1},... | collective-permute-start | bytes 786440 | tf_op jit(solution)/shard_map/ppermute | solution.py:22
  112.8 13.1 %collective-permute-start.15 = (f32[1,128,512]{2,1,0:T(8,128)S(1)}, f32[1,128,512]{2,1,0:T(8,128)S(1)}, u32[]{:S(2)}, u32[]{:S(2)}) collective-permute-start(f32[1,128,512]{2,1,0:T(8,128)S(1)} %slice_add_fusion.2), channel_id=1, source_target_pairs={{0,8},{1,9},{2,10},{3,11},{4,12},{5,13},{6,14},{7,15},{8,0},{9,1},... | collective-permute-start | bytes 786440 | tf_op jit(solution)/shard_map/ppermute | solution.py:22

commit v9 on v8

--- a/solution.py
+++ b/solution.py
@@ -184,7 +184,7 @@
 
 
 def near_kernel(
-    orders_ref, gen_ref, tok_ref, inv_ref, near_ref, xs_ref, packed_ref,
+    orders_ref, gen_ref, tok_ref, inv_ref, near_ref, xs_ref,
     lo_ref, hi_ref, a_ref, b_ref, row_ref,
 ):
     sections, block = orders_ref.shape
@@ -215,7 +215,6 @@
         for k in range(sections - 1, 0, -1):
             value = dot(value, near_ref[k - 1, start:stop, :])
             xs_ref[k - 1, :, start:stop] = value
-    write_packed(packed_ref, xs_ref[0])
 
 
 def far_rotations_kernel(
@@ -270,7 +269,7 @@
     for start in range(0, rows, GROUP):
         stop = start + GROUP
         value = dot(
-            beside(own_ref[0, :, start:stop], read_packed(oth_ref, start, stop)),
+            beside(own_ref[0, :, start:stop], oth_ref[:, start:stop]),
             beside(far_ref[0, start:stop, :], far_ref[1, start:stop, :]),
             NT,
         )
@@ -281,7 +280,7 @@
         )
 
 
-def project_kernel(places_ref, x_ref, w_ref, *refs):
+def project_kernel(slots, places_ref, x_ref, w_ref, *refs):
     *out_refs, held_ref, made_ref, sems, out_sems = refs
     pieces, count, width = made_ref.shape
     half = pieces // 2
@@ -294,7 +293,7 @@
     def leave(p, chunk):
         return pltpu.make_async_copy(
             made_ref.at[p, :, pl.ds(chunk * part, part)],
-            out_refs[2 * chunk + p // half].at[p % half],
+            out_refs[2 * chunk + p // half].at[slots[chunk][p]],
             out_sems.at[chunk, p],
         )
 
@@ -311,13 +310,13 @@
             leave(p, chunk).wait()
 
 
-def project(x_both, weight, places):
+def project(x_both, weight, places, slots):
     pieces = places.shape[0]
     count2, rows = x_both.shape
     count = count2 // 2
     width = weight.shape[1] // lax.axis_size("tensor")
     outs = pl.pallas_call(
-        project_kernel,
+        functools.partial(project_kernel, slots),
         out_shape=(jax.ShapeDtypeStruct((pieces // 2, count, width // CHUNKS), jnp.float32),)
         * (2 * CHUNKS),
         in_specs=[
@@ -446,7 +445,7 @@
     same = jnp.concatenate([beside(same, same)] * 2, axis=0)
     for start in range(0, rows, GROUP):
         stop = start + GROUP
-        x_pair = beside(xs_ref[0, :, start:stop], read_packed(x_oth_ref, start, stop))
+        x_pair = beside(xs_ref[0, :, start:stop], x_oth_ref[:, start:stop])
         g_pair = beside(own_ref[:, start:stop], read_packed(oth_ref, start, stop))
         both = pick(jnp.where(same, dot(x_pair, g_pair, TN), 0.0), far_chooser)
         mine, theirs = both[:GROUP], both[GROUP:]
@@ -512,6 +511,16 @@
         send_ref[p] = keep_ref[half + p] + got_ref[top : top + count, :] * scale
 
 
+def last_kernel(*refs):
+    *in_refs, out_ref = refs
+    chunks = len(in_refs) // 2
+    width = in_refs[0].shape[2]
+    for chunk in range(chunks):
+        out_ref[:, chunk * width : (chunk + 1) * width] = in_refs[chunk][0] + read_packed(
+            in_refs[chunks + chunk], 0, width
+        )
+
+
 def summed(kernel, name, keep, got, first):
     pieces, count, width = keep.shape
     full = pl.BlockSpec(memory_space=pltpu.VMEM)
@@ -562,16 +571,15 @@
     flat = stored.reshape(sections * block, rows)
     square = (block * block, lanes)
     far_square = (block * block, lanes // sections)
-    inv, near, xs, x_packed = pl.pallas_call(
+    inv, near, xs = pl.pallas_call(
         near_kernel,
         out_shape=(
             jax.ShapeDtypeStruct(square, f32),
             jax.ShapeDtypeStruct((sections - 1, rows, GROUP), f32),
             jax.ShapeDtypeStruct((sections - 1, count, rows), f32),
-            jax.ShapeDtypeStruct((count + 16, rows), f32),
         ),
         in_specs=[scalars, full, full],
-        out_specs=(full,) * 4,
+        out_specs=(full,) * 3,
         scratch_shapes=[
             pltpu.VMEM((sections * rows, block), f32),
             pltpu.VMEM((sections * rows, block), f32),
@@ -582,9 +590,9 @@
         compiler_params=params,
         name="near_rotations",
     )(orders, flat, tokens)
-    x_packed, pieces, far_gen = lax.optimization_barrier((x_packed, pieces, far_gen))
+    x_last, pieces, far_gen = lax.optimization_barrier((xs[0], pieces, far_gen))
     near_news, side_news = exchange(pieces, order[-3]), exchange(pieces, order[-2])
-    x_other = exchange_packed(x_packed, pair_bit)
+    x_other = exchange(x_last, pair_bit)
     inv_far, ffar, bfar = pl.pallas_call(
         far_rotations_kernel,
         out_shape=(
@@ -617,23 +625,24 @@
         name="far_apply",
     )(xs, x_other, ffar)
 
-    reverse = np.array(
-        [sum(((p >> b) & 1) << (bits - 1 - b) for b in range(bits)) for p in range(size)], np.int32
-    )
+    stages = [tuple(range(bits)), (0, 2, 1) + tuple(range(3, bits))]
+
+    def slot_of(offset, bits_in_order):
+        return sum(((offset >> bit) & 1) << (bits - 1 - n) for n, bit in enumerate(bits_in_order))
+
+    offsets = sorted(range(size), key=lambda o: (1 - (o & 1), slot_of(o, stages[0])))
+    slots = [[slot_of(o, bits_in_order) % (size // 2) for o in offsets] for bits_in_order in stages]
     fixed = here.astype(jnp.int32)
-    places = jnp.bitwise_xor(fixed, jnp.asarray(np.roll(reverse, size // 2)))
+    places = jnp.bitwise_xor(fixed, jnp.asarray(np.array(offsets, np.int32)))
     back_places = jnp.bitwise_xor(fixed, jnp.arange(size, dtype=jnp.int32))
-    outs = project(after(x_both, near_news, side_news), weight, places)
-
-    def stage(pair, got):
-        send, keep = pair
-        if keep.shape[0] == 1:
-            return None, keep + got
+    outs = project(after(x_both, near_news, side_news), weight, places, slots)
+
+    def stage(keep, got):
         mid = keep.shape[0] // 2
         return keep[mid:] + got[mid:], keep[:mid] + got[:mid]
 
     outs = [pack(keep, exchange(send, 0)) for send, keep in outs]
-    gots = [exchange(send, 1) for send, _ in outs]
+    gots = [exchange(send, order_[1]) for (send, _), order_ in zip(outs, stages)]
     last_news = after(last_news, *[send for send, _ in outs])
     pieces = jnp.concatenate([pieces, near_news, side_news, last_news], axis=0)
     gathered = [pieces, exchange(pieces, 0)]
@@ -665,12 +674,20 @@
         name="gradients",
     )(inverse, high, grad_cols, grad_other, x_other, tokens, xs, near, bfar, inv_far, inv)
     outs = [unpack(keep, got) for (_, keep), got in zip(outs, gots)]
-    for bit in range(2, bits):
-        gots = [exchange(send, bit) for send, _ in outs]
-        if bit == 2:
-            gots[-1] = after(gots[-1], grad_tokens, grad_gens)
-        outs = [stage(pair, got) for pair, got in zip(outs, gots)]
-    outputs = jnp.concatenate([keep[0] for _, keep in outs], axis=1)
+    for n in range(2, bits - 1):
+        gots = [exchange(send, order_[n]) for (send, _), order_ in zip(outs, stages)]
+        merge = pack if n == bits - 2 else stage
+        outs = [merge(keep, got) for (_, keep), got in zip(outs, gots)]
+    lasts = [exchange(send, bits - 1).astype(f32) for send, _ in outs]
+    lasts[-1] = after(lasts[-1], grad_tokens, grad_gens)
+    outputs = pl.pallas_call(
+        last_kernel,
+        out_shape=jax.ShapeDtypeStruct((count, cotangent.shape[1]), f32),
+        in_specs=[full] * (2 * CHUNKS),
+        out_specs=full,
+        compiler_params=params,
+        name="last_sums",
+    )(*[keep for _, keep in outs], *lasts)
     return outputs, grad_tokens, jnp.swapaxes(grad_gens.reshape(sections, block, rows), 1, 2)
 
 

time: 127 us -> 119 us (0.937)
  the two profiles are of different devices: /device:TPU:0 before, /device:TPU:8 now
where the time goes in v9:
time: 119 us; the launch traced here: 118 us
  Pallas kernels  47.6 us (40%)
  waiting for transfers between devices  36.5 us (31%)
  starting transfers between devices  21.8 us (18%)
  local copies, waits for them, and re-layouts  8.75 us (7%)
  other arithmetic  2.5 us (2%)
    ppermute x16, waiting for transfers between devices, exchange(): lax.ppermute(array, 'tensor', [(i, i ^ 1 << bit) for i in range(size)])  36.5 us
    ppermute x16, starting transfers between devices, exchange(): lax.ppermute(array, 'tensor', [(i, i ^ 1 << bit) for i in range(size)])  21.8 us
    pallas_call x1, Pallas kernels, local(): pl.pallas_call(grads_kernel, out_shape=(jax.ShapeDtypeStruct((count, rows...  12.9 us
    pallas_call x1, Pallas kernels, project(): pl.pallas_call(functools.partial(project_kernel, slots), out_shape=(jax.S...  10.4 us
    pallas_call x1, Pallas kernels, project_back(): pl.pallas_call(functools.partial(back_kernel, order), out_shape=(jax.Shap...  8.38 us
    pallas_call x1, Pallas kernels, local(): pl.pallas_call(near_kernel, out_shape=(jax.ShapeDtypeStruct(square, f32),...  7.4 us
    unnamed x21, local copies, waits for them, and re-layouts  7.15 us
    pallas_call x1, Pallas kernels, local(): pl.pallas_call(far_rotations_kernel, out_shape=(jax.ShapeDtypeStruct(far_...  5.25 us
  transfers between devices with their start and end apart: 16, of which 8 were waited for; matrix products, arithmetic and copies ran while one was open for 6% of the time, Pallas kernels for 31%

profile of v9, /device:TPU:8, one launch (start us, length us, event | category | flops | bytes accessed | tf_op | source)
XLA Modules:
  0.0 118.2 jit_solution(10158129215618373807)
XLA Ops:
  0.6 2.7 %collective-permute-start = (bf16[1,128,1024]{2,1,0:T(8,128)(2,1)}, bf16[1,128,1024]{2,1,0:T(8,128)(2,1)S(1)}, u32[]{:S(2)}, u32[]{:S(2)}) collective-permute-start(bf16[1,128,1024]{2,1,0:T(8,128)(2,1)} %bitcast.14), channel_id=1, source_target_pairs={{0,8},{1,9},{2,10},{3,11},{4,12},{5,13},{6,14},{7,15},{8,0},{9,1},... | collective-permute-start | bytes 786440 | tf_op jit(solution)/shard_map/ppermute | solution.py:22
  3.3 0.8 slice_bitcast_fusion.1.own_ref
  4.1 0.3 collective-permute-start.1
  4.5 0.9 copy-done.2
  5.4 0.9 copy-done.4
  6.3 0.7 copy-done.5
  7.0 7.4 %near_rotations.1 = (f32[1024,128]{1,0:T(8,128)S(1)}, f32[3,512,128]{2,1,0:T(8,128)S(1)}, f32[3,128,512]{2,1,0:T(8,128)S(1)}) custom-call(s32[4,32]{1,0:T(4,128)S(1)} %copy-done.5, f32[128,512]{1,0:T(8,128)S(1)} %bitcast.13, bf16[128,512]{1,0:T(8,128)(2,1)S(1)} %copy-done.2), custom_call_target="tpu_custom_call" | custom-call | tf_op jit(solution)/shard_map/near_rotations/pallas_call | solution.py:574
  14.4 0.7 slice_bitcast_fusion
  15.2 1.0 collective-permute-done
  16.2 1.8 %pad_maximum_fusion = bf16[2,128,1024]{2,1,0:T(8,128)(2,1)} fusion(bf16[1,128,1024]{2,1,0:T(8,128)(2,1)S(1)} %collective-permute-done, bf16[1,128,1024]{2,1,0:T(8,128)(2,1)} %bitcast.15), kind=kLoop, calls=%fused_computation | loop fusion | flops 262144 | bytes 1048576 | tf_op jit(solution)/shard_map/concatenate | solution.py:402
  18.0 1.8 %collective-permute-start.3 = (bf16[2,128,1024]{2,1,0:T(8,128)(2,1)}, bf16[2,128,1024]{2,1,0:T(8,128)(2,1)}, u32[]{:S(2)}, u32[]{:S(2)}) collective-permute-start(bf16[2,128,1024]{2,1,0:T(8,128)(2,1)} %pad_maximum_fusion), channel_id=1, source_target_pairs={{0,4},{1,5},{2,6},{3,7},{4,0},{5,1},{6,2},{7,3},{8,12},{9,13},{10,... | collective-permute-start | bytes 1572872 | tf_op jit(solution)/shard_map/ppermute | solution.py:22
  19.8 1.6 %collective-permute-start.4 = (bf16[2,128,1024]{2,1,0:T(8,128)(2,1)}, bf16[2,128,1024]{2,1,0:T(8,128)(2,1)}, u32[]{:S(2)}, u32[]{:S(2)}) collective-permute-start(bf16[2,128,1024]{2,1,0:T(8,128)(2,1)} %pad_maximum_fusion), channel_id=1, source_target_pairs={{0,2},{1,3},{2,0},{3,1},{4,6},{5,7},{6,4},{7,5},{8,10},{9,11},{10,... | collective-permute-start | bytes 1572872 | tf_op jit(solution)/shard_map/ppermute | solution.py:22
  21.4 1.4 %collective-permute-start.2 = (f32[128,512]{1,0:T(8,128)}, f32[128,512]{1,0:T(8,128)S(1)}, u32[]{:S(2)}, u32[]{:S(2)}) collective-permute-start(f32[128,512]{1,0:T(8,128)} %slice_bitcast_fusion), channel_id=1, source_target_pairs={{0,8},{1,9},{2,10},{3,11},{4,12},{5,13},{6,14},{7,15},{8,0},{9,1},... | collective-permute-start | bytes 786440 | tf_op jit(solution)/shard_map/ppermute | solution.py:22
  22.8 5.3 %far_rotations.1 = (f32[1024,32]{1,0:T(8,128)S(1)}, f32[2,512,128]{2,1,0:T(8,128)S(1)}, f32[2,512,128]{2,1,0:T(8,128)S(1)}) custom-call(s32[1,32]{1,0:T(1,128)S(1)} %slice.12.orders_ref, s32[1]{0:T(128)} %bitcast.5.high_ref, f32[32,512]{1,0:T(8,128)S(1)} %slice_bitcast_fusion.1.own_ref, f32[32,512]{1,0:T(8,128)S(1)} %collective-permute-done.1.far_ref), custom_call_target="tpu_custom_call" | custom-call | flops 10000000 | bytes 10000000 | tf_op jit(solution)/shard_map/far_rotations/pallas_call | solution.py:596
  28.0 11.0 %collective-permute-done.2.oth_ref.x_oth_ref = f32[128,512]{1,0:T(8,128)S(1)} collective-permute-done((f32[128,512]{1,0:T(8,128)}, f32[128,512]{1,0:T(8,128)S(1)}, u32[]{:S(2)}, u32[]{:S(2)}) %collective-permute-start.2) | collective-permute-done | bytes 262176 | tf_op jit(solution)/shard_map/ppermute | solution.py:22
  39.1 0.4 far_apply.1.x_ref
  39.5 10.4 %project.1 = (f32[8,128,512]{2,1,0:T(8,128)}, f32[8,128,512]{2,1,0:T(8,128)}, f32[8,128,512]{2,1,0:T(8,128)}, f32[8,128,512]{2,1,0:T(8,128)}) custom-call(s32[16]{0:T(128)S(1)} %broadcast_xor_fusion.places_ref, bf16[256,512]{1,0:T(8,128)(2,1)S(1)} %far_apply.1.x_ref, bf16[512,16384]{1,0:T(8,128)(2,1)} %w_ref.3), custom_call_target="tpu_custom_call" | custom-call | flops 4294967296 | bytes 25165824 | tf_op jit(solution)/shard_map/project/pallas_call | solution.py:318
  49.9 0.5 collective-permute-start.5
  50.4 1.5 %collective-permute-start.7 = (bf16[2,128,1024]{2,1,0:T(8,128)(2,1)}, bf16[2,128,1024]{2,1,0:T(8,128)(2,1)S(1)}, u32[]{:S(2)}, u32[]{:S(2)}) collective-permute-start(bf16[2,128,1024]{2,1,0:T(8,128)(2,1)} %collective-permute-done.3), channel_id=1, source_target_pairs={{0,2},{1,3},{2,0},{3,1},{4,6},{5,7},{6,4},{7,5},{8,10},{9,11},{10,... | collective-permute-start | bytes 1572872 | tf_op jit(solution)/shard_map/ppermute | solution.py:22
  52.0 1.1 constant_dynamic-update-slice_fusion.3
  53.0 1.1 constant_dynamic-update-slice_fusion.2
  54.1 1.1 constant_dynamic-update-slice_fusion.1
  55.2 0.6 sum_pack.5
  55.8 0.1 convert_element_type.31
  55.9 1.4 %collective-permute-done.5.got_ref = f32[8,128,512]{2,1,0:T(8,128)S(1)} collective-permute-done((f32[8,128,512]{2,1,0:T(8,128)}, f32[8,128,512]{2,1,0:T(8,128)S(1)}, u32[]{:S(2)}, u32[]{:S(2)}) %collective-permute-start.5) | collective-permute-done | bytes 2097184 | tf_op jit(solution)/shard_map/ppermute | solution.py:22
  57.3 0.5 sum_pack.4
  57.9 0.1 convert_element_type.30
  58.0 6.6 %collective-permute-done.7 = bf16[2,128,1024]{2,1,0:T(8,128)(2,1)S(1)} collective-permute-done((bf16[2,128,1024]{2,1,0:T(8,128)(2,1)}, bf16[2,128,1024]{2,1,0:T(8,128)(2,1)S(1)}, u32[]{:S(2)}, u32[]{:S(2)}) %collective-permute-start.7) | collective-permute-done | bytes 524320 | tf_op jit(solution)/shard_map/ppermute | solution.py:22
  64.7 1.6 %collective-permute-start.6 = (f16[528,512]{1,0:T(8,128)(2,1)S(1)}, f16[528,512]{1,0:T(8,128)(2,1)S(1)}, u32[]{:S(2)}, u32[]{:S(2)}) collective-permute-start(f16[528,512]{1,0:T(8,128)(2,1)S(1)} %convert_element_type.30), channel_id=1, source_target_pairs={{0,2},{1,3},{2,0},{3,1},{4,6},{5,7},{6,4},{7,5},{8,10},{9,11},{10,... | collective-permute-start | bytes 1622024 | tf_op jit(solution)/shard_map/ppermute | solution.py:22
  66.3 2.6 %collective-permute-done.9.high_ref = bf16[8,128,1024]{2,1,0:T(8,128)(2,1)S(1)} collective-permute-done((bf16[8,128,1024]{2,1,0:T(8,128)(2,1)S(1)}, bf16[8,128,1024]{2,1,0:T(8,128)(2,1)S(1)}, u32[]{:S(2)}, u32[]{:S(2)}) %collective-permute-start.9) | collective-permute-done | bytes 2097184 | tf_op jit(solution)/shard_map/ppermute | solution.py:22
  68.8 1.4 %copy-done.7 = bf16[8,128,1024]{2,1,0:T(8,128)(2,1)} copy-done((bf16[8,128,1024]{2,1,0:T(8,128)(2,1)}, bf16[8,128,1024]{2,1,0:T(8,128)(2,1)S(1)}, u32[]{:S(2)}) %copy-start.7) | copy-done | bytes 2097176
  70.2 8.4 %project_back.1 = (f32[128,512]{1,0:T(8,128)S(1)}, f32[144,512]{1,0:T(8,128)S(1)}) custom-call(s32[16]{0:T(128)S(1)} %iota_xor_fusion.places_ref, bf16[8,128,1024]{2,1,0:T(8,128)(2,1)S(1)} %constant_dynamic-update-slice_fusion.low_ref, bf16[8,128,1024]{2,1,0:T(8,128)(2,1)} %copy-done.7, bf16[512,16384]{1,0:T(8,128)(2,1)} %w_ref.3), custom_call_target="tpu_custom_call" | custom-call | flops 2147483648 | bytes 20971520 | tf_op jit(solution)/shard_map/project_back/pallas_call | solution.py:376
  78.6 1.5 %collective-permute-start.12 = (f16[144,512]{1,0:T(8,128)(2,1)S(1)}, f16[144,512]{1,0:T(8,128)(2,1)S(1)}, u32[]{:S(2)}, u32[]{:S(2)}) collective-permute-start(f16[144,512]{1,0:T(8,128)(2,1)S(1)} %convert_element_type.33), channel_id=1, source_target_pairs={{0,8},{1,9},{2,10},{3,11},{4,12},{5,13},{6,14},{7,15},{8,0},{9,1},... | collective-permute-start | bytes 442376 | tf_op jit(solution)/shard_map/ppermute | solution.py:22
  80.1 0.1 convert_element_type.32.got_ref
  80.3 0.2 sum_unpack.2
  80.6 5.8 %collective-permute-done.12 = f16[144,512]{1,0:T(8,128)(2,1)S(1)} collective-permute-done((f16[144,512]{1,0:T(8,128)(2,1)S(1)}, f16[144,512]{1,0:T(8,128)(2,1)S(1)}, u32[]{:S(2)}, u32[]{:S(2)}) %collective-permute-start.12) | collective-permute-done | bytes 147488 | tf_op jit(solution)/shard_map/ppermute | solution.py:22
  86.3 0.1 convert_element_type.35.got_ref
  86.5 0.2 sum_unpack.3
  86.7 1.6 %collective-permute-start.13 = (f32[2,128,512]{2,1,0:T(8,128)S(1)}, f32[2,128,512]{2,1,0:T(8,128)S(1)}, u32[]{:S(2)}, u32[]{:S(2)}) collective-permute-start(f32[2,128,512]{2,1,0:T(8,128)S(1)} %get-tuple-element.62), channel_id=1, source_target_pairs={{0,2},{1,3},{2,0},{3,1},{4,6},{5,7},{6,4},{7,5},{8,10},{9,11},{10,... | collective-permute-start | bytes 1572872 | tf_op jit(solution)/shard_map/ppermute | solution.py:22
  88.3 6.9 %collective-permute-done.10.got_ref = f32[2,128,512]{2,1,0:T(8,128)S(1)} collective-permute-done((f32[2,128,512]{2,1,0:T(8,128)S(1)}, f32[2,128,512]{2,1,0:T(8,128)S(1)}, u32[]{:S(2)}, u32[]{:S(2)}) %collective-permute-start.10) | collective-permute-done | bytes 524320 | tf_op jit(solution)/shard_map/ppermute | solution.py:22
  95.2 0.3 sum_pack.6
  95.5 3.7 %collective-permute-start.14 = (f16[144,512]{1,0:T(8,128)(2,1)S(1)}, f16[144,512]{1,0:T(8,128)(2,1)S(1)}, u32[]{:S(2)}, u32[]{:S(2)}) collective-permute-start(f16[144,512]{1,0:T(8,128)(2,1)S(1)} %convert_element_type.36), channel_id=1, source_target_pairs={{0,8},{1,9},{2,10},{3,11},{4,12},{5,13},{6,14},{7,15},{8,0},{9,1},... | collective-permute-start | bytes 442376 | tf_op jit(solution)/shard_map/ppermute | solution.py:22
  99.2 1.3 %collective-permute-done.13.got_ref = f32[2,128,512]{2,1,0:T(8,128)S(1)} collective-permute-done((f32[2,128,512]{2,1,0:T(8,128)S(1)}, f32[2,128,512]{2,1,0:T(8,128)S(1)}, u32[]{:S(2)}, u32[]{:S(2)}) %collective-permute-start.13) | collective-permute-done | bytes 524320 | tf_op jit(solution)/shard_map/ppermute | solution.py:22
  100.5 0.2 sum_pack.7
  100.8 3.4 %collective-permute-start.15 = (f16[144,512]{1,0:T(8,128)(2,1)S(1)}, f16[144,512]{1,0:T(8,128)(2,1)S(1)}, u32[]{:S(2)}, u32[]{:S(2)}) collective-permute-start(f16[144,512]{1,0:T(8,128)(2,1)S(1)} %convert_element_type.38), channel_id=1, source_target_pairs={{0,8},{1,9},{2,10},{3,11},{4,12},{5,13},{6,14},{7,15},{8,0},{9,1},... | collective-permute-start | bytes 442376 | tf_op jit(solution)/shard_map/ppermute | solution.py:22
  104.2 0.1 select_reduce_fusion.inverse_ref
  104.3 12.9 %gradients.1 = (f32[128,512]{1,0:T(8,128)}, f32[128,512]{1,0:T(8,128)}) custom-call(s32[4,32]{1,0:T(4,128)S(1)} %select_reduce_fusion.inverse_ref, s32[1]{0:T(128)} %bitcast.5.high_ref, f32[128,512]{1,0:T(8,128)S(1)} %get-tuple-element.53.own_ref, f32[144,512]{1,0:T(8,128)S(1)} %convert_element_type.34.oth_ref, ...), custom_call_target="tpu_custom_call" | custom-call | tf_op jit(solution)/shard_map/gradients/pallas_call | solution.py:657
  117.2 0.9 last_sums.1
  (36 shorter events, 0.4 us)
Async XLA Ops:
  0.6 22.1 %copy-start.8 = (s32[16]{0:T(128)S(1)}, s32[16]{0:T(128)}, u32[]{:S(2)}) copy-start(s32[16]{0:T(128)} %constant.12.clone) | copy-start | bytes 196
  0.6 15.5 %collective-permute-start = (bf16[1,128,1024]{2,1,0:T(8,128)(2,1)}, bf16[1,128,1024]{2,1,0:T(8,128)(2,1)S(1)}, u32[]{:S(2)}, u32[]{:S(2)}) collective-permute-start(bf16[1,128,1024]{2,1,0:T(8,128)(2,1)} %bitcast.14), channel_id=1, source_target_pairs={{0,8},{1,9},{2,10},{3,11},{4,12},{5,13},{6,14},{7,15},{8,0},{9,1},... | collective-permute-start | bytes 786440 | tf_op jit(solution)/shard_map/ppermute | solution.py:22
  4.1 13.8 %collective-permute-start.1 = (f32[32,512]{1,0:T(8,128)S(1)}, f32[32,512]{1,0:T(8,128)S(1)}, u32[]{:S(2)}, u32[]{:S(2)}) collective-permute-start(f32[32,512]{1,0:T(8,128)S(1)} %slice_bitcast_fusion.1.own_ref), channel_id=1, source_target_pairs={{0,8},{1,9},{2,10},{3,11},{4,12},{5,13},{6,14},{7,15},{8,0},{9,1},... | collective-permute-start | bytes 196616 | tf_op jit(solution)/shard_map/ppermute | solution.py:22
  4.5 0.9 copy-start.2
  5.4 0.9 copy-start.4
  6.3 0.7 copy-start.5
  18.0 21.5 %collective-permute-start.3 = (bf16[2,128,1024]{2,1,0:T(8,128)(2,1)}, bf16[2,128,1024]{2,1,0:T(8,128)(2,1)}, u32[]{:S(2)}, u32[]{:S(2)}) collective-permute-start(bf16[2,128,1024]{2,1,0:T(8,128)(2,1)} %pad_maximum_fusion), channel_id=1, source_target_pairs={{0,4},{1,5},{2,6},{3,7},{4,0},{5,1},{6,2},{7,3},{8,12},{9,13},{10,... | collective-permute-start | bytes 1572872 | tf_op jit(solution)/shard_map/ppermute | solution.py:22
  19.8 19.7 %collective-permute-start.4 = (bf16[2,128,1024]{2,1,0:T(8,128)(2,1)}, bf16[2,128,1024]{2,1,0:T(8,128)(2,1)}, u32[]{:S(2)}, u32[]{:S(2)}) collective-permute-start(bf16[2,128,1024]{2,1,0:T(8,128)(2,1)} %pad_maximum_fusion), channel_id=1, source_target_pairs={{0,2},{1,3},{2,0},{3,1},{4,6},{5,7},{6,4},{7,5},{8,10},{9,11},{10,... | collective-permute-start | bytes 1572872 | tf_op jit(solution)/shard_map/ppermute | solution.py:22
  21.4 17.7 %collective-permute-start.2 = (f32[128,512]{1,0:T(8,128)}, f32[128,512]{1,0:T(8,128)S(1)}, u32[]{:S(2)}, u32[]{:S(2)}) collective-permute-start(f32[128,512]{1,0:T(8,128)} %slice_bitcast_fusion), channel_id=1, source_target_pairs={{0,8},{1,9},{2,10},{3,11},{4,12},{5,13},{6,14},{7,15},{8,0},{9,1},... | collective-permute-start | bytes 786440 | tf_op jit(solution)/shard_map/ppermute | solution.py:22
  49.9 5.4 %copy-start.1 = (f32[8,128,512]{2,1,0:T(8,128)S(1)}, f32[8,128,512]{2,1,0:T(8,128)}, u32[]{:S(2)}) copy-start(f32[8,128,512]{2,1,0:T(8,128)} %get-tuple-element.49.keep_ref) | copy-start | bytes 6291460
  49.9 5.3 %collective-permute-start.8 = (f32[8,128,512]{2,1,0:T(8,128)}, f32[8,128,512]{2,1,0:T(8,128)S(1)}, u32[]{:S(2)}, u32[]{:S(2)}) collective-permute-start(f32[8,128,512]{2,1,0:T(8,128)} %get-tuple-element.50), channel_id=1, source_target_pairs={{0,1},{1,0},{2,3},{3,2},{4,5},{5,4},{6,7},{7,6},{8,9},{9,8},{10,11... | collective-permute-start | bytes 6291464 | tf_op jit(solution)/shard_map/ppermute | solution.py:22
  49.9 7.4 %collective-permute-start.5 = (f32[8,128,512]{2,1,0:T(8,128)}, f32[8,128,512]{2,1,0:T(8,128)S(1)}, u32[]{:S(2)}, u32[]{:S(2)}) collective-permute-start(f32[8,128,512]{2,1,0:T(8,128)} %get-tuple-element.46), channel_id=1, source_target_pairs={{0,1},{1,0},{2,3},{3,2},{4,5},{5,4},{6,7},{7,6},{8,9},{9,8},{10,11... | collective-permute-start | bytes 6291464 | tf_op jit(solution)/shard_map/ppermute | solution.py:22
  50.4 14.1 %collective-permute-start.7 = (bf16[2,128,1024]{2,1,0:T(8,128)(2,1)}, bf16[2,128,1024]{2,1,0:T(8,128)(2,1)S(1)}, u32[]{:S(2)}, u32[]{:S(2)}) collective-permute-start(bf16[2,128,1024]{2,1,0:T(8,128)(2,1)} %collective-permute-done.3), channel_id=1, source_target_pairs={{0,2},{1,3},{2,0},{3,1},{4,6},{5,7},{6,4},{7,5},{8,10},{9,11},{10,... | collective-permute-start | bytes 1572872 | tf_op jit(solution)/shard_map/ppermute | solution.py:22
  55.2 2.1 %copy-start = (f32[8,128,512]{2,1,0:T(8,128)S(1)}, f32[8,128,512]{2,1,0:T(8,128)}, u32[]{:S(2)}) copy-start(f32[8,128,512]{2,1,0:T(8,128)} %get-tuple-element.45.keep_ref) | copy-start | bytes 6291460
  64.6 4.2 %collective-permute-start.9 = (bf16[8,128,1024]{2,1,0:T(8,128)(2,1)S(1)}, bf16[8,128,1024]{2,1,0:T(8,128)(2,1)S(1)}, u32[]{:S(2)}, u32[]{:S(2)}) collective-permute-start(bf16[8,128,1024]{2,1,0:T(8,128)(2,1)S(1)} %constant_dynamic-update-slice_fusion.low_ref), channel_id=1, source_target_pairs={{0,1},{1,0},{2,3},{3,2},{4,5},{5,4},{6,7},{7,6},{8,9},{9,8},{10,11... | collective-permute-start | bytes 6291464 | tf_op jit(solution)/shard_map/ppermute | solution.py:22
  64.7 15.4 %collective-permute-start.6 = (f16[528,512]{1,0:T(8,128)(2,1)S(1)}, f16[528,512]{1,0:T(8,128)(2,1)S(1)}, u32[]{:S(2)}, u32[]{:S(2)}) collective-permute-start(f16[528,512]{1,0:T(8,128)(2,1)S(1)} %convert_element_type.30), channel_id=1, source_target_pairs={{0,2},{1,3},{2,0},{3,1},{4,6},{5,7},{6,4},{7,5},{8,10},{9,11},{10,... | collective-permute-start | bytes 1622024 | tf_op jit(solution)/shard_map/ppermute | solution.py:22
  66.3 20.1 %collective-permute-start.11 = (f16[528,512]{1,0:T(8,128)(2,1)S(1)}, f16[528,512]{1,0:T(8,128)(2,1)S(1)}, u32[]{:S(2)}, u32[]{:S(2)}) collective-permute-start(f16[528,512]{1,0:T(8,128)(2,1)S(1)} %convert_element_type.31), channel_id=1, source_target_pairs={{0,4},{1,5},{2,6},{3,7},{4,0},{5,1},{6,2},{7,3},{8,12},{9,13},{10,... | collective-permute-start | bytes 1622024 | tf_op jit(solution)/shard_map/ppermute | solution.py:22
  68.8 1.4 %copy-start.7 = (bf16[8,128,1024]{2,1,0:T(8,128)(2,1)}, bf16[8,128,1024]{2,1,0:T(8,128)(2,1)S(1)}, u32[]{:S(2)}) copy-start(bf16[8,128,1024]{2,1,0:T(8,128)(2,1)S(1)} %collective-permute-done.9.high_ref) | copy-start | bytes 6291460
  78.6 7.7 %collective-permute-start.12 = (f16[144,512]{1,0:T(8,128)(2,1)S(1)}, f16[144,512]{1,0:T(8,128)(2,1)S(1)}, u32[]{:S(2)}, u32[]{:S(2)}) collective-permute-start(f16[144,512]{1,0:T(8,128)(2,1)S(1)} %convert_element_type.33), channel_id=1, source_target_pairs={{0,8},{1,9},{2,10},{3,11},{4,12},{5,13},{6,14},{7,15},{8,0},{9,1},... | collective-permute-start | bytes 442376 | tf_op jit(solution)/shard_map/ppermute | solution.py:22
  80.5 14.7 %collective-permute-start.10 = (f32[2,128,512]{2,1,0:T(8,128)S(1)}, f32[2,128,512]{2,1,0:T(8,128)S(1)}, u32[]{:S(2)}, u32[]{:S(2)}) collective-permute-start(f32[2,128,512]{2,1,0:T(8,128)S(1)} %get-tuple-element.56), channel_id=1, source_target_pairs={{0,4},{1,5},{2,6},{3,7},{4,0},{5,1},{6,2},{7,3},{8,12},{9,13},{10,... | collective-permute-start | bytes 1572872 | tf_op jit(solution)/shard_map/ppermute | solution.py:22
  86.5 17.7 %copy-start.6 = (s32[4,32]{1,0:T(4,128)S(1)}, s32[4,32]{1,0:T(4,128)}, u32[]{:S(2)}) copy-start(s32[4,32]{1,0:T(4,128)} %orders_ref.1) | copy-start | bytes 1540
  86.5 17.8 %copy-start.3 = (bf16[128,512]{1,0:T(8,128)(2,1)S(1)}, bf16[128,512]{1,0:T(8,128)(2,1)}, u32[]{:S(2)}) copy-start(bf16[128,512]{1,0:T(8,128)(2,1)} %tok_ref.3) | copy-start | bytes 393220
  86.7 13.7 %collective-permute-start.13 = (f32[2,128,512]{2,1,0:T(8,128)S(1)}, f32[2,128,512]{2,1,0:T(8,128)S(1)}, u32[]{:S(2)}, u32[]{:S(2)}) collective-permute-start(f32[2,128,512]{2,1,0:T(8,128)S(1)} %get-tuple-element.62), channel_id=1, source_target_pairs={{0,2},{1,3},{2,0},{3,1},{4,6},{5,7},{6,4},{7,5},{8,10},{9,11},{10,... | collective-permute-start | bytes 1572872 | tf_op jit(solution)/shard_map/ppermute | solution.py:22
  95.5 21.7 %collective-permute-start.14 = (f16[144,512]{1,0:T(8,128)(2,1)S(1)}, f16[144,512]{1,0:T(8,128)(2,1)S(1)}, u32[]{:S(2)}, u32[]{:S(2)}) collective-permute-start(f16[144,512]{1,0:T(8,128)(2,1)S(1)} %convert_element_type.36), channel_id=1, source_target_pairs={{0,8},{1,9},{2,10},{3,11},{4,12},{5,13},{6,14},{7,15},{8,0},{9,1},... | collective-permute-start | bytes 442376 | tf_op jit(solution)/shard_map/ppermute | solution.py:22
  100.8 16.4 %collective-permute-start.15 = (f16[144,512]{1,0:T(8,128)(2,1)S(1)}, f16[144,512]{1,0:T(8,128)(2,1)S(1)}, u32[]{:S(2)}, u32[]{:S(2)}) collective-permute-start(f16[144,512]{1,0:T(8,128)(2,1)S(1)} %convert_element_type.38), channel_id=1, source_target_pairs={{0,8},{1,9},{2,10},{3,11},{4,12},{5,13},{6,14},{7,15},{8,0},{9,1},... | collective-permute-start | bytes 442376 | tf_op jit(solution)/shard_map/ppermute | solution.py:22

commit v10 on v9

--- a/solution.py
+++ b/solution.py
@@ -590,9 +590,8 @@
         compiler_params=params,
         name="near_rotations",
     )(orders, flat, tokens)
-    x_last, pieces, far_gen = lax.optimization_barrier((xs[0], pieces, far_gen))
-    near_news, side_news = exchange(pieces, order[-3]), exchange(pieces, order[-2])
-    x_other = exchange(x_last, pair_bit)
+    pieces, far_gen = after(pieces, xs), after(far_gen, xs)
+    x_other = exchange(xs[0], pair_bit)
     inv_far, ffar, bfar = pl.pallas_call(
         far_rotations_kernel,
         out_shape=(
@@ -614,7 +613,8 @@
         cost_estimate=pl.CostEstimate(flops=10**7, bytes_accessed=10**7, transcendentals=0),
         name="far_rotations",
     )(orders[:1], high, stored[0], far_gen)
-    near_news = after(near_news, ffar, x_other)
+    pieces = after(pieces, ffar)
+    near_news, side_news = exchange(pieces, order[-3]), exchange(pieces, order[-2])
     last_news = exchange(near_news, order[-2])
     x_both = pl.pallas_call(
         far_kernel,
@@ -635,13 +635,13 @@
     fixed = here.astype(jnp.int32)
     places = jnp.bitwise_xor(fixed, jnp.asarray(np.array(offsets, np.int32)))
     back_places = jnp.bitwise_xor(fixed, jnp.arange(size, dtype=jnp.int32))
-    outs = project(after(x_both, near_news, side_news), weight, places, slots)
+    outs = project(x_both, weight, places, slots)
 
     def stage(keep, got):
         mid = keep.shape[0] // 2
         return keep[mid:] + got[mid:], keep[:mid] + got[:mid]
 
-    outs = [pack(keep, exchange(send, 0)) for send, keep in outs]
+    outs = [pack(keep, exchange(after(send, near_news, side_news), 0)) for send, keep in outs]
     gots = [exchange(send, order_[1]) for (send, _), order_ in zip(outs, stages)]
     last_news = after(last_news, *[send for send, _ in outs])
     pieces = jnp.concatenate([pieces, near_news, side_news, last_news], axis=0)

time: 119 us -> 113 us (0.950)
  the two profiles are of different devices: /device:TPU:8 before, /device:TPU:0 now
where the time goes in v10:
time: 113 us; the launch traced here: 112 us
  Pallas kernels  47.5 us (42%)
  waiting for transfers between devices  34.6 us (31%)
  starting transfers between devices  20.9 us (18%)
  local copies, waits for them, and re-layouts  6.7 us (6%)
  other arithmetic  1.78 us (2%)
    ppermute x16, waiting for transfers between devices, exchange(): lax.ppermute(array, 'tensor', [(i, i ^ 1 << bit) for i in range(size)])  34.6 us
    ppermute x16, starting transfers between devices, exchange(): lax.ppermute(array, 'tensor', [(i, i ^ 1 << bit) for i in range(size)])  20.9 us
    pallas_call x1, Pallas kernels, local(): pl.pallas_call(grads_kernel, out_shape=(jax.ShapeDtypeStruct((count, rows...  12.8 us
    pallas_call x1, Pallas kernels, project(): pl.pallas_call(functools.partial(project_kernel, slots), out_shape=(jax.S...  10.3 us
    pallas_call x1, Pallas kernels, project_back(): pl.pallas_call(functools.partial(back_kernel, order), out_shape=(jax.Shap...  8.39 us
    pallas_call x1, Pallas kernels, local(): pl.pallas_call(near_kernel, out_shape=(jax.ShapeDtypeStruct(square, f32),...  7.41 us
    pallas_call x1, Pallas kernels, local(): pl.pallas_call(far_rotations_kernel, out_shape=(jax.ShapeDtypeStruct(far_...  5.25 us
    unnamed x21, local copies, waits for them, and re-layouts  5.1 us
  transfers between devices with their start and end apart: 16, of which 10 were waited for; matrix products, arithmetic and copies ran while one was open for 4% of the time, Pallas kernels for 41%

profile of v10, /device:TPU:0, one launch (start us, length us, event | category | flops | bytes accessed | tf_op | source)
XLA Modules:
  0.0 112.5 jit_solution(5235621857884138516)
XLA Ops:
  0.6 4.1 %collective-permute-start.2 = (bf16[1,128,1024]{2,1,0:T(8,128)(2,1)}, bf16[1,128,1024]{2,1,0:T(8,128)(2,1)}, u32[]{:S(2)}, u32[]{:S(2)}) collective-permute-start(bf16[1,128,1024]{2,1,0:T(8,128)(2,1)} %bitcast.14), channel_id=1, source_target_pairs={{0,8},{1,9},{2,10},{3,11},{4,12},{5,13},{6,14},{7,15},{8,0},{9,1},... | collective-permute-start | bytes 786440 | tf_op jit(solution)/shard_map/ppermute | solution.py:22
  4.7 0.8 slice_bitcast_fusion.1.own_ref
  5.6 0.9 copy-done.2
  6.5 0.9 copy-done.4
  7.5 0.7 copy-done.5
  8.1 7.4 %near_rotations.1 = (f32[1024,128]{1,0:T(8,128)S(1)}, f32[3,512,128]{2,1,0:T(8,128)S(1)}, f32[3,128,512]{2,1,0:T(8,128)S(1)}) custom-call(s32[4,32]{1,0:T(4,128)S(1)} %copy-done.5, f32[128,512]{1,0:T(8,128)S(1)} %bitcast.13, bf16[128,512]{1,0:T(8,128)(2,1)S(1)} %copy-done.2), custom_call_target="tpu_custom_call" | custom-call | tf_op jit(solution)/shard_map/near_rotations/pallas_call | solution.py:574
  15.6 0.7 slice_bitcast_fusion
  16.3 2.9 %collective-permute-start = (f32[128,512]{1,0:T(8,128)}, f32[128,512]{1,0:T(8,128)S(1)}, u32[]{:S(2)}, u32[]{:S(2)}) collective-permute-start(f32[128,512]{1,0:T(8,128)} %slice_bitcast_fusion), channel_id=1, source_target_pairs={{0,8},{1,9},{2,10},{3,11},{4,12},{5,13},{6,14},{7,15},{8,0},{9,1},... | collective-permute-start | bytes 786440 | tf_op jit(solution)/shard_map/ppermute | solution.py:22
  19.2 0.6 collective-permute-done.1.far_ref
  19.8 5.3 %far_rotations.1 = (f32[1024,32]{1,0:T(8,128)S(1)}, f32[2,512,128]{2,1,0:T(8,128)S(1)}, f32[2,512,128]{2,1,0:T(8,128)S(1)}) custom-call(s32[1,32]{1,0:T(1,128)S(1)} %slice.11.orders_ref, s32[1]{0:T(128)} %bitcast.3.high_ref, f32[32,512]{1,0:T(8,128)S(1)} %slice_bitcast_fusion.1.own_ref, f32[32,512]{1,0:T(8,128)S(1)} %collective-permute-done.1.far_ref), custom_call_target="tpu_custom_call" | custom-call | flops 10000000 | bytes 10000000 | tf_op jit(solution)/shard_map/far_rotations/pallas_call | solution.py:595
  25.0 1.1 pad_maximum_fusion
  26.1 1.1 collective-permute-start.3
  27.2 1.5 %collective-permute-start.4 = (bf16[2,128,1024]{2,1,0:T(8,128)(2,1)S(1)}, bf16[2,128,1024]{2,1,0:T(8,128)(2,1)S(1)}, u32[]{:S(2)}, u32[]{:S(2)}) collective-permute-start(bf16[2,128,1024]{2,1,0:T(8,128)(2,1)S(1)} %pad_maximum_fusion), channel_id=1, source_target_pairs={{0,2},{1,3},{2,0},{3,1},{4,6},{5,7},{6,4},{7,5},{8,10},{9,11},{10,... | collective-permute-start | bytes 1572872 | tf_op jit(solution)/shard_map/ppermute | solution.py:22
  28.7 2.3 %collective-permute-done.oth_ref.x_oth_ref = f32[128,512]{1,0:T(8,128)S(1)} collective-permute-done((f32[128,512]{1,0:T(8,128)}, f32[128,512]{1,0:T(8,128)S(1)}, u32[]{:S(2)}, u32[]{:S(2)}) %collective-permute-start) | collective-permute-done | bytes 262176 | tf_op jit(solution)/shard_map/ppermute | solution.py:22
  31.0 0.4 far_apply.1.x_ref
  31.4 10.3 %project.1 = (f32[8,128,512]{2,1,0:T(8,128)}, f32[8,128,512]{2,1,0:T(8,128)}, f32[8,128,512]{2,1,0:T(8,128)}, f32[8,128,512]{2,1,0:T(8,128)}) custom-call(s32[16]{0:T(128)S(1)} %broadcast_xor_fusion.places_ref, bf16[256,512]{1,0:T(8,128)(2,1)S(1)} %far_apply.1.x_ref, bf16[512,16384]{1,0:T(8,128)(2,1)} %w_ref.3), custom_call_target="tpu_custom_call" | custom-call | flops 4294967296 | bytes 25165824 | tf_op jit(solution)/shard_map/project/pallas_call | solution.py:318
  41.8 0.5 collective-permute-done.3
  42.3 0.5 collective-permute-start.5
  42.8 1.6 %collective-permute-start.7 = (bf16[2,128,1024]{2,1,0:T(8,128)(2,1)}, bf16[2,128,1024]{2,1,0:T(8,128)(2,1)S(1)}, u32[]{:S(2)}, u32[]{:S(2)}) collective-permute-start(bf16[2,128,1024]{2,1,0:T(8,128)(2,1)} %collective-permute-done.3), channel_id=1, source_target_pairs={{0,2},{1,3},{2,0},{3,1},{4,6},{5,7},{6,4},{7,5},{8,10},{9,11},{10,... | collective-permute-start | bytes 1572872 | tf_op jit(solution)/shard_map/ppermute | solution.py:22
  44.4 1.1 constant_dynamic-update-slice_fusion.2
  45.5 1.1 collective-permute-done.8.got_ref
  46.6 0.5 sum_pack.5
  47.2 0.1 convert_element_type.31
  47.3 2.3 %collective-permute-done.5.got_ref = f32[8,128,512]{2,1,0:T(8,128)S(1)} collective-permute-done((f32[8,128,512]{2,1,0:T(8,128)}, f32[8,128,512]{2,1,0:T(8,128)S(1)}, u32[]{:S(2)}, u32[]{:S(2)}) %collective-permute-start.5) | collective-permute-done | bytes 2097184 | tf_op jit(solution)/shard_map/ppermute | solution.py:22
  49.6 0.5 sum_pack.4
  50.2 0.1 convert_element_type.30
  50.3 6.5 %collective-permute-done.7 = bf16[2,128,1024]{2,1,0:T(8,128)(2,1)S(1)} collective-permute-done((bf16[2,128,1024]{2,1,0:T(8,128)(2,1)}, bf16[2,128,1024]{2,1,0:T(8,128)(2,1)S(1)}, u32[]{:S(2)}, u32[]{:S(2)}) %collective-permute-start.7) | collective-permute-done | bytes 524320 | tf_op jit(solution)/shard_map/ppermute | solution.py:22
  56.9 0.1 collective-permute-start.9
  57.0 1.6 %collective-permute-start.6 = (f16[528,512]{1,0:T(8,128)(2,1)S(1)}, f16[528,512]{1,0:T(8,128)(2,1)S(1)}, u32[]{:S(2)}, u32[]{:S(2)}) collective-permute-start(f16[528,512]{1,0:T(8,128)(2,1)S(1)} %convert_element_type.30), channel_id=1, source_target_pairs={{0,2},{1,3},{2,0},{3,1},{4,6},{5,7},{6,4},{7,5},{8,10},{9,11},{10,... | collective-permute-start | bytes 1622024 | tf_op jit(solution)/shard_map/ppermute | solution.py:22
  58.6 0.4 collective-permute-start.11
  59.0 2.1 %collective-permute-done.9.high_ref = bf16[8,128,1024]{2,1,0:T(8,128)(2,1)S(1)} collective-permute-done((bf16[8,128,1024]{2,1,0:T(8,128)(2,1)S(1)}, bf16[8,128,1024]{2,1,0:T(8,128)(2,1)S(1)}, u32[]{:S(2)}, u32[]{:S(2)}) %collective-permute-start.9) | collective-permute-done | bytes 2097184 | tf_op jit(solution)/shard_map/ppermute | solution.py:22
  61.1 1.4 %copy-done.7 = bf16[8,128,1024]{2,1,0:T(8,128)(2,1)} copy-done((bf16[8,128,1024]{2,1,0:T(8,128)(2,1)}, bf16[8,128,1024]{2,1,0:T(8,128)(2,1)S(1)}, u32[]{:S(2)}) %copy-start.7) | copy-done | bytes 2097176
  62.5 8.4 %project_back.1 = (f32[128,512]{1,0:T(8,128)S(1)}, f32[144,512]{1,0:T(8,128)S(1)}) custom-call(s32[16]{0:T(128)S(1)} %iota_xor_fusion.places_ref, bf16[8,128,1024]{2,1,0:T(8,128)(2,1)S(1)} %constant_dynamic-update-slice_fusion.low_ref, bf16[8,128,1024]{2,1,0:T(8,128)(2,1)} %copy-done.7, bf16[512,16384]{1,0:T(8,128)(2,1)} %w_ref.3), custom_call_target="tpu_custom_call" | custom-call | flops 2147483648 | bytes 20971520 | tf_op jit(solution)/shard_map/project_back/pallas_call | solution.py:376
  70.9 6.0 %collective-permute-start.12 = (f16[144,512]{1,0:T(8,128)(2,1)S(1)}, f16[144,512]{1,0:T(8,128)(2,1)S(1)}, u32[]{:S(2)}, u32[]{:S(2)}) collective-permute-start(f16[144,512]{1,0:T(8,128)(2,1)S(1)} %convert_element_type.33), channel_id=1, source_target_pairs={{0,8},{1,9},{2,10},{3,11},{4,12},{5,13},{6,14},{7,15},{8,0},{9,1},... | collective-permute-start | bytes 442376 | tf_op jit(solution)/shard_map/ppermute | solution.py:22
  76.9 0.1 convert_element_type.32.got_ref
  77.0 0.2 sum_unpack.2
  77.2 0.2 collective-permute-start.10
  77.4 6.4 %collective-permute-done.12 = f16[144,512]{1,0:T(8,128)(2,1)S(1)} collective-permute-done((f16[144,512]{1,0:T(8,128)(2,1)S(1)}, f16[144,512]{1,0:T(8,128)(2,1)S(1)}, u32[]{:S(2)}, u32[]{:S(2)}) %collective-permute-start.12) | collective-permute-done | bytes 147488 | tf_op jit(solution)/shard_map/ppermute | solution.py:22
  83.8 0.1 convert_element_type.35.got_ref
  84.0 0.2 sum_unpack.3
  84.2 0.9 collective-permute-start.13
  85.1 8.9 %collective-permute-done.10.got_ref = f32[2,128,512]{2,1,0:T(8,128)S(1)} collective-permute-done((f32[2,128,512]{2,1,0:T(8,128)S(1)}, f32[2,128,512]{2,1,0:T(8,128)S(1)}, u32[]{:S(2)}, u32[]{:S(2)}) %collective-permute-start.10) | collective-permute-done | bytes 524320 | tf_op jit(solution)/shard_map/ppermute | solution.py:22
  94.1 0.2 sum_pack.6
  94.4 3.7 %collective-permute-done.13.got_ref = f32[2,128,512]{2,1,0:T(8,128)S(1)} collective-permute-done((f32[2,128,512]{2,1,0:T(8,128)S(1)}, f32[2,128,512]{2,1,0:T(8,128)S(1)}, u32[]{:S(2)}, u32[]{:S(2)}) %collective-permute-start.13) | collective-permute-done | bytes 524320 | tf_op jit(solution)/shard_map/ppermute | solution.py:22
  98.1 0.2 sum_pack.7
  98.5 0.1 select_reduce_fusion.inverse_ref
  98.6 12.8 %gradients.1 = (f32[128,512]{1,0:T(8,128)}, f32[128,512]{1,0:T(8,128)}) custom-call(s32[4,32]{1,0:T(4,128)S(1)} %select_reduce_fusion.inverse_ref, s32[1]{0:T(128)} %bitcast.3.high_ref, f32[128,512]{1,0:T(8,128)S(1)} %get-tuple-element.53.own_ref, f32[144,512]{1,0:T(8,128)S(1)} %convert_element_type.34.oth_ref, ...), custom_call_target="tpu_custom_call" | custom-call | tf_op jit(solution)/shard_map/gradients/pallas_call | solution.py:657
  111.5 0.9 last_sums.1
  (36 shorter events, 0.5 us)
Async XLA Ops:
  0.6 28.1 %copy-start.8 = (s32[16]{0:T(128)S(1)}, s32[16]{0:T(128)}, u32[]{:S(2)}) copy-start(s32[16]{0:T(128)} %constant.12.clone) | copy-start | bytes 196
  0.6 24.4 %collective-permute-start.2 = (bf16[1,128,1024]{2,1,0:T(8,128)(2,1)}, bf16[1,128,1024]{2,1,0:T(8,128)(2,1)}, u32[]{:S(2)}, u32[]{:S(2)}) collective-permute-start(bf16[1,128,1024]{2,1,0:T(8,128)(2,1)} %bitcast.14), channel_id=1, source_target_pairs={{0,8},{1,9},{2,10},{3,11},{4,12},{5,13},{6,14},{7,15},{8,0},{9,1},... | collective-permute-start | bytes 786440 | tf_op jit(solution)/shard_map/ppermute | solution.py:22
  5.6 14.2 %collective-permute-start.1 = (f32[32,512]{1,0:T(8,128)S(1)}, f32[32,512]{1,0:T(8,128)S(1)}, u32[]{:S(2)}, u32[]{:S(2)}) collective-permute-start(f32[32,512]{1,0:T(8,128)S(1)} %slice_bitcast_fusion.1.own_ref), channel_id=1, source_target_pairs={{0,8},{1,9},{2,10},{3,11},{4,12},{5,13},{6,14},{7,15},{8,0},{9,1},... | collective-permute-start | bytes 196616 | tf_op jit(solution)/shard_map/ppermute | solution.py:22
  5.6 0.9 copy-start.2
  6.5 0.9 copy-start.4
  7.5 0.7 copy-start.5
  16.3 14.7 %collective-permute-start = (f32[128,512]{1,0:T(8,128)}, f32[128,512]{1,0:T(8,128)S(1)}, u32[]{:S(2)}, u32[]{:S(2)}) collective-permute-start(f32[128,512]{1,0:T(8,128)} %slice_bitcast_fusion), channel_id=1, source_target_pairs={{0,8},{1,9},{2,10},{3,11},{4,12},{5,13},{6,14},{7,15},{8,0},{9,1},... | collective-permute-start | bytes 786440 | tf_op jit(solution)/shard_map/ppermute | solution.py:22
  26.1 16.1 %collective-permute-start.3 = (bf16[2,128,1024]{2,1,0:T(8,128)(2,1)S(1)}, bf16[2,128,1024]{2,1,0:T(8,128)(2,1)}, u32[]{:S(2)}, u32[]{:S(2)}) collective-permute-start(bf16[2,128,1024]{2,1,0:T(8,128)(2,1)S(1)} %pad_maximum_fusion), channel_id=1, source_target_pairs={{0,4},{1,5},{2,6},{3,7},{4,0},{5,1},{6,2},{7,3},{8,12},{9,13},{10,... | collective-permute-start | bytes 1572872 | tf_op jit(solution)/shard_map/ppermute | solution.py:22
  27.2 15.1 %collective-permute-start.4 = (bf16[2,128,1024]{2,1,0:T(8,128)(2,1)S(1)}, bf16[2,128,1024]{2,1,0:T(8,128)(2,1)S(1)}, u32[]{:S(2)}, u32[]{:S(2)}) collective-permute-start(bf16[2,128,1024]{2,1,0:T(8,128)(2,1)S(1)} %pad_maximum_fusion), channel_id=1, source_target_pairs={{0,2},{1,3},{2,0},{3,1},{4,6},{5,7},{6,4},{7,5},{8,10},{9,11},{10,... | collective-permute-start | bytes 1572872 | tf_op jit(solution)/shard_map/ppermute | solution.py:22
  41.8 4.9 %copy-start.1 = (f32[8,128,512]{2,1,0:T(8,128)S(1)}, f32[8,128,512]{2,1,0:T(8,128)}, u32[]{:S(2)}) copy-start(f32[8,128,512]{2,1,0:T(8,128)} %get-tuple-element.48.keep_ref) | copy-start | bytes 6291460
  42.3 4.4 %collective-permute-start.8 = (f32[8,128,512]{2,1,0:T(8,128)}, f32[8,128,512]{2,1,0:T(8,128)S(1)}, u32[]{:S(2)}, u32[]{:S(2)}) collective-permute-start(f32[8,128,512]{2,1,0:T(8,128)} %get-tuple-element.50), channel_id=1, source_target_pairs={{0,1},{1,0},{2,3},{3,2},{4,5},{5,4},{6,7},{7,6},{8,9},{9,8},{10,11... | collective-permute-start | bytes 6291464 | tf_op jit(solution)/shard_map/ppermute | solution.py:22
  42.3 7.4 %collective-permute-start.5 = (f32[8,128,512]{2,1,0:T(8,128)}, f32[8,128,512]{2,1,0:T(8,128)S(1)}, u32[]{:S(2)}, u32[]{:S(2)}) collective-permute-start(f32[8,128,512]{2,1,0:T(8,128)} %get-tuple-element.45), channel_id=1, source_target_pairs={{0,1},{1,0},{2,3},{3,2},{4,5},{5,4},{6,7},{7,6},{8,9},{9,8},{10,11... | collective-permute-start | bytes 6291464 | tf_op jit(solution)/shard_map/ppermute | solution.py:22
  42.8 14.1 %collective-permute-start.7 = (bf16[2,128,1024]{2,1,0:T(8,128)(2,1)}, bf16[2,128,1024]{2,1,0:T(8,128)(2,1)S(1)}, u32[]{:S(2)}, u32[]{:S(2)}) collective-permute-start(bf16[2,128,1024]{2,1,0:T(8,128)(2,1)} %collective-permute-done.3), channel_id=1, source_target_pairs={{0,2},{1,3},{2,0},{3,1},{4,6},{5,7},{6,4},{7,5},{8,10},{9,11},{10,... | collective-permute-start | bytes 1572872 | tf_op jit(solution)/shard_map/ppermute | solution.py:22
  46.6 3.0 %copy-start = (f32[8,128,512]{2,1,0:T(8,128)S(1)}, f32[8,128,512]{2,1,0:T(8,128)}, u32[]{:S(2)}) copy-start(f32[8,128,512]{2,1,0:T(8,128)} %get-tuple-element.41.keep_ref) | copy-start | bytes 6291460
  56.9 4.2 %collective-permute-start.9 = (bf16[8,128,1024]{2,1,0:T(8,128)(2,1)S(1)}, bf16[8,128,1024]{2,1,0:T(8,128)(2,1)S(1)}, u32[]{:S(2)}, u32[]{:S(2)}) collective-permute-start(bf16[8,128,1024]{2,1,0:T(8,128)(2,1)S(1)} %constant_dynamic-update-slice_fusion.low_ref), channel_id=1, source_target_pairs={{0,1},{1,0},{2,3},{3,2},{4,5},{5,4},{6,7},{7,6},{8,9},{9,8},{10,11... | collective-permute-start | bytes 6291464 | tf_op jit(solution)/shard_map/ppermute | solution.py:22
  57.0 19.9 %collective-permute-start.6 = (f16[528,512]{1,0:T(8,128)(2,1)S(1)}, f16[528,512]{1,0:T(8,128)(2,1)S(1)}, u32[]{:S(2)}, u32[]{:S(2)}) collective-permute-start(f16[528,512]{1,0:T(8,128)(2,1)S(1)} %convert_element_type.30), channel_id=1, source_target_pairs={{0,2},{1,3},{2,0},{3,1},{4,6},{5,7},{6,4},{7,5},{8,10},{9,11},{10,... | collective-permute-start | bytes 1622024 | tf_op jit(solution)/shard_map/ppermute | solution.py:22
  58.6 25.3 %collective-permute-start.11 = (f16[528,512]{1,0:T(8,128)(2,1)S(1)}, f16[528,512]{1,0:T(8,128)(2,1)S(1)}, u32[]{:S(2)}, u32[]{:S(2)}) collective-permute-start(f16[528,512]{1,0:T(8,128)(2,1)S(1)} %convert_element_type.31), channel_id=1, source_target_pairs={{0,4},{1,5},{2,6},{3,7},{4,0},{5,1},{6,2},{7,3},{8,12},{9,13},{10,... | collective-permute-start | bytes 1622024 | tf_op jit(solution)/shard_map/ppermute | solution.py:22
  61.1 1.4 %copy-start.7 = (bf16[8,128,1024]{2,1,0:T(8,128)(2,1)}, bf16[8,128,1024]{2,1,0:T(8,128)(2,1)S(1)}, u32[]{:S(2)}) copy-start(bf16[8,128,1024]{2,1,0:T(8,128)(2,1)S(1)} %collective-permute-done.9.high_ref) | copy-start | bytes 6291460
  70.9 12.9 %collective-permute-start.12 = (f16[144,512]{1,0:T(8,128)(2,1)S(1)}, f16[144,512]{1,0:T(8,128)(2,1)S(1)}, u32[]{:S(2)}, u32[]{:S(2)}) collective-permute-start(f16[144,512]{1,0:T(8,128)(2,1)S(1)} %convert_element_type.33), channel_id=1, source_target_pairs={{0,8},{1,9},{2,10},{3,11},{4,12},{5,13},{6,14},{7,15},{8,0},{9,1},... | collective-permute-start | bytes 442376 | tf_op jit(solution)/shard_map/ppermute | solution.py:22
  77.2 16.8 %collective-permute-start.10 = (f32[2,128,512]{2,1,0:T(8,128)S(1)}, f32[2,128,512]{2,1,0:T(8,128)S(1)}, u32[]{:S(2)}, u32[]{:S(2)}) collective-permute-start(f32[2,128,512]{2,1,0:T(8,128)S(1)} %get-tuple-element.56), channel_id=1, source_target_pairs={{0,4},{1,5},{2,6},{3,7},{4,0},{5,1},{6,2},{7,3},{8,12},{9,13},{10,... | collective-permute-start | bytes 1572872 | tf_op jit(solution)/shard_map/ppermute | solution.py:22
  84.0 14.5 %copy-start.6 = (s32[4,32]{1,0:T(4,128)S(1)}, s32[4,32]{1,0:T(4,128)}, u32[]{:S(2)}) copy-start(s32[4,32]{1,0:T(4,128)} %orders_ref.1) | copy-start | bytes 1540
  84.0 14.6 %copy-start.3 = (bf16[128,512]{1,0:T(8,128)(2,1)S(1)}, bf16[128,512]{1,0:T(8,128)(2,1)}, u32[]{:S(2)}) copy-start(bf16[128,512]{1,0:T(8,128)(2,1)} %tok_ref.3) | copy-start | bytes 393220
  84.2 13.9 %collective-permute-start.13 = (f32[2,128,512]{2,1,0:T(8,128)S(1)}, f32[2,128,512]{2,1,0:T(8,128)S(1)}, u32[]{:S(2)}, u32[]{:S(2)}) collective-permute-start(f32[2,128,512]{2,1,0:T(8,128)S(1)} %get-tuple-element.62), channel_id=1, source_target_pairs={{0,2},{1,3},{2,0},{3,1},{4,6},{5,7},{6,4},{7,5},{8,10},{9,11},{10,... | collective-permute-start | bytes 1572872 | tf_op jit(solution)/shard_map/ppermute | solution.py:22
  94.3 17.1 %collective-permute-start.14 = (f16[144,512]{1,0:T(8,128)(2,1)S(1)}, f16[144,512]{1,0:T(8,128)(2,1)S(1)}, u32[]{:S(2)}, u32[]{:S(2)}) collective-permute-start(f16[144,512]{1,0:T(8,128)(2,1)S(1)} %convert_element_type.36), channel_id=1, source_target_pairs={{0,8},{1,9},{2,10},{3,11},{4,12},{5,13},{6,14},{7,15},{8,0},{9,1},... | collective-permute-start | bytes 442376 | tf_op jit(solution)/shard_map/ppermute | solution.py:22
  98.4 13.1 %collective-permute-start.15 = (f16[144,512]{1,0:T(8,128)(2,1)S(1)}, f16[144,512]{1,0:T(8,128)(2,1)S(1)}, u32[]{:S(2)}, u32[]{:S(2)}) collective-permute-start(f16[144,512]{1,0:T(8,128)(2,1)S(1)} %convert_element_type.38), channel_id=1, source_target_pairs={{0,8},{1,9},{2,10},{3,11},{4,12},{5,13},{6,14},{7,15},{8,0},{9,1},... | collective-permute-start | bytes 442376 | tf_op jit(solution)/shard_map/ppermute | solution.py:22

commit v11 on v10

--- a/solution.py
+++ b/solution.py
@@ -566,8 +566,9 @@
     far_gen = exchange(stored[0], pair_bit)
     order = list(range(bits - 1, -1, -1))
     pieces = cotangent[None]
-    for bit in order[:-3]:
+    for bit in order[:-4]:
         pieces = grow(pieces, bit)
+    firsts = [exchange(pieces, bit) for bit in order[-4:-1]]
     flat = stored.reshape(sections * block, rows)
     square = (block * block, lanes)
     far_square = (block * block, lanes // sections)
@@ -590,7 +591,8 @@
         compiler_params=params,
         name="near_rotations",
     )(orders, flat, tokens)
-    pieces, far_gen = after(pieces, xs), after(far_gen, xs)
+    by_far, by_mid, by_side = [after(first, xs) for first in firsts]
+    far_gen = after(far_gen, xs, by_side)
     x_other = exchange(xs[0], pair_bit)
     inv_far, ffar, bfar = pl.pallas_call(
         far_rotations_kernel,
@@ -613,9 +615,10 @@
         cost_estimate=pl.CostEstimate(flops=10**7, bytes_accessed=10**7, transcendentals=0),
         name="far_rotations",
     )(orders[:1], high, stored[0], far_gen)
-    pieces = after(pieces, ffar)
-    near_news, side_news = exchange(pieces, order[-3]), exchange(pieces, order[-2])
-    last_news = exchange(near_news, order[-2])
+    by_far, by_mid = after(by_far, ffar), after(by_mid, ffar)
+    by_both = exchange(by_far, order[-3])
+    side_pair = exchange(jnp.concatenate([by_far, by_mid], axis=0), order[-2])
+    side_last = exchange(by_both, order[-2])
     x_both = pl.pallas_call(
         far_kernel,
         out_shape=jax.ShapeDtypeStruct((2 * count, rows), jnp.bfloat16),
@@ -641,10 +644,12 @@
         mid = keep.shape[0] // 2
         return keep[mid:] + got[mid:], keep[:mid] + got[:mid]
 
-    outs = [pack(keep, exchange(after(send, near_news, side_news), 0)) for send, keep in outs]
+    outs = [pack(keep, exchange(after(send, by_both, side_pair), 0)) for send, keep in outs]
     gots = [exchange(send, order_[1]) for (send, _), order_ in zip(outs, stages)]
-    last_news = after(last_news, *[send for send, _ in outs])
-    pieces = jnp.concatenate([pieces, near_news, side_news, last_news], axis=0)
+    side_last = after(side_last, *[send for send, _ in outs])
+    pieces = jnp.concatenate(
+        [pieces, by_far, by_mid, by_both, by_side, side_pair, side_last], axis=0
+    )
     gathered = [pieces, exchange(pieces, 0)]
     numbers = jnp.arange(block, dtype=jnp.int32)
     inverse = jnp.sum(
@@ -653,7 +658,7 @@
     grad_cols, grad_packed = project_back(back_places, gathered, gather_order(order), weight)
     grad_other = exchange_packed(grad_packed, pair_bit)
     gots[0] = after(gots[0], grad_cols)
-    gots[-1] = after(gots[-1], grad_other)
+    gots[-1] = after(gots[-1], grad_cols)
     grad_tokens, grad_gens = pl.pallas_call(
         grads_kernel,
         out_shape=(

time: 113 us -> 102 us (0.903)
  waiting for transfers between devices: 34.6 us -> 24.6 us
  starting transfers between devices: 20.9 us -> 18.8 us
  local copies, waits for them, and re-layouts: 6.7 us -> 7.99 us
    ppermute x16 -> x18, waiting for transfers between devices: 34.6 us -> 24.6 us  [exchange(): lax.ppermute(array, 'tensor', [(i, i ^ 1 << bit) for i in range(size)])]
    ppermute x16 -> x18, starting transfers between devices: 20.9 us -> 18.8 us  [exchange(): lax.ppermute(array, 'tensor', [(i, i ^ 1 << bit) for i in range(size)])]
    unnamed x21 -> x34, local copies, waits for them, and re-layouts: 5.1 us -> 6.41 us
  transfers between devices with their start and end apart: 16 -> 18, of which waited for: 10 -> 8; matrix products, arithmetic and copies ran while one was open for 4% -> 4% of each run, Pallas kernels for 41% -> 46%
where the time goes in v11:
time: 102 us
  Pallas kernels  47.7 us (47%)
  waiting for transfers between devices  24.6 us (24%)
  starting transfers between devices  18.8 us (18%)
  local copies, waits for them, and re-layouts  7.99 us (8%)
  other arithmetic  1.79 us (2%)
    ppermute x18, waiting for transfers between devices, exchange(): lax.ppermute(array, 'tensor', [(i, i ^ 1 << bit) for i in range(size)])  24.6 us
    ppermute x18, starting transfers between devices, exchange(): lax.ppermute(array, 'tensor', [(i, i ^ 1 << bit) for i in range(size)])  18.8 us
    pallas_call x1, Pallas kernels, local(): pl.pallas_call(grads_kernel, out_shape=(jax.ShapeDtypeStruct((count, rows...  12.8 us
    pallas_call x1, Pallas kernels, project(): pl.pallas_call(functools.partial(project_kernel, slots), out_shape=(jax.S...  10.3 us
    pallas_call x1, Pallas kernels, project_back(): pl.pallas_call(functools.partial(back_kernel, order), out_shape=(jax.Shap...  8.39 us
    pallas_call x1, Pallas kernels, local(): pl.pallas_call(near_kernel, out_shape=(jax.ShapeDtypeStruct(square, f32),...  7.58 us
    unnamed x34, local copies, waits for them, and re-layouts  6.41 us
    pallas_call x1, Pallas kernels, local(): pl.pallas_call(far_rotations_kernel, out_shape=(jax.ShapeDtypeStruct(far_...  5.25 us
  transfers between devices with their start and end apart: 18, of which 8 were waited for; matrix products, arithmetic and copies ran while one was open for 4% of the time, Pallas kernels for 46%

profile of v11, /device:TPU:0, one launch (start us, length us, event | category | flops | bytes accessed | tf_op | source)
XLA Modules:
  0.0 101.9 jit_solution(791169789416791904)
XLA Ops:
  0.6 3.0 %collective-permute-start.2 = (bf16[1,128,1024]{2,1,0:T(8,128)(2,1)}, bf16[1,128,1024]{2,1,0:T(8,128)(2,1)S(1)}, u32[]{:S(2)}, u32[]{:S(2)}) collective-permute-start(bf16[1,128,1024]{2,1,0:T(8,128)(2,1)} %bitcast.15), channel_id=1, source_target_pairs={{0,2},{1,3},{2,0},{3,1},{4,6},{5,7},{6,4},{7,5},{8,10},{9,11},{10,... | collective-permute-start | bytes 786440 | tf_op jit(solution)/shard_map/ppermute | solution.py:22
  3.7 2.6 %collective-permute-start.3 = (bf16[1,128,1024]{2,1,0:T(8,128)(2,1)}, bf16[1,128,1024]{2,1,0:T(8,128)(2,1)S(1)}, u32[]{:S(2)}, u32[]{:S(2)}) collective-permute-start(bf16[1,128,1024]{2,1,0:T(8,128)(2,1)} %bitcast.16), channel_id=1, source_target_pairs={{0,8},{1,9},{2,10},{3,11},{4,12},{5,13},{6,14},{7,15},{8,0},{9,1},... | collective-permute-start | bytes 786440 | tf_op jit(solution)/shard_map/ppermute | solution.py:22
  6.3 1.6 %collective-permute-start.5 = (bf16[1,128,1024]{2,1,0:T(8,128)(2,1)}, bf16[1,128,1024]{2,1,0:T(8,128)(2,1)}, u32[]{:S(2)}, u32[]{:S(2)}) collective-permute-start(bf16[1,128,1024]{2,1,0:T(8,128)(2,1)} %bitcast.17), channel_id=1, source_target_pairs={{0,4},{1,5},{2,6},{3,7},{4,0},{5,1},{6,2},{7,3},{8,12},{9,13},{10,... | collective-permute-start | bytes 786440 | tf_op jit(solution)/shard_map/ppermute | solution.py:22
  7.8 0.8 slice_bitcast_fusion.1.own_ref
  8.7 0.3 collective-permute-start.1
  9.0 0.9 copy-done.2
  9.9 0.9 copy-done.4
  10.9 0.7 copy-done.5
  11.6 7.6 %near_rotations.1 = (f32[1024,128]{1,0:T(8,128)S(1)}, f32[3,512,128]{2,1,0:T(8,128)S(1)}, f32[3,128,512]{2,1,0:T(8,128)S(1)}) custom-call(s32[4,32]{1,0:T(4,128)S(1)} %copy-done.5, f32[128,512]{1,0:T(8,128)S(1)} %bitcast.14, bf16[128,512]{1,0:T(8,128)(2,1)S(1)} %copy-done.2), custom_call_target="tpu_custom_call" | custom-call | tf_op jit(solution)/shard_map/near_rotations/pallas_call | solution.py:575
  19.1 0.7 slice_bitcast_fusion
  19.9 2.6 %collective-permute-start = (f32[128,512]{1,0:T(8,128)}, f32[128,512]{1,0:T(8,128)S(1)}, u32[]{:S(2)}, u32[]{:S(2)}) collective-permute-start(f32[128,512]{1,0:T(8,128)} %slice_bitcast_fusion), channel_id=1, source_target_pairs={{0,8},{1,9},{2,10},{3,11},{4,12},{5,13},{6,14},{7,15},{8,0},{9,1},... | collective-permute-start | bytes 786440 | tf_op jit(solution)/shard_map/ppermute | solution.py:22
  22.5 0.7 copy-done.11
  23.2 0.7 copy-done.8
  23.9 5.3 %far_rotations.1 = (f32[1024,32]{1,0:T(8,128)S(1)}, f32[2,512,128]{2,1,0:T(8,128)S(1)}, f32[2,512,128]{2,1,0:T(8,128)S(1)}) custom-call(s32[1,32]{1,0:T(1,128)S(1)} %slice.11.orders_ref, s32[1]{0:T(128)} %bitcast.3.high_ref, f32[32,512]{1,0:T(8,128)S(1)} %slice_bitcast_fusion.1.own_ref, f32[32,512]{1,0:T(8,128)S(1)} %collective-permute-done.1.far_ref), custom_call_target="tpu_custom_call" | custom-call | flops 10000000 | bytes 10000000 | tf_op jit(solution)/shard_map/far_rotations/pallas_call | solution.py:597
  29.1 1.1 %pad_maximum_fusion = bf16[2,128,1024]{2,1,0:T(8,128)(2,1)S(1)} fusion(bf16[1,128,1024]{2,1,0:T(8,128)(2,1)} %collective-permute-done.5, bf16[1,128,1024]{2,1,0:T(8,128)(2,1)} %copy-done.8), kind=kLoop, calls=%fused_computation | loop fusion | flops 262144 | bytes 1048576 | tf_op jit(solution)/shard_map/concatenate | solution.py:620
  30.2 0.6 collective-permute-start.6
  30.8 0.4 collective-permute-start.4
  31.3 2.3 %collective-permute-done.oth_ref.x_oth_ref = f32[128,512]{1,0:T(8,128)S(1)} collective-permute-done((f32[128,512]{1,0:T(8,128)}, f32[128,512]{1,0:T(8,128)S(1)}, u32[]{:S(2)}, u32[]{:S(2)}) %collective-permute-start) | collective-permute-done | bytes 262176 | tf_op jit(solution)/shard_map/ppermute | solution.py:22
  33.5 0.4 far_apply.1.x_ref
  33.9 10.3 %project.1 = (f32[8,128,512]{2,1,0:T(8,128)}, f32[8,128,512]{2,1,0:T(8,128)}, f32[8,128,512]{2,1,0:T(8,128)}, f32[8,128,512]{2,1,0:T(8,128)}) custom-call(s32[16]{0:T(128)S(1)} %broadcast_xor_fusion.places_ref, bf16[256,512]{1,0:T(8,128)(2,1)S(1)} %far_apply.1.x_ref, bf16[512,16384]{1,0:T(8,128)(2,1)} %w_ref.3), custom_call_target="tpu_custom_call" | custom-call | flops 4294967296 | bytes 25165824 | tf_op jit(solution)/shard_map/project/pallas_call | solution.py:318
  44.4 0.5 collective-permute-start.7
  45.0 1.0 constant_dynamic-update-slice_fusion.4
  45.9 0.5 collective-permute-start.9
  46.5 2.3 %collective-permute-done.10.got_ref = f32[8,128,512]{2,1,0:T(8,128)S(1)} collective-permute-done((f32[8,128,512]{2,1,0:T(8,128)}, f32[8,128,512]{2,1,0:T(8,128)S(1)}, u32[]{:S(2)}, u32[]{:S(2)}) %collective-permute-start.10) | collective-permute-done | bytes 2097184 | tf_op jit(solution)/shard_map/ppermute | solution.py:22
  48.8 0.5 sum_pack.5
  49.4 2.3 %collective-permute-done.7.got_ref = f32[8,128,512]{2,1,0:T(8,128)S(1)} collective-permute-done((f32[8,128,512]{2,1,0:T(8,128)}, f32[8,128,512]{2,1,0:T(8,128)S(1)}, u32[]{:S(2)}, u32[]{:S(2)}) %collective-permute-start.7) | collective-permute-done | bytes 2097184 | tf_op jit(solution)/shard_map/ppermute | solution.py:22
  51.8 0.5 sum_pack.4
  52.4 1.9 %collective-permute-done.9 = bf16[1,128,1024]{2,1,0:T(8,128)(2,1)S(1)} collective-permute-done((bf16[1,128,1024]{2,1,0:T(8,128)(2,1)S(1)}, bf16[1,128,1024]{2,1,0:T(8,128)(2,1)S(1)}, u32[]{:S(2)}, u32[]{:S(2)}) %collective-permute-start.9) | collective-permute-done | bytes 262176 | tf_op jit(solution)/shard_map/ppermute | solution.py:22
  54.5 0.8 collective-permute-start.8
  55.3 3.3 %collective-permute-done.11.high_ref = bf16[8,128,1024]{2,1,0:T(8,128)(2,1)S(1)} collective-permute-done((bf16[8,128,1024]{2,1,0:T(8,128)(2,1)S(1)}, bf16[8,128,1024]{2,1,0:T(8,128)(2,1)S(1)}, u32[]{:S(2)}, u32[]{:S(2)}) %collective-permute-start.11) | collective-permute-done | bytes 2097184 | tf_op jit(solution)/shard_map/ppermute | solution.py:22
  58.5 1.4 %copy-done.7 = bf16[8,128,1024]{2,1,0:T(8,128)(2,1)} copy-done((bf16[8,128,1024]{2,1,0:T(8,128)(2,1)}, bf16[8,128,1024]{2,1,0:T(8,128)(2,1)S(1)}, u32[]{:S(2)}) %copy-start.7) | copy-done | bytes 2097176
  59.9 8.4 %project_back.1 = (f32[128,512]{1,0:T(8,128)S(1)}, f32[144,512]{1,0:T(8,128)S(1)}) custom-call(s32[16]{0:T(128)S(1)} %iota_xor_fusion.places_ref, bf16[8,128,1024]{2,1,0:T(8,128)(2,1)S(1)} %constant_dynamic-update-slice_fusion.low_ref, bf16[8,128,1024]{2,1,0:T(8,128)(2,1)} %copy-done.7, bf16[512,16384]{1,0:T(8,128)(2,1)} %w_ref.3), custom_call_target="tpu_custom_call" | custom-call | flops 2147483648 | bytes 20971520 | tf_op jit(solution)/shard_map/project_back/pallas_call | solution.py:376
  68.3 0.8 collective-permute-done.13
  69.1 0.1 convert_element_type.33.got_ref
  69.2 0.2 sum_unpack.3
  69.4 0.5 collective-permute-start.14
  69.9 0.1 convert_element_type.32.got_ref
  70.1 0.2 sum_unpack.2
  70.3 1.0 collective-permute-start.12
  71.3 2.3 %collective-permute-start.17 = (f16[144,512]{1,0:T(8,128)(2,1)S(1)}, f16[144,512]{1,0:T(8,128)(2,1)S(1)}, u32[]{:S(2)}, u32[]{:S(2)}) collective-permute-start(f16[144,512]{1,0:T(8,128)(2,1)S(1)} %convert_element_type.38), channel_id=1, source_target_pairs={{0,8},{1,9},{2,10},{3,11},{4,12},{5,13},{6,14},{7,15},{8,0},{9,1},... | collective-permute-start | bytes 442376 | tf_op jit(solution)/shard_map/ppermute | solution.py:22
  73.6 9.4 %collective-permute-done.14.got_ref = f32[2,128,512]{2,1,0:T(8,128)S(1)} collective-permute-done((f32[2,128,512]{2,1,0:T(8,128)S(1)}, f32[2,128,512]{2,1,0:T(8,128)S(1)}, u32[]{:S(2)}, u32[]{:S(2)}) %collective-permute-start.14) | collective-permute-done | bytes 524320 | tf_op jit(solution)/shard_map/ppermute | solution.py:22
  83.0 0.2 sum_pack.7
  83.3 1.6 %collective-permute-start.16 = (f16[144,512]{1,0:T(8,128)(2,1)S(1)}, f16[144,512]{1,0:T(8,128)(2,1)S(1)}, u32[]{:S(2)}, u32[]{:S(2)}) collective-permute-start(f16[144,512]{1,0:T(8,128)(2,1)S(1)} %convert_element_type.36), channel_id=1, source_target_pairs={{0,8},{1,9},{2,10},{3,11},{4,12},{5,13},{6,14},{7,15},{8,0},{9,1},... | collective-permute-start | bytes 442376 | tf_op jit(solution)/shard_map/ppermute | solution.py:22
  84.9 2.5 %collective-permute-done.12.got_ref = f32[2,128,512]{2,1,0:T(8,128)S(1)} collective-permute-done((f32[2,128,512]{2,1,0:T(8,128)S(1)}, f32[2,128,512]{2,1,0:T(8,128)S(1)}, u32[]{:S(2)}, u32[]{:S(2)}) %collective-permute-start.12) | collective-permute-done | bytes 524320 | tf_op jit(solution)/shard_map/ppermute | solution.py:22
  87.4 0.2 sum_pack.6
  87.7 0.2 collective-permute-start.15
  88.0 12.8 %gradients.1 = (f32[128,512]{1,0:T(8,128)}, f32[128,512]{1,0:T(8,128)}) custom-call(s32[4,32]{1,0:T(4,128)S(1)} %select_reduce_fusion.inverse_ref, s32[1]{0:T(128)} %bitcast.3.high_ref, f32[128,512]{1,0:T(8,128)S(1)} %get-tuple-element.59.own_ref, f32[144,512]{1,0:T(8,128)S(1)} %convert_element_type.39.oth_ref, ...), custom_call_target="tpu_custom_call" | custom-call | tf_op jit(solution)/shard_map/gradients/pallas_call | solution.py:662
  101.0 0.9 last_sums.1
  (53 shorter events, 0.9 us)
Async XLA Ops:
  0.6 30.2 %copy-start.13 = (s32[16]{0:T(128)S(1)}, s32[16]{0:T(128)}, u32[]{:S(2)}) copy-start(s32[16]{0:T(128)} %constant.12.clone) | copy-start | bytes 196
  0.6 21.8 %collective-permute-start.2 = (bf16[1,128,1024]{2,1,0:T(8,128)(2,1)}, bf16[1,128,1024]{2,1,0:T(8,128)(2,1)S(1)}, u32[]{:S(2)}, u32[]{:S(2)}) collective-permute-start(bf16[1,128,1024]{2,1,0:T(8,128)(2,1)} %bitcast.15), channel_id=1, source_target_pairs={{0,2},{1,3},{2,0},{3,1},{4,6},{5,7},{6,4},{7,5},{8,10},{9,11},{10,... | collective-permute-start | bytes 786440 | tf_op jit(solution)/shard_map/ppermute | solution.py:22
  3.7 18.8 %collective-permute-start.3 = (bf16[1,128,1024]{2,1,0:T(8,128)(2,1)}, bf16[1,128,1024]{2,1,0:T(8,128)(2,1)S(1)}, u32[]{:S(2)}, u32[]{:S(2)}) collective-permute-start(bf16[1,128,1024]{2,1,0:T(8,128)(2,1)} %bitcast.16), channel_id=1, source_target_pairs={{0,8},{1,9},{2,10},{3,11},{4,12},{5,13},{6,14},{7,15},{8,0},{9,1},... | collective-permute-start | bytes 786440 | tf_op jit(solution)/shard_map/ppermute | solution.py:22
  6.3 22.9 %collective-permute-start.5 = (bf16[1,128,1024]{2,1,0:T(8,128)(2,1)}, bf16[1,128,1024]{2,1,0:T(8,128)(2,1)}, u32[]{:S(2)}, u32[]{:S(2)}) collective-permute-start(bf16[1,128,1024]{2,1,0:T(8,128)(2,1)} %bitcast.17), channel_id=1, source_target_pairs={{0,4},{1,5},{2,6},{3,7},{4,0},{5,1},{6,2},{7,3},{8,12},{9,13},{10,... | collective-permute-start | bytes 786440 | tf_op jit(solution)/shard_map/ppermute | solution.py:22
  8.7 13.8 %collective-permute-start.1 = (f32[32,512]{1,0:T(8,128)S(1)}, f32[32,512]{1,0:T(8,128)S(1)}, u32[]{:S(2)}, u32[]{:S(2)}) collective-permute-start(f32[32,512]{1,0:T(8,128)S(1)} %slice_bitcast_fusion.1.own_ref), channel_id=1, source_target_pairs={{0,8},{1,9},{2,10},{3,11},{4,12},{5,13},{6,14},{7,15},{8,0},{9,1},... | collective-permute-start | bytes 196616 | tf_op jit(solution)/shard_map/ppermute | solution.py:22
  9.0 0.9 copy-start.2
  9.9 0.9 copy-start.4
  10.9 0.7 copy-start.5
  19.9 13.6 %collective-permute-start = (f32[128,512]{1,0:T(8,128)}, f32[128,512]{1,0:T(8,128)S(1)}, u32[]{:S(2)}, u32[]{:S(2)}) collective-permute-start(f32[128,512]{1,0:T(8,128)} %slice_bitcast_fusion), channel_id=1, source_target_pairs={{0,8},{1,9},{2,10},{3,11},{4,12},{5,13},{6,14},{7,15},{8,0},{9,1},... | collective-permute-start | bytes 786440 | tf_op jit(solution)/shard_map/ppermute | solution.py:22
  22.5 0.7 copy-start.11
  23.2 0.7 copy-start.8
  30.2 14.1 %collective-permute-start.6 = (bf16[2,128,1024]{2,1,0:T(8,128)(2,1)S(1)}, bf16[2,128,1024]{2,1,0:T(8,128)(2,1)S(1)}, u32[]{:S(2)}, u32[]{:S(2)}) collective-permute-start(bf16[2,128,1024]{2,1,0:T(8,128)(2,1)S(1)} %pad_maximum_fusion), channel_id=1, source_target_pairs={{0,2},{1,3},{2,0},{3,1},{4,6},{5,7},{6,4},{7,5},{8,10},{9,11},{10,... | collective-permute-start | bytes 1572872 | tf_op jit(solution)/shard_map/ppermute | solution.py:22
  30.8 13.5 %collective-permute-start.4 = (bf16[1,128,1024]{2,1,0:T(8,128)(2,1)}, bf16[1,128,1024]{2,1,0:T(8,128)(2,1)S(1)}, u32[]{:S(2)}, u32[]{:S(2)}) collective-permute-start(bf16[1,128,1024]{2,1,0:T(8,128)(2,1)} %copy-done.8), channel_id=1, source_target_pairs={{0,4},{1,5},{2,6},{3,7},{4,0},{5,1},{6,2},{7,3},{8,12},{9,13},{10,... | collective-permute-start | bytes 786440 | tf_op jit(solution)/shard_map/ppermute | solution.py:22
  33.9 11.0 %copy-start.10 = (bf16[128,1024]{1,0:T(8,128)(2,1)S(1)}, bf16[128,1024]{1,0:T(8,128)(2,1)}, u32[]{:S(2)}) copy-start(bf16[128,1024]{1,0:T(8,128)(2,1)} %param.10) | copy-start | bytes 786436
  33.9 11.0 %copy-start.9 = (bf16[1,128,1024]{2,1,0:T(8,128)(2,1)S(1)}, bf16[1,128,1024]{2,1,0:T(8,128)(2,1)}, u32[]{:S(2)}) copy-start(bf16[1,128,1024]{2,1,0:T(8,128)(2,1)} %copy-done.8) | copy-start | bytes 786436
  33.9 12.5 %copy-start.12 = (bf16[1,128,1024]{2,1,0:T(8,128)(2,1)S(1)}, bf16[1,128,1024]{2,1,0:T(8,128)(2,1)}, u32[]{:S(2)}) copy-start(bf16[1,128,1024]{2,1,0:T(8,128)(2,1)} %copy-done.11) | copy-start | bytes 786436
  44.3 4.5 %copy-start.1 = (f32[8,128,512]{2,1,0:T(8,128)S(1)}, f32[8,128,512]{2,1,0:T(8,128)}, u32[]{:S(2)}) copy-start(f32[8,128,512]{2,1,0:T(8,128)} %get-tuple-element.54.keep_ref) | copy-start | bytes 6291460
  44.3 4.4 %collective-permute-start.10 = (f32[8,128,512]{2,1,0:T(8,128)}, f32[8,128,512]{2,1,0:T(8,128)S(1)}, u32[]{:S(2)}, u32[]{:S(2)}) collective-permute-start(f32[8,128,512]{2,1,0:T(8,128)} %get-tuple-element.56), channel_id=1, source_target_pairs={{0,1},{1,0},{2,3},{3,2},{4,5},{5,4},{6,7},{7,6},{8,9},{9,8},{10,11... | collective-permute-start | bytes 6291464 | tf_op jit(solution)/shard_map/ppermute | solution.py:22
  44.4 7.4 %collective-permute-start.7 = (f32[8,128,512]{2,1,0:T(8,128)}, f32[8,128,512]{2,1,0:T(8,128)S(1)}, u32[]{:S(2)}, u32[]{:S(2)}) collective-permute-start(f32[8,128,512]{2,1,0:T(8,128)} %get-tuple-element.51), channel_id=1, source_target_pairs={{0,1},{1,0},{2,3},{3,2},{4,5},{5,4},{6,7},{7,6},{8,9},{9,8},{10,11... | collective-permute-start | bytes 6291464 | tf_op jit(solution)/shard_map/ppermute | solution.py:22
  45.9 8.4 %collective-permute-start.9 = (bf16[1,128,1024]{2,1,0:T(8,128)(2,1)S(1)}, bf16[1,128,1024]{2,1,0:T(8,128)(2,1)S(1)}, u32[]{:S(2)}, u32[]{:S(2)}) collective-permute-start(bf16[1,128,1024]{2,1,0:T(8,128)(2,1)S(1)} %collective-permute-done.4), channel_id=1, source_target_pairs={{0,2},{1,3},{2,0},{3,1},{4,6},{5,7},{6,4},{7,5},{8,10},{9,11},{10,... | collective-permute-start | bytes 786440 | tf_op jit(solution)/shard_map/ppermute | solution.py:22
  48.8 3.0 %copy-start = (f32[8,128,512]{2,1,0:T(8,128)S(1)}, f32[8,128,512]{2,1,0:T(8,128)}, u32[]{:S(2)}) copy-start(f32[8,128,512]{2,1,0:T(8,128)} %get-tuple-element.45.keep_ref) | copy-start | bytes 6291460
  54.3 4.2 %collective-permute-start.11 = (bf16[8,128,1024]{2,1,0:T(8,128)(2,1)S(1)}, bf16[8,128,1024]{2,1,0:T(8,128)(2,1)S(1)}, u32[]{:S(2)}, u32[]{:S(2)}) collective-permute-start(bf16[8,128,1024]{2,1,0:T(8,128)(2,1)S(1)} %constant_dynamic-update-slice_fusion.low_ref), channel_id=1, source_target_pairs={{0,1},{1,0},{2,3},{3,2},{4,5},{5,4},{6,7},{7,6},{8,9},{9,8},{10,11... | collective-permute-start | bytes 6291464 | tf_op jit(solution)/shard_map/ppermute | solution.py:22
  54.4 14.7 %collective-permute-start.13 = (f16[528,512]{1,0:T(8,128)(2,1)S(1)}, f16[528,512]{1,0:T(8,128)(2,1)S(1)}, u32[]{:S(2)}, u32[]{:S(2)}) collective-permute-start(f16[528,512]{1,0:T(8,128)(2,1)S(1)} %convert_element_type.31), channel_id=1, source_target_pairs={{0,4},{1,5},{2,6},{3,7},{4,0},{5,1},{6,2},{7,3},{8,12},{9,13},{10,... | collective-permute-start | bytes 1622024 | tf_op jit(solution)/shard_map/ppermute | solution.py:22
  54.5 15.4 %collective-permute-start.8 = (f16[528,512]{1,0:T(8,128)(2,1)S(1)}, f16[528,512]{1,0:T(8,128)(2,1)S(1)}, u32[]{:S(2)}, u32[]{:S(2)}) collective-permute-start(f16[528,512]{1,0:T(8,128)(2,1)S(1)} %convert_element_type.30), channel_id=1, source_target_pairs={{0,2},{1,3},{2,0},{3,1},{4,6},{5,7},{6,4},{7,5},{8,10},{9,11},{10,... | collective-permute-start | bytes 1622024 | tf_op jit(solution)/shard_map/ppermute | solution.py:22
  58.5 1.4 %copy-start.7 = (bf16[8,128,1024]{2,1,0:T(8,128)(2,1)}, bf16[8,128,1024]{2,1,0:T(8,128)(2,1)S(1)}, u32[]{:S(2)}) copy-start(bf16[8,128,1024]{2,1,0:T(8,128)(2,1)S(1)} %collective-permute-done.11.high_ref) | copy-start | bytes 6291460
  69.4 13.6 %collective-permute-start.14 = (f32[2,128,512]{2,1,0:T(8,128)S(1)}, f32[2,128,512]{2,1,0:T(8,128)S(1)}, u32[]{:S(2)}, u32[]{:S(2)}) collective-permute-start(f32[2,128,512]{2,1,0:T(8,128)S(1)} %get-tuple-element.67), channel_id=1, source_target_pairs={{0,2},{1,3},{2,0},{3,1},{4,6},{5,7},{6,4},{7,5},{8,10},{9,11},{10,... | collective-permute-start | bytes 1572872 | tf_op jit(solution)/shard_map/ppermute | solution.py:22
  70.3 17.6 %copy-start.6 = (s32[4,32]{1,0:T(4,128)S(1)}, s32[4,32]{1,0:T(4,128)}, u32[]{:S(2)}) copy-start(s32[4,32]{1,0:T(4,128)} %orders_ref.1) | copy-start | bytes 1540
  70.3 17.7 %copy-start.3 = (bf16[128,512]{1,0:T(8,128)(2,1)S(1)}, bf16[128,512]{1,0:T(8,128)(2,1)}, u32[]{:S(2)}) copy-start(bf16[128,512]{1,0:T(8,128)(2,1)} %tok_ref.3) | copy-start | bytes 393220
  70.3 17.1 %collective-permute-start.12 = (f32[2,128,512]{2,1,0:T(8,128)S(1)}, f32[2,128,512]{2,1,0:T(8,128)S(1)}, u32[]{:S(2)}, u32[]{:S(2)}) collective-permute-start(f32[2,128,512]{2,1,0:T(8,128)S(1)} %get-tuple-element.62), channel_id=1, source_target_pairs={{0,4},{1,5},{2,6},{3,7},{4,0},{5,1},{6,2},{7,3},{8,12},{9,13},{10,... | collective-permute-start | bytes 1572872 | tf_op jit(solution)/shard_map/ppermute | solution.py:22
  71.3 16.7 %collective-permute-start.17 = (f16[144,512]{1,0:T(8,128)(2,1)S(1)}, f16[144,512]{1,0:T(8,128)(2,1)S(1)}, u32[]{:S(2)}, u32[]{:S(2)}) collective-permute-start(f16[144,512]{1,0:T(8,128)(2,1)S(1)} %convert_element_type.38), channel_id=1, source_target_pairs={{0,8},{1,9},{2,10},{3,11},{4,12},{5,13},{6,14},{7,15},{8,0},{9,1},... | collective-permute-start | bytes 442376 | tf_op jit(solution)/shard_map/ppermute | solution.py:22
  83.3 17.6 %collective-permute-start.16 = (f16[144,512]{1,0:T(8,128)(2,1)S(1)}, f16[144,512]{1,0:T(8,128)(2,1)S(1)}, u32[]{:S(2)}, u32[]{:S(2)}) collective-permute-start(f16[144,512]{1,0:T(8,128)(2,1)S(1)} %convert_element_type.36), channel_id=1, source_target_pairs={{0,8},{1,9},{2,10},{3,11},{4,12},{5,13},{6,14},{7,15},{8,0},{9,1},... | collective-permute-start | bytes 442376 | tf_op jit(solution)/shard_map/ppermute | solution.py:22
  87.7 13.3 %collective-permute-start.15 = (f16[144,512]{1,0:T(8,128)(2,1)S(1)}, f16[144,512]{1,0:T(8,128)(2,1)S(1)}, u32[]{:S(2)}, u32[]{:S(2)}) collective-permute-start(f16[144,512]{1,0:T(8,128)(2,1)S(1)} %convert_element_type.34), channel_id=1, source_target_pairs={{0,8},{1,9},{2,10},{3,11},{4,12},{5,13},{6,14},{7,15},{8,0},{9,1},... | collective-permute-start | bytes 442376 | tf_op jit(solution)/shard_map/ppermute | solution.py:22

commit v12 on v11

--- a/solution.py
+++ b/solution.py
@@ -9,7 +9,7 @@
 from jax.sharding import PartitionSpec as P
 
 VMEM_LIMIT = 16 * 2**20
-WIDE_LIMIT = 50 * 2**20
+WIDE_LIMIT = 46 * 2**20
 GROUP = 128
 NN = (((1,), (0,)), ((), ()))
 NT = (((1,), (1,)), ((), ()))
@@ -486,65 +486,59 @@
         ggen_ref[k * block : (k + 1) * block, :] = row_ref[k * rows : (k + 1) * rows, :].T
 
 
-def pack_kernel(keep_ref, got_ref, packed_ref, out_ref):
+def merge_kernel(got_packed, send_packed, keep_ref, got_ref, send_ref, out_ref):
     half, count, width = out_ref.shape
+    if got_packed:
+        got_scale = jnp.exp2(got_ref[2 * half * count : 2 * half * count + 1, 0:1])
+
+    def total(p):
+        if got_packed:
+            return keep_ref[p] + got_ref[p * count : (p + 1) * count, :] * got_scale
+        return keep_ref[p] + got_ref[p]
+
     largest = jnp.zeros((count, width), jnp.float32)
     for p in range(half):
-        total = keep_ref[half + p] + got_ref[half + p]
-        packed_ref[p * count : (p + 1) * count, :] = total
-        largest = jnp.maximum(largest, jnp.abs(total))
-        out_ref[p] = keep_ref[p] + got_ref[p]
-    peak = jnp.max(largest, axis=(0, 1), keepdims=True)
-    exponent = jnp.ceil(jnp.log2(jnp.maximum(peak, 1e-30))) - 15.0
-    scale = jnp.exp2(-exponent)
-    for p in range(half):
-        packed_ref[p * count : (p + 1) * count, :] *= scale
-    packed_ref[half * count :, :] = jnp.broadcast_to(exponent, (16, width))
-
-
-def unpack_kernel(keep_ref, got_ref, send_ref, out_ref):
-    half, count, width = out_ref.shape
-    scale = jnp.exp2(got_ref[2 * half * count : 2 * half * count + 1, 0:1])
-    for p in range(half):
-        low, top = p * count, (half + p) * count
-        out_ref[p] = keep_ref[p] + got_ref[low : low + count, :] * scale
-        send_ref[p] = keep_ref[half + p] + got_ref[top : top + count, :] * scale
-
-
-def last_kernel(*refs):
+        out_ref[p] = total(p)
+        upper = total(half + p)
+        if send_packed:
+            send_ref[p * count : (p + 1) * count, :] = upper
+            largest = jnp.maximum(largest, jnp.abs(upper))
+        else:
+            send_ref[p] = upper
+    if send_packed:
+        peak = jnp.max(largest, axis=(0, 1), keepdims=True)
+        exponent = jnp.ceil(jnp.log2(jnp.maximum(peak, 1e-30))) - 15.0
+        scale = jnp.exp2(-exponent)
+        for p in range(half):
+            send_ref[p * count : (p + 1) * count, :] *= scale
+        send_ref[half * count :, :] = jnp.broadcast_to(exponent, (16, width))
+
+
+def last_kernel(packed, *refs):
     *in_refs, out_ref = refs
     chunks = len(in_refs) // 2
     width = in_refs[0].shape[2]
     for chunk in range(chunks):
-        out_ref[:, chunk * width : (chunk + 1) * width] = in_refs[chunk][0] + read_packed(
-            in_refs[chunks + chunk], 0, width
-        )
-
-
-def summed(kernel, name, keep, got, first):
+        got_ref = in_refs[chunks + chunk]
+        got = read_packed(got_ref, 0, width) if packed[chunk] else got_ref[0]
+        out_ref[:, chunk * width : (chunk + 1) * width] = in_refs[chunk][0] + got
+
+
+def merge(keep, got, got_packed, send_packed):
     pieces, count, width = keep.shape
+    half = pieces // 2
+    kept = jax.ShapeDtypeStruct((half, count, width), jnp.float32)
+    packed = jax.ShapeDtypeStruct((half * count + 16, width), jnp.float32)
     full = pl.BlockSpec(memory_space=pltpu.VMEM)
-    return pl.pallas_call(
-        kernel,
-        out_shape=(first, jax.ShapeDtypeStruct((pieces // 2, count, width), jnp.float32)),
+    send, keep = pl.pallas_call(
+        functools.partial(merge_kernel, got_packed, send_packed),
+        out_shape=(packed if send_packed else kept, kept),
         in_specs=[full] * 2,
         out_specs=(full,) * 2,
         compiler_params=pltpu.CompilerParams(vmem_limit_bytes=VMEM_LIMIT),
-        name=name,
-    )(keep, got)
-
-
-def pack(keep, got):
-    pieces, count, width = keep.shape
-    first = jax.ShapeDtypeStruct((pieces // 2 * count + 16, width), jnp.float32)
-    packed, keep = summed(pack_kernel, "sum_pack", keep, got, first)
-    return packed.astype(jnp.float16), keep
-
-
-def unpack(keep, got):
-    pieces, count, width = keep.shape
-    first = jax.ShapeDtypeStruct((pieces // 2, count, width), jnp.float32)
-    return summed(unpack_kernel, "sum_unpack", keep, got.astype(jnp.float32), first)
+        name="merge",
+    )(keep, got.astype(jnp.float32))
+    return (send.astype(jnp.float16) if send_packed else send), keep
 
 
 def local(tokens, weight, generators, orders, cotangent):
@@ -640,11 +634,15 @@
     back_places = jnp.bitwise_xor(fixed, jnp.arange(size, dtype=jnp.int32))
     outs = project(x_both, weight, places, slots)
 
-    def stage(keep, got):
-        mid = keep.shape[0] // 2
-        return keep[mid:] + got[mid:], keep[:mid] + got[:mid]
-
-    outs = [pack(keep, exchange(after(send, by_both, side_pair), 0)) for send, keep in outs]
+    narrow = [(1, 2), (1, bits - 1)]
+
+    def merged(n, outs, gots):
+        return [
+            merge(keep, got, n in marks, n + 1 in marks)
+            for (_, keep), got, marks in zip(outs, gots, narrow)
+        ]
+
+    outs = merged(0, outs, [exchange(after(send, by_both, side_pair), 0) for send, _ in outs])
     gots = [exchange(send, order_[1]) for (send, _), order_ in zip(outs, stages)]
     side_last = after(side_last, *[send for send, _ in outs])
     pieces = jnp.concatenate(
@@ -678,15 +676,16 @@
         compiler_params=params,
         name="gradients",
     )(inverse, high, grad_cols, grad_other, x_other, tokens, xs, near, bfar, inv_far, inv)
-    outs = [unpack(keep, got) for (_, keep), got in zip(outs, gots)]
+    outs = merged(1, outs, gots)
     for n in range(2, bits - 1):
         gots = [exchange(send, order_[n]) for (send, _), order_ in zip(outs, stages)]
-        merge = pack if n == bits - 2 else stage
-        outs = [merge(keep, got) for (_, keep), got in zip(outs, gots)]
+        if n == 2:
+            gots[0] = after(gots[0], grad_other)
+        outs = merged(n, outs, gots)
     lasts = [exchange(send, bits - 1).astype(f32) for send, _ in outs]
     lasts[-1] = after(lasts[-1], grad_tokens, grad_gens)
     outputs = pl.pallas_call(
-        last_kernel,
+        functools.partial(last_kernel, [bits - 1 in marks for marks in narrow]),
         out_shape=jax.ShapeDtypeStruct((count, cotangent.shape[1]), f32),
         in_specs=[full] * (2 * CHUNKS),
         out_specs=full,

time: 102 us -> 102 us (level)
  local copies, waits for them, and re-layouts: 7.99 us -> 4.28 us
  waiting for transfers between devices: 24.6 us -> 27.8 us
    unnamed x34 -> x22, local copies, waits for them, and re-layouts: 6.41 us -> 2.69 us
    ppermute x18, waiting for transfers between devices: 24.6 us -> 27.8 us  [exchange(): lax.ppermute(array, 'tensor', [(i, i ^ 1 << bit) for i in range(size)])]
    ppermute x18, starting transfers between devices: 18.8 us -> 19.8 us  [exchange(): lax.ppermute(array, 'tensor', [(i, i ^ 1 << bit) for i in range(size)])]
    concatenate x1, other arithmetic: 1.08 us -> 0.05 us  [local(): side_pair = exchange(jnp.concatenate([by_far, by_mid], axis=0), order[-2])]
  transfers between devices with their start and end apart: 18 -> 18, of which waited for: 8 -> 9; matrix products, arithmetic and copies ran while one was open for 4% -> 2% of each run, Pallas kernels for 46% -> 46%
where the time goes in v12:
time: 102 us
  Pallas kernels  48 us (47%)
  waiting for transfers between devices  27.8 us (27%)
  starting transfers between devices  19.8 us (19%)
  local copies, waits for them, and re-layouts  4.28 us (4%)
    ppermute x18, waiting for transfers between devices, exchange(): lax.ppermute(array, 'tensor', [(i, i ^ 1 << bit) for i in range(size)])  27.8 us
    ppermute x18, starting transfers between devices, exchange(): lax.ppermute(array, 'tensor', [(i, i ^ 1 << bit) for i in range(size)])  19.8 us
    pallas_call x1, Pallas kernels, local(): pl.pallas_call(grads_kernel, out_shape=(jax.ShapeDtypeStruct((count, rows...  12.8 us
    pallas_call x1, Pallas kernels, project(): pl.pallas_call(functools.partial(project_kernel, slots), out_shape=(jax.S...  10.4 us
    pallas_call x1, Pallas kernels, project_back(): pl.pallas_call(functools.partial(back_kernel, order), out_shape=(jax.Shap...  8.39 us
    pallas_call x1, Pallas kernels, local(): pl.pallas_call(near_kernel, out_shape=(jax.ShapeDtypeStruct(square, f32),...  7.59 us
    pallas_call x1, Pallas kernels, local(): pl.pallas_call(far_rotations_kernel, out_shape=(jax.ShapeDtypeStruct(far_...  5.28 us
    unnamed x22, local copies, waits for them, and re-layouts  2.69 us
  transfers between devices with their start and end apart: 18, of which 9 were waited for; matrix products, arithmetic and copies ran while one was open for 2% of the time, Pallas kernels for 46%

profile of v12, /device:TPU:0, one launch (start us, length us, event | category | flops | bytes accessed | tf_op | source)
XLA Modules:
  0.0 101.6 jit_solution(11074306537153362430)
XLA Ops:
  0.6 3.0 %collective-permute-start.2 = (bf16[1,128,1024]{2,1,0:T(8,128)(2,1)}, bf16[1,128,1024]{2,1,0:T(8,128)(2,1)S(1)}, u32[]{:S(2)}, u32[]{:S(2)}) collective-permute-start(bf16[1,128,1024]{2,1,0:T(8,128)(2,1)} %bitcast.15), channel_id=1, source_target_pairs={{0,2},{1,3},{2,0},{3,1},{4,6},{5,7},{6,4},{7,5},{8,10},{9,11},{10,... | collective-permute-start | bytes 786440 | tf_op jit(solution)/shard_map/ppermute | solution.py:22
  3.7 2.6 %collective-permute-start.3 = (bf16[1,128,1024]{2,1,0:T(8,128)(2,1)}, bf16[1,128,1024]{2,1,0:T(8,128)(2,1)S(1)}, u32[]{:S(2)}, u32[]{:S(2)}) collective-permute-start(bf16[1,128,1024]{2,1,0:T(8,128)(2,1)} %bitcast.16), channel_id=1, source_target_pairs={{0,8},{1,9},{2,10},{3,11},{4,12},{5,13},{6,14},{7,15},{8,0},{9,1},... | collective-permute-start | bytes 786440 | tf_op jit(solution)/shard_map/ppermute | solution.py:22
  6.3 1.6 %collective-permute-start.5 = (bf16[1,128,1024]{2,1,0:T(8,128)(2,1)}, bf16[1,128,1024]{2,1,0:T(8,128)(2,1)S(1)}, u32[]{:S(2)}, u32[]{:S(2)}) collective-permute-start(bf16[1,128,1024]{2,1,0:T(8,128)(2,1)} %bitcast.17), channel_id=1, source_target_pairs={{0,4},{1,5},{2,6},{3,7},{4,0},{5,1},{6,2},{7,3},{8,12},{9,13},{10,... | collective-permute-start | bytes 786440 | tf_op jit(solution)/shard_map/ppermute | solution.py:22
  7.8 0.8 slice_bitcast_fusion.1.own_ref
  8.7 0.3 collective-permute-start.1
  9.0 0.9 copy-done.1
  9.9 0.9 copy-done.3
  10.9 0.7 copy-done.4
  11.6 7.6 %near_rotations.1 = (f32[1024,128]{1,0:T(8,128)S(1)}, f32[3,512,128]{2,1,0:T(8,128)S(1)}, f32[3,128,512]{2,1,0:T(8,128)S(1)}) custom-call(s32[4,32]{1,0:T(4,128)S(1)} %copy-done.4, f32[128,512]{1,0:T(8,128)S(1)} %bitcast.14, bf16[128,512]{1,0:T(8,128)(2,1)S(1)} %copy-done.1), custom_call_target="tpu_custom_call" | custom-call | tf_op jit(solution)/shard_map/near_rotations/pallas_call | solution.py:569
  19.2 0.7 slice_bitcast_fusion
  19.9 2.6 %collective-permute-start = (f32[128,512]{1,0:T(8,128)}, f32[128,512]{1,0:T(8,128)S(1)}, u32[]{:S(2)}, u32[]{:S(2)}) collective-permute-start(f32[128,512]{1,0:T(8,128)} %slice_bitcast_fusion), channel_id=1, source_target_pairs={{0,8},{1,9},{2,10},{3,11},{4,12},{5,13},{6,14},{7,15},{8,0},{9,1},... | collective-permute-start | bytes 786440 | tf_op jit(solution)/shard_map/ppermute | solution.py:22
  22.5 5.3 %far_rotations.1 = (f32[1024,32]{1,0:T(8,128)S(1)}, f32[2,512,128]{2,1,0:T(8,128)S(1)}, f32[2,512,128]{2,1,0:T(8,128)S(1)}) custom-call(s32[1,32]{1,0:T(1,128)S(1)} %slice.11.orders_ref, s32[1]{0:T(128)} %bitcast.3.high_ref, f32[32,512]{1,0:T(8,128)S(1)} %slice_bitcast_fusion.1.own_ref, f32[32,512]{1,0:T(8,128)S(1)} %collective-permute-done.1.far_ref), custom_call_target="tpu_custom_call" | custom-call | flops 10000000 | bytes 10000000 | tf_op jit(solution)/shard_map/far_rotations/pallas_call | solution.py:591
  27.9 0.6 collective-permute-start.6
  28.4 0.5 collective-permute-start.4
  28.9 4.6 %collective-permute-done.oth_ref.x_oth_ref = f32[128,512]{1,0:T(8,128)S(1)} collective-permute-done((f32[128,512]{1,0:T(8,128)}, f32[128,512]{1,0:T(8,128)S(1)}, u32[]{:S(2)}, u32[]{:S(2)}) %collective-permute-start) | collective-permute-done | bytes 262176 | tf_op jit(solution)/shard_map/ppermute | solution.py:22
  33.5 0.4 far_apply.1.x_ref
  33.9 10.4 %project.1 = (f32[8,128,512]{2,1,0:T(8,128)S(1)}, f32[8,128,512]{2,1,0:T(8,128)S(1)}, f32[8,128,512]{2,1,0:T(8,128)S(1)}, f32[8,128,512]{2,1,0:T(8,128)}) custom-call(s32[16]{0:T(128)S(1)} %broadcast_xor_fusion.places_ref, bf16[256,512]{1,0:T(8,128)(2,1)S(1)} %far_apply.1.x_ref, bf16[512,16384]{1,0:T(8,128)(2,1)} %w_ref.3), custom_call_target="tpu_custom_call" | custom-call | flops 4294967296 | bytes 25165824 | tf_op jit(solution)/shard_map/project/pallas_call | solution.py:318
  44.4 0.1 collective-permute-start.10
  44.4 0.5 collective-permute-start.7
  45.0 0.5 collective-permute-start.9
  45.6 3.0 %collective-permute-done.10.got_ref = f32[8,128,512]{2,1,0:T(8,128)S(1)} collective-permute-done((f32[8,128,512]{2,1,0:T(8,128)S(1)}, f32[8,128,512]{2,1,0:T(8,128)S(1)}, u32[]{:S(2)}, u32[]{:S(2)}) %collective-permute-start.10) | collective-permute-done | bytes 2097184 | tf_op jit(solution)/shard_map/ppermute | solution.py:22
  48.6 0.6 merge.7
  49.2 0.1 convert_element_type.31
  49.3 2.3 %collective-permute-done.7.got_ref = f32[8,128,512]{2,1,0:T(8,128)S(1)} collective-permute-done((f32[8,128,512]{2,1,0:T(8,128)S(1)}, f32[8,128,512]{2,1,0:T(8,128)S(1)}, u32[]{:S(2)}, u32[]{:S(2)}) %collective-permute-start.7) | collective-permute-done | bytes 2097184 | tf_op jit(solution)/shard_map/ppermute | solution.py:22
  51.6 0.6 merge.6
  52.2 0.1 convert_element_type.30
  52.3 1.1 %collective-permute-done.9 = bf16[1,128,1024]{2,1,0:T(8,128)(2,1)S(1)} collective-permute-done((bf16[1,128,1024]{2,1,0:T(8,128)(2,1)S(1)}, bf16[1,128,1024]{2,1,0:T(8,128)(2,1)S(1)}, u32[]{:S(2)}, u32[]{:S(2)}) %collective-permute-start.9) | collective-permute-done | bytes 262176 | tf_op jit(solution)/shard_map/ppermute | solution.py:22
  53.6 0.5 collective-permute-start.8
  54.1 3.5 %collective-permute-done.11.high_ref = bf16[8,128,1024]{2,1,0:T(8,128)(2,1)S(1)} collective-permute-done((bf16[8,128,1024]{2,1,0:T(8,128)(2,1)S(1)}, bf16[8,128,1024]{2,1,0:T(8,128)(2,1)S(1)}, u32[]{:S(2)}, u32[]{:S(2)}) %collective-permute-start.11) | collective-permute-done | bytes 2097184 | tf_op jit(solution)/shard_map/ppermute | solution.py:22
  57.6 8.4 %project_back.1 = (f32[128,512]{1,0:T(8,128)S(1)}, f32[144,512]{1,0:T(8,128)S(1)}) custom-call(s32[16]{0:T(128)S(1)} %iota_xor_fusion.places_ref, bf16[8,128,1024]{2,1,0:T(8,128)(2,1)S(1)} %constant_dynamic-update-slice_fusion.low_ref, bf16[8,128,1024]{2,1,0:T(8,128)(2,1)S(1)} %collective-permute-done.11.high_ref, bf16[512,16384]{1,0:T(8,128)(2,1)} %w_ref.3), custom_call_target="tpu_custom_call" | custom-call | flops 2147483648 | bytes 20971520 | tf_op jit(solution)/shard_map/project_back/pallas_call | solution.py:376
  66.0 2.2 %collective-permute-done.14 = f16[528,512]{1,0:T(8,128)(2,1)S(1)} collective-permute-done((f16[528,512]{1,0:T(8,128)(2,1)S(1)}, f16[528,512]{1,0:T(8,128)(2,1)S(1)}, u32[]{:S(2)}, u32[]{:S(2)}) %collective-permute-start.14) | collective-permute-done | bytes 540704 | tf_op jit(solution)/shard_map/ppermute | solution.py:22
  68.2 0.1 convert_element_type.37.got_ref
  68.3 0.2 merge.10
  68.5 0.5 collective-permute-start.15
  69.1 0.1 convert_element_type.32.got_ref
  69.2 0.4 merge.8
  69.7 0.9 collective-permute-start.12
  70.6 2.4 %collective-permute-start.13 = (f16[144,512]{1,0:T(8,128)(2,1)S(1)}, f16[144,512]{1,0:T(8,128)(2,1)S(1)}, u32[]{:S(2)}, u32[]{:S(2)}) collective-permute-start(f16[144,512]{1,0:T(8,128)(2,1)S(1)} %convert_element_type.34), channel_id=1, source_target_pairs={{0,8},{1,9},{2,10},{3,11},{4,12},{5,13},{6,14},{7,15},{8,0},{9,1},... | collective-permute-start | bytes 442376 | tf_op jit(solution)/shard_map/ppermute | solution.py:22
  73.1 6.1 %collective-permute-done.13 = f16[144,512]{1,0:T(8,128)(2,1)S(1)} collective-permute-done((f16[144,512]{1,0:T(8,128)(2,1)S(1)}, f16[144,512]{1,0:T(8,128)(2,1)S(1)}, u32[]{:S(2)}, u32[]{:S(2)}) %collective-permute-start.13) | collective-permute-done | bytes 147488 | tf_op jit(solution)/shard_map/ppermute | solution.py:22
  79.2 1.6 %collective-permute-done.12 = f16[272,512]{1,0:T(8,128)(2,1)S(1)} collective-permute-done((f16[272,512]{1,0:T(8,128)(2,1)S(1)}, f16[272,512]{1,0:T(8,128)(2,1)S(1)}, u32[]{:S(2)}, u32[]{:S(2)}) %collective-permute-start.12) | collective-permute-done | bytes 278560 | tf_op jit(solution)/shard_map/ppermute | solution.py:22
  80.9 0.1 merge.9
  81.1 1.8 %collective-permute-start.16 = (f32[1,128,512]{2,1,0:T(8,128)S(1)}, f32[1,128,512]{2,1,0:T(8,128)S(1)}, u32[]{:S(2)}, u32[]{:S(2)}) collective-permute-start(f32[1,128,512]{2,1,0:T(8,128)S(1)} %get-tuple-element.72), channel_id=1, source_target_pairs={{0,8},{1,9},{2,10},{3,11},{4,12},{5,13},{6,14},{7,15},{8,0},{9,1},... | collective-permute-start | bytes 786440 | tf_op jit(solution)/shard_map/ppermute | solution.py:22
  82.9 0.2 merge.11
  83.2 1.2 %collective-permute-start.17 = (f16[144,512]{1,0:T(8,128)(2,1)S(1)}, f16[144,512]{1,0:T(8,128)(2,1)S(1)}, u32[]{:S(2)}, u32[]{:S(2)}) collective-permute-start(f16[144,512]{1,0:T(8,128)(2,1)S(1)} %convert_element_type.38), channel_id=1, source_target_pairs={{0,8},{1,9},{2,10},{3,11},{4,12},{5,13},{6,14},{7,15},{8,0},{9,1},... | collective-permute-start | bytes 442376 | tf_op jit(solution)/shard_map/ppermute | solution.py:22
  84.4 0.1 select_reduce_fusion.inverse_ref
  84.5 12.8 %gradients.1 = (f32[128,512]{1,0:T(8,128)}, f32[128,512]{1,0:T(8,128)}) custom-call(s32[4,32]{1,0:T(4,128)S(1)} %select_reduce_fusion.inverse_ref, s32[1]{0:T(128)} %bitcast.3.high_ref, f32[128,512]{1,0:T(8,128)S(1)} %get-tuple-element.60.own_ref, f32[144,512]{1,0:T(8,128)S(1)} %convert_element_type.35.oth_ref, ...), custom_call_target="tpu_custom_call" | custom-call | tf_op jit(solution)/shard_map/gradients/pallas_call | solution.py:660
  97.3 3.3 %collective-permute-done.17 = f16[144,512]{1,0:T(8,128)(2,1)S(1)} collective-permute-done((f16[144,512]{1,0:T(8,128)(2,1)S(1)}, f16[144,512]{1,0:T(8,128)(2,1)S(1)}, u32[]{:S(2)}, u32[]{:S(2)}) %collective-permute-start.17) | collective-permute-done | bytes 147488 | tf_op jit(solution)/shard_map/ppermute | solution.py:22
  100.7 0.9 last_sums.1
  (41 shorter events, 0.6 us)
Async XLA Ops:
  0.6 27.8 %copy-start.7 = (s32[16]{0:T(128)S(1)}, s32[16]{0:T(128)}, u32[]{:S(2)}) copy-start(s32[16]{0:T(128)} %constant.12.clone) | copy-start | bytes 196
  0.6 21.8 %collective-permute-start.2 = (bf16[1,128,1024]{2,1,0:T(8,128)(2,1)}, bf16[1,128,1024]{2,1,0:T(8,128)(2,1)S(1)}, u32[]{:S(2)}, u32[]{:S(2)}) collective-permute-start(bf16[1,128,1024]{2,1,0:T(8,128)(2,1)} %bitcast.15), channel_id=1, source_target_pairs={{0,2},{1,3},{2,0},{3,1},{4,6},{5,7},{6,4},{7,5},{8,10},{9,11},{10,... | collective-permute-start | bytes 786440 | tf_op jit(solution)/shard_map/ppermute | solution.py:22
  3.7 18.8 %collective-permute-start.3 = (bf16[1,128,1024]{2,1,0:T(8,128)(2,1)}, bf16[1,128,1024]{2,1,0:T(8,128)(2,1)S(1)}, u32[]{:S(2)}, u32[]{:S(2)}) collective-permute-start(bf16[1,128,1024]{2,1,0:T(8,128)(2,1)} %bitcast.16), channel_id=1, source_target_pairs={{0,8},{1,9},{2,10},{3,11},{4,12},{5,13},{6,14},{7,15},{8,0},{9,1},... | collective-permute-start | bytes 786440 | tf_op jit(solution)/shard_map/ppermute | solution.py:22
  6.3 21.5 %collective-permute-start.5 = (bf16[1,128,1024]{2,1,0:T(8,128)(2,1)}, bf16[1,128,1024]{2,1,0:T(8,128)(2,1)S(1)}, u32[]{:S(2)}, u32[]{:S(2)}) collective-permute-start(bf16[1,128,1024]{2,1,0:T(8,128)(2,1)} %bitcast.17), channel_id=1, source_target_pairs={{0,4},{1,5},{2,6},{3,7},{4,0},{5,1},{6,2},{7,3},{8,12},{9,13},{10,... | collective-permute-start | bytes 786440 | tf_op jit(solution)/shard_map/ppermute | solution.py:22
  8.7 13.8 %collective-permute-start.1 = (f32[32,512]{1,0:T(8,128)S(1)}, f32[32,512]{1,0:T(8,128)S(1)}, u32[]{:S(2)}, u32[]{:S(2)}) collective-permute-start(f32[32,512]{1,0:T(8,128)S(1)} %slice_bitcast_fusion.1.own_ref), channel_id=1, source_target_pairs={{0,8},{1,9},{2,10},{3,11},{4,12},{5,13},{6,14},{7,15},{8,0},{9,1},... | collective-permute-start | bytes 196616 | tf_op jit(solution)/shard_map/ppermute | solution.py:22
  9.0 0.9 copy-start.1
  9.9 0.9 copy-start.3
  10.9 0.7 copy-start.4
  19.9 13.6 %collective-permute-start = (f32[128,512]{1,0:T(8,128)}, f32[128,512]{1,0:T(8,128)S(1)}, u32[]{:S(2)}, u32[]{:S(2)}) collective-permute-start(f32[128,512]{1,0:T(8,128)} %slice_bitcast_fusion), channel_id=1, source_target_pairs={{0,8},{1,9},{2,10},{3,11},{4,12},{5,13},{6,14},{7,15},{8,0},{9,1},... | collective-permute-start | bytes 786440 | tf_op jit(solution)/shard_map/ppermute | solution.py:22
  27.9 16.5 %collective-permute-start.6 = (bf16[2,128,1024]{2,1,0:T(8,128)(2,1)S(1)}, bf16[2,128,1024]{2,1,0:T(8,128)(2,1)S(1)}, u32[]{:S(2)}, u32[]{:S(2)}) collective-permute-start(bf16[2,128,1024]{2,1,0:T(8,128)(2,1)S(1)} %pad_maximum_fusion), channel_id=1, source_target_pairs={{0,2},{1,3},{2,0},{3,1},{4,6},{5,7},{6,4},{7,5},{8,10},{9,11},{10,... | collective-permute-start | bytes 1572872 | tf_op jit(solution)/shard_map/ppermute | solution.py:22
  28.4 15.9 %collective-permute-start.4 = (bf16[1,128,1024]{2,1,0:T(8,128)(2,1)S(1)}, bf16[1,128,1024]{2,1,0:T(8,128)(2,1)S(1)}, u32[]{:S(2)}, u32[]{:S(2)}) collective-permute-start(bf16[1,128,1024]{2,1,0:T(8,128)(2,1)S(1)} %collective-permute-done.3), channel_id=1, source_target_pairs={{0,4},{1,5},{2,6},{3,7},{4,0},{5,1},{6,2},{7,3},{8,12},{9,13},{10,... | collective-permute-start | bytes 786440 | tf_op jit(solution)/shard_map/ppermute | solution.py:22
  33.9 11.0 %copy-start.6 = (bf16[128,1024]{1,0:T(8,128)(2,1)S(1)}, bf16[128,1024]{1,0:T(8,128)(2,1)}, u32[]{:S(2)}) copy-start(bf16[128,1024]{1,0:T(8,128)(2,1)} %param.10) | copy-start | bytes 786436
  44.3 4.3 %copy-start = (f32[8,128,512]{2,1,0:T(8,128)S(1)}, f32[8,128,512]{2,1,0:T(8,128)}, u32[]{:S(2)}) copy-start(f32[8,128,512]{2,1,0:T(8,128)} %get-tuple-element.55.keep_ref) | copy-start | bytes 6291460
  44.4 4.2 %collective-permute-start.10 = (f32[8,128,512]{2,1,0:T(8,128)S(1)}, f32[8,128,512]{2,1,0:T(8,128)S(1)}, u32[]{:S(2)}, u32[]{:S(2)}) collective-permute-start(f32[8,128,512]{2,1,0:T(8,128)S(1)} %get-tuple-element.57), channel_id=1, source_target_pairs={{0,1},{1,0},{2,3},{3,2},{4,5},{5,4},{6,7},{7,6},{8,9},{9,8},{10,11... | collective-permute-start | bytes 6291464 | tf_op jit(solution)/shard_map/ppermute | solution.py:22
  44.4 7.1 %collective-permute-start.7 = (f32[8,128,512]{2,1,0:T(8,128)S(1)}, f32[8,128,512]{2,1,0:T(8,128)S(1)}, u32[]{:S(2)}, u32[]{:S(2)}) collective-permute-start(f32[8,128,512]{2,1,0:T(8,128)S(1)} %get-tuple-element.52), channel_id=1, source_target_pairs={{0,1},{1,0},{2,3},{3,2},{4,5},{5,4},{6,7},{7,6},{8,9},{9,8},{10,11... | collective-permute-start | bytes 6291464 | tf_op jit(solution)/shard_map/ppermute | solution.py:22
  45.0 8.4 %collective-permute-start.9 = (bf16[1,128,1024]{2,1,0:T(8,128)(2,1)S(1)}, bf16[1,128,1024]{2,1,0:T(8,128)(2,1)S(1)}, u32[]{:S(2)}, u32[]{:S(2)}) collective-permute-start(bf16[1,128,1024]{2,1,0:T(8,128)(2,1)S(1)} %collective-permute-done.4), channel_id=1, source_target_pairs={{0,2},{1,3},{2,0},{3,1},{4,6},{5,7},{6,4},{7,5},{8,10},{9,11},{10,... | collective-permute-start | bytes 786440 | tf_op jit(solution)/shard_map/ppermute | solution.py:22
  53.4 4.2 %collective-permute-start.11 = (bf16[8,128,1024]{2,1,0:T(8,128)(2,1)S(1)}, bf16[8,128,1024]{2,1,0:T(8,128)(2,1)S(1)}, u32[]{:S(2)}, u32[]{:S(2)}) collective-permute-start(bf16[8,128,1024]{2,1,0:T(8,128)(2,1)S(1)} %constant_dynamic-update-slice_fusion.low_ref), channel_id=1, source_target_pairs={{0,1},{1,0},{2,3},{3,2},{4,5},{5,4},{6,7},{7,6},{8,9},{9,8},{10,11... | collective-permute-start | bytes 6291464 | tf_op jit(solution)/shard_map/ppermute | solution.py:22
  53.5 14.7 %collective-permute-start.14 = (f16[528,512]{1,0:T(8,128)(2,1)S(1)}, f16[528,512]{1,0:T(8,128)(2,1)S(1)}, u32[]{:S(2)}, u32[]{:S(2)}) collective-permute-start(f16[528,512]{1,0:T(8,128)(2,1)S(1)} %convert_element_type.31), channel_id=1, source_target_pairs={{0,4},{1,5},{2,6},{3,7},{4,0},{5,1},{6,2},{7,3},{8,12},{9,13},{10,... | collective-permute-start | bytes 1622024 | tf_op jit(solution)/shard_map/ppermute | solution.py:22
  53.6 15.5 %collective-permute-start.8 = (f16[528,512]{1,0:T(8,128)(2,1)S(1)}, f16[528,512]{1,0:T(8,128)(2,1)S(1)}, u32[]{:S(2)}, u32[]{:S(2)}) collective-permute-start(f16[528,512]{1,0:T(8,128)(2,1)S(1)} %convert_element_type.30), channel_id=1, source_target_pairs={{0,2},{1,3},{2,0},{3,1},{4,6},{5,7},{6,4},{7,5},{8,10},{9,11},{10,... | collective-permute-start | bytes 1622024 | tf_op jit(solution)/shard_map/ppermute | solution.py:22
  68.5 14.4 %collective-permute-start.15 = (f32[2,128,512]{2,1,0:T(8,128)S(1)}, f32[2,128,512]{2,1,0:T(8,128)S(1)}, u32[]{:S(2)}, u32[]{:S(2)}) collective-permute-start(f32[2,128,512]{2,1,0:T(8,128)S(1)} %get-tuple-element.70), channel_id=1, source_target_pairs={{0,2},{1,3},{2,0},{3,1},{4,6},{5,7},{6,4},{7,5},{8,10},{9,11},{10,... | collective-permute-start | bytes 1572872 | tf_op jit(solution)/shard_map/ppermute | solution.py:22
  69.7 11.2 %collective-permute-start.12 = (f16[272,512]{1,0:T(8,128)(2,1)S(1)}, f16[272,512]{1,0:T(8,128)(2,1)S(1)}, u32[]{:S(2)}, u32[]{:S(2)}) collective-permute-start(f16[272,512]{1,0:T(8,128)(2,1)S(1)} %convert_element_type.33), channel_id=1, source_target_pairs={{0,4},{1,5},{2,6},{3,7},{4,0},{5,1},{6,2},{7,3},{8,12},{9,13},{10,... | collective-permute-start | bytes 835592 | tf_op jit(solution)/shard_map/ppermute | solution.py:22
  70.6 13.8 %copy-start.5 = (s32[4,32]{1,0:T(4,128)S(1)}, s32[4,32]{1,0:T(4,128)}, u32[]{:S(2)}) copy-start(s32[4,32]{1,0:T(4,128)} %orders_ref.1) | copy-start | bytes 1540
  70.6 13.9 %copy-start.2 = (bf16[128,512]{1,0:T(8,128)(2,1)S(1)}, bf16[128,512]{1,0:T(8,128)(2,1)}, u32[]{:S(2)}) copy-start(bf16[128,512]{1,0:T(8,128)(2,1)} %tok_ref.3) | copy-start | bytes 393220
  70.6 8.5 %collective-permute-start.13 = (f16[144,512]{1,0:T(8,128)(2,1)S(1)}, f16[144,512]{1,0:T(8,128)(2,1)S(1)}, u32[]{:S(2)}, u32[]{:S(2)}) collective-permute-start(f16[144,512]{1,0:T(8,128)(2,1)S(1)} %convert_element_type.34), channel_id=1, source_target_pairs={{0,8},{1,9},{2,10},{3,11},{4,12},{5,13},{6,14},{7,15},{8,0},{9,1},... | collective-permute-start | bytes 442376 | tf_op jit(solution)/shard_map/ppermute | solution.py:22
  81.1 19.6 %collective-permute-start.16 = (f32[1,128,512]{2,1,0:T(8,128)S(1)}, f32[1,128,512]{2,1,0:T(8,128)S(1)}, u32[]{:S(2)}, u32[]{:S(2)}) collective-permute-start(f32[1,128,512]{2,1,0:T(8,128)S(1)} %get-tuple-element.72), channel_id=1, source_target_pairs={{0,8},{1,9},{2,10},{3,11},{4,12},{5,13},{6,14},{7,15},{8,0},{9,1},... | collective-permute-start | bytes 786440 | tf_op jit(solution)/shard_map/ppermute | solution.py:22
  83.2 17.5 %collective-permute-start.17 = (f16[144,512]{1,0:T(8,128)(2,1)S(1)}, f16[144,512]{1,0:T(8,128)(2,1)S(1)}, u32[]{:S(2)}, u32[]{:S(2)}) collective-permute-start(f16[144,512]{1,0:T(8,128)(2,1)S(1)} %convert_element_type.38), channel_id=1, source_target_pairs={{0,8},{1,9},{2,10},{3,11},{4,12},{5,13},{6,14},{7,15},{8,0},{9,1},... | collective-permute-start | bytes 442376 | tf_op jit(solution)/shard_map/ppermute | solution.py:22

commit v13 on v12

--- a/solution.py
+++ b/solution.py
@@ -281,33 +281,26 @@
 
 
 def project_kernel(slots, places_ref, x_ref, w_ref, *refs):
-    *out_refs, held_ref, made_ref, sems, out_sems = refs
-    pieces, count, width = made_ref.shape
+    *out_refs, held_ref, sems = refs
+    pieces, _, width = held_ref.shape
+    count = x_ref.shape[0] // 2
     half = pieces // 2
     part = width // CHUNKS
 
     def fetch(p):
         at = pl.multiple_of(places_ref[p] * width, width)
         return pltpu.make_async_copy(w_ref.at[:, pl.ds(at, width)], held_ref.at[p], sems.at[p])
-
-    def leave(p, chunk):
-        return pltpu.make_async_copy(
-            made_ref.at[p, :, pl.ds(chunk * part, part)],
-            out_refs[2 * chunk + p // half].at[slots[chunk][p]],
-            out_sems.at[chunk, p],
-        )
 
     for p in range(pieces):
         fetch(p).start()
     for p in range(pieces):
         fetch(p).wait()
         both = one_dot(x_ref[...], held_ref[p])
-        made_ref[p] = both[:count] + both[count:]
+        total = both[:count] + both[count:]
         for chunk in range(CHUNKS):
-            leave(p, chunk).start()
-    for p in range(pieces):
-        for chunk in range(CHUNKS):
-            leave(p, chunk).wait()
+            out_refs[2 * chunk + p // half][slots[chunk][p]] = total[
+                :, chunk * part : (chunk + 1) * part
+            ]
 
 
 def project(x_both, weight, places, slots):
@@ -324,12 +317,10 @@
             pl.BlockSpec(memory_space=pltpu.VMEM),
             pl.BlockSpec(memory_space=pl.ANY),
         ],
-        out_specs=(pl.BlockSpec(memory_space=pl.ANY),) * (2 * CHUNKS),
+        out_specs=(pl.BlockSpec(memory_space=pltpu.VMEM),) * (2 * CHUNKS),
         scratch_shapes=[
             pltpu.VMEM((pieces, rows, width), weight.dtype),
-            pltpu.VMEM((pieces, count, width), jnp.float32),
             pltpu.SemaphoreType.DMA((pieces,)),
-            pltpu.SemaphoreType.DMA((CHUNKS, pieces)),
         ],
         compiler_params=pltpu.CompilerParams(vmem_limit_bytes=WIDE_LIMIT),
         cost_estimate=pl.CostEstimate(

time: 102 us -> 102 us (level)
  no operation moved by 1% of the time
where the time goes in v13:
time: 102 us
  Pallas kernels  47.9 us (47%)
  waiting for transfers between devices  27.8 us (27%)
  starting transfers between devices  19.8 us (19%)
  local copies, waits for them, and re-layouts  4.28 us (4%)
    ppermute x18, waiting for transfers between devices, exchange(): lax.ppermute(array, 'tensor', [(i, i ^ 1 << bit) for i in range(size)])  27.8 us
    ppermute x18, starting transfers between devices, exchange(): lax.ppermute(array, 'tensor', [(i, i ^ 1 << bit) for i in range(size)])  19.8 us
    pallas_call x1, Pallas kernels, local(): pl.pallas_call(grads_kernel, out_shape=(jax.ShapeDtypeStruct((count, rows...  12.8 us
    pallas_call x1, Pallas kernels, project(): pl.pallas_call(functools.partial(project_kernel, slots), out_shape=(jax.S...  10.3 us
    pallas_call x1, Pallas kernels, project_back(): pl.pallas_call(functools.partial(back_kernel, order), out_shape=(jax.Shap...  8.39 us
    pallas_call x1, Pallas kernels, local(): pl.pallas_call(near_kernel, out_shape=(jax.ShapeDtypeStruct(square, f32),...  7.59 us
    pallas_call x1, Pallas kernels, local(): pl.pallas_call(far_rotations_kernel, out_shape=(jax.ShapeDtypeStruct(far_...  5.29 us
    unnamed x22, local copies, waits for them, and re-layouts  2.69 us
  transfers between devices with their start and end apart: 18, of which 9 were waited for; matrix products, arithmetic and copies ran while one was open for 2% of the time, Pallas kernels for 46%

profile of v13, /device:TPU:0, one launch (start us, length us, event | category | flops | bytes accessed | tf_op | source)
XLA Modules:
  0.0 101.5 jit_solution(9142533961521059742)
XLA Ops:
  0.6 3.0 %collective-permute-start.2 = (bf16[1,128,1024]{2,1,0:T(8,128)(2,1)}, bf16[1,128,1024]{2,1,0:T(8,128)(2,1)S(1)}, u32[]{:S(2)}, u32[]{:S(2)}) collective-permute-start(bf16[1,128,1024]{2,1,0:T(8,128)(2,1)} %bitcast.15), channel_id=1, source_target_pairs={{0,2},{1,3},{2,0},{3,1},{4,6},{5,7},{6,4},{7,5},{8,10},{9,11},{10,... | collective-permute-start | bytes 786440 | tf_op jit(solution)/shard_map/ppermute | solution.py:22
  3.7 2.6 %collective-permute-start.3 = (bf16[1,128,1024]{2,1,0:T(8,128)(2,1)}, bf16[1,128,1024]{2,1,0:T(8,128)(2,1)S(1)}, u32[]{:S(2)}, u32[]{:S(2)}) collective-permute-start(bf16[1,128,1024]{2,1,0:T(8,128)(2,1)} %bitcast.16), channel_id=1, source_target_pairs={{0,8},{1,9},{2,10},{3,11},{4,12},{5,13},{6,14},{7,15},{8,0},{9,1},... | collective-permute-start | bytes 786440 | tf_op jit(solution)/shard_map/ppermute | solution.py:22
  6.3 1.6 %collective-permute-start.5 = (bf16[1,128,1024]{2,1,0:T(8,128)(2,1)}, bf16[1,128,1024]{2,1,0:T(8,128)(2,1)S(1)}, u32[]{:S(2)}, u32[]{:S(2)}) collective-permute-start(bf16[1,128,1024]{2,1,0:T(8,128)(2,1)} %bitcast.17), channel_id=1, source_target_pairs={{0,4},{1,5},{2,6},{3,7},{4,0},{5,1},{6,2},{7,3},{8,12},{9,13},{10,... | collective-permute-start | bytes 786440 | tf_op jit(solution)/shard_map/ppermute | solution.py:22
  7.8 0.8 slice_bitcast_fusion.1.own_ref
  8.7 0.3 collective-permute-start.1
  9.0 0.9 copy-done.1
  9.9 0.9 copy-done.3
  10.9 0.7 copy-done.4
  11.6 7.6 %near_rotations.1 = (f32[1024,128]{1,0:T(8,128)S(1)}, f32[3,512,128]{2,1,0:T(8,128)S(1)}, f32[3,128,512]{2,1,0:T(8,128)S(1)}) custom-call(s32[4,32]{1,0:T(4,128)S(1)} %copy-done.4, f32[128,512]{1,0:T(8,128)S(1)} %bitcast.14, bf16[128,512]{1,0:T(8,128)(2,1)S(1)} %copy-done.1), custom_call_target="tpu_custom_call" | custom-call | tf_op jit(solution)/shard_map/near_rotations/pallas_call | solution.py:560
  19.2 0.7 slice_bitcast_fusion
  19.9 2.6 %collective-permute-start = (f32[128,512]{1,0:T(8,128)}, f32[128,512]{1,0:T(8,128)S(1)}, u32[]{:S(2)}, u32[]{:S(2)}) collective-permute-start(f32[128,512]{1,0:T(8,128)} %slice_bitcast_fusion), channel_id=1, source_target_pairs={{0,8},{1,9},{2,10},{3,11},{4,12},{5,13},{6,14},{7,15},{8,0},{9,1},... | collective-permute-start | bytes 786440 | tf_op jit(solution)/shard_map/ppermute | solution.py:22
  22.5 5.3 %far_rotations.1 = (f32[1024,32]{1,0:T(8,128)S(1)}, f32[2,512,128]{2,1,0:T(8,128)S(1)}, f32[2,512,128]{2,1,0:T(8,128)S(1)}) custom-call(s32[1,32]{1,0:T(1,128)S(1)} %slice.11.orders_ref, s32[1]{0:T(128)} %bitcast.3.high_ref, f32[32,512]{1,0:T(8,128)S(1)} %slice_bitcast_fusion.1.own_ref, f32[32,512]{1,0:T(8,128)S(1)} %collective-permute-done.1.far_ref), custom_call_target="tpu_custom_call" | custom-call | flops 10000000 | bytes 10000000 | tf_op jit(solution)/shard_map/far_rotations/pallas_call | solution.py:582
  27.9 0.6 collective-permute-start.6
  28.4 0.5 collective-permute-start.4
  28.9 4.6 %collective-permute-done.oth_ref.x_oth_ref = f32[128,512]{1,0:T(8,128)S(1)} collective-permute-done((f32[128,512]{1,0:T(8,128)}, f32[128,512]{1,0:T(8,128)S(1)}, u32[]{:S(2)}, u32[]{:S(2)}) %collective-permute-start) | collective-permute-done | bytes 262176 | tf_op jit(solution)/shard_map/ppermute | solution.py:22
  33.5 0.4 far_apply.1.x_ref
  33.9 10.3 %project.1 = (f32[8,128,512]{2,1,0:T(8,128)S(1)}, f32[8,128,512]{2,1,0:T(8,128)S(1)}, f32[8,128,512]{2,1,0:T(8,128)S(1)}, f32[8,128,512]{2,1,0:T(8,128)}) custom-call(s32[16]{0:T(128)S(1)} %broadcast_xor_fusion.places_ref, bf16[256,512]{1,0:T(8,128)(2,1)S(1)} %far_apply.1.x_ref, bf16[512,16384]{1,0:T(8,128)(2,1)} %w_ref.3), custom_call_target="tpu_custom_call" | custom-call | flops 4294967296 | bytes 25165824 | tf_op jit(solution)/shard_map/project/pallas_call | solution.py:311
  44.4 0.5 collective-permute-start.7
  44.9 0.5 collective-permute-start.9
  45.6 3.0 %collective-permute-done.10.got_ref = f32[8,128,512]{2,1,0:T(8,128)S(1)} collective-permute-done((f32[8,128,512]{2,1,0:T(8,128)S(1)}, f32[8,128,512]{2,1,0:T(8,128)S(1)}, u32[]{:S(2)}, u32[]{:S(2)}) %collective-permute-start.10) | collective-permute-done | bytes 2097184 | tf_op jit(solution)/shard_map/ppermute | solution.py:22
  48.5 0.6 merge.7
  49.1 0.1 convert_element_type.31
  49.2 2.3 %collective-permute-done.7.got_ref = f32[8,128,512]{2,1,0:T(8,128)S(1)} collective-permute-done((f32[8,128,512]{2,1,0:T(8,128)S(1)}, f32[8,128,512]{2,1,0:T(8,128)S(1)}, u32[]{:S(2)}, u32[]{:S(2)}) %collective-permute-start.7) | collective-permute-done | bytes 2097184 | tf_op jit(solution)/shard_map/ppermute | solution.py:22
  51.5 0.6 merge.6
  52.1 0.1 convert_element_type.30
  52.2 1.1 %collective-permute-done.9 = bf16[1,128,1024]{2,1,0:T(8,128)(2,1)S(1)} collective-permute-done((bf16[1,128,1024]{2,1,0:T(8,128)(2,1)S(1)}, bf16[1,128,1024]{2,1,0:T(8,128)(2,1)S(1)}, u32[]{:S(2)}, u32[]{:S(2)}) %collective-permute-start.9) | collective-permute-done | bytes 262176 | tf_op jit(solution)/shard_map/ppermute | solution.py:22
  53.4 0.1 collective-permute-start.14
  53.5 0.5 collective-permute-start.8
  54.0 3.5 %collective-permute-done.11.high_ref = bf16[8,128,1024]{2,1,0:T(8,128)(2,1)S(1)} collective-permute-done((bf16[8,128,1024]{2,1,0:T(8,128)(2,1)S(1)}, bf16[8,128,1024]{2,1,0:T(8,128)(2,1)S(1)}, u32[]{:S(2)}, u32[]{:S(2)}) %collective-permute-start.11) | collective-permute-done | bytes 2097184 | tf_op jit(solution)/shard_map/ppermute | solution.py:22
  57.5 8.4 %project_back.1 = (f32[128,512]{1,0:T(8,128)S(1)}, f32[144,512]{1,0:T(8,128)S(1)}) custom-call(s32[16]{0:T(128)S(1)} %iota_xor_fusion.places_ref, bf16[8,128,1024]{2,1,0:T(8,128)(2,1)S(1)} %constant_dynamic-update-slice_fusion.low_ref, bf16[8,128,1024]{2,1,0:T(8,128)(2,1)S(1)} %collective-permute-done.11.high_ref, bf16[512,16384]{1,0:T(8,128)(2,1)} %w_ref.3), custom_call_target="tpu_custom_call" | custom-call | flops 2147483648 | bytes 20971520 | tf_op jit(solution)/shard_map/project_back/pallas_call | solution.py:367
  65.9 2.1 %collective-permute-done.14 = f16[528,512]{1,0:T(8,128)(2,1)S(1)} collective-permute-done((f16[528,512]{1,0:T(8,128)(2,1)S(1)}, f16[528,512]{1,0:T(8,128)(2,1)S(1)}, u32[]{:S(2)}, u32[]{:S(2)}) %collective-permute-start.14) | collective-permute-done | bytes 540704 | tf_op jit(solution)/shard_map/ppermute | solution.py:22
  68.1 0.1 convert_element_type.37.got_ref
  68.2 0.2 merge.10
  68.5 0.5 collective-permute-start.15
  69.0 0.1 convert_element_type.32.got_ref
  69.1 0.4 merge.8
  69.6 0.9 collective-permute-start.12
  70.6 2.4 %collective-permute-start.13 = (f16[144,512]{1,0:T(8,128)(2,1)S(1)}, f16[144,512]{1,0:T(8,128)(2,1)S(1)}, u32[]{:S(2)}, u32[]{:S(2)}) collective-permute-start(f16[144,512]{1,0:T(8,128)(2,1)S(1)} %convert_element_type.34), channel_id=1, source_target_pairs={{0,8},{1,9},{2,10},{3,11},{4,12},{5,13},{6,14},{7,15},{8,0},{9,1},... | collective-permute-start | bytes 442376 | tf_op jit(solution)/shard_map/ppermute | solution.py:22
  73.0 6.1 %collective-permute-done.13 = f16[144,512]{1,0:T(8,128)(2,1)S(1)} collective-permute-done((f16[144,512]{1,0:T(8,128)(2,1)S(1)}, f16[144,512]{1,0:T(8,128)(2,1)S(1)}, u32[]{:S(2)}, u32[]{:S(2)}) %collective-permute-start.13) | collective-permute-done | bytes 147488 | tf_op jit(solution)/shard_map/ppermute | solution.py:22
  79.1 1.6 %collective-permute-done.12 = f16[272,512]{1,0:T(8,128)(2,1)S(1)} collective-permute-done((f16[272,512]{1,0:T(8,128)(2,1)S(1)}, f16[272,512]{1,0:T(8,128)(2,1)S(1)}, u32[]{:S(2)}, u32[]{:S(2)}) %collective-permute-start.12) | collective-permute-done | bytes 278560 | tf_op jit(solution)/shard_map/ppermute | solution.py:22
  80.9 0.1 merge.9
  81.0 1.8 %collective-permute-start.16 = (f32[1,128,512]{2,1,0:T(8,128)S(1)}, f32[1,128,512]{2,1,0:T(8,128)S(1)}, u32[]{:S(2)}, u32[]{:S(2)}) collective-permute-start(f32[1,128,512]{2,1,0:T(8,128)S(1)} %get-tuple-element.72), channel_id=1, source_target_pairs={{0,8},{1,9},{2,10},{3,11},{4,12},{5,13},{6,14},{7,15},{8,0},{9,1},... | collective-permute-start | bytes 786440 | tf_op jit(solution)/shard_map/ppermute | solution.py:22
  82.8 0.2 merge.11
  83.1 1.2 %collective-permute-start.17 = (f16[144,512]{1,0:T(8,128)(2,1)S(1)}, f16[144,512]{1,0:T(8,128)(2,1)S(1)}, u32[]{:S(2)}, u32[]{:S(2)}) collective-permute-start(f16[144,512]{1,0:T(8,128)(2,1)S(1)} %convert_element_type.38), channel_id=1, source_target_pairs={{0,8},{1,9},{2,10},{3,11},{4,12},{5,13},{6,14},{7,15},{8,0},{9,1},... | collective-permute-start | bytes 442376 | tf_op jit(solution)/shard_map/ppermute | solution.py:22
  84.3 0.1 select_reduce_fusion.inverse_ref
  84.4 12.8 %gradients.1 = (f32[128,512]{1,0:T(8,128)}, f32[128,512]{1,0:T(8,128)}) custom-call(s32[4,32]{1,0:T(4,128)S(1)} %select_reduce_fusion.inverse_ref, s32[1]{0:T(128)} %bitcast.3.high_ref, f32[128,512]{1,0:T(8,128)S(1)} %get-tuple-element.60.own_ref, f32[144,512]{1,0:T(8,128)S(1)} %convert_element_type.35.oth_ref, ...), custom_call_target="tpu_custom_call" | custom-call | tf_op jit(solution)/shard_map/gradients/pallas_call | solution.py:651
  97.3 3.3 %collective-permute-done.17 = f16[144,512]{1,0:T(8,128)(2,1)S(1)} collective-permute-done((f16[144,512]{1,0:T(8,128)(2,1)S(1)}, f16[144,512]{1,0:T(8,128)(2,1)S(1)}, u32[]{:S(2)}, u32[]{:S(2)}) %collective-permute-start.17) | collective-permute-done | bytes 147488 | tf_op jit(solution)/shard_map/ppermute | solution.py:22
  100.6 0.9 last_sums.1
  (41 shorter events, 0.6 us)
Async XLA Ops:
  0.6 27.8 %copy-start.7 = (s32[16]{0:T(128)S(1)}, s32[16]{0:T(128)}, u32[]{:S(2)}) copy-start(s32[16]{0:T(128)} %constant.12.clone) | copy-start | bytes 196
  0.6 21.8 %collective-permute-start.2 = (bf16[1,128,1024]{2,1,0:T(8,128)(2,1)}, bf16[1,128,1024]{2,1,0:T(8,128)(2,1)S(1)}, u32[]{:S(2)}, u32[]{:S(2)}) collective-permute-start(bf16[1,128,1024]{2,1,0:T(8,128)(2,1)} %bitcast.15), channel_id=1, source_target_pairs={{0,2},{1,3},{2,0},{3,1},{4,6},{5,7},{6,4},{7,5},{8,10},{9,11},{10,... | collective-permute-start | bytes 786440 | tf_op jit(solution)/shard_map/ppermute | solution.py:22
  3.7 18.8 %collective-permute-start.3 = (bf16[1,128,1024]{2,1,0:T(8,128)(2,1)}, bf16[1,128,1024]{2,1,0:T(8,128)(2,1)S(1)}, u32[]{:S(2)}, u32[]{:S(2)}) collective-permute-start(bf16[1,128,1024]{2,1,0:T(8,128)(2,1)} %bitcast.16), channel_id=1, source_target_pairs={{0,8},{1,9},{2,10},{3,11},{4,12},{5,13},{6,14},{7,15},{8,0},{9,1},... | collective-permute-start | bytes 786440 | tf_op jit(solution)/shard_map/ppermute | solution.py:22
  6.3 21.5 %collective-permute-start.5 = (bf16[1,128,1024]{2,1,0:T(8,128)(2,1)}, bf16[1,128,1024]{2,1,0:T(8,128)(2,1)S(1)}, u32[]{:S(2)}, u32[]{:S(2)}) collective-permute-start(bf16[1,128,1024]{2,1,0:T(8,128)(2,1)} %bitcast.17), channel_id=1, source_target_pairs={{0,4},{1,5},{2,6},{3,7},{4,0},{5,1},{6,2},{7,3},{8,12},{9,13},{10,... | collective-permute-start | bytes 786440 | tf_op jit(solution)/shard_map/ppermute | solution.py:22
  8.7 13.8 %collective-permute-start.1 = (f32[32,512]{1,0:T(8,128)S(1)}, f32[32,512]{1,0:T(8,128)S(1)}, u32[]{:S(2)}, u32[]{:S(2)}) collective-permute-start(f32[32,512]{1,0:T(8,128)S(1)} %slice_bitcast_fusion.1.own_ref), channel_id=1, source_target_pairs={{0,8},{1,9},{2,10},{3,11},{4,12},{5,13},{6,14},{7,15},{8,0},{9,1},... | collective-permute-start | bytes 196616 | tf_op jit(solution)/shard_map/ppermute | solution.py:22
  9.0 0.9 copy-start.1
  9.9 0.9 copy-start.3
  10.9 0.7 copy-start.4
  19.9 13.6 %collective-permute-start = (f32[128,512]{1,0:T(8,128)}, f32[128,512]{1,0:T(8,128)S(1)}, u32[]{:S(2)}, u32[]{:S(2)}) collective-permute-start(f32[128,512]{1,0:T(8,128)} %slice_bitcast_fusion), channel_id=1, source_target_pairs={{0,8},{1,9},{2,10},{3,11},{4,12},{5,13},{6,14},{7,15},{8,0},{9,1},... | collective-permute-start | bytes 786440 | tf_op jit(solution)/shard_map/ppermute | solution.py:22
  27.9 16.4 %collective-permute-start.6 = (bf16[2,128,1024]{2,1,0:T(8,128)(2,1)S(1)}, bf16[2,128,1024]{2,1,0:T(8,128)(2,1)S(1)}, u32[]{:S(2)}, u32[]{:S(2)}) collective-permute-start(bf16[2,128,1024]{2,1,0:T(8,128)(2,1)S(1)} %pad_maximum_fusion), channel_id=1, source_target_pairs={{0,2},{1,3},{2,0},{3,1},{4,6},{5,7},{6,4},{7,5},{8,10},{9,11},{10,... | collective-permute-start | bytes 1572872 | tf_op jit(solution)/shard_map/ppermute | solution.py:22
  28.4 15.8 %collective-permute-start.4 = (bf16[1,128,1024]{2,1,0:T(8,128)(2,1)S(1)}, bf16[1,128,1024]{2,1,0:T(8,128)(2,1)S(1)}, u32[]{:S(2)}, u32[]{:S(2)}) collective-permute-start(bf16[1,128,1024]{2,1,0:T(8,128)(2,1)S(1)} %collective-permute-done.3), channel_id=1, source_target_pairs={{0,4},{1,5},{2,6},{3,7},{4,0},{5,1},{6,2},{7,3},{8,12},{9,13},{10,... | collective-permute-start | bytes 786440 | tf_op jit(solution)/shard_map/ppermute | solution.py:22
  33.9 11.0 %copy-start.6 = (bf16[128,1024]{1,0:T(8,128)(2,1)S(1)}, bf16[128,1024]{1,0:T(8,128)(2,1)}, u32[]{:S(2)}) copy-start(bf16[128,1024]{1,0:T(8,128)(2,1)} %param.10) | copy-start | bytes 786436
  44.3 4.3 %copy-start = (f32[8,128,512]{2,1,0:T(8,128)S(1)}, f32[8,128,512]{2,1,0:T(8,128)}, u32[]{:S(2)}) copy-start(f32[8,128,512]{2,1,0:T(8,128)} %get-tuple-element.55.keep_ref) | copy-start | bytes 6291460
  44.3 4.2 %collective-permute-start.10 = (f32[8,128,512]{2,1,0:T(8,128)S(1)}, f32[8,128,512]{2,1,0:T(8,128)S(1)}, u32[]{:S(2)}, u32[]{:S(2)}) collective-permute-start(f32[8,128,512]{2,1,0:T(8,128)S(1)} %get-tuple-element.57), channel_id=1, source_target_pairs={{0,1},{1,0},{2,3},{3,2},{4,5},{5,4},{6,7},{7,6},{8,9},{9,8},{10,11... | collective-permute-start | bytes 6291464 | tf_op jit(solution)/shard_map/ppermute | solution.py:22
  44.4 7.1 %collective-permute-start.7 = (f32[8,128,512]{2,1,0:T(8,128)S(1)}, f32[8,128,512]{2,1,0:T(8,128)S(1)}, u32[]{:S(2)}, u32[]{:S(2)}) collective-permute-start(f32[8,128,512]{2,1,0:T(8,128)S(1)} %get-tuple-element.52), channel_id=1, source_target_pairs={{0,1},{1,0},{2,3},{3,2},{4,5},{5,4},{6,7},{7,6},{8,9},{9,8},{10,11... | collective-permute-start | bytes 6291464 | tf_op jit(solution)/shard_map/ppermute | solution.py:22
  44.9 8.4 %collective-permute-start.9 = (bf16[1,128,1024]{2,1,0:T(8,128)(2,1)S(1)}, bf16[1,128,1024]{2,1,0:T(8,128)(2,1)S(1)}, u32[]{:S(2)}, u32[]{:S(2)}) collective-permute-start(bf16[1,128,1024]{2,1,0:T(8,128)(2,1)S(1)} %collective-permute-done.4), channel_id=1, source_target_pairs={{0,2},{1,3},{2,0},{3,1},{4,6},{5,7},{6,4},{7,5},{8,10},{9,11},{10,... | collective-permute-start | bytes 786440 | tf_op jit(solution)/shard_map/ppermute | solution.py:22
  53.3 4.2 %collective-permute-start.11 = (bf16[8,128,1024]{2,1,0:T(8,128)(2,1)S(1)}, bf16[8,128,1024]{2,1,0:T(8,128)(2,1)S(1)}, u32[]{:S(2)}, u32[]{:S(2)}) collective-permute-start(bf16[8,128,1024]{2,1,0:T(8,128)(2,1)S(1)} %constant_dynamic-update-slice_fusion.low_ref), channel_id=1, source_target_pairs={{0,1},{1,0},{2,3},{3,2},{4,5},{5,4},{6,7},{7,6},{8,9},{9,8},{10,11... | collective-permute-start | bytes 6291464 | tf_op jit(solution)/shard_map/ppermute | solution.py:22
  53.4 14.7 %collective-permute-start.14 = (f16[528,512]{1,0:T(8,128)(2,1)S(1)}, f16[528,512]{1,0:T(8,128)(2,1)S(1)}, u32[]{:S(2)}, u32[]{:S(2)}) collective-permute-start(f16[528,512]{1,0:T(8,128)(2,1)S(1)} %convert_element_type.31), channel_id=1, source_target_pairs={{0,4},{1,5},{2,6},{3,7},{4,0},{5,1},{6,2},{7,3},{8,12},{9,13},{10,... | collective-permute-start | bytes 1622024 | tf_op jit(solution)/shard_map/ppermute | solution.py:22
  53.5 15.5 %collective-permute-start.8 = (f16[528,512]{1,0:T(8,128)(2,1)S(1)}, f16[528,512]{1,0:T(8,128)(2,1)S(1)}, u32[]{:S(2)}, u32[]{:S(2)}) collective-permute-start(f16[528,512]{1,0:T(8,128)(2,1)S(1)} %convert_element_type.30), channel_id=1, source_target_pairs={{0,2},{1,3},{2,0},{3,1},{4,6},{5,7},{6,4},{7,5},{8,10},{9,11},{10,... | collective-permute-start | bytes 1622024 | tf_op jit(solution)/shard_map/ppermute | solution.py:22
  68.5 14.4 %collective-permute-start.15 = (f32[2,128,512]{2,1,0:T(8,128)S(1)}, f32[2,128,512]{2,1,0:T(8,128)S(1)}, u32[]{:S(2)}, u32[]{:S(2)}) collective-permute-start(f32[2,128,512]{2,1,0:T(8,128)S(1)} %get-tuple-element.70), channel_id=1, source_target_pairs={{0,2},{1,3},{2,0},{3,1},{4,6},{5,7},{6,4},{7,5},{8,10},{9,11},{10,... | collective-permute-start | bytes 1572872 | tf_op jit(solution)/shard_map/ppermute | solution.py:22
  69.6 11.2 %collective-permute-start.12 = (f16[272,512]{1,0:T(8,128)(2,1)S(1)}, f16[272,512]{1,0:T(8,128)(2,1)S(1)}, u32[]{:S(2)}, u32[]{:S(2)}) collective-permute-start(f16[272,512]{1,0:T(8,128)(2,1)S(1)} %convert_element_type.33), channel_id=1, source_target_pairs={{0,4},{1,5},{2,6},{3,7},{4,0},{5,1},{6,2},{7,3},{8,12},{9,13},{10,... | collective-permute-start | bytes 835592 | tf_op jit(solution)/shard_map/ppermute | solution.py:22
  70.5 13.8 %copy-start.5 = (s32[4,32]{1,0:T(4,128)S(1)}, s32[4,32]{1,0:T(4,128)}, u32[]{:S(2)}) copy-start(s32[4,32]{1,0:T(4,128)} %orders_ref.1) | copy-start | bytes 1540
  70.5 13.9 %copy-start.2 = (bf16[128,512]{1,0:T(8,128)(2,1)S(1)}, bf16[128,512]{1,0:T(8,128)(2,1)}, u32[]{:S(2)}) copy-start(bf16[128,512]{1,0:T(8,128)(2,1)} %tok_ref.3) | copy-start | bytes 393220
  70.6 8.5 %collective-permute-start.13 = (f16[144,512]{1,0:T(8,128)(2,1)S(1)}, f16[144,512]{1,0:T(8,128)(2,1)S(1)}, u32[]{:S(2)}, u32[]{:S(2)}) collective-permute-start(f16[144,512]{1,0:T(8,128)(2,1)S(1)} %convert_element_type.34), channel_id=1, source_target_pairs={{0,8},{1,9},{2,10},{3,11},{4,12},{5,13},{6,14},{7,15},{8,0},{9,1},... | collective-permute-start | bytes 442376 | tf_op jit(solution)/shard_map/ppermute | solution.py:22
  81.0 19.6 %collective-permute-start.16 = (f32[1,128,512]{2,1,0:T(8,128)S(1)}, f32[1,128,512]{2,1,0:T(8,128)S(1)}, u32[]{:S(2)}, u32[]{:S(2)}) collective-permute-start(f32[1,128,512]{2,1,0:T(8,128)S(1)} %get-tuple-element.72), channel_id=1, source_target_pairs={{0,8},{1,9},{2,10},{3,11},{4,12},{5,13},{6,14},{7,15},{8,0},{9,1},... | collective-permute-start | bytes 786440 | tf_op jit(solution)/shard_map/ppermute | solution.py:22
  83.1 17.5 %collective-permute-start.17 = (f16[144,512]{1,0:T(8,128)(2,1)S(1)}, f16[144,512]{1,0:T(8,128)(2,1)S(1)}, u32[]{:S(2)}, u32[]{:S(2)}) collective-permute-start(f16[144,512]{1,0:T(8,128)(2,1)S(1)} %convert_element_type.38), channel_id=1, source_target_pairs={{0,8},{1,9},{2,10},{3,11},{4,12},{5,13},{6,14},{7,15},{8,0},{9,1},... | collective-permute-start | bytes 442376 | tf_op jit(solution)/shard_map/ppermute | solution.py:22

commit v14 on v13

--- a/solution.py
+++ b/solution.py
@@ -10,6 +10,7 @@
 
 VMEM_LIMIT = 16 * 2**20
 WIDE_LIMIT = 46 * 2**20
+DEPTH = 4
 GROUP = 128
 NN = (((1,), (0,)), ((), ()))
 NT = (((1,), (1,)), ((), ()))
@@ -291,10 +292,12 @@
         at = pl.multiple_of(places_ref[p] * width, width)
         return pltpu.make_async_copy(w_ref.at[:, pl.ds(at, width)], held_ref.at[p], sems.at[p])
 
-    for p in range(pieces):
+    for p in range(min(DEPTH, pieces)):
         fetch(p).start()
     for p in range(pieces):
         fetch(p).wait()
+        if p + DEPTH < pieces:
+            fetch(p + DEPTH).start()
         both = one_dot(x_ref[...], held_ref[p])
         total = both[:count] + both[count:]
         for chunk in range(CHUNKS):
@@ -345,12 +348,15 @@
             pltpu.make_async_copy(w_ref.at[:, pl.ds(at, width)], held_ref.at[:, here], sems.at[slot]),
         )
 
-    for slot in range(2 * half):
+    for slot in range(min(DEPTH, 2 * half)):
         for copy in fetches(slot):
             copy.start()
     for slot in range(2 * half):
         for copy in fetches(slot):
             copy.wait()
+        if slot + DEPTH < 2 * half:
+            for copy in fetches(slot + DEPTH):
+                copy.start()
         here = slice(slot * width, (slot + 1) * width)
         product = one_dot(cots_ref[:, here], held_ref[:, here], NT)
         if slot == 0:

time: 102 us -> 102 us (level)
  transfers between devices with their start and end apart: 18 -> 18, of which waited for: 9 -> 9; matrix products, arithmetic and copies ran while one was open for 2% -> 2% of each run, Pallas kernels for 46% -> 47%
where the time goes in v14:
time: 102 us
  Pallas kernels  48.3 us (47%)
  waiting for transfers between devices  27.4 us (27%)
  starting transfers between devices  19.8 us (19%)
  local copies, waits for them, and re-layouts  4.28 us (4%)
    ppermute x18, waiting for transfers between devices, exchange(): lax.ppermute(array, 'tensor', [(i, i ^ 1 << bit) for i in range(size)])  27.4 us
    ppermute x18, starting transfers between devices, exchange(): lax.ppermute(array, 'tensor', [(i, i ^ 1 << bit) for i in range(size)])  19.8 us
    pallas_call x1, Pallas kernels, local(): pl.pallas_call(grads_kernel, out_shape=(jax.ShapeDtypeStruct((count, rows...  12.9 us
    pallas_call x1, Pallas kernels, project(): pl.pallas_call(functools.partial(project_kernel, slots), out_shape=(jax.S...  10.3 us
    pallas_call x1, Pallas kernels, project_back(): pl.pallas_call(functools.partial(back_kernel, order), out_shape=(jax.Shap...  8.79 us
    pallas_call x1, Pallas kernels, local(): pl.pallas_call(near_kernel, out_shape=(jax.ShapeDtypeStruct(square, f32),...  7.59 us
    pallas_call x1, Pallas kernels, local(): pl.pallas_call(far_rotations_kernel, out_shape=(jax.ShapeDtypeStruct(far_...  5.29 us
    unnamed x22, local copies, waits for them, and re-layouts  2.69 us
  transfers between devices with their start and end apart: 18, of which 9 were waited for; matrix products, arithmetic and copies ran while one was open for 2% of the time, Pallas kernels for 47%

profile of v14, /device:TPU:0, one launch (start us, length us, event | category | flops | bytes accessed | tf_op | source)
XLA Modules:
  0.0 101.5 jit_solution(10562216095516745546)
XLA Ops:
  0.6 3.0 %collective-permute-start.2 = (bf16[1,128,1024]{2,1,0:T(8,128)(2,1)}, bf16[1,128,1024]{2,1,0:T(8,128)(2,1)S(1)}, u32[]{:S(2)}, u32[]{:S(2)}) collective-permute-start(bf16[1,128,1024]{2,1,0:T(8,128)(2,1)} %bitcast.15), channel_id=1, source_target_pairs={{0,2},{1,3},{2,0},{3,1},{4,6},{5,7},{6,4},{7,5},{8,10},{9,11},{10,... | collective-permute-start | bytes 786440 | tf_op jit(solution)/shard_map/ppermute | solution.py:23
  3.7 2.6 %collective-permute-start.3 = (bf16[1,128,1024]{2,1,0:T(8,128)(2,1)}, bf16[1,128,1024]{2,1,0:T(8,128)(2,1)S(1)}, u32[]{:S(2)}, u32[]{:S(2)}) collective-permute-start(bf16[1,128,1024]{2,1,0:T(8,128)(2,1)} %bitcast.16), channel_id=1, source_target_pairs={{0,8},{1,9},{2,10},{3,11},{4,12},{5,13},{6,14},{7,15},{8,0},{9,1},... | collective-permute-start | bytes 786440 | tf_op jit(solution)/shard_map/ppermute | solution.py:23
  6.3 1.6 %collective-permute-start.5 = (bf16[1,128,1024]{2,1,0:T(8,128)(2,1)}, bf16[1,128,1024]{2,1,0:T(8,128)(2,1)S(1)}, u32[]{:S(2)}, u32[]{:S(2)}) collective-permute-start(bf16[1,128,1024]{2,1,0:T(8,128)(2,1)} %bitcast.17), channel_id=1, source_target_pairs={{0,4},{1,5},{2,6},{3,7},{4,0},{5,1},{6,2},{7,3},{8,12},{9,13},{10,... | collective-permute-start | bytes 786440 | tf_op jit(solution)/shard_map/ppermute | solution.py:23
  7.8 0.8 slice_bitcast_fusion.1.own_ref
  8.7 0.3 collective-permute-start.1
  9.0 0.9 copy-done.1
  9.9 0.9 copy-done.3
  10.9 0.7 copy-done.4
  11.6 7.6 %near_rotations.1 = (f32[1024,128]{1,0:T(8,128)S(1)}, f32[3,512,128]{2,1,0:T(8,128)S(1)}, f32[3,128,512]{2,1,0:T(8,128)S(1)}) custom-call(s32[4,32]{1,0:T(4,128)S(1)} %copy-done.4, f32[128,512]{1,0:T(8,128)S(1)} %bitcast.14, bf16[128,512]{1,0:T(8,128)(2,1)S(1)} %copy-done.1), custom_call_target="tpu_custom_call" | custom-call | tf_op jit(solution)/shard_map/near_rotations/pallas_call | solution.py:566
  19.2 0.7 slice_bitcast_fusion
  19.9 2.6 %collective-permute-start = (f32[128,512]{1,0:T(8,128)}, f32[128,512]{1,0:T(8,128)S(1)}, u32[]{:S(2)}, u32[]{:S(2)}) collective-permute-start(f32[128,512]{1,0:T(8,128)} %slice_bitcast_fusion), channel_id=1, source_target_pairs={{0,8},{1,9},{2,10},{3,11},{4,12},{5,13},{6,14},{7,15},{8,0},{9,1},... | collective-permute-start | bytes 786440 | tf_op jit(solution)/shard_map/ppermute | solution.py:23
  22.5 5.3 %far_rotations.1 = (f32[1024,32]{1,0:T(8,128)S(1)}, f32[2,512,128]{2,1,0:T(8,128)S(1)}, f32[2,512,128]{2,1,0:T(8,128)S(1)}) custom-call(s32[1,32]{1,0:T(1,128)S(1)} %slice.11.orders_ref, s32[1]{0:T(128)} %bitcast.3.high_ref, f32[32,512]{1,0:T(8,128)S(1)} %slice_bitcast_fusion.1.own_ref, f32[32,512]{1,0:T(8,128)S(1)} %collective-permute-done.1.far_ref), custom_call_target="tpu_custom_call" | custom-call | flops 10000000 | bytes 10000000 | tf_op jit(solution)/shard_map/far_rotations/pallas_call | solution.py:588
  27.9 0.6 collective-permute-start.6
  28.4 0.4 collective-permute-start.4
  28.9 4.6 %collective-permute-done.oth_ref.x_oth_ref = f32[128,512]{1,0:T(8,128)S(1)} collective-permute-done((f32[128,512]{1,0:T(8,128)}, f32[128,512]{1,0:T(8,128)S(1)}, u32[]{:S(2)}, u32[]{:S(2)}) %collective-permute-start) | collective-permute-done | bytes 262176 | tf_op jit(solution)/shard_map/ppermute | solution.py:23
  33.5 0.4 far_apply.1.x_ref
  33.9 10.3 %project.1 = (f32[8,128,512]{2,1,0:T(8,128)S(1)}, f32[8,128,512]{2,1,0:T(8,128)S(1)}, f32[8,128,512]{2,1,0:T(8,128)S(1)}, f32[8,128,512]{2,1,0:T(8,128)}) custom-call(s32[16]{0:T(128)S(1)} %broadcast_xor_fusion.places_ref, bf16[256,512]{1,0:T(8,128)(2,1)S(1)} %far_apply.1.x_ref, bf16[512,16384]{1,0:T(8,128)(2,1)} %w_ref.3), custom_call_target="tpu_custom_call" | custom-call | flops 4294967296 | bytes 25165824 | tf_op jit(solution)/shard_map/project/pallas_call | solution.py:314
  44.3 0.1 collective-permute-start.10
  44.4 0.5 collective-permute-start.7
  45.0 0.5 collective-permute-start.9
  45.6 3.0 %collective-permute-done.10.got_ref = f32[8,128,512]{2,1,0:T(8,128)S(1)} collective-permute-done((f32[8,128,512]{2,1,0:T(8,128)S(1)}, f32[8,128,512]{2,1,0:T(8,128)S(1)}, u32[]{:S(2)}, u32[]{:S(2)}) %collective-permute-start.10) | collective-permute-done | bytes 2097184 | tf_op jit(solution)/shard_map/ppermute | solution.py:23
  48.5 0.6 merge.7
  49.1 0.1 convert_element_type.31
  49.3 2.3 %collective-permute-done.7.got_ref = f32[8,128,512]{2,1,0:T(8,128)S(1)} collective-permute-done((f32[8,128,512]{2,1,0:T(8,128)S(1)}, f32[8,128,512]{2,1,0:T(8,128)S(1)}, u32[]{:S(2)}, u32[]{:S(2)}) %collective-permute-start.7) | collective-permute-done | bytes 2097184 | tf_op jit(solution)/shard_map/ppermute | solution.py:23
  51.5 0.6 merge.6
  52.1 0.1 convert_element_type.30
  52.2 1.1 %collective-permute-done.9 = bf16[1,128,1024]{2,1,0:T(8,128)(2,1)S(1)} collective-permute-done((bf16[1,128,1024]{2,1,0:T(8,128)(2,1)S(1)}, bf16[1,128,1024]{2,1,0:T(8,128)(2,1)S(1)}, u32[]{:S(2)}, u32[]{:S(2)}) %collective-permute-start.9) | collective-permute-done | bytes 262176 | tf_op jit(solution)/shard_map/ppermute | solution.py:23
  53.5 0.5 collective-permute-start.8
  54.0 3.5 %collective-permute-done.11.high_ref = bf16[8,128,1024]{2,1,0:T(8,128)(2,1)S(1)} collective-permute-done((bf16[8,128,1024]{2,1,0:T(8,128)(2,1)S(1)}, bf16[8,128,1024]{2,1,0:T(8,128)(2,1)S(1)}, u32[]{:S(2)}, u32[]{:S(2)}) %collective-permute-start.11) | collective-permute-done | bytes 2097184 | tf_op jit(solution)/shard_map/ppermute | solution.py:23
  57.6 8.8 %project_back.1 = (f32[128,512]{1,0:T(8,128)S(1)}, f32[144,512]{1,0:T(8,128)S(1)}) custom-call(s32[16]{0:T(128)S(1)} %iota_xor_fusion.places_ref, bf16[8,128,1024]{2,1,0:T(8,128)(2,1)S(1)} %constant_dynamic-update-slice_fusion.low_ref, bf16[8,128,1024]{2,1,0:T(8,128)(2,1)S(1)} %collective-permute-done.11.high_ref, bf16[512,16384]{1,0:T(8,128)(2,1)} %w_ref.3), custom_call_target="tpu_custom_call" | custom-call | flops 2147483648 | bytes 20971520 | tf_op jit(solution)/shard_map/project_back/pallas_call | solution.py:373
  66.4 1.7 %collective-permute-done.14 = f16[528,512]{1,0:T(8,128)(2,1)S(1)} collective-permute-done((f16[528,512]{1,0:T(8,128)(2,1)S(1)}, f16[528,512]{1,0:T(8,128)(2,1)S(1)}, u32[]{:S(2)}, u32[]{:S(2)}) %collective-permute-start.14) | collective-permute-done | bytes 540704 | tf_op jit(solution)/shard_map/ppermute | solution.py:23
  68.1 0.1 convert_element_type.37.got_ref
  68.2 0.2 merge.10
  68.5 0.5 collective-permute-start.15
  69.0 0.1 convert_element_type.32.got_ref
  69.1 0.4 merge.8
  69.6 0.9 collective-permute-start.12
  70.6 2.4 %collective-permute-start.13 = (f16[144,512]{1,0:T(8,128)(2,1)S(1)}, f16[144,512]{1,0:T(8,128)(2,1)S(1)}, u32[]{:S(2)}, u32[]{:S(2)}) collective-permute-start(f16[144,512]{1,0:T(8,128)(2,1)S(1)} %convert_element_type.34), channel_id=1, source_target_pairs={{0,8},{1,9},{2,10},{3,11},{4,12},{5,13},{6,14},{7,15},{8,0},{9,1},... | collective-permute-start | bytes 442376 | tf_op jit(solution)/shard_map/ppermute | solution.py:23
  73.0 6.1 %collective-permute-done.13 = f16[144,512]{1,0:T(8,128)(2,1)S(1)} collective-permute-done((f16[144,512]{1,0:T(8,128)(2,1)S(1)}, f16[144,512]{1,0:T(8,128)(2,1)S(1)}, u32[]{:S(2)}, u32[]{:S(2)}) %collective-permute-start.13) | collective-permute-done | bytes 147488 | tf_op jit(solution)/shard_map/ppermute | solution.py:23
  79.2 1.6 %collective-permute-done.12 = f16[272,512]{1,0:T(8,128)(2,1)S(1)} collective-permute-done((f16[272,512]{1,0:T(8,128)(2,1)S(1)}, f16[272,512]{1,0:T(8,128)(2,1)S(1)}, u32[]{:S(2)}, u32[]{:S(2)}) %collective-permute-start.12) | collective-permute-done | bytes 278560 | tf_op jit(solution)/shard_map/ppermute | solution.py:23
  80.9 0.1 merge.9
  81.0 1.8 %collective-permute-start.16 = (f32[1,128,512]{2,1,0:T(8,128)S(1)}, f32[1,128,512]{2,1,0:T(8,128)S(1)}, u32[]{:S(2)}, u32[]{:S(2)}) collective-permute-start(f32[1,128,512]{2,1,0:T(8,128)S(1)} %get-tuple-element.72), channel_id=1, source_target_pairs={{0,8},{1,9},{2,10},{3,11},{4,12},{5,13},{6,14},{7,15},{8,0},{9,1},... | collective-permute-start | bytes 786440 | tf_op jit(solution)/shard_map/ppermute | solution.py:23
  82.8 0.2 merge.11
  83.1 1.2 %collective-permute-start.17 = (f16[144,512]{1,0:T(8,128)(2,1)S(1)}, f16[144,512]{1,0:T(8,128)(2,1)S(1)}, u32[]{:S(2)}, u32[]{:S(2)}) collective-permute-start(f16[144,512]{1,0:T(8,128)(2,1)S(1)} %convert_element_type.38), channel_id=1, source_target_pairs={{0,8},{1,9},{2,10},{3,11},{4,12},{5,13},{6,14},{7,15},{8,0},{9,1},... | collective-permute-start | bytes 442376 | tf_op jit(solution)/shard_map/ppermute | solution.py:23
  84.3 0.1 select_reduce_fusion.inverse_ref
  84.4 12.9 %gradients.1 = (f32[128,512]{1,0:T(8,128)}, f32[128,512]{1,0:T(8,128)}) custom-call(s32[4,32]{1,0:T(4,128)S(1)} %select_reduce_fusion.inverse_ref, s32[1]{0:T(128)} %bitcast.3.high_ref, f32[128,512]{1,0:T(8,128)S(1)} %get-tuple-element.60.own_ref, f32[144,512]{1,0:T(8,128)S(1)} %convert_element_type.35.oth_ref, ...), custom_call_target="tpu_custom_call" | custom-call | tf_op jit(solution)/shard_map/gradients/pallas_call | solution.py:657
  97.3 3.3 %collective-permute-done.17 = f16[144,512]{1,0:T(8,128)(2,1)S(1)} collective-permute-done((f16[144,512]{1,0:T(8,128)(2,1)S(1)}, f16[144,512]{1,0:T(8,128)(2,1)S(1)}, u32[]{:S(2)}, u32[]{:S(2)}) %collective-permute-start.17) | collective-permute-done | bytes 147488 | tf_op jit(solution)/shard_map/ppermute | solution.py:23
  100.6 0.9 last_sums.1
  (41 shorter events, 0.6 us)
Async XLA Ops:
  0.6 27.8 %copy-start.7 = (s32[16]{0:T(128)S(1)}, s32[16]{0:T(128)}, u32[]{:S(2)}) copy-start(s32[16]{0:T(128)} %constant.12.clone) | copy-start | bytes 196
  0.6 21.8 %collective-permute-start.2 = (bf16[1,128,1024]{2,1,0:T(8,128)(2,1)}, bf16[1,128,1024]{2,1,0:T(8,128)(2,1)S(1)}, u32[]{:S(2)}, u32[]{:S(2)}) collective-permute-start(bf16[1,128,1024]{2,1,0:T(8,128)(2,1)} %bitcast.15), channel_id=1, source_target_pairs={{0,2},{1,3},{2,0},{3,1},{4,6},{5,7},{6,4},{7,5},{8,10},{9,11},{10,... | collective-permute-start | bytes 786440 | tf_op jit(solution)/shard_map/ppermute | solution.py:23
  3.7 18.8 %collective-permute-start.3 = (bf16[1,128,1024]{2,1,0:T(8,128)(2,1)}, bf16[1,128,1024]{2,1,0:T(8,128)(2,1)S(1)}, u32[]{:S(2)}, u32[]{:S(2)}) collective-permute-start(bf16[1,128,1024]{2,1,0:T(8,128)(2,1)} %bitcast.16), channel_id=1, source_target_pairs={{0,8},{1,9},{2,10},{3,11},{4,12},{5,13},{6,14},{7,15},{8,0},{9,1},... | collective-permute-start | bytes 786440 | tf_op jit(solution)/shard_map/ppermute | solution.py:23
  6.3 21.5 %collective-permute-start.5 = (bf16[1,128,1024]{2,1,0:T(8,128)(2,1)}, bf16[1,128,1024]{2,1,0:T(8,128)(2,1)S(1)}, u32[]{:S(2)}, u32[]{:S(2)}) collective-permute-start(bf16[1,128,1024]{2,1,0:T(8,128)(2,1)} %bitcast.17), channel_id=1, source_target_pairs={{0,4},{1,5},{2,6},{3,7},{4,0},{5,1},{6,2},{7,3},{8,12},{9,13},{10,... | collective-permute-start | bytes 786440 | tf_op jit(solution)/shard_map/ppermute | solution.py:23
  8.7 13.8 %collective-permute-start.1 = (f32[32,512]{1,0:T(8,128)S(1)}, f32[32,512]{1,0:T(8,128)S(1)}, u32[]{:S(2)}, u32[]{:S(2)}) collective-permute-start(f32[32,512]{1,0:T(8,128)S(1)} %slice_bitcast_fusion.1.own_ref), channel_id=1, source_target_pairs={{0,8},{1,9},{2,10},{3,11},{4,12},{5,13},{6,14},{7,15},{8,0},{9,1},... | collective-permute-start | bytes 196616 | tf_op jit(solution)/shard_map/ppermute | solution.py:23
  9.0 0.9 copy-start.1
  9.9 0.9 copy-start.3
  10.9 0.7 copy-start.4
  19.9 13.6 %collective-permute-start = (f32[128,512]{1,0:T(8,128)}, f32[128,512]{1,0:T(8,128)S(1)}, u32[]{:S(2)}, u32[]{:S(2)}) collective-permute-start(f32[128,512]{1,0:T(8,128)} %slice_bitcast_fusion), channel_id=1, source_target_pairs={{0,8},{1,9},{2,10},{3,11},{4,12},{5,13},{6,14},{7,15},{8,0},{9,1},... | collective-permute-start | bytes 786440 | tf_op jit(solution)/shard_map/ppermute | solution.py:23
  27.9 16.4 %collective-permute-start.6 = (bf16[2,128,1024]{2,1,0:T(8,128)(2,1)S(1)}, bf16[2,128,1024]{2,1,0:T(8,128)(2,1)S(1)}, u32[]{:S(2)}, u32[]{:S(2)}) collective-permute-start(bf16[2,128,1024]{2,1,0:T(8,128)(2,1)S(1)} %pad_maximum_fusion), channel_id=1, source_target_pairs={{0,2},{1,3},{2,0},{3,1},{4,6},{5,7},{6,4},{7,5},{8,10},{9,11},{10,... | collective-permute-start | bytes 1572872 | tf_op jit(solution)/shard_map/ppermute | solution.py:23
  28.4 15.9 %collective-permute-start.4 = (bf16[1,128,1024]{2,1,0:T(8,128)(2,1)S(1)}, bf16[1,128,1024]{2,1,0:T(8,128)(2,1)S(1)}, u32[]{:S(2)}, u32[]{:S(2)}) collective-permute-start(bf16[1,128,1024]{2,1,0:T(8,128)(2,1)S(1)} %collective-permute-done.3), channel_id=1, source_target_pairs={{0,4},{1,5},{2,6},{3,7},{4,0},{5,1},{6,2},{7,3},{8,12},{9,13},{10,... | collective-permute-start | bytes 786440 | tf_op jit(solution)/shard_map/ppermute | solution.py:23
  33.9 11.0 %copy-start.6 = (bf16[128,1024]{1,0:T(8,128)(2,1)S(1)}, bf16[128,1024]{1,0:T(8,128)(2,1)}, u32[]{:S(2)}) copy-start(bf16[128,1024]{1,0:T(8,128)(2,1)} %param.10) | copy-start | bytes 786436
  44.3 4.3 %copy-start = (f32[8,128,512]{2,1,0:T(8,128)S(1)}, f32[8,128,512]{2,1,0:T(8,128)}, u32[]{:S(2)}) copy-start(f32[8,128,512]{2,1,0:T(8,128)} %get-tuple-element.55.keep_ref) | copy-start | bytes 6291460
  44.3 4.2 %collective-permute-start.10 = (f32[8,128,512]{2,1,0:T(8,128)S(1)}, f32[8,128,512]{2,1,0:T(8,128)S(1)}, u32[]{:S(2)}, u32[]{:S(2)}) collective-permute-start(f32[8,128,512]{2,1,0:T(8,128)S(1)} %get-tuple-element.57), channel_id=1, source_target_pairs={{0,1},{1,0},{2,3},{3,2},{4,5},{5,4},{6,7},{7,6},{8,9},{9,8},{10,11... | collective-permute-start | bytes 6291464 | tf_op jit(solution)/shard_map/ppermute | solution.py:23
  44.4 7.1 %collective-permute-start.7 = (f32[8,128,512]{2,1,0:T(8,128)S(1)}, f32[8,128,512]{2,1,0:T(8,128)S(1)}, u32[]{:S(2)}, u32[]{:S(2)}) collective-permute-start(f32[8,128,512]{2,1,0:T(8,128)S(1)} %get-tuple-element.52), channel_id=1, source_target_pairs={{0,1},{1,0},{2,3},{3,2},{4,5},{5,4},{6,7},{7,6},{8,9},{9,8},{10,11... | collective-permute-start | bytes 6291464 | tf_op jit(solution)/shard_map/ppermute | solution.py:23
  45.0 8.4 %collective-permute-start.9 = (bf16[1,128,1024]{2,1,0:T(8,128)(2,1)S(1)}, bf16[1,128,1024]{2,1,0:T(8,128)(2,1)S(1)}, u32[]{:S(2)}, u32[]{:S(2)}) collective-permute-start(bf16[1,128,1024]{2,1,0:T(8,128)(2,1)S(1)} %collective-permute-done.4), channel_id=1, source_target_pairs={{0,2},{1,3},{2,0},{3,1},{4,6},{5,7},{6,4},{7,5},{8,10},{9,11},{10,... | collective-permute-start | bytes 786440 | tf_op jit(solution)/shard_map/ppermute | solution.py:23
  53.3 4.2 %collective-permute-start.11 = (bf16[8,128,1024]{2,1,0:T(8,128)(2,1)S(1)}, bf16[8,128,1024]{2,1,0:T(8,128)(2,1)S(1)}, u32[]{:S(2)}, u32[]{:S(2)}) collective-permute-start(bf16[8,128,1024]{2,1,0:T(8,128)(2,1)S(1)} %constant_dynamic-update-slice_fusion.low_ref), channel_id=1, source_target_pairs={{0,1},{1,0},{2,3},{3,2},{4,5},{5,4},{6,7},{7,6},{8,9},{9,8},{10,11... | collective-permute-start | bytes 6291464 | tf_op jit(solution)/shard_map/ppermute | solution.py:23
  53.4 14.7 %collective-permute-start.14 = (f16[528,512]{1,0:T(8,128)(2,1)S(1)}, f16[528,512]{1,0:T(8,128)(2,1)S(1)}, u32[]{:S(2)}, u32[]{:S(2)}) collective-permute-start(f16[528,512]{1,0:T(8,128)(2,1)S(1)} %convert_element_type.31), channel_id=1, source_target_pairs={{0,4},{1,5},{2,6},{3,7},{4,0},{5,1},{6,2},{7,3},{8,12},{9,13},{10,... | collective-permute-start | bytes 1622024 | tf_op jit(solution)/shard_map/ppermute | solution.py:23
  53.5 15.5 %collective-permute-start.8 = (f16[528,512]{1,0:T(8,128)(2,1)S(1)}, f16[528,512]{1,0:T(8,128)(2,1)S(1)}, u32[]{:S(2)}, u32[]{:S(2)}) collective-permute-start(f16[528,512]{1,0:T(8,128)(2,1)S(1)} %convert_element_type.30), channel_id=1, source_target_pairs={{0,2},{1,3},{2,0},{3,1},{4,6},{5,7},{6,4},{7,5},{8,10},{9,11},{10,... | collective-permute-start | bytes 1622024 | tf_op jit(solution)/shard_map/ppermute | solution.py:23
  68.5 14.4 %collective-permute-start.15 = (f32[2,128,512]{2,1,0:T(8,128)S(1)}, f32[2,128,512]{2,1,0:T(8,128)S(1)}, u32[]{:S(2)}, u32[]{:S(2)}) collective-permute-start(f32[2,128,512]{2,1,0:T(8,128)S(1)} %get-tuple-element.70), channel_id=1, source_target_pairs={{0,2},{1,3},{2,0},{3,1},{4,6},{5,7},{6,4},{7,5},{8,10},{9,11},{10,... | collective-permute-start | bytes 1572872 | tf_op jit(solution)/shard_map/ppermute | solution.py:23
  69.6 11.2 %collective-permute-start.12 = (f16[272,512]{1,0:T(8,128)(2,1)S(1)}, f16[272,512]{1,0:T(8,128)(2,1)S(1)}, u32[]{:S(2)}, u32[]{:S(2)}) collective-permute-start(f16[272,512]{1,0:T(8,128)(2,1)S(1)} %convert_element_type.33), channel_id=1, source_target_pairs={{0,4},{1,5},{2,6},{3,7},{4,0},{5,1},{6,2},{7,3},{8,12},{9,13},{10,... | collective-permute-start | bytes 835592 | tf_op jit(solution)/shard_map/ppermute | solution.py:23
  70.6 13.8 %copy-start.5 = (s32[4,32]{1,0:T(4,128)S(1)}, s32[4,32]{1,0:T(4,128)}, u32[]{:S(2)}) copy-start(s32[4,32]{1,0:T(4,128)} %orders_ref.1) | copy-start | bytes 1540
  70.6 13.9 %copy-start.2 = (bf16[128,512]{1,0:T(8,128)(2,1)S(1)}, bf16[128,512]{1,0:T(8,128)(2,1)}, u32[]{:S(2)}) copy-start(bf16[128,512]{1,0:T(8,128)(2,1)} %tok_ref.3) | copy-start | bytes 393220
  70.6 8.5 %collective-permute-start.13 = (f16[144,512]{1,0:T(8,128)(2,1)S(1)}, f16[144,512]{1,0:T(8,128)(2,1)S(1)}, u32[]{:S(2)}, u32[]{:S(2)}) collective-permute-start(f16[144,512]{1,0:T(8,128)(2,1)S(1)} %convert_element_type.34), channel_id=1, source_target_pairs={{0,8},{1,9},{2,10},{3,11},{4,12},{5,13},{6,14},{7,15},{8,0},{9,1},... | collective-permute-start | bytes 442376 | tf_op jit(solution)/shard_map/ppermute | solution.py:23
  81.0 19.6 %collective-permute-start.16 = (f32[1,128,512]{2,1,0:T(8,128)S(1)}, f32[1,128,512]{2,1,0:T(8,128)S(1)}, u32[]{:S(2)}, u32[]{:S(2)}) collective-permute-start(f32[1,128,512]{2,1,0:T(8,128)S(1)} %get-tuple-element.72), channel_id=1, source_target_pairs={{0,8},{1,9},{2,10},{3,11},{4,12},{5,13},{6,14},{7,15},{8,0},{9,1},... | collective-permute-start | bytes 786440 | tf_op jit(solution)/shard_map/ppermute | solution.py:23
  83.1 17.5 %collective-permute-start.17 = (f16[144,512]{1,0:T(8,128)(2,1)S(1)}, f16[144,512]{1,0:T(8,128)(2,1)S(1)}, u32[]{:S(2)}, u32[]{:S(2)}) collective-permute-start(f16[144,512]{1,0:T(8,128)(2,1)S(1)} %convert_element_type.38), channel_id=1, source_target_pairs={{0,8},{1,9},{2,10},{3,11},{4,12},{5,13},{6,14},{7,15},{8,0},{9,1},... | collective-permute-start | bytes 442376 | tf_op jit(solution)/shard_map/ppermute | solution.py:23

commit v15 on v13

--- a/solution.py
+++ b/solution.py
@@ -667,7 +667,9 @@
         compiler_params=params,
         name="gradients",
     )(inverse, high, grad_cols, grad_other, x_other, tokens, xs, near, bfar, inv_far, inv)
-    outs = merged(1, outs, gots)
+    ahead = merge(outs[0][1], gots[0], True, 2 in narrow[0])
+    gots = [gots[0]] + [after(got, ahead[0]) for got in gots[1:]]
+    outs = [ahead] + merged(1, outs, gots)[1:]
     for n in range(2, bits - 1):
         gots = [exchange(send, order_[n]) for (send, _), order_ in zip(outs, stages)]
         if n == 2:

time: 102 us -> 102 us (level)
  waiting for transfers between devices: 27.8 us -> 26.5 us
  starting transfers between devices: 19.8 us -> 21 us
    ppermute x18, waiting for transfers between devices: 27.8 us -> 26.5 us  [exchange(): lax.ppermute(array, 'tensor', [(i, i ^ 1 << bit) for i in range(size)])]
    ppermute x18, starting transfers between devices: 19.8 us -> 21 us  [exchange(): lax.ppermute(array, 'tensor', [(i, i ^ 1 << bit) for i in range(size)])]
where the time goes in v15:
time: 102 us; the launch traced here: 101 us
  Pallas kernels  47.9 us (47%)
  waiting for transfers between devices  26.5 us (26%)
  starting transfers between devices  21 us (21%)
  local copies, waits for them, and re-layouts  4.28 us (4%)
    ppermute x18, waiting for transfers between devices, exchange(): lax.ppermute(array, 'tensor', [(i, i ^ 1 << bit) for i in range(size)])  26.5 us
    ppermute x18, starting transfers between devices, exchange(): lax.ppermute(array, 'tensor', [(i, i ^ 1 << bit) for i in range(size)])  21 us
    pallas_call x1, Pallas kernels, local(): pl.pallas_call(grads_kernel, out_shape=(jax.ShapeDtypeStruct((count, rows...  12.8 us
    pallas_call x1, Pallas kernels, project(): pl.pallas_call(functools.partial(project_kernel, slots), out_shape=(jax.S...  10.3 us
    pallas_call x1, Pallas kernels, project_back(): pl.pallas_call(functools.partial(back_kernel, order), out_shape=(jax.Shap...  8.38 us
    pallas_call x1, Pallas kernels, local(): pl.pallas_call(near_kernel, out_shape=(jax.ShapeDtypeStruct(square, f32),...  7.59 us
    pallas_call x1, Pallas kernels, local(): pl.pallas_call(far_rotations_kernel, out_shape=(jax.ShapeDtypeStruct(far_...  5.29 us
    unnamed x22, local copies, waits for them, and re-layouts  2.69 us
  transfers between devices with their start and end apart: 18, of which 9 were waited for; matrix products, arithmetic and copies ran while one was open for 2% of the time, Pallas kernels for 46%

profile of v15, /device:TPU:0, one launch (start us, length us, event | category | flops | bytes accessed | tf_op | source)
XLA Modules:
  0.0 101.4 jit_solution(2085800574035154883)
XLA Ops:
  0.6 3.0 %collective-permute-start.2 = (bf16[1,128,1024]{2,1,0:T(8,128)(2,1)}, bf16[1,128,1024]{2,1,0:T(8,128)(2,1)S(1)}, u32[]{:S(2)}, u32[]{:S(2)}) collective-permute-start(bf16[1,128,1024]{2,1,0:T(8,128)(2,1)} %bitcast.15), channel_id=1, source_target_pairs={{0,2},{1,3},{2,0},{3,1},{4,6},{5,7},{6,4},{7,5},{8,10},{9,11},{10,... | collective-permute-start | bytes 786440 | tf_op jit(solution)/shard_map/ppermute | solution.py:22
  3.7 2.6 %collective-permute-start.3 = (bf16[1,128,1024]{2,1,0:T(8,128)(2,1)}, bf16[1,128,1024]{2,1,0:T(8,128)(2,1)S(1)}, u32[]{:S(2)}, u32[]{:S(2)}) collective-permute-start(bf16[1,128,1024]{2,1,0:T(8,128)(2,1)} %bitcast.16), channel_id=1, source_target_pairs={{0,8},{1,9},{2,10},{3,11},{4,12},{5,13},{6,14},{7,15},{8,0},{9,1},... | collective-permute-start | bytes 786440 | tf_op jit(solution)/shard_map/ppermute | solution.py:22
  6.3 1.6 %collective-permute-start.5 = (bf16[1,128,1024]{2,1,0:T(8,128)(2,1)}, bf16[1,128,1024]{2,1,0:T(8,128)(2,1)S(1)}, u32[]{:S(2)}, u32[]{:S(2)}) collective-permute-start(bf16[1,128,1024]{2,1,0:T(8,128)(2,1)} %bitcast.17), channel_id=1, source_target_pairs={{0,4},{1,5},{2,6},{3,7},{4,0},{5,1},{6,2},{7,3},{8,12},{9,13},{10,... | collective-permute-start | bytes 786440 | tf_op jit(solution)/shard_map/ppermute | solution.py:22
  7.8 0.8 slice_bitcast_fusion.1.own_ref
  8.7 0.3 collective-permute-start.1
  9.0 0.9 copy-done.1
  9.9 0.9 copy-done.3
  10.9 0.7 copy-done.4
  11.6 7.6 %near_rotations.1 = (f32[1024,128]{1,0:T(8,128)S(1)}, f32[3,512,128]{2,1,0:T(8,128)S(1)}, f32[3,128,512]{2,1,0:T(8,128)S(1)}) custom-call(s32[4,32]{1,0:T(4,128)S(1)} %copy-done.4, f32[128,512]{1,0:T(8,128)S(1)} %bitcast.14, bf16[128,512]{1,0:T(8,128)(2,1)S(1)} %copy-done.1), custom_call_target="tpu_custom_call" | custom-call | tf_op jit(solution)/shard_map/near_rotations/pallas_call | solution.py:560
  19.2 0.7 slice_bitcast_fusion
  19.9 2.6 %collective-permute-start = (f32[128,512]{1,0:T(8,128)}, f32[128,512]{1,0:T(8,128)S(1)}, u32[]{:S(2)}, u32[]{:S(2)}) collective-permute-start(f32[128,512]{1,0:T(8,128)} %slice_bitcast_fusion), channel_id=1, source_target_pairs={{0,8},{1,9},{2,10},{3,11},{4,12},{5,13},{6,14},{7,15},{8,0},{9,1},... | collective-permute-start | bytes 786440 | tf_op jit(solution)/shard_map/ppermute | solution.py:22
  22.5 5.3 %far_rotations.1 = (f32[1024,32]{1,0:T(8,128)S(1)}, f32[2,512,128]{2,1,0:T(8,128)S(1)}, f32[2,512,128]{2,1,0:T(8,128)S(1)}) custom-call(s32[1,32]{1,0:T(1,128)S(1)} %slice.11.orders_ref, s32[1]{0:T(128)} %bitcast.3.high_ref, f32[32,512]{1,0:T(8,128)S(1)} %slice_bitcast_fusion.1.own_ref, f32[32,512]{1,0:T(8,128)S(1)} %collective-permute-done.1.far_ref), custom_call_target="tpu_custom_call" | custom-call | flops 10000000 | bytes 10000000 | tf_op jit(solution)/shard_map/far_rotations/pallas_call | solution.py:582
  27.9 0.6 collective-permute-start.6
  28.4 0.4 collective-permute-start.4
  28.9 4.6 %collective-permute-done.oth_ref.x_oth_ref = f32[128,512]{1,0:T(8,128)S(1)} collective-permute-done((f32[128,512]{1,0:T(8,128)}, f32[128,512]{1,0:T(8,128)S(1)}, u32[]{:S(2)}, u32[]{:S(2)}) %collective-permute-start) | collective-permute-done | bytes 262176 | tf_op jit(solution)/shard_map/ppermute | solution.py:22
  33.5 0.4 far_apply.1.x_ref
  33.9 10.3 %project.1 = (f32[8,128,512]{2,1,0:T(8,128)S(1)}, f32[8,128,512]{2,1,0:T(8,128)S(1)}, f32[8,128,512]{2,1,0:T(8,128)S(1)}, f32[8,128,512]{2,1,0:T(8,128)}) custom-call(s32[16]{0:T(128)S(1)} %broadcast_xor_fusion.places_ref, bf16[256,512]{1,0:T(8,128)(2,1)S(1)} %far_apply.1.x_ref, bf16[512,16384]{1,0:T(8,128)(2,1)} %w_ref.3), custom_call_target="tpu_custom_call" | custom-call | flops 4294967296 | bytes 25165824 | tf_op jit(solution)/shard_map/project/pallas_call | solution.py:311
  44.4 0.5 collective-permute-start.7
  44.9 0.5 collective-permute-start.9
  45.6 3.0 %collective-permute-done.10.got_ref = f32[8,128,512]{2,1,0:T(8,128)S(1)} collective-permute-done((f32[8,128,512]{2,1,0:T(8,128)S(1)}, f32[8,128,512]{2,1,0:T(8,128)S(1)}, u32[]{:S(2)}, u32[]{:S(2)}) %collective-permute-start.10) | collective-permute-done | bytes 2097184 | tf_op jit(solution)/shard_map/ppermute | solution.py:22
  48.5 0.6 merge.7
  49.1 0.1 convert_element_type.31
  49.2 2.3 %collective-permute-done.7.got_ref = f32[8,128,512]{2,1,0:T(8,128)S(1)} collective-permute-done((f32[8,128,512]{2,1,0:T(8,128)S(1)}, f32[8,128,512]{2,1,0:T(8,128)S(1)}, u32[]{:S(2)}, u32[]{:S(2)}) %collective-permute-start.7) | collective-permute-done | bytes 2097184 | tf_op jit(solution)/shard_map/ppermute | solution.py:22
  51.5 0.6 merge.6
  52.1 0.1 convert_element_type.30
  52.2 1.1 %collective-permute-done.9 = bf16[1,128,1024]{2,1,0:T(8,128)(2,1)S(1)} collective-permute-done((bf16[1,128,1024]{2,1,0:T(8,128)(2,1)S(1)}, bf16[1,128,1024]{2,1,0:T(8,128)(2,1)S(1)}, u32[]{:S(2)}, u32[]{:S(2)}) %collective-permute-start.9) | collective-permute-done | bytes 262176 | tf_op jit(solution)/shard_map/ppermute | solution.py:22
  53.4 0.1 collective-permute-start.14
  53.5 0.5 collective-permute-start.8
  54.0 3.5 %collective-permute-done.11.high_ref = bf16[8,128,1024]{2,1,0:T(8,128)(2,1)S(1)} collective-permute-done((bf16[8,128,1024]{2,1,0:T(8,128)(2,1)S(1)}, bf16[8,128,1024]{2,1,0:T(8,128)(2,1)S(1)}, u32[]{:S(2)}, u32[]{:S(2)}) %collective-permute-start.11) | collective-permute-done | bytes 2097184 | tf_op jit(solution)/shard_map/ppermute | solution.py:22
  57.5 8.4 %project_back.1 = (f32[128,512]{1,0:T(8,128)S(1)}, f32[144,512]{1,0:T(8,128)S(1)}) custom-call(s32[16]{0:T(128)S(1)} %iota_xor_fusion.places_ref, bf16[8,128,1024]{2,1,0:T(8,128)(2,1)S(1)} %constant_dynamic-update-slice_fusion.low_ref, bf16[8,128,1024]{2,1,0:T(8,128)(2,1)S(1)} %collective-permute-done.11.high_ref, bf16[512,16384]{1,0:T(8,128)(2,1)} %w_ref.3), custom_call_target="tpu_custom_call" | custom-call | flops 2147483648 | bytes 20971520 | tf_op jit(solution)/shard_map/project_back/pallas_call | solution.py:367
  65.9 2.2 %collective-permute-done.14 = f16[528,512]{1,0:T(8,128)(2,1)S(1)} collective-permute-done((f16[528,512]{1,0:T(8,128)(2,1)S(1)}, f16[528,512]{1,0:T(8,128)(2,1)S(1)}, u32[]{:S(2)}, u32[]{:S(2)}) %collective-permute-start.14) | collective-permute-done | bytes 540704 | tf_op jit(solution)/shard_map/ppermute | solution.py:22
  68.1 0.1 convert_element_type.32.got_ref
  68.2 0.4 merge.8
  68.7 0.1 convert_element_type.37.got_ref
  68.9 0.2 merge.10
  69.1 0.5 collective-permute-start.15
  69.6 1.7 %collective-permute-start.12 = (f16[272,512]{1,0:T(8,128)(2,1)S(1)}, f16[272,512]{1,0:T(8,128)(2,1)S(1)}, u32[]{:S(2)}, u32[]{:S(2)}) collective-permute-start(f16[272,512]{1,0:T(8,128)(2,1)S(1)} %convert_element_type.33), channel_id=1, source_target_pairs={{0,4},{1,5},{2,6},{3,7},{4,0},{5,1},{6,2},{7,3},{8,12},{9,13},{10,... | collective-permute-start | bytes 835592 | tf_op jit(solution)/shard_map/ppermute | solution.py:22
  71.4 1.5 %collective-permute-start.13 = (f16[144,512]{1,0:T(8,128)(2,1)S(1)}, f16[144,512]{1,0:T(8,128)(2,1)S(1)}, u32[]{:S(2)}, u32[]{:S(2)}) collective-permute-start(f16[144,512]{1,0:T(8,128)(2,1)S(1)} %convert_element_type.34), channel_id=1, source_target_pairs={{0,8},{1,9},{2,10},{3,11},{4,12},{5,13},{6,14},{7,15},{8,0},{9,1},... | collective-permute-start | bytes 442376 | tf_op jit(solution)/shard_map/ppermute | solution.py:22
  72.9 6.7 %collective-permute-done.13 = f16[144,512]{1,0:T(8,128)(2,1)S(1)} collective-permute-done((f16[144,512]{1,0:T(8,128)(2,1)S(1)}, f16[144,512]{1,0:T(8,128)(2,1)S(1)}, u32[]{:S(2)}, u32[]{:S(2)}) %collective-permute-start.13) | collective-permute-done | bytes 147488 | tf_op jit(solution)/shard_map/ppermute | solution.py:22
  79.7 1.0 %collective-permute-done.12 = f16[272,512]{1,0:T(8,128)(2,1)S(1)} collective-permute-done((f16[272,512]{1,0:T(8,128)(2,1)S(1)}, f16[272,512]{1,0:T(8,128)(2,1)S(1)}, u32[]{:S(2)}, u32[]{:S(2)}) %collective-permute-start.12) | collective-permute-done | bytes 278560 | tf_op jit(solution)/shard_map/ppermute | solution.py:22
  80.8 0.1 merge.9
  80.9 2.4 %collective-permute-start.16 = (f32[1,128,512]{2,1,0:T(8,128)S(1)}, f32[1,128,512]{2,1,0:T(8,128)S(1)}, u32[]{:S(2)}, u32[]{:S(2)}) collective-permute-start(f32[1,128,512]{2,1,0:T(8,128)S(1)} %get-tuple-element.74), channel_id=1, source_target_pairs={{0,8},{1,9},{2,10},{3,11},{4,12},{5,13},{6,14},{7,15},{8,0},{9,1},... | collective-permute-start | bytes 786440 | tf_op jit(solution)/shard_map/ppermute | solution.py:22
  83.4 0.2 merge.11
  83.6 1.9 %collective-permute-start.17 = (f16[144,512]{1,0:T(8,128)(2,1)S(1)}, f16[144,512]{1,0:T(8,128)(2,1)S(1)}, u32[]{:S(2)}, u32[]{:S(2)}) collective-permute-start(f16[144,512]{1,0:T(8,128)(2,1)S(1)} %convert_element_type.38), channel_id=1, source_target_pairs={{0,8},{1,9},{2,10},{3,11},{4,12},{5,13},{6,14},{7,15},{8,0},{9,1},... | collective-permute-start | bytes 442376 | tf_op jit(solution)/shard_map/ppermute | solution.py:22
  85.5 0.1 select_reduce_fusion.inverse_ref
  85.6 12.8 %gradients.1 = (f32[128,512]{1,0:T(8,128)}, f32[128,512]{1,0:T(8,128)}) custom-call(s32[4,32]{1,0:T(4,128)S(1)} %select_reduce_fusion.inverse_ref, s32[1]{0:T(128)} %bitcast.3.high_ref, f32[128,512]{1,0:T(8,128)S(1)} %get-tuple-element.61.own_ref, f32[144,512]{1,0:T(8,128)S(1)} %convert_element_type.35.oth_ref, ...), custom_call_target="tpu_custom_call" | custom-call | tf_op jit(solution)/shard_map/gradients/pallas_call | solution.py:651
  98.5 2.0 %collective-permute-done.17 = f16[144,512]{1,0:T(8,128)(2,1)S(1)} collective-permute-done((f16[144,512]{1,0:T(8,128)(2,1)S(1)}, f16[144,512]{1,0:T(8,128)(2,1)S(1)}, u32[]{:S(2)}, u32[]{:S(2)}) %collective-permute-start.17) | collective-permute-done | bytes 147488 | tf_op jit(solution)/shard_map/ppermute | solution.py:22
  100.5 0.9 last_sums.1
  (41 shorter events, 0.6 us)
Async XLA Ops:
  0.6 27.8 %copy-start.7 = (s32[16]{0:T(128)S(1)}, s32[16]{0:T(128)}, u32[]{:S(2)}) copy-start(s32[16]{0:T(128)} %constant.12.clone) | copy-start | bytes 196
  0.6 21.8 %collective-permute-start.2 = (bf16[1,128,1024]{2,1,0:T(8,128)(2,1)}, bf16[1,128,1024]{2,1,0:T(8,128)(2,1)S(1)}, u32[]{:S(2)}, u32[]{:S(2)}) collective-permute-start(bf16[1,128,1024]{2,1,0:T(8,128)(2,1)} %bitcast.15), channel_id=1, source_target_pairs={{0,2},{1,3},{2,0},{3,1},{4,6},{5,7},{6,4},{7,5},{8,10},{9,11},{10,... | collective-permute-start | bytes 786440 | tf_op jit(solution)/shard_map/ppermute | solution.py:22
  3.7 18.8 %collective-permute-start.3 = (bf16[1,128,1024]{2,1,0:T(8,128)(2,1)}, bf16[1,128,1024]{2,1,0:T(8,128)(2,1)S(1)}, u32[]{:S(2)}, u32[]{:S(2)}) collective-permute-start(bf16[1,128,1024]{2,1,0:T(8,128)(2,1)} %bitcast.16), channel_id=1, source_target_pairs={{0,8},{1,9},{2,10},{3,11},{4,12},{5,13},{6,14},{7,15},{8,0},{9,1},... | collective-permute-start | bytes 786440 | tf_op jit(solution)/shard_map/ppermute | solution.py:22
  6.3 21.5 %collective-permute-start.5 = (bf16[1,128,1024]{2,1,0:T(8,128)(2,1)}, bf16[1,128,1024]{2,1,0:T(8,128)(2,1)S(1)}, u32[]{:S(2)}, u32[]{:S(2)}) collective-permute-start(bf16[1,128,1024]{2,1,0:T(8,128)(2,1)} %bitcast.17), channel_id=1, source_target_pairs={{0,4},{1,5},{2,6},{3,7},{4,0},{5,1},{6,2},{7,3},{8,12},{9,13},{10,... | collective-permute-start | bytes 786440 | tf_op jit(solution)/shard_map/ppermute | solution.py:22
  8.7 13.8 %collective-permute-start.1 = (f32[32,512]{1,0:T(8,128)S(1)}, f32[32,512]{1,0:T(8,128)S(1)}, u32[]{:S(2)}, u32[]{:S(2)}) collective-permute-start(f32[32,512]{1,0:T(8,128)S(1)} %slice_bitcast_fusion.1.own_ref), channel_id=1, source_target_pairs={{0,8},{1,9},{2,10},{3,11},{4,12},{5,13},{6,14},{7,15},{8,0},{9,1},... | collective-permute-start | bytes 196616 | tf_op jit(solution)/shard_map/ppermute | solution.py:22
  9.0 0.9 copy-start.1
  9.9 0.9 copy-start.3
  10.9 0.7 copy-start.4
  19.9 13.6 %collective-permute-start = (f32[128,512]{1,0:T(8,128)}, f32[128,512]{1,0:T(8,128)S(1)}, u32[]{:S(2)}, u32[]{:S(2)}) collective-permute-start(f32[128,512]{1,0:T(8,128)} %slice_bitcast_fusion), channel_id=1, source_target_pairs={{0,8},{1,9},{2,10},{3,11},{4,12},{5,13},{6,14},{7,15},{8,0},{9,1},... | collective-permute-start | bytes 786440 | tf_op jit(solution)/shard_map/ppermute | solution.py:22
  27.9 16.4 %collective-permute-start.6 = (bf16[2,128,1024]{2,1,0:T(8,128)(2,1)S(1)}, bf16[2,128,1024]{2,1,0:T(8,128)(2,1)S(1)}, u32[]{:S(2)}, u32[]{:S(2)}) collective-permute-start(bf16[2,128,1024]{2,1,0:T(8,128)(2,1)S(1)} %pad_maximum_fusion), channel_id=1, source_target_pairs={{0,2},{1,3},{2,0},{3,1},{4,6},{5,7},{6,4},{7,5},{8,10},{9,11},{10,... | collective-permute-start | bytes 1572872 | tf_op jit(solution)/shard_map/ppermute | solution.py:22
  28.4 15.8 %collective-permute-start.4 = (bf16[1,128,1024]{2,1,0:T(8,128)(2,1)S(1)}, bf16[1,128,1024]{2,1,0:T(8,128)(2,1)S(1)}, u32[]{:S(2)}, u32[]{:S(2)}) collective-permute-start(bf16[1,128,1024]{2,1,0:T(8,128)(2,1)S(1)} %collective-permute-done.3), channel_id=1, source_target_pairs={{0,4},{1,5},{2,6},{3,7},{4,0},{5,1},{6,2},{7,3},{8,12},{9,13},{10,... | collective-permute-start | bytes 786440 | tf_op jit(solution)/shard_map/ppermute | solution.py:22
  33.9 11.0 %copy-start.6 = (bf16[128,1024]{1,0:T(8,128)(2,1)S(1)}, bf16[128,1024]{1,0:T(8,128)(2,1)}, u32[]{:S(2)}) copy-start(bf16[128,1024]{1,0:T(8,128)(2,1)} %param.10) | copy-start | bytes 786436
  44.3 4.3 %copy-start = (f32[8,128,512]{2,1,0:T(8,128)S(1)}, f32[8,128,512]{2,1,0:T(8,128)}, u32[]{:S(2)}) copy-start(f32[8,128,512]{2,1,0:T(8,128)} %get-tuple-element.56.keep_ref) | copy-start | bytes 6291460
  44.3 4.2 %collective-permute-start.10 = (f32[8,128,512]{2,1,0:T(8,128)S(1)}, f32[8,128,512]{2,1,0:T(8,128)S(1)}, u32[]{:S(2)}, u32[]{:S(2)}) collective-permute-start(f32[8,128,512]{2,1,0:T(8,128)S(1)} %get-tuple-element.58), channel_id=1, source_target_pairs={{0,1},{1,0},{2,3},{3,2},{4,5},{5,4},{6,7},{7,6},{8,9},{9,8},{10,11... | collective-permute-start | bytes 6291464 | tf_op jit(solution)/shard_map/ppermute | solution.py:22
  44.4 7.1 %collective-permute-start.7 = (f32[8,128,512]{2,1,0:T(8,128)S(1)}, f32[8,128,512]{2,1,0:T(8,128)S(1)}, u32[]{:S(2)}, u32[]{:S(2)}) collective-permute-start(f32[8,128,512]{2,1,0:T(8,128)S(1)} %get-tuple-element.53), channel_id=1, source_target_pairs={{0,1},{1,0},{2,3},{3,2},{4,5},{5,4},{6,7},{7,6},{8,9},{9,8},{10,11... | collective-permute-start | bytes 6291464 | tf_op jit(solution)/shard_map/ppermute | solution.py:22
  44.9 8.4 %collective-permute-start.9 = (bf16[1,128,1024]{2,1,0:T(8,128)(2,1)S(1)}, bf16[1,128,1024]{2,1,0:T(8,128)(2,1)S(1)}, u32[]{:S(2)}, u32[]{:S(2)}) collective-permute-start(bf16[1,128,1024]{2,1,0:T(8,128)(2,1)S(1)} %collective-permute-done.4), channel_id=1, source_target_pairs={{0,2},{1,3},{2,0},{3,1},{4,6},{5,7},{6,4},{7,5},{8,10},{9,11},{10,... | collective-permute-start | bytes 786440 | tf_op jit(solution)/shard_map/ppermute | solution.py:22
  53.3 4.2 %collective-permute-start.11 = (bf16[8,128,1024]{2,1,0:T(8,128)(2,1)S(1)}, bf16[8,128,1024]{2,1,0:T(8,128)(2,1)S(1)}, u32[]{:S(2)}, u32[]{:S(2)}) collective-permute-start(bf16[8,128,1024]{2,1,0:T(8,128)(2,1)S(1)} %constant_dynamic-update-slice_fusion.low_ref), channel_id=1, source_target_pairs={{0,1},{1,0},{2,3},{3,2},{4,5},{5,4},{6,7},{7,6},{8,9},{9,8},{10,11... | collective-permute-start | bytes 6291464 | tf_op jit(solution)/shard_map/ppermute | solution.py:22
  53.4 14.7 %collective-permute-start.14 = (f16[528,512]{1,0:T(8,128)(2,1)S(1)}, f16[528,512]{1,0:T(8,128)(2,1)S(1)}, u32[]{:S(2)}, u32[]{:S(2)}) collective-permute-start(f16[528,512]{1,0:T(8,128)(2,1)S(1)} %convert_element_type.31), channel_id=1, source_target_pairs={{0,4},{1,5},{2,6},{3,7},{4,0},{5,1},{6,2},{7,3},{8,12},{9,13},{10,... | collective-permute-start | bytes 1622024 | tf_op jit(solution)/shard_map/ppermute | solution.py:22
  53.5 14.6 %collective-permute-start.8 = (f16[528,512]{1,0:T(8,128)(2,1)S(1)}, f16[528,512]{1,0:T(8,128)(2,1)S(1)}, u32[]{:S(2)}, u32[]{:S(2)}) collective-permute-start(f16[528,512]{1,0:T(8,128)(2,1)S(1)} %convert_element_type.30), channel_id=1, source_target_pairs={{0,2},{1,3},{2,0},{3,1},{4,6},{5,7},{6,4},{7,5},{8,10},{9,11},{10,... | collective-permute-start | bytes 1622024 | tf_op jit(solution)/shard_map/ppermute | solution.py:22
  69.1 14.3 %collective-permute-start.15 = (f32[2,128,512]{2,1,0:T(8,128)S(1)}, f32[2,128,512]{2,1,0:T(8,128)S(1)}, u32[]{:S(2)}, u32[]{:S(2)}) collective-permute-start(f32[2,128,512]{2,1,0:T(8,128)S(1)} %get-tuple-element.72), channel_id=1, source_target_pairs={{0,2},{1,3},{2,0},{3,1},{4,6},{5,7},{6,4},{7,5},{8,10},{9,11},{10,... | collective-permute-start | bytes 1572872 | tf_op jit(solution)/shard_map/ppermute | solution.py:22
  69.6 11.1 %collective-permute-start.12 = (f16[272,512]{1,0:T(8,128)(2,1)S(1)}, f16[272,512]{1,0:T(8,128)(2,1)S(1)}, u32[]{:S(2)}, u32[]{:S(2)}) collective-permute-start(f16[272,512]{1,0:T(8,128)(2,1)S(1)} %convert_element_type.33), channel_id=1, source_target_pairs={{0,4},{1,5},{2,6},{3,7},{4,0},{5,1},{6,2},{7,3},{8,12},{9,13},{10,... | collective-permute-start | bytes 835592 | tf_op jit(solution)/shard_map/ppermute | solution.py:22
  71.4 14.2 %copy-start.5 = (s32[4,32]{1,0:T(4,128)S(1)}, s32[4,32]{1,0:T(4,128)}, u32[]{:S(2)}) copy-start(s32[4,32]{1,0:T(4,128)} %orders_ref.1) | copy-start | bytes 1540
  71.4 14.3 %copy-start.2 = (bf16[128,512]{1,0:T(8,128)(2,1)S(1)}, bf16[128,512]{1,0:T(8,128)(2,1)}, u32[]{:S(2)}) copy-start(bf16[128,512]{1,0:T(8,128)(2,1)} %tok_ref.3) | copy-start | bytes 393220
  71.4 8.3 %collective-permute-start.13 = (f16[144,512]{1,0:T(8,128)(2,1)S(1)}, f16[144,512]{1,0:T(8,128)(2,1)S(1)}, u32[]{:S(2)}, u32[]{:S(2)}) collective-permute-start(f16[144,512]{1,0:T(8,128)(2,1)S(1)} %convert_element_type.34), channel_id=1, source_target_pairs={{0,8},{1,9},{2,10},{3,11},{4,12},{5,13},{6,14},{7,15},{8,0},{9,1},... | collective-permute-start | bytes 442376 | tf_op jit(solution)/shard_map/ppermute | solution.py:22
  80.9 19.6 %collective-permute-start.16 = (f32[1,128,512]{2,1,0:T(8,128)S(1)}, f32[1,128,512]{2,1,0:T(8,128)S(1)}, u32[]{:S(2)}, u32[]{:S(2)}) collective-permute-start(f32[1,128,512]{2,1,0:T(8,128)S(1)} %get-tuple-element.74), channel_id=1, source_target_pairs={{0,8},{1,9},{2,10},{3,11},{4,12},{5,13},{6,14},{7,15},{8,0},{9,1},... | collective-permute-start | bytes 786440 | tf_op jit(solution)/shard_map/ppermute | solution.py:22
  83.6 16.9 %collective-permute-start.17 = (f16[144,512]{1,0:T(8,128)(2,1)S(1)}, f16[144,512]{1,0:T(8,128)(2,1)S(1)}, u32[]{:S(2)}, u32[]{:S(2)}) collective-permute-start(f16[144,512]{1,0:T(8,128)(2,1)S(1)} %convert_element_type.38), channel_id=1, source_target_pairs={{0,8},{1,9},{2,10},{3,11},{4,12},{5,13},{6,14},{7,15},{8,0},{9,1},... | collective-permute-start | bytes 442376 | tf_op jit(solution)/shard_map/ppermute | solution.py:22
